TPU v7x, 32 devices: a whole 2x2x4 slice. The times are simulated.
32 devices in a mesh: dp: 8 (over z, y), mp: 4 (over x, core).
Axes of the slice: x: 2, y: 2, z: 4, core: 2. Of those that a mesh axis runs over, the one named last changes fastest.
Arguments:
- inputs: bfloat16 [1024, 4, 5632], P('mp', None, 'dp'), may hold values from -13 to 13
- pixel_mask: int32 [4, 5632], P(None, 'dp'), may hold values from 0 to 1, as said below
- widths: int32 [2], replicated, may hold values from 288 to 512, as said below
- output_grad: bfloat16 [2048, 5632], P('mp', 'dp'), may hold values from -6 to 6
- first_weight: float32 [1024, 512], P('dp', 'mp'), may hold values from -1.5 to 1.5
- shortcut_weight: float32 [1024, 2048], P('dp', 'mp'), may hold values from -1.5 to 1.5
- middle_weight: float32 [2, 9, 512, 512], P(None, None, 'dp', 'mp'), may hold values from -1.5 to 1.5
- last_weight: float32 [2, 512, 2048], P(None, 'mp', 'dp'), may hold values from -1.5 to 1.5
- second_weight: float32 [2048, 512], P('dp', 'mp'), may hold values from -1.5 to 1.5
- narrow_norms: float32 [4, 2, 512], P(None, None, 'mp'), may hold values from -2 to 5, as said below
- wide_norms: float32 [3, 2, 2048], P(None, None, 'mp'), may hold values from -2 to 5, as said below
- first_mean: float32 [1024, 512], P('dp', 'mp'), may hold values from -38 to 38
- first_square: float32 [1024, 512], P('dp', 'mp'), may hold values from 0 to 19
- shortcut_mean: float32 [1024, 2048], P('dp', 'mp'), may hold values from -38 to 38
- shortcut_square: float32 [1024, 2048], P('dp', 'mp'), may hold values from 0 to 19
- middle_mean: float32 [2, 9, 512, 512], P(None, None, 'dp', 'mp'), may hold values from -38 to 38
- middle_square: float32 [2, 9, 512, 512], P(None, None, 'dp', 'mp'), may hold values from 0 to 19
- last_mean: float32 [2, 512, 2048], P(None, 'mp', 'dp'), may hold values from -38 to 38
- last_square: float32 [2, 512, 2048], P(None, 'mp', 'dp'), may hold values from 0 to 19
- second_mean: float32 [2048, 512], P('dp', 'mp'), may hold values from -38 to 38
- second_square: float32 [2048, 512], P('dp', 'mp'), may hold values from 0 to 19
- narrow_mean: float32 [4, 2, 512], P(None, None, 'mp'), may hold values from -38 to 38
- narrow_square: float32 [4, 2, 512], P(None, None, 'mp'), may hold values from 0 to 19
- wide_mean: float32 [3, 2, 2048], P(None, None, 'mp'), may hold values from -38 to 38
- wide_square: float32 [3, 2, 2048], P(None, None, 'mp'), may hold values from 0 to 19
Outputs:
- block_output: bfloat16 [2048, 5632], P('mp', 'dp')
- input_grad: bfloat16 [1024, 4, 5632], P('mp', None, 'dp')
- first_mean_next: float32 [1024, 512], P('dp', 'mp')
- first_square_next: float32 [1024, 512], P('dp', 'mp')
- first_weight_next: float32 [1024, 512], P('dp', 'mp')
- shortcut_mean_next: float32 [1024, 2048], P('dp', 'mp')
- shortcut_square_next: float32 [1024, 2048], P('dp', 'mp')
- shortcut_weight_next: float32 [1024, 2048], P('dp', 'mp')
- middle_mean_next: float32 [2, 9, 512, 512], P(None, None, 'dp', 'mp')
- middle_square_next: float32 [2, 9, 512, 512], P(None, None, 'dp', 'mp')
- middle_weight_next: float32 [2, 9, 512, 512], P(None, None, 'dp', 'mp')
- last_mean_next: float32 [2, 512, 2048], P(None, 'mp', 'dp')
- last_square_next: float32 [2, 512, 2048], P(None, 'mp', 'dp')
- last_weight_next: float32 [2, 512, 2048], P(None, 'mp', 'dp')
- second_mean_next: float32 [2048, 512], P('dp', 'mp')
- second_square_next: float32 [2048, 512], P('dp', 'mp')
- second_weight_next: float32 [2048, 512], P('dp', 'mp')
- narrow_mean_next: float32 [4, 2, 512], P(None, None, 'mp')
- narrow_square_next: float32 [4, 2, 512], P(None, None, 'mp')
- narrow_norms_next: float32 [4, 2, 512], P(None, None, 'mp')
- wide_mean_next: float32 [3, 2, 2048], P(None, None, 'mp')
- wide_square_next: float32 [3, 2, 2048], P(None, None, 'mp')
- wide_norms_next: float32 [3, 2, 2048], P(None, None, 'mp')
- matrix_norms: float32 [7, 2], replicated
- first_weight_copy: bfloat16 [1024, 512], P('dp', 'mp')
- shortcut_weight_copy: bfloat16 [1024, 2048], P('dp', 'mp')
- middle_weight_copy: bfloat16 [2, 9, 512, 512], P(None, None, 'dp', 'mp')
- last_weight_copy: bfloat16 [2, 512, 2048], P(None, 'mp', 'dp')
- second_weight_copy: bfloat16 [2048, 512], P('dp', 'mp')
Inputs may be any that keep to these rules, and one draw needn't show every extreme that they name: `pixel_mask`: each image's ones form the top-left rectangle of its 32 x 2 * 11 pixels, seen through the four phases; every image of the last index of dp is all ones. `widths`: both are multiples of 32, at least 288; one of the two is 512. `narrow_norms`: index 0 of the second dimension holds gains, index 1 biases. `wide_norms`: index 0 of the second dimension holds gains, index 1 biases.
All inputs are finite; a program needn't handle non-finite values.
Results may differ from a plain program's by a relative error of at most 0.02.
Values may be sent and summed in bfloat16 or wider, within the bound.
No kernel may reach another device: no remote copies, remote signals or barrier semaphores. Data moves between devices by JAX's collectives and lax.ppermute only.
A program may use at most 192 MiB of HBM per device.

v0:
```python
import jax
import jax.numpy as jnp
from jax import lax
from jax.sharding import PartitionSpec as P

HO = 16
WO = 11
STEP = 10


EPS_NORM = 1e-05
BETA_ONE = 0.9
BETA_TWO = 0.999
EPS_ADAM = 1e-06
DECAY = 0.01
RATE = 0.3
RATE_NORM = 0.3
EPS_TRUST = 1e-06
PHASES = ((1, -1), (0, 0), (1, 0))
STRIDED_TAPS = tuple(
    (
        (
            3 * above + beside,
            2 * PHASES[above][0] + PHASES[beside][0],
            PHASES[above][1],
            PHASES[beside][1],
        )
        for above in range(3)
        for beside in range(3)
    )
)
PLAIN_TAPS = tuple(
    ((3 * above + beside, 0, above - 1, beside - 1) for above in range(3) for beside in range(3))
)


def slope(values):
    gate = jax.nn.sigmoid(values)
    return gate * (1.0 + values * (1.0 - gate))


def shifted(values, drow, dcol):
    length = values.shape[1]
    offset = drow * WO + dcol
    place = lax.iota(jnp.int32, length)
    row_at = place // WO % HO + drow
    col_at = place % WO + dcol
    inside = (row_at >= 0) & (row_at < HO) & (col_at >= 0) & (col_at < WO)
    moved = jnp.roll(values, -offset, axis=1)
    return jnp.where(inside[None, :], moved, jnp.zeros_like(moved))


def over_images(first, second):
    return lax.psum((first, second), "dp")


def moments(values, mask):
    weighted = values * mask[None, :]
    return over_images(jnp.sum(weighted, 1), jnp.sum(weighted * values, 1))


def normalize(values, totals, squares, count, gain, bias):
    mean = totals / count
    scale = lax.rsqrt(squares / count - mean * mean + EPS_NORM)
    centred = (values - mean[:, None]) * scale[:, None]
    return (centred, scale, centred * gain[:, None] + bias[:, None])


def back_sums(grad_in, centred):
    return over_images(jnp.sum(grad_in * centred, 1), jnp.sum(grad_in, 1))


def norm_back(grad_in, centred, scale, gain, mask, gain_sum, bias_sum, count):
    return (gain * scale)[:, None] * (
        grad_in - mask[None, :] * (bias_sum[:, None] + centred * gain_sum[:, None]) / count
    )


def input_mix(values, weight, side_weight, pixels):
    start_sum = (jnp.zeros((weight.shape[1], values.shape[1]), jnp.float32),)
    if side_weight is not None:
        start_sum = start_sum + (jnp.zeros((side_weight.shape[1], pixels), jnp.float32),)
    piece = lax.all_gather(values, "mp", axis=0, tiled=True)
    result = (jnp.einsum("kc,kp->cp", weight, piece, preferred_element_type=jnp.float32),)
    if side_weight is not None:
        result = result + (
            jnp.einsum(
                "kc,kp->cp", side_weight, piece[:, :pixels], preferred_element_type=jnp.float32
            ),
        )
    return result


def mid_gathered(hidden):
    return lax.all_gather(hidden, "mp", axis=0, tiled=True)


def conv_forward(gathered, kernel, taps, pixels):
    result = jnp.zeros((kernel.shape[2], pixels), jnp.float32)
    for tap, phase, drow, dcol in taps:
        source = gathered[:, phase * pixels : (phase + 1) * pixels]
        part = jnp.einsum("kc,kp->cp", kernel[tap], source, preferred_element_type=jnp.float32)
        result = result + shifted(part, drow, dcol)
    return result


def conv_backward(grad_b, gathered, kernel, taps, pixels, phases):
    moved = [shifted(grad_b, -drow, -dcol) for tap, phase, drow, dcol in taps]
    count = gathered.shape[0] // lax.axis_size("mp") * lax.axis_size("mp")
    blocks = []
    for target in range(phases):
        result = jnp.zeros((count, pixels), jnp.float32)
        for conv_index, (conv_tap, conv_phase, conv_drow, conv_dcol) in enumerate(taps):
            if conv_phase == target:
                part = kernel[conv_tap]
                result = result + jnp.dot(
                    part, moved[conv_index], preferred_element_type=jnp.float32
                )
        blocks.append(result)
    hidden_grad = lax.psum_scatter(
        jnp.concatenate(blocks, 1), "mp", scatter_dimension=0, tiled=True
    )
    kernel_grad = jnp.stack(
        [
            jnp.einsum(
                "kp,cp->kc",
                gathered[:, phase * pixels : (phase + 1) * pixels],
                moved[index],
                preferred_element_type=jnp.float32,
            )
            for index, (tap, phase, drow, dcol) in enumerate(taps)
        ]
    )
    return (hidden_grad, kernel_grad)


def output_mix(hidden, kernel):
    return lax.psum_scatter(
        jnp.einsum("kc,kp->cp", kernel, hidden, preferred_element_type=jnp.float32),
        "mp",
        scatter_dimension=0,
        tiled=True,
    )


def output_back(grad_b, kernel, hidden):
    piece = lax.all_gather(grad_b, "mp", axis=0, tiled=True)
    hidden_grad = jnp.dot(kernel, piece, preferred_element_type=jnp.float32)
    columns = jnp.einsum("cp,kp->ck", hidden, piece, preferred_element_type=jnp.float32)
    return (hidden_grad, columns)


def input_back(values, grad_b, side_b, weight, side_weight, pixels):
    width = weight.shape[1]
    result = jnp.dot(weight, grad_b, preferred_element_type=jnp.float32)
    if side_weight is not None:
        result = jnp.concatenate(
            [
                result[:, :pixels]
                + jnp.dot(side_weight, side_b, preferred_element_type=jnp.float32),
                result[:, pixels:],
            ],
            1,
        )
    values_grad = lax.psum_scatter(result, "mp", scatter_dimension=0, tiled=True)
    piece = lax.all_gather(values, "mp", axis=0, tiled=True)
    blocks = [jnp.einsum("kp,cp->kc", piece, grad_b, preferred_element_type=jnp.float32)]
    if side_weight is not None:
        blocks.append(
            jnp.einsum("kp,cp->kc", piece[:, :pixels], side_b, preferred_element_type=jnp.float32)
        )
    joined = jnp.concatenate(blocks, 1)
    return (values_grad, joined[:, :width], joined[:, width:])


def adapt(grad_in, mean, square, first_fix, second_fix):
    mean_next = BETA_ONE * mean + (1.0 - BETA_ONE) * grad_in
    square_next = BETA_TWO * square + (1.0 - BETA_TWO) * grad_in * grad_in
    step = mean_next / first_fix / (jnp.sqrt(square_next / second_fix) + EPS_ADAM)
    return (mean_next, square_next, step)


def shards(
    inputs,
    pixel_mask,
    widths,
    output_grad,
    first_weight,
    shortcut_weight,
    middle_weight,
    last_weight,
    second_weight,
    narrow_norms,
    wide_norms,
    first_mean,
    first_square,
    shortcut_mean,
    shortcut_square,
    middle_mean,
    middle_square,
    last_mean,
    last_square,
    second_mean,
    second_square,
    narrow_mean,
    narrow_square,
    wide_mean,
    wide_square,
):
    pixels = pixel_mask.shape[1]
    width = first_weight.shape[1]
    rank = lax.axis_index("mp")
    channel = rank * width + lax.iota(jnp.int32, width)
    keep_one = (channel < widths[0]).astype(jnp.float32)[:, None]
    keep_two = (channel < widths[1]).astype(jnp.float32)[:, None]
    masks = pixel_mask.astype(jnp.float32)
    mask_in = masks.reshape(-1)
    mask_out = masks[0]
    field = (inputs * pixel_mask.astype(jnp.bfloat16)[None]).reshape(inputs.shape[0], -1)
    first_w, short_w, middle_w, last_w, second_w = (
        lax.all_gather(first_weight.astype(jnp.bfloat16), "dp", axis=0, tiled=True),
        lax.all_gather(shortcut_weight.astype(jnp.bfloat16), "dp", axis=0, tiled=True),
        lax.all_gather(middle_weight.astype(jnp.bfloat16), "dp", axis=2, tiled=True),
        lax.all_gather(last_weight.astype(jnp.bfloat16), "dp", axis=2, tiled=True),
        lax.all_gather(second_weight.astype(jnp.bfloat16), "dp", axis=0, tiled=True),
    )
    count_in, count_out = over_images(jnp.sum(mask_in), jnp.sum(mask_out))
    pre_one, pre_side = input_mix(field, first_w, short_w, pixels)
    totals, squares = moments(pre_one, mask_in)
    cen_one, scale_one, act_one = normalize(
        pre_one, totals, squares, count_in, narrow_norms[0, 0], narrow_norms[0, 1]
    )
    hid_one = (jax.nn.silu(act_one) * mask_in[None, :] * keep_one).astype(jnp.bfloat16)
    gat_one = mid_gathered(hid_one)
    pre_two = conv_forward(gat_one, middle_w[0], STRIDED_TAPS, pixels)
    totals, squares = moments(pre_two, mask_out)
    cen_two, scale_two, act_two = normalize(
        pre_two, totals, squares, count_out, narrow_norms[1, 0], narrow_norms[1, 1]
    )
    hid_two = (jax.nn.silu(act_two) * mask_out[None, :] * keep_one).astype(jnp.bfloat16)
    pre_three = output_mix(hid_two, last_w[0])
    weighted_three = pre_three * mask_out[None, :]
    weighted_side = pre_side * mask_out[None, :]
    totals, squares = over_images(
        jnp.stack([jnp.sum(weighted_three, 1), jnp.sum(weighted_side, 1)]),
        jnp.stack([jnp.sum(weighted_three * pre_three, 1), jnp.sum(weighted_side * pre_side, 1)]),
    )
    cen_three, scale_three, act_three = normalize(
        pre_three, totals[0], squares[0], count_out, wide_norms[0, 0], wide_norms[0, 1]
    )
    cen_side, scale_side, act_side = normalize(
        pre_side, totals[1], squares[1], count_out, wide_norms[1, 0], wide_norms[1, 1]
    )
    total_one = act_three + act_side
    out_one = (jax.nn.silu(total_one) * mask_out[None, :]).astype(jnp.bfloat16)
    (pre_four,) = input_mix(out_one, second_w, None, pixels)
    totals, squares = moments(pre_four, mask_out)
    cen_four, scale_four, act_four = normalize(
        pre_four, totals, squares, count_out, narrow_norms[2, 0], narrow_norms[2, 1]
    )
    hid_four = (jax.nn.silu(act_four) * mask_out[None, :] * keep_two).astype(jnp.bfloat16)
    gat_four = mid_gathered(hid_four)
    pre_five = conv_forward(gat_four, middle_w[1], PLAIN_TAPS, pixels)
    totals, squares = moments(pre_five, mask_out)
    cen_five, scale_five, act_five = normalize(
        pre_five, totals, squares, count_out, narrow_norms[3, 0], narrow_norms[3, 1]
    )
    hid_five = (jax.nn.silu(act_five) * mask_out[None, :] * keep_two).astype(jnp.bfloat16)
    pre_six = output_mix(hid_five, last_w[1])
    totals, squares = moments(pre_six, mask_out)
    cen_six, scale_six, act_six = normalize(
        pre_six, totals, squares, count_out, wide_norms[2, 0], wide_norms[2, 1]
    )
    total_two = act_six + out_one.astype(jnp.float32)
    block_output = (jax.nn.silu(total_two) * mask_out[None, :]).astype(jnp.bfloat16)
    grad_two = output_grad.astype(jnp.float32) * mask_out[None, :] * slope(total_two)
    gain_six, bias_six = back_sums(grad_two, cen_six)
    grad_six = norm_back(
        grad_two, cen_six, scale_six, wide_norms[2, 0], mask_out, gain_six, bias_six, count_out
    ).astype(jnp.bfloat16)
    hid_five_grad, last_one_grad = output_back(grad_six, last_w[1], hid_five)
    act_five_grad = hid_five_grad * keep_two * mask_out[None, :] * slope(act_five)
    gain_five, bias_five = back_sums(act_five_grad, cen_five)
    grad_five = norm_back(
        act_five_grad,
        cen_five,
        scale_five,
        narrow_norms[3, 0],
        mask_out,
        gain_five,
        bias_five,
        count_out,
    ).astype(jnp.bfloat16)
    hid_four_grad, middle_one_grad = conv_backward(
        grad_five, gat_four, middle_w[1], PLAIN_TAPS, pixels, 1
    )
    act_four_grad = hid_four_grad * keep_two * mask_out[None, :] * slope(act_four)
    gain_four, bias_four = back_sums(act_four_grad, cen_four)
    grad_four = norm_back(
        act_four_grad,
        cen_four,
        scale_four,
        narrow_norms[2, 0],
        mask_out,
        gain_four,
        bias_four,
        count_out,
    ).astype(jnp.bfloat16)
    out_one_grad, second_grad, unused_side = input_back(
        out_one, grad_four, None, second_w, None, pixels
    )
    grad_one = (grad_two + out_one_grad) * mask_out[None, :] * slope(total_one)
    gains_pair, bias_pair = over_images(
        jnp.stack([jnp.sum(grad_one * cen_three, 1), jnp.sum(grad_one * cen_side, 1)]),
        jnp.sum(grad_one, 1),
    )
    grad_three = norm_back(
        grad_one,
        cen_three,
        scale_three,
        wide_norms[0, 0],
        mask_out,
        gains_pair[0],
        bias_pair,
        count_out,
    ).astype(jnp.bfloat16)
    grad_side = norm_back(
        grad_one,
        cen_side,
        scale_side,
        wide_norms[1, 0],
        mask_out,
        gains_pair[1],
        bias_pair,
        count_out,
    ).astype(jnp.bfloat16)
    hid_two_grad, last_zero_grad = output_back(grad_three, last_w[0], hid_two)
    act_two_grad = hid_two_grad * keep_one * mask_out[None, :] * slope(act_two)
    gain_two, bias_two = back_sums(act_two_grad, cen_two)
    grad_mid = norm_back(
        act_two_grad,
        cen_two,
        scale_two,
        narrow_norms[1, 0],
        mask_out,
        gain_two,
        bias_two,
        count_out,
    ).astype(jnp.bfloat16)
    hid_one_grad, middle_zero_grad = conv_backward(
        grad_mid, gat_one, middle_w[0], STRIDED_TAPS, pixels, 4
    )
    act_one_grad = hid_one_grad * keep_one * mask_in[None, :] * slope(act_one)
    gain_one, bias_one = back_sums(act_one_grad, cen_one)
    grad_first = norm_back(
        act_one_grad, cen_one, scale_one, narrow_norms[0, 0], mask_in, gain_one, bias_one, count_in
    ).astype(jnp.bfloat16)
    field_grad, first_grad, short_grad = input_back(
        field, grad_first, grad_side, first_w, short_w, pixels
    )
    input_grad = (field_grad * mask_in[None, :]).astype(jnp.bfloat16).reshape(inputs.shape)
    grads = (
        lax.psum_scatter(first_grad, "dp", scatter_dimension=0, tiled=True),
        lax.psum_scatter(short_grad, "dp", scatter_dimension=0, tiled=True),
        lax.psum_scatter(
            jnp.stack([middle_zero_grad, middle_one_grad]), "dp", scatter_dimension=2, tiled=True
        ),
        lax.psum_scatter(
            jnp.stack([last_zero_grad, last_one_grad]), "dp", scatter_dimension=2, tiled=True
        ),
        lax.psum_scatter(second_grad, "dp", scatter_dimension=0, tiled=True),
    )
    first_fix = 1.0 - BETA_ONE**STEP
    second_fix = 1.0 - BETA_TWO**STEP
    weights = (first_weight, shortcut_weight, middle_weight, last_weight, second_weight)
    means = (first_mean, shortcut_mean, middle_mean, last_mean, second_mean)
    squares_old = (first_square, shortcut_square, middle_square, last_square, second_square)
    states = []
    updates = []
    for index in range(5):
        mean_next, square_next, step = adapt(
            grads[index], means[index], squares_old[index], first_fix, second_fix
        )
        states.append((mean_next, square_next))
        updates.append(step + DECAY * weights[index])
    pairs = [
        (weights[0], updates[0]),
        (weights[1], updates[1]),
        (weights[2][0], updates[2][0]),
        (weights[2][1], updates[2][1]),
        (weights[3][0], updates[3][0]),
        (weights[3][1], updates[3][1]),
        (weights[4], updates[4]),
    ]
    partial_value = jnp.stack(
        [
            jnp.stack([jnp.sum(weight * weight), jnp.sum(update * update)])
            for weight, update in pairs
        ]
    )
    matrix_norms = jnp.sqrt(lax.psum(partial_value, ("dp", "mp")))
    ratio = matrix_norms[:, 0] / (matrix_norms[:, 1] + EPS_TRUST)
    first_next = first_weight - RATE * ratio[0] * updates[0]
    short_next = shortcut_weight - RATE * ratio[1] * updates[1]
    middle_next = middle_weight - RATE * ratio[2:4].reshape(2, 1, 1, 1) * updates[2]
    last_next = last_weight - RATE * ratio[4:6].reshape(2, 1, 1) * updates[3]
    second_next = second_weight - RATE * ratio[6] * updates[4]
    narrow_grad = jnp.stack(
        [
            jnp.stack([gain_one, bias_one]),
            jnp.stack([gain_two, bias_two]),
            jnp.stack([gain_four, bias_four]),
            jnp.stack([gain_five, bias_five]),
        ]
    )
    wide_grad = jnp.stack(
        [
            jnp.stack([gains_pair[0], bias_pair]),
            jnp.stack([gains_pair[1], bias_pair]),
            jnp.stack([gain_six, bias_six]),
        ]
    )
    narrow_mean_next, narrow_square_next, narrow_step = adapt(
        narrow_grad, narrow_mean, narrow_square, first_fix, second_fix
    )
    wide_mean_next, wide_square_next, wide_step = adapt(
        wide_grad, wide_mean, wide_square, first_fix, second_fix
    )
    return (
        block_output,
        input_grad,
        states[0][0],
        states[0][1],
        first_next,
        states[1][0],
        states[1][1],
        short_next,
        states[2][0],
        states[2][1],
        middle_next,
        states[3][0],
        states[3][1],
        last_next,
        states[4][0],
        states[4][1],
        second_next,
        narrow_mean_next,
        narrow_square_next,
        narrow_norms - RATE_NORM * narrow_step,
        wide_mean_next,
        wide_square_next,
        wide_norms - RATE_NORM * wide_step,
        matrix_norms,
        first_next.astype(jnp.bfloat16),
        short_next.astype(jnp.bfloat16),
        middle_next.astype(jnp.bfloat16),
        last_next.astype(jnp.bfloat16),
        second_next.astype(jnp.bfloat16),
    )


def solution(mesh):
    in_specs = (
        P("mp", None, "dp"),
        P(None, "dp"),
        P(),
        P("mp", "dp"),
        P("dp", "mp"),
        P("dp", "mp"),
        P(None, None, "dp", "mp"),
        P(None, "mp", "dp"),
        P("dp", "mp"),
        P(None, None, "mp"),
        P(None, None, "mp"),
        P("dp", "mp"),
        P("dp", "mp"),
        P("dp", "mp"),
        P("dp", "mp"),
        P(None, None, "dp", "mp"),
        P(None, None, "dp", "mp"),
        P(None, "mp", "dp"),
        P(None, "mp", "dp"),
        P("dp", "mp"),
        P("dp", "mp"),
        P(None, None, "mp"),
        P(None, None, "mp"),
        P(None, None, "mp"),
        P(None, None, "mp"),
    )
    out_specs = (
        P("mp", "dp"),
        P("mp", None, "dp"),
        P("dp", "mp"),
        P("dp", "mp"),
        P("dp", "mp"),
        P("dp", "mp"),
        P("dp", "mp"),
        P("dp", "mp"),
        P(None, None, "dp", "mp"),
        P(None, None, "dp", "mp"),
        P(None, None, "dp", "mp"),
        P(None, "mp", "dp"),
        P(None, "mp", "dp"),
        P(None, "mp", "dp"),
        P("dp", "mp"),
        P("dp", "mp"),
        P("dp", "mp"),
        P(None, None, "mp"),
        P(None, None, "mp"),
        P(None, None, "mp"),
        P(None, None, "mp"),
        P(None, None, "mp"),
        P(None, None, "mp"),
        P(),
        P("dp", "mp"),
        P("dp", "mp"),
        P(None, None, "dp", "mp"),
        P(None, "mp", "dp"),
        P("dp", "mp"),
    )
    return jax.shard_map(shards, mesh=mesh, in_specs=in_specs, out_specs=out_specs, check_vma=False)
```

profile of v0, /device:TPU:0, one launch (start us, length us, event | category | flops | bytes accessed | tf_op | source)
XLA Modules:
  0.0 1309.8 jit_solution(6673871898393225484)
XLA Ops:
  8.0 2.9 broadcast_multiply_fusion
  14.8 32.5 %all_gather.36 = bf16[1024,128]{1,0:T(8,128)(2,1)S(1)} all-gather(bf16[128,128]{1,0:T(8,128)(2,1)S(1)} %convert_element_type.99), channel_id=1, replica_groups=mesh['dp'=8,'mp'=4] {'dp'}, dimensions={0}, use_global_device_ids=true | all-gather | bytes 294912 | tf_op jit(solution)/shard_map/all_gather | solution.py:221
  48.0 10.0 all-gather.9.cloned.1.call-done
  58.0 4.3 fusion.4
  62.3 22.1 %all-reduce.11 = (f32[128]{0:T(128)S(1)}, f32[]{:T(128)}, f32[128]{0:T(128)S(1)}) all-reduce(f32[128]{0:T(128)S(1)} %get-tuple-element.88, f32[]{:T(128)} %convert_reduce_fusion, f32[128]{0:T(128)S(1)} %get-tuple-element.87), channel_id=1, replica_groups=mesh['dp'=8,'mp'=4] {'dp'}, use_global_device_ids=true, to_apply=%region_1.0 | all-reduce | flops 257 | bytes 2056 | tf_op jit(solution)/shard_map/psum | solution.py:54
  89.4 23.4 %all-gather.13.cloned.1.call-done = bf16[2,9,512,128]{3,2,1,0:T(8,128)(2,1)} async-done(((bf16[2,9,64,128]{3,2,1,0:T(8,128)(2,1)}), bf16[2,9,512,128]{3,2,1,0:T(8,128)(2,1)}) %all-gather.13.cloned.1.call-update) | async-done | bytes 2359312 | tf_op jit(solution)/shard_map/all_gather | solution.py:223
  112.9 28.1 %all-gather.11.cloned.1.call-done = bf16[512,2816]{0,1:T(8,128)(2,1)} async-done(((bf16[128,2816]{0,1:T(8,128)(2,1)}), bf16[512,2816]{0,1:T(8,128)(2,1)}) %all-gather.11.cloned.1.call-update) | async-done | bytes 2883600 | tf_op jit(solution)/shard_map/all_gather | solution.py:95
  153.8 22.2 %all-reduce.10 = (f32[128]{0:T(128)S(1)}, f32[]{:T(128)}, f32[128]{0:T(128)S(1)}) all-reduce(f32[128]{0:T(128)S(1)} %get-tuple-element.111, f32[]{:T(128)} %get-tuple-element.128, f32[128]{0:T(128)S(1)} %get-tuple-element.110), channel_id=1, replica_groups=mesh['dp'=8,'mp'=4] {'dp'}, use_global_device_ids=true, to_apply=%region_7.0 | all-reduce | flops 257 | bytes 2056 | tf_op jit(solution)/shard_map/psum | solution.py:54
  177.2 5.9 all-gather.15.cloned.1.call-done
  183.2 4.4 convolution_bitcast_fusion.4
  188.9 35.8 %all-gather.17.cloned.1.call-done = bf16[1024,512]{1,0:T(8,128)(2,1)} async-done(((bf16[128,512]{1,0:T(8,128)(2,1)}), bf16[1024,512]{1,0:T(8,128)(2,1)}) %all-gather.17.cloned.1.call-update) | async-done | bytes 1048592 | tf_op jit(solution)/shard_map/all_gather | solution.py:222
  224.7 56.0 %reduce-scatter.12.cloned.1.call-done = f32[512,704]{0,1:T(8,128)} async-done(((f32[2048,704]{0,1:T(8,128)}), f32[512,704]{0,1:T(8,128)}) %reduce-scatter.12.cloned.1.call-update) | async-done | bytes 1441808 | tf_op jit(solution)/shard_map/reduce_scatter | solution.py:138
  280.8 4.3 multiply_reduce_fusion.2
  285.1 21.6 %all-reduce.9 = (f32[2,512]{1,0:T(2,128)S(1)}, f32[2,512]{1,0:T(2,128)S(1)}) all-reduce(f32[2,512]{1,0:T(2,128)S(1)} %pad_maximum_fusion.8, f32[2,512]{1,0:T(2,128)S(1)} %pad_maximum_fusion.7), channel_id=1, replica_groups=mesh['dp'=8,'mp'=4] {'dp'}, use_global_device_ids=true, to_apply=%region_18.19 | all-reduce | flops 2048 | bytes 16384 | tf_op jit(solution)/shard_map/psum | solution.py:54
  309.3 3.0 multiply_convert_fusion.6
  313.2 33.3 %all_gather.42 = bf16[2048,128]{1,0:T(8,128)(2,1)} all-gather(bf16[256,128]{1,0:T(8,128)(2,1)S(1)} %convert_element_type.108), channel_id=1, replica_groups=mesh['dp'=8,'mp'=4] {'dp'}, dimensions={0}, use_global_device_ids=true | all-gather | bytes 589824 | tf_op jit(solution)/shard_map/all_gather | solution.py:225
  346.5 2.8 fusion.62
  349.4 17.4 %all-reduce.8 = (f32[128]{0:T(128)S(1)}, f32[128]{0:T(128)S(1)}) all-reduce(f32[128]{0:T(128)S(1)} %get-tuple-element.109, f32[128]{0:T(128)S(1)} %get-tuple-element.108), channel_id=1, replica_groups=mesh['dp'=8,'mp'=4] {'dp'}, use_global_device_ids=true, to_apply=%region_20.21 | all-reduce | flops 256 | bytes 2048 | tf_op jit(solution)/shard_map/psum | solution.py:54
  368.1 7.8 all_gather.43
  387.1 3.3 fusion.63
  390.4 18.9 %all-reduce.7 = (f32[128]{0:T(128)S(1)}, f32[128]{0:T(128)S(1)}) all-reduce(f32[128]{0:T(128)S(1)} %get-tuple-element.107, f32[128]{0:T(128)S(1)} %get-tuple-element.106), channel_id=1, replica_groups=mesh['dp'=8,'mp'=4] {'dp'}, use_global_device_ids=true, to_apply=%region_24.25 | all-reduce | flops 256 | bytes 2048 | tf_op jit(solution)/shard_map/psum | solution.py:54
  410.4 4.5 convolution_bitcast_fusion.3
  415.1 52.2 %reduce-scatter.14.cloned.1.call-done = f32[512,704]{0,1:T(8,128)} async-done(((f32[2048,704]{0,1:T(8,128)}), f32[512,704]{0,1:T(8,128)}) %reduce-scatter.14.cloned.1.call-update) | async-done | bytes 1441808 | tf_op jit(solution)/shard_map/reduce_scatter | solution.py:138
  468.9 21.4 %all-reduce.6 = (f32[512]{0:T(512)S(1)}, f32[512]{0:T(512)S(1)}) all-reduce(f32[512]{0:T(512)S(1)} %get-tuple-element.90, f32[512]{0:T(512)S(1)} %get-tuple-element.89), channel_id=1, replica_groups=mesh['dp'=8,'mp'=4] {'dp'}, use_global_device_ids=true, to_apply=%region_31.32 | all-reduce | flops 1024 | bytes 8192 | tf_op jit(solution)/shard_map/psum | solution.py:54
  490.9 4.2 fusion.156
  495.1 17.1 %all-reduce.5 = (f32[512]{0:T(512)S(1)}, f32[512]{0:T(512)S(1)}) all-reduce(f32[512]{0:T(512)S(1)} %get-tuple-element.101, f32[512]{0:T(512)S(1)} %get-tuple-element.100), channel_id=1, replica_groups=mesh['dp'=8,'mp'=4] {'dp'}, use_global_device_ids=true, to_apply=%region_35.36 | all-reduce | flops 1024 | bytes 8192 | tf_op jit(solution)/shard_map/psum | solution.py:54
  512.2 3.7 multiply_convert_fusion.4
  516.0 24.9 %all-gather.21.cloned.1.call-done = bf16[2048,704]{0,1:T(8,128)(2,1)} async-done(((bf16[512,704]{0,1:T(8,128)(2,1)}), bf16[2048,704]{0,1:T(8,128)(2,1)}) %all-gather.21.cloned.1.call-update) | async-done | bytes 2883600 | tf_op jit(solution)/shard_map/all_gather | solution.py:147
  540.9 3.7 fusion.159
  544.6 21.9 %all-reduce.4 = (f32[128]{0:T(128)}, f32[128]{0:T(128)}) all-reduce(f32[128]{0:T(128)S(1)} %get-tuple-element.117, f32[128]{0:T(128)S(1)} %get-tuple-element.116), channel_id=1, replica_groups=mesh['dp'=8,'mp'=4] {'dp'}, use_global_device_ids=true, to_apply=%region_39.40 | all-reduce | flops 256 | bytes 2048 | tf_op jit(solution)/shard_map/psum | solution.py:54
  577.3 23.8 %reduce-scatter.16.cloned.1.call-done = f32[128,704]{0,1:T(8,128)} async-done(((f32[512,704]{0,1:T(8,128)}), f32[128,704]{0,1:T(8,128)}) %reduce-scatter.16.cloned.1.call-update) | async-done | bytes 360464 | tf_op jit(solution)/shard_map/reduce_scatter | solution.py:120
  601.1 2.6 fusion.158
  603.7 22.2 %all-reduce.3 = (f32[128]{0:T(128)}, f32[128]{0:T(128)}) all-reduce(f32[128]{0:T(128)} %get-tuple-element.115, f32[128]{0:T(128)} %get-tuple-element.114), channel_id=1, replica_groups=mesh['dp'=8,'mp'=4] {'dp'}, use_global_device_ids=true, to_apply=%region_44.45 | all-reduce | flops 256 | bytes 2048 | tf_op jit(solution)/shard_map/psum | solution.py:54
  628.5 4.4 convolution_bitcast_fusion.2
  633.0 51.3 %reduce-scatter.18.cloned.1.call-done = f32[512,704]{0,1:T(8,128)} async-done(((f32[2048,704]{0,1:T(8,128)}), f32[512,704]{0,1:T(8,128)}) %reduce-scatter.18.cloned.1.call-update) | async-done | bytes 1441808 | tf_op jit(solution)/shard_map/reduce_scatter | solution.py:165
  684.2 5.2 fusion.155
  690.1 22.3 %all-reduce.2 = (f32[2,512]{1,0:T(2,128)}, f32[512]{0:T(512)}) all-reduce(f32[2,512]{1,0:T(2,128)} %pad_maximum_fusion.9, f32[512]{0:T(512)} %get-tuple-element.97), channel_id=1, replica_groups=mesh['dp'=8,'mp'=4] {'dp'}, use_global_device_ids=true, to_apply=%region_50.51 | all-reduce | flops 1536 | bytes 12288 | tf_op jit(solution)/shard_map/psum | solution.py:54
  713.2 4.4 multiply_convert_fusion.1
  717.7 23.4 %all-gather.23.cloned.1.call-done = bf16[2048,704]{0,1:T(8,128)(2,1)} async-done(((bf16[512,704]{0,1:T(8,128)(2,1)}), bf16[2048,704]{0,1:T(8,128)(2,1)}) %all-gather.23.cloned.1.call-update) | async-done | bytes 2883600 | tf_op jit(solution)/shard_map/all_gather | solution.py:147
  741.1 2.9 fusion.157
  744.1 21.4 %all-reduce.1 = (f32[128]{0:T(128)S(1)}, f32[128]{0:T(128)S(1)}) all-reduce(f32[128]{0:T(128)S(1)} %get-tuple-element.113, f32[128]{0:T(128)S(1)} %get-tuple-element.112), channel_id=1, replica_groups=mesh['dp'=8,'mp'=4] {'dp'}, use_global_device_ids=true, to_apply=%region_54.55 | all-reduce | flops 256 | bytes 2048 | tf_op jit(solution)/shard_map/psum | solution.py:54
  778.9 2.9 pad_maximum_fusion.1
  782.7 4.7 fusion.187
  787.5 4.0 fusion.8
  795.0 2.7 convolution_bitcast_fusion.5
  815.1 4.2 pad_maximum_fusion.2
  819.4 13.7 %reduce-scatter.20.cloned.1.call-done = f32[128,2816]{0,1:T(8,128)} async-done(((f32[512,2816]{0,1:T(8,128)}), f32[128,2816]{0,1:T(8,128)}) %reduce-scatter.20.cloned.1.call-update) | async-done | bytes 1441808 | tf_op jit(solution)/shard_map/reduce_scatter | solution.py:120
  833.2 3.3 fusion.154
  836.5 21.6 %all-reduce = (f32[128]{0:T(128)S(1)}, f32[128]{0:T(128)S(1)}) all-reduce(f32[128]{0:T(128)S(1)} %get-tuple-element.96, f32[128]{0:T(128)S(1)} %get-tuple-element.95), channel_id=1, replica_groups=mesh['dp'=8,'mp'=4] {'dp'}, use_global_device_ids=true, to_apply=%region_59.60 | all-reduce | flops 256 | bytes 2048 | tf_op jit(solution)/shard_map/psum | solution.py:54
  858.1 2.5 multiply_convert_fusion.2
  862.3 4.3 slice.658
  866.6 2.8 copy-done
  869.4 2.5 fusion.186
  872.0 3.3 slice_add_fusion
  875.3 10.1 pad_maximum_fusion
  887.0 13.3 %reduce-scatter.32.cloned.1.call-done = f32[256,128]{1,0:T(8,128)} async-done(((f32[2048,128]{1,0:T(8,128)}), f32[256,128]{1,0:T(8,128)}) %reduce-scatter.32.cloned.1.call-update) | async-done | bytes 131088 | tf_op jit(solution)/shard_map/reduce_scatter | solution.py:371
  904.7 65.8 %reduce-scatter.26.cloned.1.call-done = f32[128,512]{1,0:T(8,128)} async-done(((f32[1024,512]{1,0:T(8,128)}), f32[128,512]{1,0:T(8,128)}) %reduce-scatter.26.cloned.1.call-update) | async-done | bytes 262160 | tf_op jit(solution)/shard_map/reduce_scatter | solution.py:364
  973.9 67.3 %reduce-scatter.30.cloned.1.call-done = f32[2,128,256]{2,1,0:T(8,128)} async-done(((f32[2,128,2048]{2,1,0:T(8,128)}), f32[2,128,256]{2,1,0:T(8,128)}) %reduce-scatter.30.cloned.1.call-update) | async-done | bytes 262160 | tf_op jit(solution)/shard_map/reduce_scatter | solution.py:368
  1046.7 92.7 %reduce-scatter.28.cloned.1.call-done = f32[2,9,64,128]{3,2,1,0:T(8,128)} async-done(((f32[2,9,512,128]{3,2,1,0:T(8,128)}), f32[2,9,64,128]{3,2,1,0:T(8,128)}) %reduce-scatter.28.cloned.1.call-update) | async-done | bytes 589840 | tf_op jit(solution)/shard_map/reduce_scatter | solution.py:365
  1139.4 2.7 multiply_add_fusion.1
  1145.7 59.2 %reduce-scatter.24.cloned.1.call-done = f32[128,128]{1,0:T(8,128)} async-done(((f32[1024,128]{1,0:T(8,128)}), f32[128,128]{1,0:T(8,128)}) %reduce-scatter.24.cloned.1.call-update) | async-done | bytes 65552 | tf_op jit(solution)/shard_map/reduce_scatter | solution.py:363
  1208.6 40.3 %psum.215 = f32[7,2]{0,1:T(2,128)S(1)} all-reduce(f32[7,2]{0,1:T(2,128)S(1)} %stack.337), channel_id=1, replica_groups=mesh['dp'=8,'mp'=4] {'dp','mp'}, use_global_device_ids=true, to_apply=%region_80.81 | all-reduce | flops 14 | bytes 112 | tf_op jit(solution)/shard_map/psum | solution.py:401
  1255.9 43.6 %reduce-scatter.22.cloned.1.call-done = f32[256,2816]{0,1:T(8,128)} async-done(((f32[1024,2816]{0,1:T(8,128)}), f32[256,2816]{0,1:T(8,128)}) %reduce-scatter.22.cloned.1.call-update) | async-done | bytes 2883600 | tf_op jit(solution)/shard_map/reduce_scatter | solution.py:165
  1299.5 3.4 multiply_convert_fusion
  (616 shorter events, 122.2 us)
Async XLA Ops:
  7.2 50.8 %all-gather.9.cloned.1.call-start = ((), (), s32[]{:S(2)}) async-start(), calls=%async_computation.11 | async-start | bytes 7208960 | tf_op jit(solution)/shard_map/all_gather | solution.py:83
  11.0 101.9 %all-gather.13.cloned.1.call-start = ((), (), s32[]{:S(2)}) async-start(), calls=%async_computation.13 | async-start | bytes 2654208 | tf_op jit(solution)/shard_map/all_gather | solution.py:223
  12.8 128.2 %all-gather.11.cloned.1.call-start = ((), (), s32[]{:S(2)}) async-start(), calls=%async_computation.12 | async-start | bytes 3604480 | tf_op jit(solution)/shard_map/all_gather | solution.py:95
  12.9 72.7 %copy-start.56 = (f32[2816]{0:T(1024)}, f32[2816]{0:T(1024)S(1)}, u32[]{:S(2)}) copy-start(f32[2816]{0:T(1024)S(1)} %mul.1028) | copy-start | bytes 33796
  14.2 168.9 %copy-start.122 = (f32[128]{0:T(128)}, f32[128]{0:T(128)S(1)}, u32[]{:S(2)}) copy-start(f32[128]{0:T(128)S(1)} %compare_convert_fusion.1) | copy-start | bytes 1540
  48.0 135.2 %copy-start.129 = (f32[128]{0:T(128)}, f32[128]{0:T(128)S(1)}, u32[]{:S(2)}) copy-start(f32[128]{0:T(128)S(1)} %get-tuple-element.240) | copy-start | bytes 1540
  48.0 135.2 %copy-start.131 = (f32[128]{0:T(128)}, f32[128]{0:T(128)S(1)}, u32[]{:S(2)}) copy-start(f32[128]{0:T(128)S(1)} %get-tuple-element.241) | copy-start | bytes 1540
  87.2 96.0 %all-gather.15.cloned.1.call-start = ((), (), s32[]{:S(2)}) async-start(), calls=%async_computation.14 | async-start | bytes 1179648 | tf_op jit(solution)/shard_map/all_gather | solution.py:224
  87.9 136.8 %all-gather.17.cloned.1.call-start = ((), (), s32[]{:S(2)}) async-start(), calls=%async_computation.16 | async-start | bytes 1179648 | tf_op jit(solution)/shard_map/all_gather | solution.py:222
  88.7 192.1 %reduce-scatter.12.cloned.1.call-start = ((), (), s32[]{:S(2)}) async-start(), calls=%async_computation.15 | async-start | bytes 7208960 | tf_op jit(solution)/shard_map/reduce_scatter | solution.py:138
  88.8 63.5 %copy-start.153 = (pred[704]{0:T(1024)(128)(4,1)}, pred[704]{0:T(1024)(128)(4,1)S(1)}, u32[]{:S(2)}) copy-start(pred[704]{0:T(1024)(128)(4,1)S(1)} %get-tuple-element.269) | copy-start | bytes 2116
  88.8 63.5 %copy-start.157 = (pred[704]{0:T(1024)(128)(4,1)}, pred[704]{0:T(1024)(128)(4,1)S(1)}, u32[]{:S(2)}) copy-start(pred[704]{0:T(1024)(128)(4,1)S(1)} %get-tuple-element.268) | copy-start | bytes 2116
  88.8 63.5 %copy-start.161 = (pred[704]{0:T(1024)(128)(4,1)}, pred[704]{0:T(1024)(128)(4,1)S(1)}, u32[]{:S(2)}) copy-start(pred[704]{0:T(1024)(128)(4,1)S(1)} %get-tuple-element.267) | copy-start | bytes 2116
  88.8 298.1 %copy-start.68 = (pred[704]{0:T(1024)(128)(4,1)}, pred[704]{0:T(1024)(128)(4,1)S(1)}, u32[]{:S(2)}) copy-start(pred[704]{0:T(1024)(128)(4,1)S(1)} %get-tuple-element.266) | copy-start | bytes 2116
  89.4 451.5 %copy-start.15 = (f32[704]{0:T(1024)}, f32[704]{0:T(1024)S(1)}, u32[]{:S(2)}) copy-start(f32[704]{0:T(1024)S(1)} %get-tuple-element.129) | copy-start | bytes 8452
  187.6 158.9 %all-gather.19.cloned.1.call-start = ((), (), s32[]{:S(2)}) async-start(), calls=%async_computation.17 | async-start | bytes 3604480 | tf_op jit(solution)/shard_map/all_gather | solution.py:83
  188.9 120.3 %copy-start.79 = (f32[1,1,512]{2,1,0:T(1,128)}, f32[1,1,512]{2,1,0:T(1,128)S(1)}, u32[]{:S(2)}) copy-start(f32[1,1,512]{2,1,0:T(1,128)S(1)} %get-tuple-element.225) | copy-start | bytes 6148
  188.9 120.3 %copy-start.80 = (f32[1,1,512]{2,1,0:T(1,128)}, f32[1,1,512]{2,1,0:T(1,128)S(1)}, u32[]{:S(2)}) copy-start(f32[1,1,512]{2,1,0:T(1,128)S(1)} %get-tuple-element.227) | copy-start | bytes 6148
  188.9 120.3 %copy-start.87 = (f32[1,1,512]{2,1,0:T(1,128)}, f32[1,1,512]{2,1,0:T(1,128)S(1)}, u32[]{:S(2)}) copy-start(f32[1,1,512]{2,1,0:T(1,128)S(1)} %get-tuple-element.224) | copy-start | bytes 6148
  188.9 120.3 %copy-start.88 = (f32[1,1,512]{2,1,0:T(1,128)}, f32[1,1,512]{2,1,0:T(1,128)S(1)}, u32[]{:S(2)}) copy-start(f32[1,1,512]{2,1,0:T(1,128)S(1)} %get-tuple-element.226) | copy-start | bytes 6148
  312.3 154.9 %reduce-scatter.14.cloned.1.call-start = ((), (), s32[]{:S(2)}) async-start(), calls=%async_computation.18 | async-start | bytes 7208960 | tf_op jit(solution)/shard_map/reduce_scatter | solution.py:138
  313.0 227.9 %copy-start.111 = (f32[128]{0:T(128)}, f32[128]{0:T(128)S(1)}, u32[]{:S(2)}) copy-start(f32[128]{0:T(128)S(1)} %compare_convert_fusion) | copy-start | bytes 1540
  313.1 73.9 %copy-start.171 = (pred[704]{0:T(1024)(128)(4,1)}, pred[704]{0:T(1024)(128)(4,1)S(1)}, u32[]{:S(2)}) copy-start(pred[704]{0:T(1024)(128)(4,1)S(1)} %and_and_fusion) | copy-start | bytes 2116
  313.1 73.8 %copy-start.165 = (pred[704]{0:T(1024)(128)(4,1)}, pred[704]{0:T(1024)(128)(4,1)S(1)}, u32[]{:S(2)}) copy-start(pred[704]{0:T(1024)(128)(4,1)S(1)} %get-tuple-element.273) | copy-start | bytes 2116
  313.1 73.8 %copy-start.168 = (pred[704]{0:T(1024)(128)(4,1)}, pred[704]{0:T(1024)(128)(4,1)S(1)}, u32[]{:S(2)}) copy-start(pred[704]{0:T(1024)(128)(4,1)S(1)} %get-tuple-element.272) | copy-start | bytes 2116
  313.2 73.8 %copy-start.89 = (pred[704]{0:T(1024)(128)(4,1)}, pred[704]{0:T(1024)(128)(4,1)S(1)}, u32[]{:S(2)}) copy-start(pred[704]{0:T(1024)(128)(4,1)S(1)} %get-tuple-element.270) | copy-start | bytes 2116
  313.2 73.8 %copy-start.93 = (pred[704]{0:T(1024)(128)(4,1)}, pred[704]{0:T(1024)(128)(4,1)S(1)}, u32[]{:S(2)}) copy-start(pred[704]{0:T(1024)(128)(4,1)S(1)} %get-tuple-element.271) | copy-start | bytes 2116
  410.4 130.5 %copy-start.118 = (f32[128]{0:T(128)}, f32[128]{0:T(128)S(1)}, u32[]{:S(2)}) copy-start(f32[128]{0:T(128)S(1)} %get-tuple-element.199) | copy-start | bytes 1540
  410.4 130.5 %copy-start.120 = (f32[128]{0:T(128)}, f32[128]{0:T(128)S(1)}, u32[]{:S(2)}) copy-start(f32[128]{0:T(128)S(1)} %get-tuple-element.200) | copy-start | bytes 1540
  415.0 75.9 %copy-start.128 = (f32[1,1,512]{2,1,0:T(1,128)S(1)}, f32[1,1,512]{2,1,0:T(1,128)}, u32[]{:S(2)}) copy-start(f32[1,1,512]{2,1,0:T(1,128)} %get-tuple-element.228) | copy-start | bytes 6148
  415.0 125.9 %all-gather.21.cloned.1.call-start = ((), (), s32[]{:S(2)}) async-start(), calls=%async_computation.19 | async-start | bytes 3604480 | tf_op jit(solution)/shard_map/all_gather | solution.py:147
  515.9 85.2 %reduce-scatter.16.cloned.1.call-start = ((), (), s32[]{:S(2)}) async-start(), calls=%async_computation.20 | async-start | bytes 1802240 | tf_op jit(solution)/shard_map/reduce_scatter | solution.py:120
  577.3 107.0 %reduce-scatter.18.cloned.1.call-start = ((), (), s32[]{:S(2)}) async-start(), calls=%async_computation.21 | async-start | bytes 7208960 | tf_op jit(solution)/shard_map/reduce_scatter | solution.py:165
  632.9 108.2 %all-gather.23.cloned.1.call-start = ((), (), s32[]{:S(2)}) async-start(), calls=%async_computation.22 | async-start | bytes 3604480 | tf_op jit(solution)/shard_map/all_gather | solution.py:147
  717.6 48.4 %copy-start.16 = (f32[704]{0:T(1024)S(1)}, f32[704]{0:T(1024)}, u32[]{:S(2)}) copy-start(f32[704]{0:T(1024)} %copy-done.15) | copy-start | bytes 8452
  717.6 48.3 %copy-start.114 = (f32[128]{0:T(128)S(1)}, f32[128]{0:T(128)}, u32[]{:S(2)}) copy-start(f32[128]{0:T(128)} %copy-done.113) | copy-start | bytes 1540
  717.6 48.3 %copy-start.116 = (f32[128]{0:T(128)S(1)}, f32[128]{0:T(128)}, u32[]{:S(2)}) copy-start(f32[128]{0:T(128)} %copy-done.115) | copy-start | bytes 1540
  717.6 48.3 %copy-start.180 = (f32[128]{0:T(128)S(1)}, f32[128]{0:T(128)}, u32[]{:S(2)}) copy-start(f32[128]{0:T(128)} %get-tuple-element.190) | copy-start | bytes 1540
  717.6 115.5 %reduce-scatter.20.cloned.1.call-start = ((), (), s32[]{:S(2)}) async-start(), calls=%async_computation.23 | async-start | bytes 7208960 | tf_op jit(solution)/shard_map/reduce_scatter | solution.py:120
  781.8 118.5 %reduce-scatter.32.cloned.1.call-start = ((), (), s32[]{:S(2)}) async-start(), calls=%async_computation.29 | async-start | bytes 1179648 | tf_op jit(solution)/shard_map/reduce_scatter | solution.py:371
  787.4 183.2 %reduce-scatter.26.cloned.1.call-start = ((), (), s32[]{:S(2)}) async-start(), calls=%async_computation.26 | async-start | bytes 2359296 | tf_op jit(solution)/shard_map/reduce_scatter | solution.py:364
  791.6 249.6 %reduce-scatter.30.cloned.1.call-start = ((), (), s32[]{:S(2)}) async-start(), calls=%async_computation.28 | async-start | bytes 2359296 | tf_op jit(solution)/shard_map/reduce_scatter | solution.py:368
  800.0 339.4 %reduce-scatter.28.cloned.1.call-start = ((), (), s32[]{:S(2)}) async-start(), calls=%async_computation.27 | async-start | bytes 5308416 | tf_op jit(solution)/shard_map/reduce_scatter | solution.py:365
  819.4 38.7 %copy-start.179 = (f32[128]{0:T(128)S(1)}, f32[128]{0:T(128)}, u32[]{:S(2)}) copy-start(f32[128]{0:T(128)} %get-tuple-element.186) | copy-start | bytes 1540
  819.4 385.5 %reduce-scatter.24.cloned.1.call-start = ((), (), s32[]{:S(2)}) async-start(), calls=%async_computation.25 | async-start | bytes 589824 | tf_op jit(solution)/shard_map/reduce_scatter | solution.py:363
  871.9 427.5 %reduce-scatter.22.cloned.1.call-start = ((), (), s32[]{:S(2)}) async-start(), calls=%async_computation.24 | async-start | bytes 14417920 | tf_op jit(solution)/shard_map/reduce_scatter | solution.py:165
  885.6 85.0 %copy-start.14 = (f32[128,512]{1,0:T(8,128)S(1)}, f32[128,512]{1,0:T(8,128)}, u32[]{:S(2)}) copy-start(f32[128,512]{1,0:T(8,128)} %param.30) | copy-start | bytes 786436
  885.6 85.0 %copy-start.60 = (f32[128,512]{1,0:T(8,128)S(1)}, f32[128,512]{1,0:T(8,128)}, u32[]{:S(2)}) copy-start(f32[128,512]{1,0:T(8,128)} %param.38) | copy-start | bytes 786436
  885.6 85.0 %copy-start.61 = (f32[128,512]{1,0:T(8,128)S(1)}, f32[128,512]{1,0:T(8,128)}, u32[]{:S(2)}) copy-start(f32[128,512]{1,0:T(8,128)} %param.39) | copy-start | bytes 786436
  886.2 87.7 %copy-start.186 = (f32[128]{0:T(128)S(1)}, f32[128]{0:T(128)}, u32[]{:S(2)}) copy-start(f32[128]{0:T(128)} %copy-done.185) | copy-start | bytes 1540
  886.2 87.7 %copy-start.188 = (f32[128]{0:T(128)S(1)}, f32[128]{0:T(128)}, u32[]{:S(2)}) copy-start(f32[128]{0:T(128)} %copy-done.187) | copy-start | bytes 1540
  886.2 155.0 %copy-start.58 = (f32[2,128,256]{2,1,0:T(8,128)S(1)}, f32[2,128,256]{2,1,0:T(8,128)}, u32[]{:S(2)}) copy-start(f32[2,128,256]{2,1,0:T(8,128)} %param.42) | copy-start | bytes 786436
  886.2 155.0 %copy-start.59 = (f32[2,128,256]{2,1,0:T(8,128)S(1)}, f32[2,128,256]{2,1,0:T(8,128)}, u32[]{:S(2)}) copy-start(f32[2,128,256]{2,1,0:T(8,128)} %param.43) | copy-start | bytes 786436
  902.6 349.7 %copy-start.51 = (f32[256,128]{1,0:T(8,128)}, f32[256,128]{1,0:T(8,128)S(1)}, u32[]{:S(2)}) copy-start(f32[256,128]{1,0:T(8,128)S(1)} %get-tuple-element.174) | copy-start | bytes 393220
  972.3 281.5 %copy-start.28 = (f32[128,512]{1,0:T(8,128)}, f32[128,512]{1,0:T(8,128)S(1)}, u32[]{:S(2)}) copy-start(f32[128,512]{1,0:T(8,128)S(1)} %get-tuple-element.182) | copy-start | bytes 786436
  972.3 281.5 %copy-start.29 = (f32[128,512]{1,0:T(8,128)}, f32[128,512]{1,0:T(8,128)S(1)}, u32[]{:S(2)}) copy-start(f32[128,512]{1,0:T(8,128)S(1)} %get-tuple-element.183) | copy-start | bytes 786436
  972.3 167.1 %copy-start.48 = (f32[2,9,64,128]{3,2,1,0:T(8,128)S(1)}, f32[2,9,64,128]{3,2,1,0:T(8,128)}, u32[]{:S(2)}) copy-start(f32[2,9,64,128]{3,2,1,0:T(8,128)} %param.40) | copy-start | bytes 1769476
  1046.7 158.2 %copy-start.50 = (f32[128,128]{1,0:T(8,128)S(1)}, f32[128,128]{1,0:T(8,128)}, u32[]{:S(2)}) copy-start(f32[128,128]{1,0:T(8,128)} %param.29) | copy-start | bytes 196612
  1046.7 161.3 %copy-start.82 = (f32[4,2,128]{2,1,0:T(2,128)S(1)}, f32[4,2,128]{2,1,0:T(2,128)}, u32[]{:S(2)}) copy-start(f32[4,2,128]{2,1,0:T(2,128)} %param.34) | copy-start | bytes 12292
  1046.7 161.3 %copy-start.175 = (f32[4,2,128]{2,1,0:T(2,128)S(1)}, f32[4,2,128]{2,1,0:T(2,128)}, u32[]{:S(2)}) copy-start(f32[4,2,128]{2,1,0:T(2,128)} %param.47) | copy-start | bytes 12292
  1046.7 161.3 %copy-start.176 = (f32[4,2,128]{2,1,0:T(2,128)S(1)}, f32[4,2,128]{2,1,0:T(2,128)}, u32[]{:S(2)}) copy-start(f32[4,2,128]{2,1,0:T(2,128)} %param.46) | copy-start | bytes 12292
  1142.1 110.2 %copy-start.52 = (f32[256,128]{1,0:T(8,128)S(1)}, f32[256,128]{1,0:T(8,128)}, u32[]{:S(2)}) copy-start(f32[256,128]{1,0:T(8,128)} %get-tuple-element.175) | copy-start | bytes 393220
  1206.4 48.3 %copy-start.62 = (f32[128,128]{1,0:T(8,128)}, f32[128,128]{1,0:T(8,128)S(1)}, u32[]{:S(2)}) copy-start(f32[128,128]{1,0:T(8,128)S(1)} %get-tuple-element.184) | copy-start | bytes 196612
  1206.4 48.3 %copy-start.63 = (f32[128,128]{1,0:T(8,128)}, f32[128,128]{1,0:T(8,128)S(1)}, u32[]{:S(2)}) copy-start(f32[128,128]{1,0:T(8,128)S(1)} %get-tuple-element.185) | copy-start | bytes 196612
  (162 other events, 969.4 us)
Sparse Core Ops, SparseCore 0:
  11.1 46.8 all-gather.8
  60.8 52.0 all-gather.12
  115.0 25.9 all-gather.10
  143.5 39.6 all-gather.14
  185.7 38.9 all-gather.16
  227.1 53.5 reduce-scatter.11
  312.4 23.3 all-gather.18
  415.1 52.0 reduce-scatter.13
  516.1 24.8 all-gather.20
  577.4 23.6 reduce-scatter.15
  633.0 51.1 reduce-scatter.17
  717.7 23.3 all-gather.22
  781.9 51.1 reduce-scatter.19
  836.8 63.4 reduce-scatter.31
  903.7 66.8 reduce-scatter.25
  973.9 67.2 reduce-scatter.29
  1044.7 94.6 reduce-scatter.27
  1143.2 61.6 reduce-scatter.23
  1207.6 91.8 reduce-scatter.21
where the time goes:
time: 1320 us; the launch traced here: 1310 us
  waiting for transfers between devices  691 us (52%)
  blocking collectives  364 us (28%)
  matrix products  110 us (8%)
  other arithmetic  104 us (8%)
  local copies, waits for them, and re-layouts  21 us (2%)
  between operations  19 us (1%)
    psum x12, blocking collectives, over_images(): return lax.psum((first, second), 'dp')  250 us
    reduce_scatter x2, waiting for transfers between devices, output_mix(): lax.psum_scatter(jnp.einsum('kc,kp->cp', kernel, hidden, preferred_elemen...  108 us
    reduce_scatter x2, waiting for transfers between devices, input_back(): lax.psum_scatter(result, 'mp', scatter_dimension=0, tiled=True)  94.9 us
    reduce_scatter x1, waiting for transfers between devices, shards(): lax.psum_scatter(jnp.stack([middle_zero_grad, middle_one_grad]), 'dp', sc...  92.7 us
    reduce_scatter x1, waiting for transfers between devices, shards(): lax.psum_scatter(jnp.stack([last_zero_grad, last_one_grad]), 'dp', scatte...  67.3 us
    reduce_scatter x1, waiting for transfers between devices, shards(): lax.psum_scatter(short_grad, 'dp', scatter_dimension=0, tiled=True)  65.8 us
    reduce_scatter x1, waiting for transfers between devices, shards(): lax.psum_scatter(first_grad, 'dp', scatter_dimension=0, tiled=True)  59.2 us
    all_gather x2, waiting for transfers between devices, output_back(): piece = lax.all_gather(grad_b, 'mp', axis=0, tiled=True)  48.4 us
  transfers between devices with their start and end apart: 19, of which 18 were waited for; matrix products, arithmetic and copies ran while one was open for 9% of the time, Pallas kernels for 0%

commit v1 on v0

--- a/solution.py
+++ b/solution.py
@@ -459,6 +459,469 @@
     )
 
 
+def fits(mesh, pixel_mask):
+    sizes = (mesh.shape["dp"], mesh.shape["mp"])
+    powers = all(size >= 2 and size & (size - 1) == 0 for size in sizes)
+    return powers and pixel_mask.shape[1] % (HO * WO * sizes[1]) == 0
+
+
+def swap(values, axis, mask):
+    size = lax.axis_size(axis)
+    return lax.ppermute(values, axis, [(place, place ^ mask) for place in range(size)])
+
+
+def bit_of(axis, mask):
+    return (lax.axis_index(axis) & mask) // mask
+
+
+def high_bits(axis):
+    masks = []
+    mask = lax.axis_size(axis) // 2
+    while mask:
+        masks.append(mask)
+        mask //= 2
+    return masks
+
+
+def tree_sum(terms):
+    while len(terms) > 1:
+        terms = [terms[place] + terms[place + 1] for place in range(0, len(terms), 2)]
+    return terms[0]
+
+
+def everywhere(values):
+    for axis in ("mp", "dp"):
+        values = tree_sum(
+            [values] + [swap(values, axis, mask) for mask in range(1, lax.axis_size(axis))]
+        )
+    return values
+
+
+def sum_all(parts):
+    flat = [part.reshape(-1, 128) for part in parts]
+    total = everywhere(jnp.concatenate(flat, 0))
+    result = []
+    start = 0
+    for part, rows in zip(parts, flat):
+        result.append(total[start : start + rows.shape[0]].reshape(part.shape))
+        start += rows.shape[0]
+    return result
+
+
+def routes(late_rows):
+    rows = high_bits("dp")
+    columns = high_bits("mp")[:-1]
+    order = [("dp", mask) for mask in rows[:-1]]
+    last_row = [("dp", rows[-1])]
+    sides = [("mp", mask) for mask in reversed(columns)]
+    return order + (sides + last_row if late_rows else last_row + sides)
+
+
+def gather(block, late_rows):
+    lead, _, _ = block.shape
+    outer = 1
+    for axis, mask in routes(late_rows):
+        other = swap(block, axis, mask)
+        high = bit_of(axis, mask) > 0
+        first = jnp.where(high, other, block)
+        second = jnp.where(high, block, other)
+        if axis == "dp":
+            rows, cols = block.shape[1:]
+            pair = [part.reshape(lead, outer, rows // outer, cols) for part in (first, second)]
+            block = jnp.stack(pair, 2).reshape(lead, 2 * rows, cols)
+            outer *= 2
+        else:
+            block = jnp.concatenate([first, second], 2)
+    return (block, swap(block, "mp", 1))
+
+
+def scatter(keep, send, late_rows):
+    masks = high_bits("dp")
+    lead, rows, cols = keep.shape
+    unit = rows >> len(masks)
+    shape = (lead,) + (2,) * len(masks) + (unit, cols)
+    terms = [keep.reshape(shape), swap(send, "mp", 1).reshape(shape)]
+    for axis, mask in reversed(routes(late_rows)):
+        place = bit_of(axis, mask)
+        if axis == "dp":
+            dim = 1 + masks.index(mask)
+            size = 1
+        else:
+            dim = len(shape) - 1
+            size = terms[0].shape[dim] // 2
+
+        def pick(term, which):
+            return lax.dynamic_slice_in_dim(term, which * size, size, dim)
+
+        out = sum(pick(term, 1 - place).astype(jnp.float32) for term in terms)
+        arrived = swap(out.astype(jnp.bfloat16), axis, mask)
+        terms = [pick(term, place) for term in terms] + [arrived]
+    total = sum(term.astype(jnp.float32) for term in terms)
+    return total.reshape(lead, unit, -1)
+
+
+def halves(values):
+    count = lax.axis_size("mp")
+    width = values.shape[-1] // count
+    blocks = [values[..., place * width : (place + 1) * width] for place in range(count)]
+    even = jnp.concatenate(blocks[0::2], -1)
+    odd = jnp.concatenate(blocks[1::2], -1)
+    high = bit_of("mp", 1) > 0
+    return (jnp.where(high, odd, even), jnp.where(high, even, odd))
+
+
+def joined(mine, other):
+    count = lax.axis_size("mp")
+    width = 2 * mine.shape[-1] // count
+    high = bit_of("mp", 1) > 0
+    even = jnp.where(high, other, mine)
+    odd = jnp.where(high, mine, other)
+    blocks = []
+    for place in range(count // 2):
+        blocks.append(even[..., place * width : (place + 1) * width])
+        blocks.append(odd[..., place * width : (place + 1) * width])
+    return jnp.concatenate(blocks, -1)
+
+
+def dot(first, second, dims):
+    return lax.dot_general(first, second, (dims, ((), ())), preferred_element_type=jnp.float32)
+
+
+def times(values, weight):
+    return joined(*[dot(values, part, ((1,), (0,))) for part in weight])
+
+
+def times_turned(values, weight):
+    parts = [
+        dot(value, part, ((1,), (1,))) for value, part in zip(halves(values), weight)
+    ]
+    return parts[0] + parts[1]
+
+
+def outer_parts(rows_of, cols_of):
+    return [
+        dot(rows_of, part, ((0,), (0,))).astype(jnp.bfloat16) for part in halves(cols_of)
+    ]
+
+
+def reach(values, drow, dcol):
+    offset = drow * WO + dcol
+    count = values.shape[0]
+    place = lax.iota(jnp.int32, count)
+    row_at = place // WO % HO + drow
+    col_at = place % WO + dcol
+    inside = (row_at >= 0) & (row_at < HO) & (col_at >= 0) & (col_at < WO)
+    moved = jnp.roll(values, -offset, axis=0)
+    return jnp.where(inside[:, None], moved, jnp.zeros_like(moved))
+
+
+def tap_columns(values, taps, pixels):
+    return jnp.concatenate(
+        [
+            reach(values[phase * pixels : (phase + 1) * pixels], drow, dcol)
+            for tap, phase, drow, dcol in taps
+        ],
+        1,
+    )
+
+
+def tap_back(columns, taps, width, phases):
+    blocks = []
+    for target in range(phases):
+        total = 0.0
+        for tap, phase, drow, dcol in taps:
+            if phase == target:
+                total = total + reach(columns[:, tap * width : (tap + 1) * width], -drow, -dcol)
+        blocks.append(total)
+    return jnp.concatenate(blocks, 0)
+
+
+def flat_pair(pair):
+    return [part.reshape(-1, part.shape[-1]) for part in pair]
+
+
+def sums_of(values, mask):
+    weighted = values * mask
+    return [jnp.sum(weighted, 0), jnp.sum(weighted * values, 0)]
+
+
+def normed(values, totals, count, table):
+    mean = totals[0] / count
+    scale = lax.rsqrt(totals[1] / count - mean * mean + EPS_NORM)
+    centred = (values - mean[None]) * scale[None]
+    return (centred, scale, centred * table[0][None] + table[1][None])
+
+
+def grad_sums(grad_in, centred):
+    return [jnp.sum(grad_in * centred, 0), jnp.sum(grad_in, 0)]
+
+
+def normed_back(grad_in, centred, scale, gain, mask, totals, count):
+    return (
+        (gain * scale)[None]
+        * (grad_in - mask * (totals[1][None] + centred * totals[0][None]) / count)
+    ).astype(jnp.bfloat16)
+
+
+def by_image(
+    inputs,
+    pixel_mask,
+    widths,
+    output_grad,
+    first_weight,
+    shortcut_weight,
+    middle_weight,
+    last_weight,
+    second_weight,
+    narrow_norms,
+    wide_norms,
+    first_mean,
+    first_square,
+    shortcut_mean,
+    shortcut_square,
+    middle_mean,
+    middle_square,
+    last_mean,
+    last_square,
+    second_mean,
+    second_square,
+    narrow_mean,
+    narrow_square,
+    wide_mean,
+    wide_square,
+):
+    ranks = lax.axis_size("mp")
+    rank = lax.axis_index("mp")
+    pixels = pixel_mask.shape[1] // ranks
+    narrow = first_weight.shape[1] * ranks
+    wide = shortcut_weight.shape[1] * ranks
+    low = jnp.bfloat16
+    first_w = gather(first_weight.astype(low)[None], False)
+    mid_zero_w = gather(middle_weight[0].astype(low), True)
+    last_zero_w = gather(last_weight[0].astype(low).T[None], False)
+    short_w = gather(shortcut_weight.astype(low)[None], True)
+    second_w = gather(second_weight.astype(low)[None], False)
+    mid_one_w = gather(middle_weight[1].astype(low), False)
+    last_one_w = gather(last_weight[1].astype(low).T[None], True)
+    first_w, short_w, second_w, mid_zero_w, mid_one_w, last_zero_w, last_one_w = [
+        flat_pair(pair)
+        for pair in (first_w, short_w, second_w, mid_zero_w, mid_one_w, last_zero_w, last_one_w)
+    ]
+    tables = lax.all_gather(
+        jnp.concatenate([narrow_norms.reshape(-1, 128), wide_norms.reshape(-1, 128)], 0), "mp"
+    )
+    split = narrow_norms.size // 128
+    narrow_all = (
+        tables[:, :split].reshape(ranks, 4, 2, -1).transpose(1, 2, 0, 3).reshape(4, 2, narrow)
+    )
+    wide_all = tables[:, split:].reshape(ranks, 3, 2, -1).transpose(1, 2, 0, 3).reshape(3, 2, wide)
+
+    own_mask = lax.dynamic_slice_in_dim(pixel_mask, rank * pixels, pixels, 1).astype(jnp.float32)
+    mask_in = own_mask.reshape(-1, 1)
+    mask_out = own_mask[0][:, None]
+    channel = lax.iota(jnp.int32, narrow)
+    keep_one = (channel < widths[0]).astype(jnp.float32)[None]
+    keep_two = (channel < widths[1]).astype(jnp.float32)[None]
+
+    field = lax.all_to_all(inputs, "mp", split_axis=2, concat_axis=0, tiled=True)
+    field = field.transpose(1, 2, 0).reshape(4 * pixels, -1) * mask_in.astype(low)
+    above = lax.all_to_all(output_grad, "mp", split_axis=1, concat_axis=0, tiled=True).T
+
+    pre_one = times(field, first_w)
+    counts = jnp.stack([jnp.sum(mask_in), jnp.sum(mask_out)])
+    counts = jnp.concatenate([counts, jnp.zeros(126, jnp.float32)])
+    *totals, counts = sum_all(sums_of(pre_one, mask_in) + [counts])
+    count_in, count_out = counts[0], counts[1]
+    cen_one, scale_one, act_one = normed(pre_one, totals, count_in, narrow_all[0])
+    hid_one = (jax.nn.silu(act_one) * mask_in * keep_one).astype(low)
+    cols_one = tap_columns(hid_one, STRIDED_TAPS, pixels)
+    pre_two = times(cols_one, mid_zero_w)
+    totals = sum_all(sums_of(pre_two, mask_out))
+    cen_two, scale_two, act_two = normed(pre_two, totals, count_out, narrow_all[1])
+    hid_two = (jax.nn.silu(act_two) * mask_out * keep_one).astype(low)
+    pre_three = times_turned(hid_two, last_zero_w)
+    pre_side = times(field[:pixels], short_w)
+    totals = sum_all(sums_of(pre_three, mask_out) + sums_of(pre_side, mask_out))
+    cen_three, scale_three, act_three = normed(pre_three, totals[:2], count_out, wide_all[0])
+    cen_side, scale_side, act_side = normed(pre_side, totals[2:], count_out, wide_all[1])
+    total_one = act_three + act_side
+    out_one = (jax.nn.silu(total_one) * mask_out).astype(low)
+    pre_four = times(out_one, second_w)
+    totals = sum_all(sums_of(pre_four, mask_out))
+    cen_four, scale_four, act_four = normed(pre_four, totals, count_out, narrow_all[2])
+    hid_four = (jax.nn.silu(act_four) * mask_out * keep_two).astype(low)
+    cols_four = tap_columns(hid_four, PLAIN_TAPS, pixels)
+    pre_five = times(cols_four, mid_one_w)
+    totals = sum_all(sums_of(pre_five, mask_out))
+    cen_five, scale_five, act_five = normed(pre_five, totals, count_out, narrow_all[3])
+    hid_five = (jax.nn.silu(act_five) * mask_out * keep_two).astype(low)
+    pre_six = times_turned(hid_five, last_one_w)
+    totals = sum_all(sums_of(pre_six, mask_out))
+    cen_six, scale_six, act_six = normed(pre_six, totals, count_out, wide_all[2])
+    total_two = act_six + out_one.astype(jnp.float32)
+    block_output = (jax.nn.silu(total_two) * mask_out).astype(low)
+    block_output = lax.all_to_all(block_output.T, "mp", split_axis=0, concat_axis=1, tiled=True)
+
+    grad_two = above.astype(jnp.float32) * mask_out * slope(total_two)
+    sums_six = sum_all(grad_sums(grad_two, cen_six))
+    grad_six = normed_back(
+        grad_two, cen_six, scale_six, wide_all[2, 0], mask_out, sums_six, count_out
+    )
+    hid_five_grad = times(grad_six, last_one_w)
+    keep, send = outer_parts(grad_six, hid_five)
+    last_one_grad = scatter(keep[None], send[None], True)
+    act_five_grad = hid_five_grad * keep_two * mask_out * slope(act_five)
+    sums_five = sum_all(grad_sums(act_five_grad, cen_five))
+    grad_five = normed_back(
+        act_five_grad, cen_five, scale_five, narrow_all[3, 0], mask_out, sums_five, count_out
+    )
+    keep, send = outer_parts(cols_four, grad_five)
+    mid_one_grad = scatter(keep.reshape(9, narrow, -1), send.reshape(9, narrow, -1), False)
+    hid_four_grad = tap_back(times_turned(grad_five, mid_one_w), PLAIN_TAPS, narrow, 1)
+    act_four_grad = hid_four_grad * keep_two * mask_out * slope(act_four)
+    sums_four = sum_all(grad_sums(act_four_grad, cen_four))
+    grad_four = normed_back(
+        act_four_grad, cen_four, scale_four, narrow_all[2, 0], mask_out, sums_four, count_out
+    )
+    keep, send = outer_parts(out_one, grad_four)
+    second_grad = scatter(keep[None], send[None], False)
+    grad_one = (
+        (grad_two + times_turned(grad_four, second_w)) * mask_out * slope(total_one)
+    )
+    gain_three, gain_side, bias_pair = sum_all(
+        [
+            jnp.sum(grad_one * cen_three, 0),
+            jnp.sum(grad_one * cen_side, 0),
+            jnp.sum(grad_one, 0),
+        ]
+    )
+    grad_three = normed_back(
+        grad_one, cen_three, scale_three, wide_all[0, 0], mask_out, (gain_three, bias_pair), count_out
+    )
+    grad_side = normed_back(
+        grad_one, cen_side, scale_side, wide_all[1, 0], mask_out, (gain_side, bias_pair), count_out
+    )
+    hid_two_grad = times(grad_three, last_zero_w)
+    keep, send = outer_parts(grad_three, hid_two)
+    last_zero_grad = scatter(keep[None], send[None], False)
+    keep, send = outer_parts(field[:pixels], grad_side)
+    short_grad = scatter(keep[None], send[None], True)
+    act_two_grad = hid_two_grad * keep_one * mask_out * slope(act_two)
+    sums_two = sum_all(grad_sums(act_two_grad, cen_two))
+    grad_mid = normed_back(
+        act_two_grad, cen_two, scale_two, narrow_all[1, 0], mask_out, sums_two, count_out
+    )
+    keep, send = outer_parts(cols_one, grad_mid)
+    mid_zero_grad = scatter(keep.reshape(9, narrow, -1), send.reshape(9, narrow, -1), True)
+    hid_one_grad = tap_back(times_turned(grad_mid, mid_zero_w), STRIDED_TAPS, narrow, 4)
+    act_one_grad = hid_one_grad * keep_one * mask_in * slope(act_one)
+    sums_one = sum_all(grad_sums(act_one_grad, cen_one))
+    grad_first = normed_back(
+        act_one_grad, cen_one, scale_one, narrow_all[0, 0], mask_in, sums_one, count_in
+    )
+    keep, send = outer_parts(field, grad_first)
+    first_grad = scatter(keep[None], send[None], False)
+    field_grad = times_turned(grad_first, first_w)
+    side_grad = times_turned(grad_side, short_w)
+    field_grad = jnp.concatenate([field_grad[:pixels] + side_grad, field_grad[pixels:]], 0)
+    field_grad = (field_grad * mask_in).astype(low).reshape(4, pixels, -1).transpose(2, 0, 1)
+    input_grad = lax.all_to_all(field_grad, "mp", split_axis=0, concat_axis=2, tiled=True)
+
+    grads = (
+        first_grad[0],
+        short_grad[0],
+        jnp.stack([mid_zero_grad, mid_one_grad]),
+        jnp.stack([last_zero_grad[0].T, last_one_grad[0].T]),
+        second_grad[0],
+    )
+    first_fix = 1.0 - BETA_ONE**STEP
+    second_fix = 1.0 - BETA_TWO**STEP
+    weights = (first_weight, shortcut_weight, middle_weight, last_weight, second_weight)
+    means = (first_mean, shortcut_mean, middle_mean, last_mean, second_mean)
+    squares_old = (first_square, shortcut_square, middle_square, last_square, second_square)
+    states = []
+    updates = []
+    for index in range(5):
+        mean_next, square_next, step = adapt(
+            grads[index], means[index], squares_old[index], first_fix, second_fix
+        )
+        states.append((mean_next, square_next))
+        updates.append(step + DECAY * weights[index])
+    pairs = [
+        (weights[0], updates[0]),
+        (weights[1], updates[1]),
+        (weights[2][0], updates[2][0]),
+        (weights[2][1], updates[2][1]),
+        (weights[3][0], updates[3][0]),
+        (weights[3][1], updates[3][1]),
+        (weights[4], updates[4]),
+    ]
+    own = [jnp.sum(value * value) for pair in pairs for value in pair]
+    own = jnp.concatenate([jnp.stack(own), jnp.zeros(128 - len(own), jnp.float32)])
+    (powers,) = sum_all([own])
+    matrix_norms = jnp.sqrt(powers[: 2 * len(pairs)].reshape(-1, 2))
+    ratio = matrix_norms[:, 0] / (matrix_norms[:, 1] + EPS_TRUST)
+    first_next = first_weight - RATE * ratio[0] * updates[0]
+    short_next = shortcut_weight - RATE * ratio[1] * updates[1]
+    middle_next = middle_weight - RATE * ratio[2:4].reshape(2, 1, 1, 1) * updates[2]
+    last_next = last_weight - RATE * ratio[4:6].reshape(2, 1, 1) * updates[3]
+    second_next = second_weight - RATE * ratio[6] * updates[4]
+
+    def own_channels(values):
+        width = values.shape[-1] // ranks
+        return lax.dynamic_slice_in_dim(values, rank * width, width, values.ndim - 1)
+
+    narrow_grad = own_channels(
+        jnp.stack([jnp.stack(pair) for pair in (sums_one, sums_two, sums_four, sums_five)])
+    )
+    wide_grad = own_channels(
+        jnp.stack(
+            [
+                jnp.stack([gain_three, bias_pair]),
+                jnp.stack([gain_side, bias_pair]),
+                jnp.stack(sums_six),
+            ]
+        )
+    )
+    narrow_mean_next, narrow_square_next, narrow_step = adapt(
+        narrow_grad, narrow_mean, narrow_square, first_fix, second_fix
+    )
+    wide_mean_next, wide_square_next, wide_step = adapt(
+        wide_grad, wide_mean, wide_square, first_fix, second_fix
+    )
+    return (
+        block_output,
+        input_grad,
+        states[0][0],
+        states[0][1],
+        first_next,
+        states[1][0],
+        states[1][1],
+        short_next,
+        states[2][0],
+        states[2][1],
+        middle_next,
+        states[3][0],
+        states[3][1],
+        last_next,
+        states[4][0],
+        states[4][1],
+        second_next,
+        narrow_mean_next,
+        narrow_square_next,
+        narrow_norms - RATE_NORM * narrow_step,
+        wide_mean_next,
+        wide_square_next,
+        wide_norms - RATE_NORM * wide_step,
+        matrix_norms,
+        first_next.astype(jnp.bfloat16),
+        short_next.astype(jnp.bfloat16),
+        middle_next.astype(jnp.bfloat16),
+        last_next.astype(jnp.bfloat16),
+        second_next.astype(jnp.bfloat16),
+    )
+
+
 def solution(mesh):
     in_specs = (
         P("mp", None, "dp"),
@@ -518,4 +981,10 @@
         P(None, "mp", "dp"),
         P("dp", "mp"),
     )
-    return jax.shard_map(shards, mesh=mesh, in_specs=in_specs, out_specs=out_specs, check_vma=False)
+    return jax.shard_map(
+        lambda *values: (by_image if fits(mesh, values[1]) else shards)(*values),
+        mesh=mesh,
+        in_specs=in_specs,
+        out_specs=out_specs,
+        check_vma=False,
+    )

time: 1320 us -> 800 us (0.61)
  waiting for transfers between devices: 691 us -> 219 us
  blocking collectives: 364 us -> 19.8 us
  starting transfers between devices: 1 us -> 251 us
  local copies, waits for them, and re-layouts: 21 us -> 97.5 us
  matrix products: 110 us -> 45.9 us
  other arithmetic: 104 us -> 148 us
    reduce_scatter x11 -> x0, waiting for transfers between devices: 539 us -> none  [the longest x2 108 us: output_mix(): lax.psum_scatter(jnp.einsum('kc,kp->cp', kernel, hidden, preferred_elemen...]
    psum x13 -> x0, blocking collectives: 290 us -> none  [the longest x12 250 us: over_images(): return lax.psum((first, second), 'dp')]
    ppermute x0 -> x200, starting transfers between devices: none -> 236 us  [swap(): lax.ppermute(values, axis, [(place, place ^ mask) for place in range(size)])]
    ppermute x0 -> x200, waiting for transfers between devices: none -> 219 us  [swap(): lax.ppermute(values, axis, [(place, place ^ mask) for place in range(size)])]
    all_gather x8 -> x0, waiting for transfers between devices: 152 us -> none  [the longest x2 48.4 us: output_back(): piece = lax.all_gather(grad_b, 'mp', axis=0, tiled=True)]
    dot_general x69 -> x42, matrix products: 110 us -> 45.9 us  [dot(): lax.dot_general(first, second, (dims, ((), ())), preferred_element_type=j...]
    all_gather x3 -> x1, blocking collectives: 73.7 us -> 19.8 us  [by_image(): lax.all_gather(jnp.concatenate([narrow_norms.reshape(-1, 128), wide_norms...]
    unnamed x398 -> x589, local copies, waits for them, and re-layouts: 12 us -> 48.5 us
  transfers between devices with their start and end apart: 19 -> 204, of which waited for: 18 -> 54; matrix products, arithmetic and copies ran while one was open for 9% -> 32% of each run, Pallas kernels for 0% -> 0%
where the time goes in v1:
time: 800 us; the launch traced here: 790 us
  starting transfers between devices  251 us (31%)
  waiting for transfers between devices  219 us (27%)
  other arithmetic  148 us (18%)
  local copies, waits for them, and re-layouts  97.5 us (12%)
  matrix products  45.9 us (6%)
  blocking collectives  19.8 us (2%)
  between operations  8.01 us (1%)
    ppermute x200, starting transfers between devices, swap(): lax.ppermute(values, axis, [(place, place ^ mask) for place in range(size)])  236 us
    ppermute x200, waiting for transfers between devices, swap(): lax.ppermute(values, axis, [(place, place ^ mask) for place in range(size)])  219 us
    unnamed x589, local copies, waits for them, and re-layouts  48.5 us
    dot_general x42, matrix products, dot(): lax.dot_general(first, second, (dims, ((), ())), preferred_element_type=j...  45.9 us
    convert_element_type x28, other arithmetic, scatter(): arrived = swap(out.astype(jnp.bfloat16), axis, mask)  31.8 us
    all_gather x1, blocking collectives, by_image(): lax.all_gather(jnp.concatenate([narrow_norms.reshape(-1, 128), wide_norms...  19.8 us
    dynamic_slice x16, local copies, waits for them, and re-layouts, pick(): return lax.dynamic_slice_in_dim(term, which * size, size, dim)  17.6 us
  transfers between devices with their start and end apart: 204, of which 54 were waited for; matrix products, arithmetic and copies ran while one was open for 32% of the time, Pallas kernels for 0%

profile of v1, /device:TPU:0, one launch (start us, length us, event | category | flops | bytes accessed | tf_op | source)
XLA Modules:
  0.0 789.7 jit_solution(6120895605718973434)
XLA Ops:
  1.9 4.1 collective-permute-start.65
  7.9 2.8 collective-permute-start.80
  10.9 2.9 collective-permute-start
  16.0 3.7 all-to-all-start
  19.8 19.8 %all-gather = f32[128,128]{1,0:T(8,128)S(1)} all-gather(f32[32,128]{1,0:T(8,128)S(1)} %pad_maximum_fusion.54), channel_id=2, replica_groups=mesh['dp'=8,'mp'=4] {'mp'}, dimensions={0}, use_global_device_ids=true | all-gather | bytes 81920 | tf_op jit(solution)/shard_map/all_gather | solution.py:710
  53.2 2.9 collective-permute-start.35
  57.7 5.4 collective-permute-done.30
  71.7 2.7 collective-permute-done.81
  76.7 3.3 collective-permute-done.36
  80.5 5.8 collective-permute-done.66
  86.7 3.9 collective-permute-done.16
  98.7 6.7 collective-permute-done.37
  106.9 32.2 %collective-permute-done.33 = bf16[1,2048,128]{2,1,0:T(8,128)(2,1)S(1)} collective-permute-done((bf16[1,2048,128]{2,1,0:T(8,128)(2,1)S(1)}, bf16[1,2048,128]{2,1,0:T(8,128)(2,1)S(1)}, u32[]{:S(2)}, u32[]{:S(2)}) %collective-permute-start.33) | collective-permute-done | bytes 524320 | tf_op jit(solution)/shard_map/ppermute | solution.py:470
  153.1 3.4 collective-permute-start.11
  170.1 41.7 %collective-permute-done.18 = bf16[9,256,256]{2,1,0:T(8,128)(2,1)S(1)} collective-permute-done((bf16[9,256,256]{2,1,0:T(8,128)(2,1)S(1)}, bf16[9,256,256]{2,1,0:T(8,128)(2,1)S(1)}, u32[]{:S(2)}, u32[]{:S(2)}) %collective-permute-start.18) | collective-permute-done | bytes 1179680 | tf_op jit(solution)/shard_map/ppermute | solution.py:470
  251.0 2.6 collective-permute-start.45
  254.3 2.5 collective-permute-start.47
  258.4 2.8 collective-permute-start.49
  267.0 13.1 %multiply_convert_fusion.6 = bf16[176,2048]{1,0:T(8,128)(2,1)S(1)} fusion(f32[176]{0:T(256)S(1)} %bitcast.731, f32[2048]{0:T(1024)S(1)} %bitcast.763, f32[2048]{0:T(1024)S(1)} %bitcast.765, f32[2048]{0:T(1024)S(1)} %get-tuple-element.439, f32[2048]{0:T(1024)S(1)} %get-tuple-element.442, f32[2048]{0:T(1024)S(1)} %bitcast.767, f32[2048]{0:T(1024)S(1)} %bitcast.769, ...), kind=kLoop, calls=%fused_computation.71 | loop fusion | flops 6488064 | bytes 3670720 | tf_op jit(solution)/shard_map/convert_element_type | solution.py:748
  284.5 5.4 collective-permute-done.56
  291.2 2.6 collective-permute-start.60
  294.2 3.0 collective-permute-start.62
  298.7 2.8 collective-permute-start.64
  314.5 4.2 all-to-all-start.2
  325.4 2.8 collective-permute-start.77
  333.7 2.9 collective-permute-done.79
  348.1 2.5 collective-permute-start.90
  351.0 3.0 collective-permute-start.92
  355.5 2.8 collective-permute-start.94
  365.0 2.5 multiply_reduce_fusion.7
  372.2 3.4 collective-permute-start.101
  384.3 4.2 all-to-all-start.1
  389.4 2.9 multiply_convert_fusion.4
  426.8 2.6 fusion.147
  445.0 2.8 collective-permute-start.122
  453.2 2.9 collective-permute-done.124
  467.4 2.5 collective-permute-start.130
  470.2 3.0 collective-permute-start.132
  474.7 2.8 collective-permute-start.134
  502.5 2.8 collective-permute-start.142
  510.7 2.9 collective-permute-done.144
  519.2 3.2 multiply_reduce_fusion.4
  535.8 3.1 convolution_convert_fusion.3
  539.0 2.6 collective-permute-start.150
  541.9 3.0 collective-permute-start.152
  546.4 2.8 collective-permute-start.154
  563.9 3.4 copy.222
  567.4 3.1 collective-permute-done.156
  573.1 4.3 fusion.6
  604.1 3.9 collective-permute-done.181
  619.7 4.1 collective-permute-done.176
  655.8 11.0 %collective-permute-done.161 = bf16[1,2,2,1,128,1024]{5,4,3,2,1,0:T(8,128)(2,1)S(1)} collective-permute-done((bf16[1,2,2,1,128,1024]{5,4,3,2,1,0:T(8,128)(2,1)S(1)}, bf16[1,2,2,1,128,1024]{5,4,3,2,1,0:T(8,128)(2,1)S(1)}, u32[]{:S(2)}, u32[]{:S(2)}) %collective-permute-start.161) | collective-permute-done | bytes 1048608 | tf_op jit(solution)/shard_map/ppermute | solution.py:470
  676.5 15.7 %collective-permute-done.166 = bf16[9,2,2,1,64,256]{5,4,3,2,1,0:T(8,128)(2,1)S(1)} collective-permute-done((bf16[9,2,2,1,64,256]{5,4,3,2,1,0:T(8,128)(2,1)S(1)}, bf16[9,2,2,1,64,256]{5,4,3,2,1,0:T(8,128)(2,1)S(1)}, u32[]{:S(2)}, u32[]{:S(2)}) %collective-permute-start.166) | collective-permute-done | bytes 1179680 | tf_op jit(solution)/shard_map/ppermute | solution.py:470
  697.0 5.0 collective-permute-done.172
  709.9 7.6 collective-permute-done.173
  718.8 2.7 multiply_reduce_fusion.16
  721.8 3.0 collective-permute-start.169
  724.8 2.9 collective-permute-done.174
  731.8 3.7 all-to-all-start.3
  735.6 2.8 multiply_add_fusion.1
  739.6 10.3 %concatenate.324 = f32[128]{0:T(128)} concatenate(f32[1]{0:T(128)} %bitcast.218, f32[1]{0:T(128)} %bitcast.219, f32[1]{0:T(128)} %bitcast.220, f32[1]{0:T(128)} %bitcast.225, f32[1]{0:T(128)} %bitcast.226, f32[1]{0:T(128)} %bitcast.235, f32[1]{0:T(128)} %bitcast.236, f32[1]{0:T(128)} %bitcast.237, f32[1]{0:T(128)} %bitcast.238, f32[1]{0:T(128)} %bitcast.251, f32[1]{0:T(128)} %bitcast.252, ...), dimensions={0} | concatenate | bytes 1024 | tf_op jit(solution)/shard_map/concatenate | solution.py:860
  752.7 8.5 %collective-permute-done.191 = f32[1,128]{1,0:T(1,128)S(1)} collective-permute-done((f32[1,128]{1,0:T(1,128)}, f32[1,128]{1,0:T(1,128)S(1)}, u32[]{:S(2)}, u32[]{:S(2)}) %collective-permute-start.191) | collective-permute-done | bytes 544 | tf_op jit(solution)/shard_map/ppermute | solution.py:470
  762.7 3.4 collective-permute-start.195
  770.7 3.1 collective-permute-start.199
  (1298 shorter events, 438.3 us)
Async XLA Ops:
  1.9 63.6 %collective-permute-start.65 = (bf16[9,64,128]{2,1,0:T(8,128)(2,1)S(1)}, bf16[9,64,128]{2,1,0:T(8,128)(2,1)S(1)}, u32[]{:S(2)}, u32[]{:S(2)}) collective-permute-start(bf16[9,64,128]{2,1,0:T(8,128)(2,1)S(1)} %get-tuple-element.318), channel_id=1, source_target_pairs={{0,16},{4,20},{8,24},{12,28},{16,0},{20,4},{24,8},{28,12},{1,17},{... | collective-permute-start | bytes 442376 | tf_op jit(solution)/shard_map/ppermute | solution.py:470
  6.0 61.1 %collective-permute-start.15 = (bf16[9,64,128]{2,1,0:T(8,128)(2,1)S(1)}, bf16[9,64,128]{2,1,0:T(8,128)(2,1)S(1)}, u32[]{:S(2)}, u32[]{:S(2)}) collective-permute-start(bf16[9,64,128]{2,1,0:T(8,128)(2,1)S(1)} %get-tuple-element.319), channel_id=1, source_target_pairs={{0,16},{4,20},{8,24},{12,28},{16,0},{20,4},{24,8},{28,12},{1,17},{... | collective-permute-start | bytes 442376 | tf_op jit(solution)/shard_map/ppermute | solution.py:470
  7.9 45.3 %collective-permute-start.80 = (bf16[1,256,128]{2,1,0:T(8,128)(2,1)S(1)}, bf16[1,256,128]{2,1,0:T(8,128)(2,1)S(1)}, u32[]{:S(2)}, u32[]{:S(2)}) collective-permute-start(bf16[1,256,128]{2,1,0:T(8,128)(2,1)S(1)} %get-tuple-element.415), channel_id=1, source_target_pairs={{0,16},{4,20},{8,24},{12,28},{16,0},{20,4},{24,8},{28,12},{1,17},{... | collective-permute-start | bytes 196616 | tf_op jit(solution)/shard_map/ppermute | solution.py:470
  10.8 45.3 %collective-permute-start.50 = (bf16[1,256,128]{2,1,0:T(8,128)(2,1)S(1)}, bf16[1,256,128]{2,1,0:T(8,128)(2,1)S(1)}, u32[]{:S(2)}, u32[]{:S(2)}) collective-permute-start(bf16[1,256,128]{2,1,0:T(8,128)(2,1)S(1)} %convert_bitcast_fusion.4), channel_id=1, source_target_pairs={{0,16},{4,20},{8,24},{12,28},{16,0},{20,4},{24,8},{28,12},{1,17},{... | collective-permute-start | bytes 196616 | tf_op jit(solution)/shard_map/ppermute | solution.py:470
  10.9 42.1 %collective-permute-start = (bf16[1,128,128]{2,1,0:T(8,128)(2,1)S(1)}, bf16[1,128,128]{2,1,0:T(8,128)(2,1)S(1)}, u32[]{:S(2)}, u32[]{:S(2)}) collective-permute-start(bf16[1,128,128]{2,1,0:T(8,128)(2,1)S(1)} %convert_bitcast_fusion.6), channel_id=1, source_target_pairs={{0,16},{4,20},{8,24},{12,28},{16,0},{20,4},{24,8},{28,12},{1,17},{... | collective-permute-start | bytes 98312 | tf_op jit(solution)/shard_map/ppermute | solution.py:470
  16.0 125.5 %all-to-all-start = ((bf16[256,4,704]{0,1,2:T(4,128)(2,1)}), bf16[256,4,704]{0,1,2:T(4,128)(2,1)S(1)}, u32[]{:S(2)}, u32[]{:S(2)}) async-start(bf16[256,4,704]{0,1,2:T(4,128)(2,1)} %copy.195), calls=%async_computation | async-start | bytes 2883584 | tf_op jit(solution)/shard_map/all_to_all | solution.py:726
  53.2 12.2 %collective-permute-start.35 = (bf16[1,128,512]{2,1,0:T(8,128)(2,1)S(1)}, bf16[1,128,512]{2,1,0:T(8,128)(2,1)S(1)}, u32[]{:S(2)}, u32[]{:S(2)}) collective-permute-start(bf16[1,128,512]{2,1,0:T(8,128)(2,1)S(1)} %convert_bitcast_fusion.2), channel_id=1, source_target_pairs={{0,16},{4,20},{8,24},{12,28},{16,0},{20,4},{24,8},{28,12},{1,17},{... | collective-permute-start | bytes 393224 | tf_op jit(solution)/shard_map/ppermute | solution.py:470
  67.1 12.9 %collective-permute-start.36 = (bf16[1,256,512]{2,1,0:T(8,128)(2,1)S(1)}, bf16[1,256,512]{2,1,0:T(8,128)(2,1)S(1)}, u32[]{:S(2)}, u32[]{:S(2)}) collective-permute-start(bf16[1,256,512]{2,1,0:T(8,128)(2,1)S(1)} %bitcast.692), channel_id=1, source_target_pairs={{0,8},{4,12},{8,0},{12,4},{16,24},{20,28},{24,16},{28,20},{1,9},{5... | collective-permute-start | bytes 786440 | tf_op jit(solution)/shard_map/ppermute | solution.py:470
  69.4 17.0 %collective-permute-start.66 = (bf16[9,128,128]{2,1,0:T(8,128)(2,1)S(1)}, bf16[9,128,128]{2,1,0:T(8,128)(2,1)S(1)}, u32[]{:S(2)}, u32[]{:S(2)}) collective-permute-start(bf16[9,128,128]{2,1,0:T(8,128)(2,1)S(1)} %bitcast.671), channel_id=1, source_target_pairs={{0,8},{4,12},{8,0},{12,4},{16,24},{20,28},{24,16},{28,20},{1,9},{5... | collective-permute-start | bytes 884744 | tf_op jit(solution)/shard_map/ppermute | solution.py:470
  71.6 19.0 %collective-permute-start.16 = (bf16[9,128,128]{2,1,0:T(8,128)(2,1)S(1)}, bf16[9,128,128]{2,1,0:T(8,128)(2,1)S(1)}, u32[]{:S(2)}, u32[]{:S(2)}) collective-permute-start(bf16[9,128,128]{2,1,0:T(8,128)(2,1)S(1)} %bitcast.673), channel_id=1, source_target_pairs={{0,8},{4,12},{8,0},{12,4},{16,24},{20,28},{24,16},{28,20},{1,9},{5... | collective-permute-start | bytes 884744 | tf_op jit(solution)/shard_map/ppermute | solution.py:470
  74.4 18.3 %collective-permute-start.52 = (bf16[1,1024,128]{2,1,0:T(8,128)(2,1)S(1)}, bf16[1,1024,128]{2,1,0:T(8,128)(2,1)S(1)}, u32[]{:S(2)}, u32[]{:S(2)}) collective-permute-start(bf16[1,1024,128]{2,1,0:T(8,128)(2,1)S(1)} %bitcast.695), channel_id=1, source_target_pairs={{0,4},{4,0},{8,12},{12,8},{16,20},{20,16},{24,28},{28,24},{1,5},{5... | collective-permute-start | bytes 786440 | tf_op jit(solution)/shard_map/ppermute | solution.py:470
  76.1 18.5 %collective-permute-start.32 = (bf16[1,1024,128]{2,1,0:T(8,128)(2,1)S(1)}, bf16[1,1024,128]{2,1,0:T(8,128)(2,1)S(1)}, u32[]{:S(2)}, u32[]{:S(2)}) collective-permute-start(bf16[1,1024,128]{2,1,0:T(8,128)(2,1)S(1)} %bitcast.696), channel_id=1, source_target_pairs={{0,4},{4,0},{8,12},{12,8},{16,20},{20,16},{24,28},{28,24},{1,5},{5... | collective-permute-start | bytes 786440 | tf_op jit(solution)/shard_map/ppermute | solution.py:470
  80.0 15.1 %collective-permute-start.82 = (bf16[1,1024,128]{2,1,0:T(8,128)(2,1)S(1)}, bf16[1,1024,128]{2,1,0:T(8,128)(2,1)S(1)}, u32[]{:S(2)}, u32[]{:S(2)}) collective-permute-start(bf16[1,1024,128]{2,1,0:T(8,128)(2,1)S(1)} %bitcast.693), channel_id=1, source_target_pairs={{0,2},{1,3},{2,0},{3,1},{4,6},{5,7},{6,4},{7,5},{8,10},{9,11},{10,... | collective-permute-start | bytes 786440 | tf_op jit(solution)/shard_map/ppermute | solution.py:470
  86.4 11.3 %collective-permute-start.3 = (bf16[1,1024,128]{2,1,0:T(8,128)(2,1)S(1)}, bf16[1,1024,128]{2,1,0:T(8,128)(2,1)S(1)}, u32[]{:S(2)}, u32[]{:S(2)}) collective-permute-start(bf16[1,1024,128]{2,1,0:T(8,128)(2,1)S(1)} %bitcast.694), channel_id=1, source_target_pairs={{0,2},{1,3},{2,0},{3,1},{4,6},{5,7},{6,4},{7,5},{8,10},{9,11},{10,... | collective-permute-start | bytes 786440 | tf_op jit(solution)/shard_map/ppermute | solution.py:470
  90.6 14.9 %collective-permute-start.37 = (bf16[1,512,512]{2,1,0:T(8,128)(2,1)S(1)}, bf16[1,512,512]{2,1,0:T(8,128)(2,1)S(1)}, u32[]{:S(2)}, u32[]{:S(2)}) collective-permute-start(bf16[1,512,512]{2,1,0:T(8,128)(2,1)S(1)} %bitcast.660), channel_id=1, source_target_pairs={{0,2},{1,3},{2,0},{3,1},{4,6},{5,7},{6,4},{7,5},{8,10},{9,11},{10,... | collective-permute-start | bytes 1572872 | tf_op jit(solution)/shard_map/ppermute | solution.py:470
  92.8 57.4 %collective-permute-start.17 = (bf16[9,256,128]{2,1,0:T(8,128)(2,1)}, bf16[9,256,128]{2,1,0:T(8,128)(2,1)}, u32[]{:S(2)}, u32[]{:S(2)}) collective-permute-start(bf16[9,256,128]{2,1,0:T(8,128)(2,1)} %bitcast.41), channel_id=1, source_target_pairs={{0,2},{1,3},{2,0},{3,1},{4,6},{5,7},{6,4},{7,5},{8,10},{9,11},{10,... | collective-permute-start | bytes 1769480 | tf_op jit(solution)/shard_map/ppermute | solution.py:470
  94.6 45.9 %collective-permute-start.53 = (bf16[1,2048,128]{2,1,0:T(8,128)(2,1)S(1)}, bf16[1,2048,128]{2,1,0:T(8,128)(2,1)S(1)}, u32[]{:S(2)}, u32[]{:S(2)}) collective-permute-start(bf16[1,2048,128]{2,1,0:T(8,128)(2,1)S(1)} %bitcast.661), channel_id=1, source_target_pairs={{0,2},{1,3},{2,0},{3,1},{4,6},{5,7},{6,4},{7,5},{8,10},{9,11},{10,... | collective-permute-start | bytes 1572872 | tf_op jit(solution)/shard_map/ppermute | solution.py:470
  95.1 44.0 %collective-permute-start.33 = (bf16[1,2048,128]{2,1,0:T(8,128)(2,1)S(1)}, bf16[1,2048,128]{2,1,0:T(8,128)(2,1)S(1)}, u32[]{:S(2)}, u32[]{:S(2)}) collective-permute-start(bf16[1,2048,128]{2,1,0:T(8,128)(2,1)S(1)} %bitcast.662), channel_id=1, source_target_pairs={{0,2},{1,3},{2,0},{3,1},{4,6},{5,7},{6,4},{7,5},{8,10},{9,11},{10,... | collective-permute-start | bytes 1572872 | tf_op jit(solution)/shard_map/ppermute | solution.py:470
  98.7 46.7 %collective-permute-start.4 = (bf16[1,1024,256]{2,1,0:T(8,128)(2,1)}, bf16[1,1024,256]{2,1,0:T(8,128)(2,1)}, u32[]{:S(2)}, u32[]{:S(2)}) collective-permute-start(bf16[1,1024,256]{2,1,0:T(8,128)(2,1)} %pad_maximum_fusion.15), channel_id=1, source_target_pairs={{0,1},{1,0},{2,3},{3,2},{4,5},{5,4},{6,7},{7,6},{8,9},{9,8},{10,11... | collective-permute-start | bytes 1572872 | tf_op jit(solution)/shard_map/ppermute | solution.py:470
  162.5 51.0 %collective-permute-start.38 = (bf16[1,512,1024]{2,1,0:T(8,128)(2,1)S(1)}, bf16[1,512,1024]{2,1,0:T(8,128)(2,1)S(1)}, u32[]{:S(2)}, u32[]{:S(2)}) collective-permute-start(bf16[1,512,1024]{2,1,0:T(8,128)(2,1)S(1)} %copy-done.113), channel_id=1, source_target_pairs={{0,4},{4,0},{8,12},{12,8},{16,20},{20,16},{24,28},{28,24},{1,5},{5... | collective-permute-start | bytes 3145736 | tf_op jit(solution)/shard_map/ppermute | solution.py:470
  163.9 47.9 %collective-permute-start.18 = (bf16[9,256,256]{2,1,0:T(8,128)(2,1)S(1)}, bf16[9,256,256]{2,1,0:T(8,128)(2,1)S(1)}, u32[]{:S(2)}, u32[]{:S(2)}) collective-permute-start(bf16[9,256,256]{2,1,0:T(8,128)(2,1)S(1)} %pad_maximum_fusion.6), channel_id=1, source_target_pairs={{0,4},{4,0},{8,12},{12,8},{16,20},{20,16},{24,28},{28,24},{1,5},{5... | collective-permute-start | bytes 3538952 | tf_op jit(solution)/shard_map/ppermute | solution.py:470
  215.3 11.3 %collective-permute-start.39 = (bf16[1,1024,1024]{2,1,0:T(8,128)(2,1)S(1)}, bf16[1,1024,1024]{2,1,0:T(8,128)(2,1)S(1)}, u32[]{:S(2)}, u32[]{:S(2)}) collective-permute-start(bf16[1,1024,1024]{2,1,0:T(8,128)(2,1)S(1)} %bitcast.618), channel_id=1, source_target_pairs={{0,1},{1,0},{2,3},{3,2},{4,5},{5,4},{6,7},{7,6},{8,9},{9,8},{10,11... | collective-permute-start | bytes 6291464 | tf_op jit(solution)/shard_map/ppermute | solution.py:470
  237.3 13.5 %collective-permute-start.67 = (bf16[9,256,128]{2,1,0:T(8,128)(2,1)S(1)}, bf16[9,256,128]{2,1,0:T(8,128)(2,1)S(1)}, u32[]{:S(2)}, u32[]{:S(2)}) collective-permute-start(bf16[9,256,128]{2,1,0:T(8,128)(2,1)S(1)} %bitcast.642), channel_id=1, source_target_pairs={{0,4},{4,0},{8,12},{12,8},{16,20},{20,16},{24,28},{28,24},{1,5},{5... | collective-permute-start | bytes 1769480 | tf_op jit(solution)/shard_map/ppermute | solution.py:470
  261.3 19.2 %collective-permute-start.54 = (bf16[1,2048,256]{2,1,0:T(8,128)(2,1)S(1)}, bf16[1,2048,256]{2,1,0:T(8,128)(2,1)S(1)}, u32[]{:S(2)}, u32[]{:S(2)}) collective-permute-start(bf16[1,2048,256]{2,1,0:T(8,128)(2,1)S(1)} %pad_maximum_fusion.10), channel_id=1, source_target_pairs={{0,1},{1,0},{2,3},{3,2},{4,5},{5,4},{6,7},{7,6},{8,9},{9,8},{10,11... | collective-permute-start | bytes 3145736 | tf_op jit(solution)/shard_map/ppermute | solution.py:470
  261.4 29.6 %collective-permute-start.68 = (bf16[9,512,128]{2,1,0:T(8,128)(2,1)S(1)}, bf16[9,512,128]{2,1,0:T(8,128)(2,1)S(1)}, u32[]{:S(2)}, u32[]{:S(2)}) collective-permute-start(bf16[9,512,128]{2,1,0:T(8,128)(2,1)S(1)} %bitcast.635), channel_id=1, source_target_pairs={{0,2},{1,3},{2,0},{3,1},{4,6},{5,7},{6,4},{7,5},{8,10},{9,11},{10,... | collective-permute-start | bytes 3538952 | tf_op jit(solution)/shard_map/ppermute | solution.py:470
  301.8 19.1 %collective-permute-start.83 = (bf16[1,1024,256]{2,1,0:T(8,128)(2,1)}, bf16[1,1024,256]{2,1,0:T(8,128)(2,1)}, u32[]{:S(2)}, u32[]{:S(2)}) collective-permute-start(bf16[1,1024,256]{2,1,0:T(8,128)(2,1)} %pad_maximum_fusion.19), channel_id=1, source_target_pairs={{0,4},{4,0},{8,12},{12,8},{16,20},{20,16},{24,28},{28,24},{1,5},{5... | collective-permute-start | bytes 1572872 | tf_op jit(solution)/shard_map/ppermute | solution.py:470
  314.5 43.8 %all-to-all-start.2 = ((bf16[512,4,176]{0,2,1:T(8,128)(2,1)}), bf16[512,4,176]{0,2,1:T(8,128)(2,1)}, u32[]{:S(2)}, u32[]{:S(2)}) async-start(bf16[512,4,176]{0,2,1:T(8,128)(2,1)} %bitcast.703), calls=%async_computation.2 | async-start | bytes 1441792 | tf_op jit(solution)/shard_map/all_to_all | solution.py:728
  348.1 11.6 %collective-permute-start.90 = (f32[32,128]{1,0:T(8,128)}, f32[32,128]{1,0:T(8,128)}, u32[]{:S(2)}, u32[]{:S(2)}) collective-permute-start(f32[32,128]{1,0:T(8,128)} %add_add_fusion.8), channel_id=1, source_target_pairs={{0,12},{4,8},{8,4},{12,0},{16,28},{20,24},{24,20},{28,16},{1,13},{... | collective-permute-start | bytes 49160 | tf_op jit(solution)/shard_map/ppermute | solution.py:470
  375.5 13.0 %collective-permute-start.102 = (f32[32,128]{1,0:T(8,128)}, f32[32,128]{1,0:T(8,128)}, u32[]{:S(2)}, u32[]{:S(2)}) collective-permute-start(f32[32,128]{1,0:T(8,128)} %add_add_fusion.6), channel_id=1, source_target_pairs={{0,20},{4,16},{8,28},{12,24},{16,4},{20,0},{24,12},{28,8},{1,21},{... | collective-permute-start | bytes 49160 | tf_op jit(solution)/shard_map/ppermute | solution.py:470
  376.0 12.6 %collective-permute-start.103 = (f32[32,128]{1,0:T(8,128)}, f32[32,128]{1,0:T(8,128)}, u32[]{:S(2)}, u32[]{:S(2)}) collective-permute-start(f32[32,128]{1,0:T(8,128)} %add_add_fusion.6), channel_id=1, source_target_pairs={{0,24},{4,28},{8,16},{12,20},{16,8},{20,12},{24,0},{28,4},{1,25},{... | collective-permute-start | bytes 49160 | tf_op jit(solution)/shard_map/ppermute | solution.py:470
  384.3 347.4 %all-to-all-start.1 = ((bf16[4,512,176]{1,2,0:T(8,128)(2,1)}), bf16[4,512,176]{1,2,0:T(8,128)(2,1)}, u32[]{:S(2)}, u32[]{:S(2)}) async-start(bf16[4,512,176]{1,2,0:T(8,128)(2,1)} %bitcast.640), calls=%async_computation.1 | async-start | bytes 1441792 | tf_op jit(solution)/shard_map/all_to_all | solution.py:763
  406.3 17.7 %collective-permute-start.110 = (f32[8,128]{1,0:T(8,128)}, f32[8,128]{1,0:T(8,128)}, u32[]{:S(2)}, u32[]{:S(2)}) collective-permute-start(f32[8,128]{1,0:T(8,128)} %add_add_fusion.18), channel_id=1, source_target_pairs={{0,12},{4,8},{8,4},{12,0},{16,28},{20,24},{24,20},{28,16},{1,13},{... | collective-permute-start | bytes 12296 | tf_op jit(solution)/shard_map/ppermute | solution.py:470
  407.0 17.1 %collective-permute-start.111 = (f32[8,128]{1,0:T(8,128)}, f32[8,128]{1,0:T(8,128)}, u32[]{:S(2)}, u32[]{:S(2)}) collective-permute-start(f32[8,128]{1,0:T(8,128)} %add_add_fusion.18), channel_id=1, source_target_pairs={{0,16},{4,20},{8,24},{12,28},{16,0},{20,4},{24,8},{28,12},{1,17},{... | collective-permute-start | bytes 12296 | tf_op jit(solution)/shard_map/ppermute | solution.py:470
  409.3 14.8 %collective-permute-start.112 = (f32[8,128]{1,0:T(8,128)}, f32[8,128]{1,0:T(8,128)}, u32[]{:S(2)}, u32[]{:S(2)}) collective-permute-start(f32[8,128]{1,0:T(8,128)} %add_add_fusion.18), channel_id=1, source_target_pairs={{0,20},{4,16},{8,28},{12,24},{16,4},{20,0},{24,12},{28,8},{1,21},{... | collective-permute-start | bytes 12296 | tf_op jit(solution)/shard_map/ppermute | solution.py:470
  410.7 13.4 %collective-permute-start.113 = (f32[8,128]{1,0:T(8,128)}, f32[8,128]{1,0:T(8,128)}, u32[]{:S(2)}, u32[]{:S(2)}) collective-permute-start(f32[8,128]{1,0:T(8,128)} %add_add_fusion.18), channel_id=1, source_target_pairs={{0,24},{4,28},{8,16},{12,20},{16,8},{20,12},{24,0},{28,4},{1,25},{... | collective-permute-start | bytes 12296 | tf_op jit(solution)/shard_map/ppermute | solution.py:470
  412.8 11.3 %collective-permute-start.114 = (f32[8,128]{1,0:T(8,128)}, f32[8,128]{1,0:T(8,128)}, u32[]{:S(2)}, u32[]{:S(2)}) collective-permute-start(f32[8,128]{1,0:T(8,128)} %add_add_fusion.18), channel_id=1, source_target_pairs={{0,28},{4,24},{8,20},{12,16},{16,12},{20,8},{24,4},{28,0},{1,29},{... | collective-permute-start | bytes 12296 | tf_op jit(solution)/shard_map/ppermute | solution.py:470
  485.4 11.6 %collective-permute-start.135 = (f32[8,128]{1,0:T(8,128)S(1)}, f32[8,128]{1,0:T(8,128)S(1)}, u32[]{:S(2)}, u32[]{:S(2)}) collective-permute-start(f32[8,128]{1,0:T(8,128)S(1)} %pad_maximum_fusion.63), channel_id=1, source_target_pairs={{0,1},{1,0},{2,3},{3,2},{4,5},{5,4},{6,7},{7,6},{8,9},{9,8},{10,11... | collective-permute-start | bytes 12296 | tf_op jit(solution)/shard_map/ppermute | solution.py:470
  485.5 11.6 %collective-permute-start.136 = (f32[8,128]{1,0:T(8,128)S(1)}, f32[8,128]{1,0:T(8,128)S(1)}, u32[]{:S(2)}, u32[]{:S(2)}) collective-permute-start(f32[8,128]{1,0:T(8,128)S(1)} %pad_maximum_fusion.63), channel_id=1, source_target_pairs={{0,2},{1,3},{2,0},{3,1},{4,6},{5,7},{6,4},{7,5},{8,10},{9,11},{10,... | collective-permute-start | bytes 12296 | tf_op jit(solution)/shard_map/ppermute | solution.py:470
  539.0 12.5 %collective-permute-start.150 = (f32[8,128]{1,0:T(8,128)S(1)}, f32[8,128]{1,0:T(8,128)S(1)}, u32[]{:S(2)}, u32[]{:S(2)}) collective-permute-start(f32[8,128]{1,0:T(8,128)S(1)} %add_add_fusion.12), channel_id=1, source_target_pairs={{0,12},{4,8},{8,4},{12,0},{16,28},{20,24},{24,20},{28,16},{1,13},{... | collective-permute-start | bytes 12296 | tf_op jit(solution)/shard_map/ppermute | solution.py:470
  551.5 27.1 %collective-permute-start.180 = (bf16[1,2048,256]{2,1,0:T(8,128)(2,1)}, bf16[1,2048,256]{2,1,0:T(8,128)(2,1)}, u32[]{:S(2)}, u32[]{:S(2)}) collective-permute-start(bf16[1,2048,256]{2,1,0:T(8,128)(2,1)} %fusion.4), channel_id=1, source_target_pairs={{0,1},{1,0},{2,3},{3,2},{4,5},{5,4},{6,7},{7,6},{8,9},{9,8},{10,11... | collective-permute-start | bytes 3145736 | tf_op jit(solution)/shard_map/ppermute | solution.py:470
  551.5 89.2 %collective-permute-start.170 = (bf16[9,512,256]{2,1,0:T(8,128)(2,1)}, bf16[9,512,256]{2,1,0:T(8,128)(2,1)}, u32[]{:S(2)}, u32[]{:S(2)}) collective-permute-start(bf16[9,512,256]{2,1,0:T(8,128)(2,1)} %bitcast.232), channel_id=1, source_target_pairs={{0,1},{1,0},{2,3},{3,2},{4,5},{5,4},{6,7},{7,6},{8,9},{9,8},{10,11... | collective-permute-start | bytes 7077896 | tf_op jit(solution)/shard_map/ppermute | solution.py:470
  552.0 37.5 %collective-permute-start.185 = (bf16[1,2048,256]{2,1,0:T(8,128)(2,1)}, bf16[1,2048,256]{2,1,0:T(8,128)(2,1)}, u32[]{:S(2)}, u32[]{:S(2)}) collective-permute-start(bf16[1,2048,256]{2,1,0:T(8,128)(2,1)} %fusion.5), channel_id=1, source_target_pairs={{0,1},{1,0},{2,3},{3,2},{4,5},{5,4},{6,7},{7,6},{8,9},{9,8},{10,11... | collective-permute-start | bytes 3145736 | tf_op jit(solution)/shard_map/ppermute | solution.py:470
  552.1 45.4 %collective-permute-start.175 = (bf16[1,2048,256]{2,1,0:T(8,128)(2,1)}, bf16[1,2048,256]{2,1,0:T(8,128)(2,1)}, u32[]{:S(2)}, u32[]{:S(2)}) collective-permute-start(bf16[1,2048,256]{2,1,0:T(8,128)(2,1)} %fusion.3), channel_id=1, source_target_pairs={{0,1},{1,0},{2,3},{3,2},{4,5},{5,4},{6,7},{7,6},{8,9},{9,8},{10,11... | collective-permute-start | bytes 3145736 | tf_op jit(solution)/shard_map/ppermute | solution.py:470
  577.4 60.7 %collective-permute-start.160 = (bf16[1,1024,1024]{2,1,0:T(8,128)(2,1)}, bf16[1,1024,1024]{2,1,0:T(8,128)(2,1)}, u32[]{:S(2)}, u32[]{:S(2)}) collective-permute-start(bf16[1,1024,1024]{2,1,0:T(8,128)(2,1)} %convert_bitcast_fusion), channel_id=1, source_target_pairs={{0,1},{1,0},{2,3},{3,2},{4,5},{5,4},{6,7},{7,6},{8,9},{9,8},{10,11... | collective-permute-start | bytes 6291464 | tf_op jit(solution)/shard_map/ppermute | solution.py:470
  588.0 60.7 %collective-permute-start.165 = (bf16[9,512,256]{2,1,0:T(8,128)(2,1)}, bf16[9,512,256]{2,1,0:T(8,128)(2,1)S(1)}, u32[]{:S(2)}, u32[]{:S(2)}) collective-permute-start(bf16[9,512,256]{2,1,0:T(8,128)(2,1)} %bitcast.843), channel_id=1, source_target_pairs={{0,1},{1,0},{2,3},{3,2},{4,5},{5,4},{6,7},{7,6},{8,9},{9,8},{10,11... | collective-permute-start | bytes 7077896 | tf_op jit(solution)/shard_map/ppermute | solution.py:470
  594.4 13.6 %collective-permute-start.181 = (bf16[1,2,2,1,256,256]{4,5,3,2,1,0:T(8,128)(2,1)}, bf16[1,2,2,1,256,256]{4,5,3,2,1,0:T(8,128)(2,1)}, u32[]{:S(2)}, u32[]{:S(2)}) collective-permute-start(bf16[1,2,2,1,256,256]{4,5,3,2,1,0:T(8,128)(2,1)} %add_convert_fusion.6), channel_id=1, source_target_pairs={{0,4},{4,0},{8,12},{12,8},{16,20},{20,16},{24,28},{28,24},{1,5},{5... | collective-permute-start | bytes 1572872 | tf_op jit(solution)/shard_map/ppermute | solution.py:470
  597.5 19.6 %collective-permute-start.186 = (bf16[1,2,2,2,256,128]{5,4,3,2,1,0:T(8,128)(2,1)}, bf16[1,2,2,2,256,128]{5,4,3,2,1,0:T(8,128)(2,1)}, u32[]{:S(2)}, u32[]{:S(2)}) collective-permute-start(bf16[1,2,2,2,256,128]{5,4,3,2,1,0:T(8,128)(2,1)} %add_convert_fusion.5), channel_id=1, source_target_pairs={{0,2},{1,3},{2,0},{3,1},{4,6},{5,7},{6,4},{7,5},{8,10},{9,11},{10,... | collective-permute-start | bytes 1572872 | tf_op jit(solution)/shard_map/ppermute | solution.py:470
  608.0 15.8 %collective-permute-start.176 = (bf16[1,2,2,2,256,128]{4,5,3,2,1,0:T(8,128)(2,1)}, bf16[1,2,2,2,256,128]{4,5,3,2,1,0:T(8,128)(2,1)}, u32[]{:S(2)}, u32[]{:S(2)}) collective-permute-start(bf16[1,2,2,2,256,128]{4,5,3,2,1,0:T(8,128)(2,1)} %add_convert_fusion.7), channel_id=1, source_target_pairs={{0,2},{1,3},{2,0},{3,1},{4,6},{5,7},{6,4},{7,5},{8,10},{9,11},{10,... | collective-permute-start | bytes 1572872 | tf_op jit(solution)/shard_map/ppermute | solution.py:470
  631.3 12.5 %collective-permute-start.183 = (bf16[1,2,1,1,256,128]{4,5,3,2,1,0:T(8,128)(2,1)S(1)}, bf16[1,2,1,1,256,128]{4,5,3,2,1,0:T(8,128)(2,1)S(1)}, u32[]{:S(2)}, u32[]{:S(2)}) collective-permute-start(bf16[1,2,1,1,256,128]{4,5,3,2,1,0:T(8,128)(2,1)S(1)} %add_convert_fusion.19), channel_id=1, source_target_pairs={{0,8},{4,12},{8,0},{12,4},{16,24},{20,28},{24,16},{28,20},{1,9},{5... | collective-permute-start | bytes 393224 | tf_op jit(solution)/shard_map/ppermute | solution.py:470
  638.1 15.8 %collective-permute-start.178 = (bf16[1,2,1,1,256,128]{4,5,3,2,1,0:T(8,128)(2,1)S(1)}, bf16[1,2,1,1,256,128]{4,5,3,2,1,0:T(8,128)(2,1)S(1)}, u32[]{:S(2)}, u32[]{:S(2)}) collective-permute-start(bf16[1,2,1,1,256,128]{4,5,3,2,1,0:T(8,128)(2,1)S(1)} %add_convert_fusion.20), channel_id=1, source_target_pairs={{0,8},{4,12},{8,0},{12,4},{16,24},{20,28},{24,16},{28,20},{1,9},{5... | collective-permute-start | bytes 393224 | tf_op jit(solution)/shard_map/ppermute | solution.py:470
  640.7 26.2 %collective-permute-start.161 = (bf16[1,2,2,1,128,1024]{5,4,3,2,1,0:T(8,128)(2,1)S(1)}, bf16[1,2,2,1,128,1024]{5,4,3,2,1,0:T(8,128)(2,1)S(1)}, u32[]{:S(2)}, u32[]{:S(2)}) collective-permute-start(bf16[1,2,2,1,128,1024]{5,4,3,2,1,0:T(8,128)(2,1)S(1)} %add_convert_fusion.2), channel_id=1, source_target_pairs={{0,4},{4,0},{8,12},{12,8},{16,20},{20,16},{24,28},{28,24},{1,5},{5... | collective-permute-start | bytes 3145736 | tf_op jit(solution)/shard_map/ppermute | solution.py:470
  643.8 28.7 %collective-permute-start.171 = (bf16[9,2,2,2,64,128]{5,4,0,3,2,1:T(8,128)(2,1)S(1)}, bf16[9,2,2,2,64,128]{5,4,0,3,2,1:T(8,128)(2,1)S(1)}, u32[]{:S(2)}, u32[]{:S(2)}) collective-permute-start(bf16[9,2,2,2,64,128]{5,4,0,3,2,1:T(8,128)(2,1)S(1)} %add_convert_fusion), channel_id=1, source_target_pairs={{0,2},{1,3},{2,0},{3,1},{4,6},{5,7},{6,4},{7,5},{8,10},{9,11},{10,... | collective-permute-start | bytes 3538952 | tf_op jit(solution)/shard_map/ppermute | solution.py:470
  648.8 20.4 %collective-permute-start.189 = (bf16[1,1,1,1,256,128]{5,4,3,2,1,0:T(8,128)(2,1)S(1)}, bf16[1,1,1,1,256,128]{5,4,3,2,1,0:T(8,128)(2,1)S(1)}, u32[]{:S(2)}, u32[]{:S(2)}) collective-permute-start(bf16[1,1,1,1,256,128]{5,4,3,2,1,0:T(8,128)(2,1)S(1)} %add_convert_fusion.23), channel_id=1, source_target_pairs={{0,16},{4,20},{8,24},{12,28},{16,0},{20,4},{24,8},{28,12},{1,17},{... | collective-permute-start | bytes 196616 | tf_op jit(solution)/shard_map/ppermute | solution.py:470
  651.2 41.0 %collective-permute-start.166 = (bf16[9,2,2,1,64,256]{5,4,3,2,1,0:T(8,128)(2,1)S(1)}, bf16[9,2,2,1,64,256]{5,4,3,2,1,0:T(8,128)(2,1)S(1)}, u32[]{:S(2)}, u32[]{:S(2)}) collective-permute-start(bf16[9,2,2,1,64,256]{5,4,3,2,1,0:T(8,128)(2,1)S(1)} %add_convert_fusion.1), channel_id=1, source_target_pairs={{0,4},{4,0},{8,12},{12,8},{16,20},{20,16},{24,28},{28,24},{1,5},{5... | collective-permute-start | bytes 3538952 | tf_op jit(solution)/shard_map/ppermute | solution.py:470
  654.8 20.7 %collective-permute-start.179 = (bf16[1,1,1,1,256,128]{4,5,3,2,1,0:T(8,128)(2,1)S(1)}, bf16[1,1,1,1,256,128]{4,5,3,2,1,0:T(8,128)(2,1)S(1)}, u32[]{:S(2)}, u32[]{:S(2)}) collective-permute-start(bf16[1,1,1,1,256,128]{4,5,3,2,1,0:T(8,128)(2,1)S(1)} %add_convert_fusion.25), channel_id=1, source_target_pairs={{0,16},{4,20},{8,24},{12,28},{16,0},{20,4},{24,8},{28,12},{1,17},{... | collective-permute-start | bytes 196616 | tf_op jit(solution)/shard_map/ppermute | solution.py:470
  668.5 24.8 %collective-permute-start.162 = (bf16[1,2,2,1,128,512]{5,4,3,2,1,0:T(8,128)(2,1)S(1)}, bf16[1,2,2,1,128,512]{5,4,3,2,1,0:T(8,128)(2,1)S(1)}, u32[]{:S(2)}, u32[]{:S(2)}) collective-permute-start(bf16[1,2,2,1,128,512]{5,4,3,2,1,0:T(8,128)(2,1)S(1)} %add_convert_fusion.8), channel_id=1, source_target_pairs={{0,2},{1,3},{2,0},{3,1},{4,6},{5,7},{6,4},{7,5},{8,10},{9,11},{10,... | collective-permute-start | bytes 1572872 | tf_op jit(solution)/shard_map/ppermute | solution.py:470
  674.4 27.7 %collective-permute-start.172 = (bf16[9,2,2,1,64,128]{5,4,0,3,2,1:T(8,128)(2,1)S(1)}, bf16[9,2,2,1,64,128]{5,4,0,3,2,1:T(8,128)(2,1)S(1)}, u32[]{:S(2)}, u32[]{:S(2)}) collective-permute-start(bf16[9,2,2,1,64,128]{5,4,0,3,2,1:T(8,128)(2,1)S(1)} %add_convert_fusion.3), channel_id=1, source_target_pairs={{0,4},{4,0},{8,12},{12,8},{16,20},{20,16},{24,28},{28,24},{1,5},{5... | collective-permute-start | bytes 1769480 | tf_op jit(solution)/shard_map/ppermute | solution.py:470
  692.7 14.9 %collective-permute-start.167 = (bf16[9,2,2,1,64,128]{5,4,3,2,1,0:T(8,128)(2,1)S(1)}, bf16[9,2,2,1,64,128]{5,4,3,2,1,0:T(8,128)(2,1)S(1)}, u32[]{:S(2)}, u32[]{:S(2)}) collective-permute-start(bf16[9,2,2,1,64,128]{5,4,3,2,1,0:T(8,128)(2,1)S(1)} %add_convert_fusion.4), channel_id=1, source_target_pairs={{0,2},{1,3},{2,0},{3,1},{4,6},{5,7},{6,4},{7,5},{8,10},{9,11},{10,... | collective-permute-start | bytes 1769480 | tf_op jit(solution)/shard_map/ppermute | solution.py:470
  703.4 14.1 %collective-permute-start.173 = (bf16[9,2,1,1,64,128]{5,4,0,3,2,1:T(8,128)(2,1)S(1)}, bf16[9,2,1,1,64,128]{5,4,0,3,2,1:T(8,128)(2,1)S(1)}, u32[]{:S(2)}, u32[]{:S(2)}) collective-permute-start(bf16[9,2,1,1,64,128]{5,4,0,3,2,1:T(8,128)(2,1)S(1)} %add_convert_fusion.9), channel_id=1, source_target_pairs={{0,8},{4,12},{8,0},{12,4},{16,24},{20,28},{24,16},{28,20},{1,9},{5... | collective-permute-start | bytes 884744 | tf_op jit(solution)/shard_map/ppermute | solution.py:470
  706.6 12.2 %collective-permute-start.164 = (bf16[1,1,1,1,128,512]{5,4,3,2,1,0:T(8,128)(2,1)S(1)}, bf16[1,1,1,1,128,512]{5,4,3,2,1,0:T(8,128)(2,1)S(1)}, u32[]{:S(2)}, u32[]{:S(2)}) collective-permute-start(bf16[1,1,1,1,128,512]{5,4,3,2,1,0:T(8,128)(2,1)S(1)} %add_convert_fusion.21), channel_id=1, source_target_pairs={{0,16},{4,20},{8,24},{12,28},{16,0},{20,4},{24,8},{28,12},{1,17},{... | collective-permute-start | bytes 393224 | tf_op jit(solution)/shard_map/ppermute | solution.py:470
  708.2 13.3 %collective-permute-start.168 = (bf16[9,2,1,1,64,128]{5,4,3,2,1,0:T(8,128)(2,1)S(1)}, bf16[9,2,1,1,64,128]{5,4,3,2,1,0:T(8,128)(2,1)S(1)}, u32[]{:S(2)}, u32[]{:S(2)}) collective-permute-start(bf16[9,2,1,1,64,128]{5,4,3,2,1,0:T(8,128)(2,1)S(1)} %add_convert_fusion.10), channel_id=1, source_target_pairs={{0,8},{4,12},{8,0},{12,4},{16,24},{20,28},{24,16},{28,20},{1,9},{5... | collective-permute-start | bytes 884744 | tf_op jit(solution)/shard_map/ppermute | solution.py:470
  731.8 43.4 %all-to-all-start.3 = ((bf16[1024,4,176]{2,1,0:T(4,128)(2,1)}), bf16[1024,4,176]{2,1,0:T(4,128)(2,1)S(1)}, u32[]{:S(2)}, u32[]{:S(2)}) async-start(bf16[1024,4,176]{2,1,0:T(4,128)(2,1)} %fusion.6), calls=%async_computation.3 | async-start | bytes 4194304 | tf_op jit(solution)/shard_map/all_to_all | solution.py:828
  762.7 14.9 %collective-permute-start.195 = (f32[1,128]{1,0:T(1,128)S(1)}, f32[1,128]{1,0:T(1,128)}, u32[]{:S(2)}, u32[]{:S(2)}) collective-permute-start(f32[1,128]{1,0:T(1,128)S(1)} %add_add_fusion.26), channel_id=1, source_target_pairs={{0,12},{4,8},{8,4},{12,0},{16,28},{20,24},{24,20},{28,16},{1,13},{... | collective-permute-start | bytes 1544 | tf_op jit(solution)/shard_map/ppermute | solution.py:470
  766.1 11.5 %collective-permute-start.196 = (f32[1,128]{1,0:T(1,128)S(1)}, f32[1,128]{1,0:T(1,128)}, u32[]{:S(2)}, u32[]{:S(2)}) collective-permute-start(f32[1,128]{1,0:T(1,128)S(1)} %add_add_fusion.26), channel_id=1, source_target_pairs={{0,16},{4,20},{8,24},{12,28},{16,0},{20,4},{24,8},{28,12},{1,17},{... | collective-permute-start | bytes 1544 | tf_op jit(solution)/shard_map/ppermute | solution.py:470
  (422 other events, 3707.6 us)

commit v2 on v1

--- a/solution.py
+++ b/solution.py
@@ -1,6 +1,10 @@
+import functools
+
 import jax
 import jax.numpy as jnp
 from jax import lax
+from jax.experimental import pallas as pl
+from jax.experimental.pallas import tpu as pltpu
 from jax.sharding import PartitionSpec as P
 
 HO = 16
@@ -490,10 +494,15 @@
 
 
 def everywhere(values):
+    if values.shape[0] <= 16:
+        count = lax.axis_size("dp") * lax.axis_size("mp")
+        copies = jnp.broadcast_to(values[None], (count,) + values.shape)
+        return jnp.sum(lax.all_to_all(copies, ("dp", "mp"), 0, 0, tiled=True), 0)
     for axis in ("mp", "dp"):
-        values = tree_sum(
-            [values] + [swap(values, axis, mask) for mask in range(1, lax.axis_size(axis))]
-        )
+        mask = 1
+        while mask < lax.axis_size(axis):
+            values = values + swap(values, axis, mask)
+            mask *= 2
     return values
 
 
@@ -508,56 +517,218 @@
     return result
 
 
-def routes(late_rows):
-    rows = high_bits("dp")
-    columns = high_bits("mp")[:-1]
-    order = [("dp", mask) for mask in rows[:-1]]
-    last_row = [("dp", rows[-1])]
-    sides = [("mp", mask) for mask in reversed(columns)]
-    return order + (sides + last_row if late_rows else last_row + sides)
-
-
-def gather(block, late_rows):
-    lead, _, _ = block.shape
-    outer = 1
-    for axis, mask in routes(late_rows):
-        other = swap(block, axis, mask)
-        high = bit_of(axis, mask) > 0
-        first = jnp.where(high, other, block)
-        second = jnp.where(high, block, other)
-        if axis == "dp":
-            rows, cols = block.shape[1:]
-            pair = [part.reshape(lead, outer, rows // outer, cols) for part in (first, second)]
-            block = jnp.stack(pair, 2).reshape(lead, 2 * rows, cols)
-            outer *= 2
+def pack(block):
+    lead, rows, cols = block.shape
+    parts = block.reshape(lead, rows, cols // 128, 128).transpose(0, 2, 1, 3)
+    return parts.reshape(-1, 128)
+
+
+def column_bits():
+    return [("mp", mask) for mask in high_bits("mp")[:-1]]
+
+
+def row_bits():
+    return [("dp", mask) for mask in high_bits("dp")]
+
+
+def lanes_of(rows):
+    first = rows // 32 * 16
+    return ((0, first), (first, rows))
+
+
+def merge(mine, other, bit, dim):
+    high = bit_of(*bit) > 0
+    pair = [jnp.where(high, other, mine), jnp.where(high, mine, other)]
+    return jnp.concatenate(pair, dim)
+
+
+class Gather:
+    def __init__(self, rows, lanes=True):
+        self.bits = column_bits() + row_bits()
+        self.common = row_bits()[:-1]
+        near = row_bits()[-1:]
+        self.orders = [near + column_bits(), column_bits() + near]
+        if not lanes:
+            self.orders = self.orders[:1]
+        self.value = rows.reshape((1,) * len(self.bits) + rows.shape)
+        self.parts = None
+        self.step = 0
+
+    def operands(self):
+        if self.step < len(self.common):
+            return [self.value]
+        if self.step < len(self.common) + len(self.orders[0]):
+            if self.parts is None:
+                spans = lanes_of(self.value.shape[-2])
+                if len(self.orders) == 1:
+                    spans = ((0, self.value.shape[-2]),)
+                self.parts = [self.value[..., low:high, :] for low, high in spans]
+            return self.parts
+        if self.parts is not None:
+            self.value = jnp.concatenate(self.parts, -2)
+            self.parts = None
+        return [self.value]
+
+    def launch(self, operands):
+        if self.step < len(self.common):
+            bit = self.common[self.step]
+            self.value = merge(operands[0], swap(operands[0], *bit), bit, self.bits.index(bit))
+        elif self.step < len(self.common) + len(self.orders[0]):
+            bits = [order[self.step - len(self.common)] for order in self.orders]
+            self.parts = [
+                merge(part, swap(part, *bit), bit, self.bits.index(bit))
+                for part, bit in zip(operands, bits)
+            ]
         else:
-            block = jnp.concatenate([first, second], 2)
-    return (block, swap(block, "mp", 1))
-
-
-def scatter(keep, send, late_rows):
-    masks = high_bits("dp")
-    lead, rows, cols = keep.shape
-    unit = rows >> len(masks)
-    shape = (lead,) + (2,) * len(masks) + (unit, cols)
-    terms = [keep.reshape(shape), swap(send, "mp", 1).reshape(shape)]
-    for axis, mask in reversed(routes(late_rows)):
-        place = bit_of(axis, mask)
-        if axis == "dp":
-            dim = 1 + masks.index(mask)
-            size = 1
+            self.value = operands[0]
+            self.other = swap(operands[0], "mp", 1)
+        self.step += 1
+
+    def matrix(self, start, lead, units, columns):
+        columns = columns // 128
+        result = []
+        for value in (self.value, self.other):
+            value = value[..., start : start + lead * columns * units, :]
+            value = value.reshape(
+                1 << len(column_bits()), lax.axis_size("dp"), lead, columns, units, 128
+            )
+            value = value.transpose(2, 1, 4, 0, 3, 5)
+            result.append(value.reshape(lead * value.shape[1] * units, -1))
+        return result
+
+
+class Scatter:
+    def __init__(self, keep, send, lanes=True):
+        self.bits = column_bits() + row_bits()
+        shape = (2,) * len(self.bits) + keep.shape[2:]
+        self.keep = keep.reshape(shape)
+        self.send = send.reshape(shape)
+        self.orders = [column_bits() + row_bits()[-1:], row_bits()[-1:] + column_bits()]
+        if not lanes:
+            self.orders = self.orders[:1]
+        self.common = row_bits()[:-1][::-1]
+        rows = keep.shape[-2]
+        self.spans = lanes_of(rows) if lanes else ((0, rows),)
+        self.step = 0
+
+    def pick(self, term, bit, turn):
+        place = bit_of(*bit)
+        place = 1 - place if turn else place
+        return lax.dynamic_slice_in_dim(term, place, 1, self.bits.index(bit))
+
+    def total(self, terms):
+        result = terms[0].astype(jnp.float32)
+        for term in terms[1:]:
+            result = result + term.astype(jnp.float32)
+        return result
+
+    def operands(self):
+        step = self.step - 1
+        if step < 0:
+            return [self.send]
+        if step < len(self.orders[0]):
+            return [
+                self.total([self.pick(term, order[step], True) for term in lane]).astype(
+                    jnp.bfloat16
+                )
+                for lane, order in zip(self.lanes, self.orders)
+            ]
+        if step == len(self.orders[0]):
+            counts = [[lane[place] for lane in self.lanes] for place in range(len(self.lanes[0]))]
+            self.terms = [
+                jnp.concatenate(parts, -2) if len(parts) > 1 else parts[0] for parts in counts
+            ]
+        bit = self.common[step - len(self.orders[0])]
+        return [self.total([self.pick(term, bit, True) for term in self.terms]).astype(jnp.bfloat16)]
+
+    def launch(self, operands):
+        step = self.step - 1
+        if step < 0:
+            other = swap(operands[0], "mp", 1).reshape(self.keep.shape)
+            self.lanes = [
+                [term[..., low:high, :] for term in (self.keep, other)] for low, high in self.spans
+            ]
+        elif step < len(self.orders[0]):
+            for place, order in enumerate(self.orders):
+                arrived = swap(operands[place], *order[step])
+                self.lanes[place] = [
+                    self.pick(term, order[step], False) for term in self.lanes[place]
+                ] + [arrived]
         else:
-            dim = len(shape) - 1
-            size = terms[0].shape[dim] // 2
-
-        def pick(term, which):
-            return lax.dynamic_slice_in_dim(term, which * size, size, dim)
-
-        out = sum(pick(term, 1 - place).astype(jnp.float32) for term in terms)
-        arrived = swap(out.astype(jnp.bfloat16), axis, mask)
-        terms = [pick(term, place) for term in terms] + [arrived]
-    total = sum(term.astype(jnp.float32) for term in terms)
-    return total.reshape(lead, unit, -1)
+            bit = self.common[step - len(self.orders[0])]
+            arrived = swap(operands[0], *bit)
+            self.terms = [self.pick(term, bit, False) for term in self.terms] + [arrived]
+        self.step += 1
+
+    def rows(self):
+        total = self.total(self.terms)
+        return total.reshape(total.shape[-2:])
+
+
+def wave(flows, anchor=()):
+    operands = [flow.operands() for flow in flows]
+    anchor, operands = lax.optimization_barrier((anchor, operands))
+    for flow, values in zip(flows, operands):
+        flow.launch(values)
+    return anchor
+
+
+def unpack(rows, start, lead, units, columns):
+    count = lead * units * columns // 128
+    value = rows[start : start + count].reshape(lead, columns // 128, units, 128)
+    return value.transpose(0, 2, 1, 3).reshape(lead, units, columns)
+
+
+def chunk_kernel(units, columns, rows_ref, cols_ref, *refs):
+    outs = refs[-2:]
+    product = lax.dot_general(
+        rows_ref[...], cols_ref[...], (((0,), (0,)), ((), ())), preferred_element_type=jnp.float32
+    ).astype(jnp.bfloat16)
+    groups = outs[0].shape[0]
+    chunks = outs[0].shape[1]
+    for half, out in enumerate(outs):
+        for group in range(groups):
+            for part in range(columns):
+                place = ((half * groups + group) * columns + part) * 128
+                block = product[:, place : place + 128].reshape(chunks, units, 128)
+                out[group, :, part * units : (part + 1) * units, :] = block
+
+
+def chunks_into(bundle, total, start, rows_of, cols_of, lead, units, columns):
+    count = lax.axis_size("dp")
+    groups = 1 << len(column_bits())
+    columns = columns // 128
+    pixels = rows_of.shape[0]
+    height = units * columns
+    if lead > 1:
+        steps, wide, chunks = lead, count * units, count
+        place = lambda step: (0, 0, start // height + step, 0)
+    else:
+        steps, wide, chunks = count, units, 1
+        place = lambda step: (0, step, start // height, 0)
+    turned = jnp.concatenate(halves(cols_of), 1)
+    shape = jax.ShapeDtypeStruct((groups, count, total, 128), jnp.bfloat16)
+    block = pl.BlockSpec((groups, chunks, height, 128), place)
+    earlier = () if bundle is None else tuple(bundle)
+    return pl.pallas_call(
+        functools.partial(chunk_kernel, units, columns),
+        grid=(steps,),
+        in_specs=[
+            pl.BlockSpec((pixels, wide), lambda step: (0, step)),
+            pl.BlockSpec(turned.shape, lambda step: (0, 0)),
+        ]
+        + [pl.BlockSpec(memory_space=pl.ANY)] * len(earlier),
+        out_specs=[block, block],
+        out_shape=[shape, shape],
+        input_output_aliases={2 + place: place for place in range(len(earlier))},
+        compiler_params=pltpu.CompilerParams(vmem_limit_bytes=40 * 2**20),
+        cost_estimate=pl.CostEstimate(
+            flops=2 * rows_of.size * cols_of.shape[1],
+            bytes_accessed=2 * (rows_of.size + cols_of.size)
+            + 2 * rows_of.shape[1] * cols_of.shape[1],
+            transcendentals=0,
+        ),
+    )(rows_of, turned, *earlier)
 
 
 def halves(values):
@@ -598,12 +769,6 @@
     return parts[0] + parts[1]
 
 
-def outer_parts(rows_of, cols_of):
-    return [
-        dot(rows_of, part, ((0,), (0,))).astype(jnp.bfloat16) for part in halves(cols_of)
-    ]
-
-
 def reach(values, drow, dcol):
     offset = drow * WO + dcol
     count = values.shape[0]
@@ -634,10 +799,6 @@
                 total = total + reach(columns[:, tap * width : (tap + 1) * width], -drow, -dcol)
         blocks.append(total)
     return jnp.concatenate(blocks, 0)
-
-
-def flat_pair(pair):
-    return [part.reshape(-1, part.shape[-1]) for part in pair]
 
 
 def sums_of(values, mask):
@@ -696,20 +857,49 @@
     narrow = first_weight.shape[1] * ranks
     wide = shortcut_weight.shape[1] * ranks
     low = jnp.bfloat16
-    first_w = gather(first_weight.astype(low)[None], False)
-    mid_zero_w = gather(middle_weight[0].astype(low), True)
-    last_zero_w = gather(last_weight[0].astype(low).T[None], False)
-    short_w = gather(shortcut_weight.astype(low)[None], True)
-    second_w = gather(second_weight.astype(low)[None], False)
-    mid_one_w = gather(middle_weight[1].astype(low), False)
-    last_one_w = gather(last_weight[1].astype(low).T[None], True)
-    first_w, short_w, second_w, mid_zero_w, mid_one_w, last_zero_w, last_one_w = [
-        flat_pair(pair)
-        for pair in (first_w, short_w, second_w, mid_zero_w, mid_one_w, last_zero_w, last_one_w)
-    ]
-    tables = lax.all_gather(
-        jnp.concatenate([narrow_norms.reshape(-1, 128), wide_norms.reshape(-1, 128)], 0), "mp"
-    )
+    flow_a = Gather(pack(first_weight.astype(low)[None]), False)
+    flow_b = Gather(pack(middle_weight[0].astype(low)))
+    flow_c = Gather(
+        jnp.concatenate(
+            [
+                pack(shortcut_weight.astype(low)[None]),
+                pack(last_weight[0].astype(low).T[None]),
+                pack(second_weight.astype(low)[None]),
+            ]
+        )
+    )
+    flow_d = Gather(
+        jnp.concatenate(
+            [pack(last_weight[1].astype(low).T[None]), pack(middle_weight[1].astype(low))]
+        )
+    )
+    wave([flow_a])
+    wave([flow_a, flow_b])
+    wave([flow_a, flow_b])
+    wave([flow_a, flow_b, flow_c])
+    wave([flow_a, flow_b, flow_c])
+    wave([flow_b, flow_c, flow_d])
+    wave([flow_c, flow_d])
+    wave([flow_c, flow_d])
+    wave([flow_d])
+    wave([flow_d])
+    unit_in, column = first_weight.shape
+    column_wide = shortcut_weight.shape[1]
+    unit_mid = middle_weight.shape[2]
+    unit_out = second_weight.shape[0]
+    size_short = unit_in * column_wide // 128
+    size_out = unit_out * column // 128
+    size_mid = 9 * unit_mid * column // 128
+    first_w = flow_a.matrix(0, 1, unit_in, column)
+    mid_zero_w = flow_b.matrix(0, 9, unit_mid, column)
+    short_w = flow_c.matrix(0, 1, unit_in, column_wide)
+    last_zero_w = flow_c.matrix(size_short, 1, unit_out, column)
+    second_w = flow_c.matrix(size_short + size_out, 1, unit_out, column)
+    last_one_w = flow_d.matrix(0, 1, unit_out, column)
+    mid_one_w = flow_d.matrix(size_out, 9, unit_mid, column)
+    tables = jnp.concatenate([narrow_norms.reshape(-1, 128), wide_norms.reshape(-1, 128)], 0)
+    tables = jnp.broadcast_to(tables[None], (ranks,) + tables.shape)
+    tables = lax.all_to_all(tables, "mp", 0, 0, tiled=True)
     split = narrow_norms.size // 128
     narrow_all = (
         tables[:, :split].reshape(ranks, 4, 2, -1).transpose(1, 2, 0, 3).reshape(4, 2, narrow)
@@ -768,32 +958,38 @@
         grad_two, cen_six, scale_six, wide_all[2, 0], mask_out, sums_six, count_out
     )
     hid_five_grad = times(grad_six, last_one_w)
-    keep, send = outer_parts(grad_six, hid_five)
-    last_one_grad = scatter(keep[None], send[None], True)
     act_five_grad = hid_five_grad * keep_two * mask_out * slope(act_five)
+    total = size_out + size_mid
+    bundle = chunks_into(None, total, 0, grad_six, hid_five, 1, unit_out, column)
     sums_five = sum_all(grad_sums(act_five_grad, cen_five))
     grad_five = normed_back(
         act_five_grad, cen_five, scale_five, narrow_all[3, 0], mask_out, sums_five, count_out
     )
-    keep, send = outer_parts(cols_four, grad_five)
-    mid_one_grad = scatter(keep.reshape(9, narrow, -1), send.reshape(9, narrow, -1), False)
+    bundle = chunks_into(bundle, total, size_out, cols_four, grad_five, 9, unit_mid, column)
+    back_a = Scatter(*bundle)
+    grad_five = wave([back_a], grad_five)
     hid_four_grad = tap_back(times_turned(grad_five, mid_one_w), PLAIN_TAPS, narrow, 1)
     act_four_grad = hid_four_grad * keep_two * mask_out * slope(act_four)
-    sums_four = sum_all(grad_sums(act_four_grad, cen_four))
+    sums_four = sum_all(wave([back_a], grad_sums(act_four_grad, cen_four)))
     grad_four = normed_back(
         act_four_grad, cen_four, scale_four, narrow_all[2, 0], mask_out, sums_four, count_out
     )
-    keep, send = outer_parts(out_one, grad_four)
-    second_grad = scatter(keep[None], send[None], False)
     grad_one = (
         (grad_two + times_turned(grad_four, second_w)) * mask_out * slope(total_one)
     )
     gain_three, gain_side, bias_pair = sum_all(
-        [
-            jnp.sum(grad_one * cen_three, 0),
-            jnp.sum(grad_one * cen_side, 0),
-            jnp.sum(grad_one, 0),
-        ]
+        wave(
+            [back_a],
+            [
+                jnp.sum(grad_one * cen_three, 0),
+                jnp.sum(grad_one * cen_side, 0),
+                jnp.sum(grad_one, 0),
+            ],
+        )
+    )
+    total = size_short + 2 * size_out
+    bundle = chunks_into(
+        None, total, size_short + size_out, out_one, grad_four, 1, unit_out, column
     )
     grad_three = normed_back(
         grad_one, cen_three, scale_three, wide_all[0, 0], mask_out, (gain_three, bias_pair), count_out
@@ -801,38 +997,54 @@
     grad_side = normed_back(
         grad_one, cen_side, scale_side, wide_all[1, 0], mask_out, (gain_side, bias_pair), count_out
     )
+    bundle = chunks_into(bundle, total, size_short, grad_three, hid_two, 1, unit_out, column)
+    bundle = chunks_into(bundle, total, 0, field[:pixels], grad_side, 1, unit_in, column_wide)
+    back_b = Scatter(*bundle)
+    grad_three = wave([back_a, back_b], grad_three)
     hid_two_grad = times(grad_three, last_zero_w)
-    keep, send = outer_parts(grad_three, hid_two)
-    last_zero_grad = scatter(keep[None], send[None], False)
-    keep, send = outer_parts(field[:pixels], grad_side)
-    short_grad = scatter(keep[None], send[None], True)
     act_two_grad = hid_two_grad * keep_one * mask_out * slope(act_two)
-    sums_two = sum_all(grad_sums(act_two_grad, cen_two))
+    sums_two = sum_all(wave([back_a, back_b], grad_sums(act_two_grad, cen_two)))
     grad_mid = normed_back(
         act_two_grad, cen_two, scale_two, narrow_all[1, 0], mask_out, sums_two, count_out
     )
-    keep, send = outer_parts(cols_one, grad_mid)
-    mid_zero_grad = scatter(keep.reshape(9, narrow, -1), send.reshape(9, narrow, -1), True)
+    bundle = chunks_into(None, size_mid, 0, cols_one, grad_mid, 9, unit_mid, column)
+    back_c = Scatter(*bundle)
+    grad_mid = wave([back_c], grad_mid)
     hid_one_grad = tap_back(times_turned(grad_mid, mid_zero_w), STRIDED_TAPS, narrow, 4)
     act_one_grad = hid_one_grad * keep_one * mask_in * slope(act_one)
-    sums_one = sum_all(grad_sums(act_one_grad, cen_one))
+    sums_one = sum_all(wave([back_b, back_c], grad_sums(act_one_grad, cen_one)))
     grad_first = normed_back(
         act_one_grad, cen_one, scale_one, narrow_all[0, 0], mask_in, sums_one, count_in
     )
-    keep, send = outer_parts(field, grad_first)
-    first_grad = scatter(keep[None], send[None], False)
+    bundle = chunks_into(None, unit_in * column // 128, 0, field, grad_first, 1, unit_in, column)
+    back_d = Scatter(*bundle, False)
+    grad_first, grad_side = wave([back_b, back_c, back_d], (grad_first, grad_side))
     field_grad = times_turned(grad_first, first_w)
     side_grad = times_turned(grad_side, short_w)
     field_grad = jnp.concatenate([field_grad[:pixels] + side_grad, field_grad[pixels:]], 0)
     field_grad = (field_grad * mask_in).astype(low).reshape(4, pixels, -1).transpose(2, 0, 1)
     input_grad = lax.all_to_all(field_grad, "mp", split_axis=0, concat_axis=2, tiled=True)
-
+    wave([back_b, back_c, back_d])
+    wave([back_c, back_d])
+    wave([back_d])
+    wave([back_d])
+    rows_a, rows_b, rows_c, rows_d = [flow.rows() for flow in (back_a, back_b, back_c, back_d)]
     grads = (
-        first_grad[0],
-        short_grad[0],
-        jnp.stack([mid_zero_grad, mid_one_grad]),
-        jnp.stack([last_zero_grad[0].T, last_one_grad[0].T]),
-        second_grad[0],
+        unpack(rows_d, 0, 1, unit_in, column)[0],
+        unpack(rows_b, 0, 1, unit_in, column_wide)[0],
+        jnp.stack(
+            [
+                unpack(rows_c, 0, 9, unit_mid, column),
+                unpack(rows_a, size_out, 9, unit_mid, column),
+            ]
+        ),
+        jnp.stack(
+            [
+                unpack(rows_b, size_short, 1, unit_out, column)[0].T,
+                unpack(rows_a, 0, 1, unit_out, column)[0].T,
+            ]
+        ),
+        unpack(rows_b, size_short + size_out, 1, unit_out, column)[0],
     )
     first_fix = 1.0 - BETA_ONE**STEP
     second_fix = 1.0 - BETA_TWO**STEP
@@ -856,10 +1068,9 @@
         (weights[3][1], updates[3][1]),
         (weights[4], updates[4]),
     ]
-    own = [jnp.sum(value * value) for pair in pairs for value in pair]
-    own = jnp.concatenate([jnp.stack(own), jnp.zeros(128 - len(own), jnp.float32)])
-    (powers,) = sum_all([own])
-    matrix_norms = jnp.sqrt(powers[: 2 * len(pairs)].reshape(-1, 2))
+    own = [jnp.sum((value * value).reshape(-1, 128), 0) for pair in pairs for value in pair]
+    powers = jnp.sum(everywhere(jnp.stack(own)), 1)
+    matrix_norms = jnp.sqrt(powers.reshape(-1, 2))
     ratio = matrix_norms[:, 0] / (matrix_norms[:, 1] + EPS_TRUST)
     first_next = first_weight - RATE * ratio[0] * updates[0]
     short_next = shortcut_weight - RATE * ratio[1] * updates[1]

time: 800 us -> 719 us (0.90)
  starting transfers between devices: 251 us -> 138 us
  local copies, waits for them, and re-layouts: 97.5 us -> 175 us
  waiting for transfers between devices: 219 us -> 177 us
  Pallas kernels: 0 us -> 25.2 us
  matrix products: 45.9 us -> 25.6 us
  blocking collectives: 19.8 us -> 0 us
  other arithmetic: 148 us -> 157 us
    ppermute x200 -> x72, starting transfers between devices: 236 us -> 78.6 us  [swap(): lax.ppermute(values, axis, [(place, place ^ mask) for place in range(size)])]
    ppermute x200 -> x72, waiting for transfers between devices: 219 us -> 159 us  [swap(): lax.ppermute(values, axis, [(place, place ^ mask) for place in range(size)])]
    all_to_all x0 -> x10, starting transfers between devices: none -> 44.5 us  [the longest x9 40.2 us: everywhere(): return jnp.sum(lax.all_to_all(copies, ('dp', 'mp'), 0, 0, tiled=True), 0)]
    pallas_call x0 -> x7, Pallas kernels: none -> 25.2 us  [chunks_into(): pl.pallas_call(functools.partial(chunk_kernel, units, columns), grid=(ste...]
    slice x2 -> x19, local copies, waits for them, and re-layouts: 1.62 us -> 26.7 us  [the longest x8 18.1 us: matrix(): value = value[..., start:start + lead * columns * units, :]]
    reshape x0 -> x12, local copies, waits for them, and re-layouts: none -> 22.3 us  [the longest x10 21.3 us: matrix(): value.reshape(1 << len(column_bits()), lax.axis_size('dp'), lead, columns...]
    dot_general x42 -> x28, matrix products: 45.9 us -> 25.6 us  [dot(): lax.dot_general(first, second, (dims, ((), ())), preferred_element_type=j...]
    all_gather x1 -> x0, blocking collectives: 19.8 us -> none  [by_image(): lax.all_gather(jnp.concatenate([narrow_norms.reshape(-1, 128), wide_norms...]
  transfers between devices with their start and end apart: 204 -> 86, of which waited for: 54 -> 42; matrix products, arithmetic and copies ran while one was open for 32% -> 35% of each run, Pallas kernels for 0% -> 3%
where the time goes in v2:
time: 719 us; the launch traced here: 707 us
  waiting for transfers between devices  177 us (25%)
  local copies, waits for them, and re-layouts  175 us (24%)
  other arithmetic  157 us (22%)
  starting transfers between devices  138 us (19%)
  matrix products  25.6 us (4%)
  Pallas kernels  25.2 us (4%)
  between operations  8.34 us (1%)
    ppermute x72, waiting for transfers between devices, swap(): lax.ppermute(values, axis, [(place, place ^ mask) for place in range(size)])  159 us
    ppermute x72, starting transfers between devices, swap(): lax.ppermute(values, axis, [(place, place ^ mask) for place in range(size)])  78.6 us
    unnamed x626, local copies, waits for them, and re-layouts  52.2 us
    all_to_all x9, starting transfers between devices, everywhere(): return jnp.sum(lax.all_to_all(copies, ('dp', 'mp'), 0, 0, tiled=True), 0)  40.2 us
    dot_general x28, matrix products, dot(): lax.dot_general(first, second, (dims, ((), ())), preferred_element_type=j...  25.6 us
    pallas_call x7, Pallas kernels, chunks_into(): pl.pallas_call(functools.partial(chunk_kernel, units, columns), grid=(ste...  25.2 us
    convert_element_type x14, other arithmetic, operands(): self.total([self.pick(term, order[step], True) for term in lane])  22.7 us
    reshape x10, local copies, waits for them, and re-layouts, matrix(): value.reshape(1 << len(column_bits()), lax.axis_size('dp'), lead, columns...  21.3 us
  transfers between devices with their start and end apart: 86, of which 42 were waited for; matrix products, arithmetic and copies ran while one was open for 35% of the time, Pallas kernels for 3%

profile of v2, /device:TPU:0, one launch (start us, length us, event | category | flops | bytes accessed | tf_op | source)
XLA Modules:
  0.0 707.0 jit_solution(17470854778034104399)
XLA Ops:
  2.8 4.2 all-to-all-start.2
  7.8 3.1 collective-permute-start
  25.6 7.5 %collective-permute-done.2 = bf16[1,1,1,1,576,128]{5,4,3,2,1,0:T(8,128)(2,1)S(1)} collective-permute-done((bf16[1,1,1,1,576,128]{5,4,3,2,1,0:T(8,128)(2,1)S(1)}, bf16[1,1,1,1,576,128]{5,4,3,2,1,0:T(8,128)(2,1)S(1)}, u32[]{:S(2)}, u32[]{:S(2)}) %collective-permute-start.2) | collective-permute-done | bytes 147488 | tf_op jit(solution)/shard_map/ppermute | solution.py:474
  40.7 3.6 all-to-all-start
  44.4 9.3 %collective-permute-done.4 = bf16[1,2,1,1,576,128]{5,4,3,2,1,0:T(8,128)(2,1)S(1)} collective-permute-done((bf16[1,2,1,1,576,128]{5,4,3,2,1,0:T(8,128)(2,1)S(1)}, bf16[1,2,1,1,576,128]{5,4,3,2,1,0:T(8,128)(2,1)S(1)}, u32[]{:S(2)}, u32[]{:S(2)}) %collective-permute-start.4) | collective-permute-done | bytes 294944 | tf_op jit(solution)/shard_map/ppermute | solution.py:474
  58.5 9.7 %collective-permute-done.8 = bf16[1,1,1,1,1024,128]{5,4,3,2,1,0:T(8,128)(2,1)S(1)} collective-permute-done((bf16[1,1,1,1,1024,128]{5,4,3,2,1,0:T(8,128)(2,1)S(1)}, bf16[1,1,1,1,1024,128]{5,4,3,2,1,0:T(8,128)(2,1)S(1)}, u32[]{:S(2)}, u32[]{:S(2)}) %collective-permute-start.8) | collective-permute-done | bytes 262176 | tf_op jit(solution)/shard_map/ppermute | solution.py:474
  70.8 4.0 collective-permute-done.7
  80.9 2.9 all_to_all.83
  90.1 2.7 collective-permute-done.12
  101.3 5.3 all-to-all-start.1
  110.0 5.5 copy.266
  130.5 9.2 %collective-permute-done.19 = bf16[1,2,1,1,832,128]{5,4,3,2,1,0:T(8,128)(2,1)S(1)} collective-permute-done((bf16[1,2,1,1,832,128]{5,4,3,2,1,0:T(8,128)(2,1)S(1)}, bf16[1,2,1,1,832,128]{5,4,3,2,1,0:T(8,128)(2,1)S(1)}, u32[]{:S(2)}, u32[]{:S(2)}) %collective-permute-start.19) | collective-permute-done | bytes 426016 | tf_op jit(solution)/shard_map/ppermute | solution.py:474
  140.7 10.8 %collective-permute-done.18 = bf16[2,2,2,1,512,128]{5,4,3,2,1,0:T(8,128)(2,1)S(1)} collective-permute-done((bf16[2,2,2,1,512,128]{5,4,3,2,1,0:T(8,128)(2,1)S(1)}, bf16[2,2,2,1,512,128]{5,4,3,2,1,0:T(8,128)(2,1)S(1)}, u32[]{:S(2)}, u32[]{:S(2)}) %collective-permute-start.18) | collective-permute-done | bytes 1048608 | tf_op jit(solution)/shard_map/ppermute | solution.py:474
  152.3 2.4 maximum_maximum_fusion
  157.4 3.1 fusion.245
  162.3 2.6 copy.270
  172.6 4.2 copy.265
  179.2 4.1 all-to-all-start.3
  185.3 6.2 all-to-all-done.3
  195.8 3.1 slice.1171
  199.0 3.1 copy.269
  202.0 3.9 fusion.244
  205.9 2.6 copy.268
  219.3 19.2 %collective-permute-done.22 = f32[64,128]{1,0:T(8,128)S(1)} collective-permute-done((f32[64,128]{1,0:T(8,128)S(1)}, f32[64,128]{1,0:T(8,128)S(1)}, u32[]{:S(2)}, u32[]{:S(2)}) %collective-permute-start.22) | collective-permute-done | bytes 32800 | tf_op jit(solution)/shard_map/ppermute | solution.py:474
  244.6 2.8 broadcast_select_fusion.5
  248.7 2.7 broadcast_select_fusion.7
  251.5 2.6 copy.272
  261.6 3.3 all-to-all-start.4
  265.0 3.4 maximum_maximum_fusion.1
  270.7 3.8 copy.275
  286.3 5.9 all-to-all-start.5
  295.2 2.5 copy.321
  302.2 4.6 all-to-all-start.7
  325.7 2.6 collective-permute-start.35
  333.1 2.5 multiply_reduce_fusion.7
  348.0 2.6 collective-permute-start.40
  353.3 2.9 multiply_convert_fusion.4.rows_ref
  359.3 6.4 all-to-all-start.8
  367.6 2.4 shard_map.464
  379.4 3.5 shard_map.465
  394.3 3.9 all-to-all-start.9
  411.2 2.7 fusion.219
  413.9 8.5 %collective-permute-done.42 = bf16[1,2,2,2,416,128]{5,4,3,2,1,0:T(8,128)(2,1)} collective-permute-done((bf16[1,2,2,2,416,128]{5,4,3,2,1,0:T(8,128)(2,1)}, bf16[1,2,2,2,416,128]{5,4,3,2,1,0:T(8,128)(2,1)}, u32[]{:S(2)}, u32[]{:S(2)}) %collective-permute-start.42) | collective-permute-done | bytes 852000 | tf_op jit(solution)/shard_map/ppermute | solution.py:474
  427.9 2.5 collective-permute-done.45
  432.2 4.0 shard_map.466
  449.3 4.1 shard_map.467
  454.3 4.6 shard_map.468
  462.2 3.5 all-to-all-start.6
  471.6 5.1 all-to-all-done.6
  476.7 2.9 fusion.242
  485.1 7.4 %collective-permute-done.51 = bf16[1,2,1,1,832,128]{5,4,3,2,1,0:T(8,128)(2,1)S(1)} collective-permute-done((bf16[1,2,1,1,832,128]{5,4,3,2,1,0:T(8,128)(2,1)S(1)}, bf16[1,2,1,1,832,128]{5,4,3,2,1,0:T(8,128)(2,1)S(1)}, u32[]{:S(2)}, u32[]{:S(2)}) %collective-permute-start.51) | collective-permute-done | bytes 426016 | tf_op jit(solution)/shard_map/ppermute | solution.py:474
  493.8 2.7 fusion.243
  500.1 5.0 all-to-all-start.10
  514.4 6.4 collective-permute-done.71
  527.0 3.5 shard_map.469
  536.1 2.6 fusion.218
  548.5 3.8 all-to-all-start.11
  566.2 3.0 shard_map.470
  573.4 9.5 %collective-permute-done.58 = bf16[1,2,2,2,288,128]{5,4,3,2,1,0:T(8,128)(2,1)} collective-permute-done((bf16[1,2,2,2,288,128]{5,4,3,2,1,0:T(8,128)(2,1)}, bf16[1,2,2,2,288,128]{5,4,3,2,1,0:T(8,128)(2,1)}, u32[]{:S(2)}, u32[]{:S(2)}) %collective-permute-start.58) | collective-permute-done | bytes 589856 | tf_op jit(solution)/shard_map/ppermute | solution.py:474
  601.2 5.0 copy.280
  619.0 3.6 all-to-all-start.12
  625.2 4.1 collective-permute-done.69
  633.2 20.7 %collective-permute-done.64 = bf16[1,2,2,2,128,128]{5,4,3,2,1,0:T(8,128)(2,1)S(1)} collective-permute-done((bf16[1,2,2,2,128,128]{5,4,3,2,1,0:T(8,128)(2,1)}, bf16[1,2,2,2,128,128]{5,4,3,2,1,0:T(8,128)(2,1)S(1)}, u32[]{:S(2)}, u32[]{:S(2)}) %collective-permute-start.64) | collective-permute-done | bytes 262176 | tf_op jit(solution)/shard_map/ppermute | solution.py:474
  683.2 2.6 all-to-all-start.13
  (1156 shorter events, 390.0 us)
Async XLA Ops:
  2.8 37.9 %all-to-all-start.2 = ((f32[4,32,128]{2,1,0:T(8,128)}), f32[4,32,128]{2,1,0:T(8,128)S(1)}, u32[]{:S(2)}, u32[]{:S(2)}) async-start(f32[4,32,128]{2,1,0:T(8,128)} %broadcast_in_dim.311), calls=%async_computation.2 | async-start | bytes 131072 | tf_op jit(solution)/shard_map/all_to_all | solution.py:902
  7.8 13.4 %collective-permute-start = (bf16[1,1,1,1,128,128]{5,4,3,2,1,0:T(8,128)(2,1)S(1)}, bf16[1,1,1,1,128,128]{5,4,3,2,1,0:T(8,128)(2,1)S(1)}, u32[]{:S(2)}, u32[]{:S(2)}) collective-permute-start(bf16[1,1,1,1,128,128]{5,4,3,2,1,0:T(8,128)(2,1)S(1)} %convert_bitcast_fusion.1), channel_id=1, source_target_pairs={{0,16},{4,20},{8,24},{12,28},{16,0},{20,4},{24,8},{28,12},{1,17},{... | collective-permute-start | bytes 98312 | tf_op jit(solution)/shard_map/ppermute | solution.py:474
  23.5 9.6 %collective-permute-start.2 = (bf16[1,1,1,1,576,128]{5,4,3,2,1,0:T(8,128)(2,1)S(1)}, bf16[1,1,1,1,576,128]{5,4,3,2,1,0:T(8,128)(2,1)S(1)}, u32[]{:S(2)}, u32[]{:S(2)}) collective-permute-start(bf16[1,1,1,1,576,128]{5,4,3,2,1,0:T(8,128)(2,1)S(1)} %bitcast.595), channel_id=1, source_target_pairs={{0,16},{4,20},{8,24},{12,28},{16,0},{20,4},{24,8},{28,12},{1,17},{... | collective-permute-start | bytes 442376 | tf_op jit(solution)/shard_map/ppermute | solution.py:474
  33.2 11.1 %collective-permute-start.3 = (bf16[1,2,2,1,128,128]{5,4,3,2,1,0:T(8,128)(2,1)S(1)}, bf16[1,2,2,1,128,128]{5,4,3,2,1,0:T(8,128)(2,1)S(1)}, u32[]{:S(2)}, u32[]{:S(2)}) collective-permute-start(bf16[1,2,2,1,128,128]{5,4,3,2,1,0:T(8,128)(2,1)S(1)} %pad_maximum_fusion.45), channel_id=1, source_target_pairs={{0,4},{4,0},{8,12},{12,8},{16,20},{20,16},{24,28},{28,24},{1,5},{5... | collective-permute-start | bytes 393224 | tf_op jit(solution)/shard_map/ppermute | solution.py:474
  40.7 38.0 %all-to-all-start = ((bf16[256,4,704]{0,1,2:T(4,128)(2,1)}), bf16[256,4,704]{0,1,2:T(4,128)(2,1)S(1)}, u32[]{:S(2)}, u32[]{:S(2)}) async-start(bf16[256,4,704]{0,1,2:T(4,128)(2,1)} %copy.255), calls=%async_computation | async-start | bytes 2883584 | tf_op jit(solution)/shard_map/all_to_all | solution.py:916
  44.3 9.4 %collective-permute-start.4 = (bf16[1,2,1,1,576,128]{5,4,3,2,1,0:T(8,128)(2,1)S(1)}, bf16[1,2,1,1,576,128]{5,4,3,2,1,0:T(8,128)(2,1)S(1)}, u32[]{:S(2)}, u32[]{:S(2)}) collective-permute-start(bf16[1,2,1,1,576,128]{5,4,3,2,1,0:T(8,128)(2,1)S(1)} %pad_maximum_fusion.29), channel_id=1, source_target_pairs={{0,8},{4,12},{8,0},{12,4},{16,24},{20,28},{24,16},{28,20},{1,9},{5... | collective-permute-start | bytes 884744 | tf_op jit(solution)/shard_map/ppermute | solution.py:474
  53.8 14.4 %collective-permute-start.8 = (bf16[1,1,1,1,1024,128]{5,4,3,2,1,0:T(8,128)(2,1)S(1)}, bf16[1,1,1,1,1024,128]{5,4,3,2,1,0:T(8,128)(2,1)S(1)}, u32[]{:S(2)}, u32[]{:S(2)}) collective-permute-start(bf16[1,1,1,1,1024,128]{5,4,3,2,1,0:T(8,128)(2,1)S(1)} %maximum_bitcast_fusion), channel_id=1, source_target_pairs={{0,16},{4,20},{8,24},{12,28},{16,0},{20,4},{24,8},{28,12},{1,17},{... | collective-permute-start | bytes 786440 | tf_op jit(solution)/shard_map/ppermute | solution.py:474
  54.5 14.4 %collective-permute-start.5 = (bf16[1,2,2,2,128,128]{5,4,3,2,1,0:T(8,128)(2,1)S(1)}, bf16[1,2,2,2,128,128]{5,4,3,2,1,0:T(8,128)(2,1)S(1)}, u32[]{:S(2)}, u32[]{:S(2)}) collective-permute-start(bf16[1,2,2,2,128,128]{5,4,3,2,1,0:T(8,128)(2,1)S(1)} %pad_maximum_fusion.30), channel_id=1, source_target_pairs={{0,2},{1,3},{2,0},{3,1},{4,6},{5,7},{6,4},{7,5},{8,10},{9,11},{10,... | collective-permute-start | bytes 786440 | tf_op jit(solution)/shard_map/ppermute | solution.py:474
  57.6 13.1 %collective-permute-start.6 = (bf16[1,2,2,1,288,128]{5,4,3,2,1,0:T(8,128)(2,1)S(1)}, bf16[1,2,2,1,288,128]{5,4,3,2,1,0:T(8,128)(2,1)S(1)}, u32[]{:S(2)}, u32[]{:S(2)}) collective-permute-start(bf16[1,2,2,1,288,128]{5,4,3,2,1,0:T(8,128)(2,1)S(1)} %get-tuple-element.110), channel_id=1, source_target_pairs={{0,4},{4,0},{8,12},{12,8},{16,20},{20,16},{24,28},{28,24},{1,5},{5... | collective-permute-start | bytes 884744 | tf_op jit(solution)/shard_map/ppermute | solution.py:474
  58.1 16.7 %collective-permute-start.7 = (bf16[1,2,2,1,288,128]{5,4,3,2,1,0:T(8,128)(2,1)S(1)}, bf16[1,2,2,1,288,128]{5,4,3,2,1,0:T(8,128)(2,1)S(1)}, u32[]{:S(2)}, u32[]{:S(2)}) collective-permute-start(bf16[1,2,2,1,288,128]{5,4,3,2,1,0:T(8,128)(2,1)S(1)} %get-tuple-element.111), channel_id=1, source_target_pairs={{0,2},{1,3},{2,0},{3,1},{4,6},{5,7},{6,4},{7,5},{8,10},{9,11},{10,... | collective-permute-start | bytes 884744 | tf_op jit(solution)/shard_map/ppermute | solution.py:474
  75.7 10.8 %collective-permute-start.9 = (bf16[2,2,2,2,128,128]{5,4,3,2,1,0:T(8,128)(2,1)}, bf16[2,2,2,2,128,128]{5,4,3,2,1,0:T(8,128)(2,1)}, u32[]{:S(2)}, u32[]{:S(2)}) collective-permute-start(bf16[2,2,2,2,128,128]{5,4,3,2,1,0:T(8,128)(2,1)} %pad_maximum_fusion.13), channel_id=1, source_target_pairs={{0,1},{1,0},{2,3},{3,2},{4,5},{5,4},{6,7},{7,6},{8,9},{9,8},{10,11... | collective-permute-start | bytes 1572872 | tf_op jit(solution)/shard_map/ppermute | solution.py:474
  77.8 17.4 %collective-permute-start.11 = (bf16[2,2,2,1,288,128]{5,4,3,2,1,0:T(8,128)(2,1)}, bf16[2,2,2,1,288,128]{5,4,3,2,1,0:T(8,128)(2,1)}, u32[]{:S(2)}, u32[]{:S(2)}) collective-permute-start(bf16[2,2,2,1,288,128]{5,4,3,2,1,0:T(8,128)(2,1)} %pad_maximum_fusion.10), channel_id=1, source_target_pairs={{0,4},{4,0},{8,12},{12,8},{16,20},{20,16},{24,28},{28,24},{1,5},{5... | collective-permute-start | bytes 1769480 | tf_op jit(solution)/shard_map/ppermute | solution.py:474
  78.3 18.7 %collective-permute-start.10 = (bf16[1,2,2,2,288,128]{5,4,3,2,1,0:T(8,128)(2,1)S(1)}, bf16[1,2,2,2,288,128]{5,4,3,2,1,0:T(8,128)(2,1)}, u32[]{:S(2)}, u32[]{:S(2)}) collective-permute-start(bf16[1,2,2,2,288,128]{5,4,3,2,1,0:T(8,128)(2,1)S(1)} %pad_maximum_fusion.9), channel_id=1, source_target_pairs={{0,2},{1,3},{2,0},{3,1},{4,6},{5,7},{6,4},{7,5},{8,10},{9,11},{10,... | collective-permute-start | bytes 1769480 | tf_op jit(solution)/shard_map/ppermute | solution.py:474
  78.7 14.1 %collective-permute-start.12 = (bf16[1,2,1,1,1024,128]{5,4,3,2,1,0:T(8,128)(2,1)}, bf16[1,2,1,1,1024,128]{5,4,3,2,1,0:T(8,128)(2,1)}, u32[]{:S(2)}, u32[]{:S(2)}) collective-permute-start(bf16[1,2,1,1,1024,128]{5,4,3,2,1,0:T(8,128)(2,1)} %pad_maximum_fusion.14), channel_id=1, source_target_pairs={{0,8},{4,12},{8,0},{12,4},{16,24},{20,28},{24,16},{28,20},{1,9},{5... | collective-permute-start | bytes 1572872 | tf_op jit(solution)/shard_map/ppermute | solution.py:474
  99.9 15.6 %collective-permute-start.16 = (bf16[1,1,1,1,832,128]{5,4,3,2,1,0:T(8,128)(2,1)}, bf16[1,1,1,1,832,128]{5,4,3,2,1,0:T(8,128)(2,1)}, u32[]{:S(2)}, u32[]{:S(2)}) collective-permute-start(bf16[1,1,1,1,832,128]{5,4,3,2,1,0:T(8,128)(2,1)} %maximum_bitcast_fusion.1), channel_id=1, source_target_pairs={{0,16},{4,20},{8,24},{12,28},{16,0},{20,4},{24,8},{28,12},{1,17},{... | collective-permute-start | bytes 638984 | tf_op jit(solution)/shard_map/ppermute | solution.py:474
  101.3 17.6 %all-to-all-start.1 = ((f32[32,9,128]{2,1,0:T(8,128)}), f32[32,9,128]{2,1,0:T(8,128)}, u32[]{:S(2)}, u32[]{:S(2)}) async-start(f32[32,9,128]{2,1,0:T(8,128)} %broadcast_in_dim.310), calls=%async_computation.1 | async-start | bytes 524288 | tf_op jit(solution)/shard_map/all_to_all | solution.py:500
  106.6 17.6 %collective-permute-start.14 = (bf16[1,2,2,1,512,128]{5,4,3,2,1,0:T(8,128)(2,1)}, bf16[1,2,2,1,512,128]{5,4,3,2,1,0:T(8,128)(2,1)}, u32[]{:S(2)}, u32[]{:S(2)}) collective-permute-start(bf16[1,2,2,1,512,128]{5,4,3,2,1,0:T(8,128)(2,1)} %get-tuple-element.118), channel_id=1, source_target_pairs={{0,4},{4,0},{8,12},{12,8},{16,20},{20,16},{24,28},{28,24},{1,5},{5... | collective-permute-start | bytes 1572872 | tf_op jit(solution)/shard_map/ppermute | solution.py:474
  108.6 16.9 %collective-permute-start.15 = (bf16[1,2,2,1,512,128]{5,4,3,2,1,0:T(8,128)(2,1)S(1)}, bf16[1,2,2,1,512,128]{5,4,3,2,1,0:T(8,128)(2,1)}, u32[]{:S(2)}, u32[]{:S(2)}) collective-permute-start(bf16[1,2,2,1,512,128]{5,4,3,2,1,0:T(8,128)(2,1)S(1)} %copy-done.145), channel_id=1, source_target_pairs={{0,2},{1,3},{2,0},{3,1},{4,6},{5,7},{6,4},{7,5},{8,10},{9,11},{10,... | collective-permute-start | bytes 1572872 | tf_op jit(solution)/shard_map/ppermute | solution.py:474
  110.0 62.6 %collective-permute-start.13 = (bf16[2,2,2,2,576,128]{5,4,3,2,1,0:T(8,128)(2,1)}, bf16[2,2,2,2,576,128]{5,4,3,2,1,0:T(8,128)(2,1)}, u32[]{:S(2)}, u32[]{:S(2)}) collective-permute-start(bf16[2,2,2,2,576,128]{5,4,3,2,1,0:T(8,128)(2,1)} %maximum_maximum_fusion.2), channel_id=1, source_target_pairs={{0,1},{1,0},{2,3},{3,2},{4,5},{5,4},{6,7},{7,6},{8,9},{9,8},{10,11... | collective-permute-start | bytes 7077896 | tf_op jit(solution)/shard_map/ppermute | solution.py:474
  126.7 24.8 %collective-permute-start.18 = (bf16[2,2,2,1,512,128]{5,4,3,2,1,0:T(8,128)(2,1)S(1)}, bf16[2,2,2,1,512,128]{5,4,3,2,1,0:T(8,128)(2,1)S(1)}, u32[]{:S(2)}, u32[]{:S(2)}) collective-permute-start(bf16[2,2,2,1,512,128]{5,4,3,2,1,0:T(8,128)(2,1)S(1)} %pad_maximum_fusion.4), channel_id=1, source_target_pairs={{0,4},{4,0},{8,12},{12,8},{16,20},{20,16},{24,28},{28,24},{1,5},{5... | collective-permute-start | bytes 3145736 | tf_op jit(solution)/shard_map/ppermute | solution.py:474
  127.8 24.4 %collective-permute-start.17 = (bf16[1,2,2,2,512,128]{5,4,3,2,1,0:T(8,128)(2,1)S(1)}, bf16[1,2,2,2,512,128]{5,4,3,2,1,0:T(8,128)(2,1)S(1)}, u32[]{:S(2)}, u32[]{:S(2)}) collective-permute-start(bf16[1,2,2,2,512,128]{5,4,3,2,1,0:T(8,128)(2,1)S(1)} %pad_maximum_fusion.3), channel_id=1, source_target_pairs={{0,2},{1,3},{2,0},{3,1},{4,6},{5,7},{6,4},{7,5},{8,10},{9,11},{10,... | collective-permute-start | bytes 3145736 | tf_op jit(solution)/shard_map/ppermute | solution.py:474
  129.1 10.6 %collective-permute-start.19 = (bf16[1,2,1,1,832,128]{5,4,3,2,1,0:T(8,128)(2,1)S(1)}, bf16[1,2,1,1,832,128]{5,4,3,2,1,0:T(8,128)(2,1)S(1)}, u32[]{:S(2)}, u32[]{:S(2)}) collective-permute-start(bf16[1,2,1,1,832,128]{5,4,3,2,1,0:T(8,128)(2,1)S(1)} %copy-done.148), channel_id=1, source_target_pairs={{0,8},{4,12},{8,0},{12,4},{16,24},{20,28},{24,16},{28,20},{1,9},{5... | collective-permute-start | bytes 1277960 | tf_op jit(solution)/shard_map/ppermute | solution.py:474
  154.7 41.1 %collective-permute-start.20 = (bf16[2,2,2,2,1024,128]{5,4,3,2,1,0:T(8,128)(2,1)}, bf16[2,2,2,2,1024,128]{5,4,3,2,1,0:T(8,128)(2,1)}, u32[]{:S(2)}, u32[]{:S(2)}) collective-permute-start(bf16[2,2,2,2,1024,128]{5,4,3,2,1,0:T(8,128)(2,1)} %maximum_maximum_fusion), channel_id=1, source_target_pairs={{0,1},{1,0},{2,3},{3,2},{4,5},{5,4},{6,7},{7,6},{8,9},{9,8},{10,11... | collective-permute-start | bytes 12582920 | tf_op jit(solution)/shard_map/ppermute | solution.py:474
  156.1 14.3 %collective-permute-start.26 = (bf16[1,2,2,1,416,128]{5,4,3,2,1,0:T(8,128)(2,1)}, bf16[1,2,2,1,416,128]{5,4,3,2,1,0:T(8,128)(2,1)}, u32[]{:S(2)}, u32[]{:S(2)}) collective-permute-start(bf16[1,2,2,1,416,128]{5,4,3,2,1,0:T(8,128)(2,1)} %get-tuple-element.125), channel_id=1, source_target_pairs={{0,4},{4,0},{8,12},{12,8},{16,20},{20,16},{24,28},{28,24},{1,5},{5... | collective-permute-start | bytes 1277960 | tf_op jit(solution)/shard_map/ppermute | solution.py:474
  167.1 16.2 %collective-permute-start.27 = (bf16[1,2,2,1,416,128]{5,4,3,2,1,0:T(8,128)(2,1)}, bf16[1,2,2,1,416,128]{5,4,3,2,1,0:T(8,128)(2,1)}, u32[]{:S(2)}, u32[]{:S(2)}) collective-permute-start(bf16[1,2,2,1,416,128]{5,4,3,2,1,0:T(8,128)(2,1)} %get-tuple-element.126), channel_id=1, source_target_pairs={{0,2},{1,3},{2,0},{3,1},{4,6},{5,7},{6,4},{7,5},{8,10},{9,11},{10,... | collective-permute-start | bytes 1277960 | tf_op jit(solution)/shard_map/ppermute | solution.py:474
  179.2 12.3 %all-to-all-start.3 = ((f32[32,8,128]{2,1,0:T(8,128)}), f32[32,8,128]{2,1,0:T(8,128)S(1)}, u32[]{:S(2)}, u32[]{:S(2)}) async-start(f32[32,8,128]{2,1,0:T(8,128)} %broadcast_in_dim.315), calls=%async_computation.3 | async-start | bytes 262144 | tf_op jit(solution)/shard_map/all_to_all | solution.py:500
  216.1 28.5 %collective-permute-start.29 = (bf16[2,2,2,1,416,128]{5,4,3,2,1,0:T(8,128)(2,1)}, bf16[2,2,2,1,416,128]{5,4,3,2,1,0:T(8,128)(2,1)}, u32[]{:S(2)}, u32[]{:S(2)}) collective-permute-start(bf16[2,2,2,1,416,128]{5,4,3,2,1,0:T(8,128)(2,1)} %pad_maximum_fusion.6), channel_id=1, source_target_pairs={{0,4},{4,0},{8,12},{12,8},{16,20},{20,16},{24,28},{28,24},{1,5},{5... | collective-permute-start | bytes 2555912 | tf_op jit(solution)/shard_map/ppermute | solution.py:474
  216.6 32.2 %collective-permute-start.28 = (bf16[1,2,2,2,416,128]{5,4,3,2,1,0:T(8,128)(2,1)}, bf16[1,2,2,2,416,128]{5,4,3,2,1,0:T(8,128)(2,1)}, u32[]{:S(2)}, u32[]{:S(2)}) collective-permute-start(bf16[1,2,2,2,416,128]{5,4,3,2,1,0:T(8,128)(2,1)} %pad_maximum_fusion.5), channel_id=1, source_target_pairs={{0,2},{1,3},{2,0},{3,1},{4,6},{5,7},{6,4},{7,5},{8,10},{9,11},{10,... | collective-permute-start | bytes 2555912 | tf_op jit(solution)/shard_map/ppermute | solution.py:474
  217.3 21.2 %collective-permute-start.22 = (f32[64,128]{1,0:T(8,128)S(1)}, f32[64,128]{1,0:T(8,128)S(1)}, u32[]{:S(2)}, u32[]{:S(2)}) collective-permute-start(f32[64,128]{1,0:T(8,128)S(1)} %fusion.214), channel_id=1, source_target_pairs={{0,2},{1,3},{2,0},{3,1},{4,6},{5,7},{6,4},{7,5},{8,10},{9,11},{10,... | collective-permute-start | bytes 98312 | tf_op jit(solution)/shard_map/ppermute | solution.py:474
  247.9 7.9 %collective-permute-start.25 = (f32[64,128]{1,0:T(8,128)S(1)}, f32[64,128]{1,0:T(8,128)S(1)}, u32[]{:S(2)}, u32[]{:S(2)}) collective-permute-start(f32[64,128]{1,0:T(8,128)S(1)} %add.1807), channel_id=1, source_target_pairs={{0,16},{4,20},{8,24},{12,28},{16,0},{20,4},{24,8},{28,12},{1,17},{... | collective-permute-start | bytes 98312 | tf_op jit(solution)/shard_map/ppermute | solution.py:474
  261.6 12.9 %all-to-all-start.4 = ((f32[32,8,128]{2,1,0:T(8,128)}), f32[32,8,128]{2,1,0:T(8,128)S(1)}, u32[]{:S(2)}, u32[]{:S(2)}) async-start(f32[32,8,128]{2,1,0:T(8,128)} %broadcast_in_dim.316), calls=%async_computation.4 | async-start | bytes 262144 | tf_op jit(solution)/shard_map/all_to_all | solution.py:500
  270.2 9.5 %collective-permute-start.30 = (bf16[2,2,2,2,832,128]{5,4,3,2,1,0:T(8,128)(2,1)}, bf16[2,2,2,2,832,128]{5,4,3,2,1,0:T(8,128)(2,1)}, u32[]{:S(2)}, u32[]{:S(2)}) collective-permute-start(bf16[2,2,2,2,832,128]{5,4,3,2,1,0:T(8,128)(2,1)} %maximum_maximum_fusion.1), channel_id=1, source_target_pairs={{0,1},{1,0},{2,3},{3,2},{4,5},{5,4},{6,7},{7,6},{8,9},{9,8},{10,11... | collective-permute-start | bytes 10223624 | tf_op jit(solution)/shard_map/ppermute | solution.py:474
  286.3 15.9 %all-to-all-start.5 = ((f32[32,8,128]{2,1,0:T(8,128)}), f32[32,8,128]{2,1,0:T(8,128)}, u32[]{:S(2)}, u32[]{:S(2)}) async-start(f32[32,8,128]{2,1,0:T(8,128)} %broadcast_in_dim.322), calls=%async_computation.5 | async-start | bytes 262144 | tf_op jit(solution)/shard_map/all_to_all | solution.py:500
  302.2 26.1 %all-to-all-start.7 = ((bf16[512,4,176]{0,2,1:T(8,128)(2,1)}), bf16[512,4,176]{0,2,1:T(8,128)(2,1)}, u32[]{:S(2)}, u32[]{:S(2)}) async-start(bf16[512,4,176]{0,2,1:T(8,128)(2,1)} %bitcast.593), calls=%async_computation.7 | async-start | bytes 1441792 | tf_op jit(solution)/shard_map/all_to_all | solution.py:918
  359.3 14.6 %all-to-all-start.8 = ((f32[32,8,128]{2,1,0:T(8,128)}), f32[32,8,128]{2,1,0:T(8,128)}, u32[]{:S(2)}, u32[]{:S(2)}) async-start(f32[32,8,128]{2,1,0:T(8,128)} %broadcast_in_dim.323), calls=%async_computation.8 | async-start | bytes 262144 | tf_op jit(solution)/shard_map/all_to_all | solution.py:500
  394.3 12.2 %all-to-all-start.9 = ((f32[32,8,128]{2,1,0:T(8,128)}), f32[32,8,128]{2,1,0:T(8,128)}, u32[]{:S(2)}, u32[]{:S(2)}) async-start(f32[32,8,128]{2,1,0:T(8,128)} %broadcast_in_dim.324), calls=%async_computation.9 | async-start | bytes 262144 | tf_op jit(solution)/shard_map/all_to_all | solution.py:500
  400.4 22.0 %collective-permute-start.42 = (bf16[1,2,2,2,416,128]{5,4,3,2,1,0:T(8,128)(2,1)}, bf16[1,2,2,2,416,128]{5,4,3,2,1,0:T(8,128)(2,1)}, u32[]{:S(2)}, u32[]{:S(2)}) collective-permute-start(bf16[1,2,2,2,416,128]{5,4,3,2,1,0:T(8,128)(2,1)} %add_convert_fusion.3), channel_id=1, source_target_pairs={{0,2},{1,3},{2,0},{3,1},{4,6},{5,7},{6,4},{7,5},{8,10},{9,11},{10,... | collective-permute-start | bytes 2555912 | tf_op jit(solution)/shard_map/ppermute | solution.py:474
  402.4 21.5 %collective-permute-start.43 = (bf16[2,2,2,1,416,128]{5,4,3,2,1,0:T(8,128)(2,1)}, bf16[2,2,2,1,416,128]{5,4,3,2,1,0:T(8,128)(2,1)}, u32[]{:S(2)}, u32[]{:S(2)}) collective-permute-start(bf16[2,2,2,1,416,128]{5,4,3,2,1,0:T(8,128)(2,1)} %add_convert_fusion.2), channel_id=1, source_target_pairs={{0,4},{4,0},{8,12},{12,8},{16,20},{20,16},{24,28},{28,24},{1,5},{5... | collective-permute-start | bytes 2555912 | tf_op jit(solution)/shard_map/ppermute | solution.py:474
  436.2 22.7 %collective-permute-start.49 = (bf16[1,2,2,1,416,128]{5,4,3,2,1,0:T(8,128)(2,1)S(1)}, bf16[1,2,2,1,416,128]{5,4,3,2,1,0:T(8,128)(2,1)S(1)}, u32[]{:S(2)}, u32[]{:S(2)}) collective-permute-start(bf16[1,2,2,1,416,128]{5,4,3,2,1,0:T(8,128)(2,1)S(1)} %add_convert_fusion.11), channel_id=1, source_target_pairs={{0,4},{4,0},{8,12},{12,8},{16,20},{20,16},{24,28},{28,24},{1,5},{5... | collective-permute-start | bytes 1277960 | tf_op jit(solution)/shard_map/ppermute | solution.py:474
  436.6 22.4 %collective-permute-start.50 = (bf16[1,2,2,1,416,128]{5,4,3,2,1,0:T(8,128)(2,1)S(1)}, bf16[1,2,2,1,416,128]{5,4,3,2,1,0:T(8,128)(2,1)S(1)}, u32[]{:S(2)}, u32[]{:S(2)}) collective-permute-start(bf16[1,2,2,1,416,128]{5,4,3,2,1,0:T(8,128)(2,1)S(1)} %add_convert_fusion.10), channel_id=1, source_target_pairs={{0,2},{1,3},{2,0},{3,1},{4,6},{5,7},{6,4},{7,5},{8,10},{9,11},{10,... | collective-permute-start | bytes 1277960 | tf_op jit(solution)/shard_map/ppermute | solution.py:474
  461.3 32.5 %collective-permute-start.52 = (bf16[2,2,2,2,1024,128]{5,4,3,2,1,0:T(8,128)(2,1)}, bf16[2,2,2,2,1024,128]{5,4,3,2,1,0:T(8,128)(2,1)}, u32[]{:S(2)}, u32[]{:S(2)}) collective-permute-start(bf16[2,2,2,2,1024,128]{5,4,3,2,1,0:T(8,128)(2,1)} %bitcast.126), channel_id=1, source_target_pairs={{0,1},{1,0},{2,3},{3,2},{4,5},{5,4},{6,7},{7,6},{8,9},{9,8},{10,11... | collective-permute-start | bytes 12582920 | tf_op jit(solution)/shard_map/ppermute | solution.py:474
  462.2 14.4 %all-to-all-start.6 = ((bf16[4,512,176]{1,2,0:T(8,128)(2,1)}), bf16[4,512,176]{1,2,0:T(8,128)(2,1)S(1)}, u32[]{:S(2)}, u32[]{:S(2)}) async-start(bf16[4,512,176]{1,2,0:T(8,128)(2,1)} %bitcast.582), calls=%async_computation.6 | async-start | bytes 1441792 | tf_op jit(solution)/shard_map/all_to_all | solution.py:953
  481.1 11.4 %collective-permute-start.51 = (bf16[1,2,1,1,832,128]{5,4,3,2,1,0:T(8,128)(2,1)S(1)}, bf16[1,2,1,1,832,128]{5,4,3,2,1,0:T(8,128)(2,1)S(1)}, u32[]{:S(2)}, u32[]{:S(2)}) collective-permute-start(bf16[1,2,1,1,832,128]{5,4,3,2,1,0:T(8,128)(2,1)S(1)} %copy-done.180), channel_id=1, source_target_pairs={{0,8},{4,12},{8,0},{12,4},{16,24},{20,28},{24,16},{28,20},{1,9},{5... | collective-permute-start | bytes 1277960 | tf_op jit(solution)/shard_map/ppermute | solution.py:474
  500.1 23.5 %all-to-all-start.10 = ((f32[32,8,128]{2,1,0:T(8,128)}), f32[32,8,128]{2,1,0:T(8,128)}, u32[]{:S(2)}, u32[]{:S(2)}) async-start(f32[32,8,128]{2,1,0:T(8,128)} %broadcast_in_dim.325), calls=%async_computation.10 | async-start | bytes 262144 | tf_op jit(solution)/shard_map/all_to_all | solution.py:500
  505.1 33.7 %collective-permute-start.53 = (bf16[1,2,2,2,512,128]{5,4,3,2,1,0:T(8,128)(2,1)}, bf16[1,2,2,2,512,128]{5,4,3,2,1,0:T(8,128)(2,1)}, u32[]{:S(2)}, u32[]{:S(2)}) collective-permute-start(bf16[1,2,2,2,512,128]{5,4,3,2,1,0:T(8,128)(2,1)} %add_convert_fusion.1), channel_id=1, source_target_pairs={{0,2},{1,3},{2,0},{3,1},{4,6},{5,7},{6,4},{7,5},{8,10},{9,11},{10,... | collective-permute-start | bytes 3145736 | tf_op jit(solution)/shard_map/ppermute | solution.py:474
  506.8 36.2 %collective-permute-start.54 = (bf16[2,2,2,1,512,128]{5,4,3,2,1,0:T(8,128)(2,1)}, bf16[2,2,2,1,512,128]{5,4,3,2,1,0:T(8,128)(2,1)}, u32[]{:S(2)}, u32[]{:S(2)}) collective-permute-start(bf16[2,2,2,1,512,128]{5,4,3,2,1,0:T(8,128)(2,1)} %add_convert_fusion), channel_id=1, source_target_pairs={{0,4},{4,0},{8,12},{12,8},{16,20},{20,16},{24,28},{28,24},{1,5},{5... | collective-permute-start | bytes 3145736 | tf_op jit(solution)/shard_map/ppermute | solution.py:474
  508.3 12.5 %collective-permute-start.71 = (bf16[1,1,1,1,832,128]{5,4,3,2,1,0:T(8,128)(2,1)S(1)}, bf16[1,1,1,1,832,128]{5,4,3,2,1,0:T(8,128)(2,1)S(1)}, u32[]{:S(2)}, u32[]{:S(2)}) collective-permute-start(bf16[1,1,1,1,832,128]{5,4,3,2,1,0:T(8,128)(2,1)S(1)} %add_convert_fusion.17), channel_id=1, source_target_pairs={{0,16},{4,20},{8,24},{12,28},{16,0},{20,4},{24,8},{28,12},{1,17},{... | collective-permute-start | bytes 638984 | tf_op jit(solution)/shard_map/ppermute | solution.py:474
  533.3 12.1 %collective-permute-start.55 = (bf16[2,2,2,2,576,128]{5,4,3,2,1,0:T(8,128)(2,1)S(1)}, bf16[2,2,2,2,576,128]{5,4,3,2,1,0:T(8,128)(2,1)S(1)}, u32[]{:S(2)}, u32[]{:S(2)}) collective-permute-start(bf16[2,2,2,2,576,128]{5,4,3,2,1,0:T(8,128)(2,1)S(1)} %bitcast.532), channel_id=1, source_target_pairs={{0,1},{1,0},{2,3},{3,2},{4,5},{5,4},{6,7},{7,6},{8,9},{9,8},{10,11... | collective-permute-start | bytes 7077896 | tf_op jit(solution)/shard_map/ppermute | solution.py:474
  548.5 13.1 %all-to-all-start.11 = ((f32[32,8,128]{2,1,0:T(8,128)}), f32[32,8,128]{2,1,0:T(8,128)S(1)}, u32[]{:S(2)}, u32[]{:S(2)}) async-start(f32[32,8,128]{2,1,0:T(8,128)} %broadcast_in_dim.326), calls=%async_computation.11 | async-start | bytes 262144 | tf_op jit(solution)/shard_map/all_to_all | solution.py:500
  554.1 15.7 %collective-permute-start.56 = (bf16[1,2,2,1,512,128]{5,4,3,2,1,0:T(8,128)(2,1)}, bf16[1,2,2,1,512,128]{5,4,3,2,1,0:T(8,128)(2,1)}, u32[]{:S(2)}, u32[]{:S(2)}) collective-permute-start(bf16[1,2,2,1,512,128]{5,4,3,2,1,0:T(8,128)(2,1)} %add_convert_fusion.8), channel_id=1, source_target_pairs={{0,4},{4,0},{8,12},{12,8},{16,20},{20,16},{24,28},{28,24},{1,5},{5... | collective-permute-start | bytes 1572872 | tf_op jit(solution)/shard_map/ppermute | solution.py:474
  556.0 15.1 %collective-permute-start.57 = (bf16[1,2,2,1,512,128]{5,4,3,2,1,0:T(8,128)(2,1)}, bf16[1,2,2,1,512,128]{5,4,3,2,1,0:T(8,128)(2,1)}, u32[]{:S(2)}, u32[]{:S(2)}) collective-permute-start(bf16[1,2,2,1,512,128]{5,4,3,2,1,0:T(8,128)(2,1)} %add_convert_fusion.7), channel_id=1, source_target_pairs={{0,2},{1,3},{2,0},{3,1},{4,6},{5,7},{6,4},{7,5},{8,10},{9,11},{10,... | collective-permute-start | bytes 1572872 | tf_op jit(solution)/shard_map/ppermute | solution.py:474
  557.5 25.4 %collective-permute-start.58 = (bf16[1,2,2,2,288,128]{5,4,3,2,1,0:T(8,128)(2,1)}, bf16[1,2,2,2,288,128]{5,4,3,2,1,0:T(8,128)(2,1)}, u32[]{:S(2)}, u32[]{:S(2)}) collective-permute-start(bf16[1,2,2,2,288,128]{5,4,3,2,1,0:T(8,128)(2,1)} %add_convert_fusion.5), channel_id=1, source_target_pairs={{0,2},{1,3},{2,0},{3,1},{4,6},{5,7},{6,4},{7,5},{8,10},{9,11},{10,... | collective-permute-start | bytes 1769480 | tf_op jit(solution)/shard_map/ppermute | solution.py:474
  558.0 26.8 %collective-permute-start.59 = (bf16[2,2,2,1,288,128]{5,4,3,2,1,0:T(8,128)(2,1)}, bf16[2,2,2,1,288,128]{5,4,3,2,1,0:T(8,128)(2,1)}, u32[]{:S(2)}, u32[]{:S(2)}) collective-permute-start(bf16[2,2,2,1,288,128]{5,4,3,2,1,0:T(8,128)(2,1)} %add_convert_fusion.4), channel_id=1, source_target_pairs={{0,4},{4,0},{8,12},{12,8},{16,20},{20,16},{24,28},{28,24},{1,5},{5... | collective-permute-start | bytes 1769480 | tf_op jit(solution)/shard_map/ppermute | solution.py:474
  592.6 20.2 %collective-permute-start.60 = (bf16[2,2,2,2,128,128]{5,4,3,2,1,0:T(8,128)(2,1)S(1)}, bf16[2,2,2,2,128,128]{5,4,3,2,1,0:T(8,128)(2,1)}, u32[]{:S(2)}, u32[]{:S(2)}) collective-permute-start(bf16[2,2,2,2,128,128]{5,4,3,2,1,0:T(8,128)(2,1)S(1)} %bitcast.533), channel_id=1, source_target_pairs={{0,1},{1,0},{2,3},{3,2},{4,5},{5,4},{6,7},{7,6},{8,9},{9,8},{10,11... | collective-permute-start | bytes 1572872 | tf_op jit(solution)/shard_map/ppermute | solution.py:474
  592.7 18.0 %collective-permute-start.61 = (bf16[1,2,1,1,1024,128]{5,4,3,2,1,0:T(8,128)(2,1)}, bf16[1,2,1,1,1024,128]{5,4,3,2,1,0:T(8,128)(2,1)}, u32[]{:S(2)}, u32[]{:S(2)}) collective-permute-start(bf16[1,2,1,1,1024,128]{5,4,3,2,1,0:T(8,128)(2,1)} %add_convert_fusion.6), channel_id=1, source_target_pairs={{0,8},{4,12},{8,0},{12,4},{16,24},{20,28},{24,16},{28,20},{1,9},{5... | collective-permute-start | bytes 1572872 | tf_op jit(solution)/shard_map/ppermute | solution.py:474
  594.1 12.2 %collective-permute-start.62 = (bf16[1,2,2,1,288,128]{5,4,3,2,1,0:T(8,128)(2,1)}, bf16[1,2,2,1,288,128]{5,4,3,2,1,0:T(8,128)(2,1)}, u32[]{:S(2)}, u32[]{:S(2)}) collective-permute-start(bf16[1,2,2,1,288,128]{5,4,3,2,1,0:T(8,128)(2,1)} %add_convert_fusion.14), channel_id=1, source_target_pairs={{0,4},{4,0},{8,12},{12,8},{16,20},{20,16},{24,28},{28,24},{1,5},{5... | collective-permute-start | bytes 884744 | tf_op jit(solution)/shard_map/ppermute | solution.py:474
  594.8 12.4 %collective-permute-start.63 = (bf16[1,2,2,1,288,128]{5,4,3,2,1,0:T(8,128)(2,1)}, bf16[1,2,2,1,288,128]{5,4,3,2,1,0:T(8,128)(2,1)}, u32[]{:S(2)}, u32[]{:S(2)}) collective-permute-start(bf16[1,2,2,1,288,128]{5,4,3,2,1,0:T(8,128)(2,1)} %add_convert_fusion.13), channel_id=1, source_target_pairs={{0,2},{1,3},{2,0},{3,1},{4,6},{5,7},{6,4},{7,5},{8,10},{9,11},{10,... | collective-permute-start | bytes 884744 | tf_op jit(solution)/shard_map/ppermute | solution.py:474
  614.6 14.8 %collective-permute-start.69 = (bf16[1,1,1,1,1024,128]{5,4,3,2,1,0:T(8,128)(2,1)}, bf16[1,1,1,1,1024,128]{5,4,3,2,1,0:T(8,128)(2,1)}, u32[]{:S(2)}, u32[]{:S(2)}) collective-permute-start(bf16[1,1,1,1,1024,128]{5,4,3,2,1,0:T(8,128)(2,1)} %add_convert_fusion.16), channel_id=1, source_target_pairs={{0,16},{4,20},{8,24},{12,28},{16,0},{20,4},{24,8},{28,12},{1,17},{... | collective-permute-start | bytes 786440 | tf_op jit(solution)/shard_map/ppermute | solution.py:474
  619.0 63.5 %all-to-all-start.12 = ((bf16[1024,4,176]{2,1,0:T(4,128)(2,1)}), bf16[1024,4,176]{2,1,0:T(4,128)(2,1)S(1)}, u32[]{:S(2)}, u32[]{:S(2)}) async-start(bf16[1024,4,176]{2,1,0:T(4,128)(2,1)} %fusion.17), calls=%async_computation.12 | async-start | bytes 4194304 | tf_op jit(solution)/shard_map/all_to_all | solution.py:1026
  622.7 34.3 %collective-permute-start.65 = (bf16[1,2,1,1,576,128]{5,4,3,2,1,0:T(8,128)(2,1)}, bf16[1,2,1,1,576,128]{5,4,3,2,1,0:T(8,128)(2,1)S(1)}, u32[]{:S(2)}, u32[]{:S(2)}) collective-permute-start(bf16[1,2,1,1,576,128]{5,4,3,2,1,0:T(8,128)(2,1)} %add_convert_fusion.12), channel_id=1, source_target_pairs={{0,8},{4,12},{8,0},{12,4},{16,24},{20,28},{24,16},{28,20},{1,9},{5... | collective-permute-start | bytes 884744 | tf_op jit(solution)/shard_map/ppermute | solution.py:474
  623.2 30.7 %collective-permute-start.64 = (bf16[1,2,2,2,128,128]{5,4,3,2,1,0:T(8,128)(2,1)}, bf16[1,2,2,2,128,128]{5,4,3,2,1,0:T(8,128)(2,1)S(1)}, u32[]{:S(2)}, u32[]{:S(2)}) collective-permute-start(bf16[1,2,2,2,128,128]{5,4,3,2,1,0:T(8,128)(2,1)} %add_convert_fusion.15), channel_id=1, source_target_pairs={{0,2},{1,3},{2,0},{3,1},{4,6},{5,7},{6,4},{7,5},{8,10},{9,11},{10,... | collective-permute-start | bytes 786440 | tf_op jit(solution)/shard_map/ppermute | solution.py:474
  659.2 8.0 %collective-permute-start.66 = (bf16[1,2,2,1,128,128]{5,4,3,2,1,0:T(8,128)(2,1)}, bf16[1,2,2,1,128,128]{5,4,3,2,1,0:T(8,128)(2,1)}, u32[]{:S(2)}, u32[]{:S(2)}) collective-permute-start(bf16[1,2,2,1,128,128]{5,4,3,2,1,0:T(8,128)(2,1)} %add_convert_fusion.19), channel_id=1, source_target_pairs={{0,4},{4,0},{8,12},{12,8},{16,20},{20,16},{24,28},{28,24},{1,5},{5... | collective-permute-start | bytes 393224 | tf_op jit(solution)/shard_map/ppermute | solution.py:474
  660.7 9.4 %collective-permute-start.70 = (bf16[1,1,1,1,576,128]{5,4,3,2,1,0:T(8,128)(2,1)}, bf16[1,1,1,1,576,128]{5,4,3,2,1,0:T(8,128)(2,1)}, u32[]{:S(2)}, u32[]{:S(2)}) collective-permute-start(bf16[1,1,1,1,576,128]{5,4,3,2,1,0:T(8,128)(2,1)} %add_convert_fusion.18), channel_id=1, source_target_pairs={{0,16},{4,20},{8,24},{12,28},{16,0},{20,4},{24,8},{28,12},{1,17},{... | collective-permute-start | bytes 442376 | tf_op jit(solution)/shard_map/ppermute | solution.py:474
  683.2 13.2 %all-to-all-start.13 = ((f32[32,14,128]{2,1,0:T(8,128)}), f32[32,14,128]{2,1,0:T(8,128)S(1)}, u32[]{:S(2)}, u32[]{:S(2)}) async-start(f32[32,14,128]{2,1,0:T(8,128)} %broadcast_in_dim.327), calls=%async_computation.13 | async-start | bytes 524288 | tf_op jit(solution)/shard_map/all_to_all | solution.py:500
  (323 other events, 2935.2 us)

commit v3 on v0

--- a/solution.py
+++ b/solution.py
@@ -1,6 +1,10 @@
+import functools
+
 import jax
 import jax.numpy as jnp
 from jax import lax
+from jax.experimental import pallas as pl
+from jax.experimental.pallas import tpu as pltpu
 from jax.sharding import PartitionSpec as P
 
 HO = 16
@@ -459,6 +463,1212 @@
     )
 
 
+def fits(mesh, pixel_mask):
+    sizes = (mesh.shape["dp"], mesh.shape["mp"])
+    powers = all(size >= 2 and size & (size - 1) == 0 for size in sizes)
+    return powers and pixel_mask.shape[1] % (HO * WO * sizes[1]) == 0
+
+
+def swap(values, *bits):
+    sizes = {axis: lax.axis_size(axis) for axis in ("dp", "mp")}
+    masks = {axis: sum(mask for at, mask in bits if at == axis) for axis in sizes}
+    if not masks["dp"]:
+        return lax.ppermute(values, "mp", [(at, at ^ masks["mp"]) for at in range(sizes["mp"])])
+    if not masks["mp"]:
+        return lax.ppermute(values, "dp", [(at, at ^ masks["dp"]) for at in range(sizes["dp"])])
+    mask = masks["dp"] * sizes["mp"] + masks["mp"]
+    return lax.ppermute(
+        values, ("dp", "mp"), [(at, at ^ mask) for at in range(sizes["dp"] * sizes["mp"])]
+    )
+
+
+def subsets(bits):
+    return [
+        [bit for place, bit in enumerate(bits) if index >> place & 1]
+        for index in range(1 << len(bits))
+    ]
+
+
+def bit_of(axis, mask):
+    return (lax.axis_index(axis) & mask) // mask
+
+
+def high_bits(axis):
+    masks = []
+    mask = lax.axis_size(axis) // 2
+    while mask:
+        masks.append(mask)
+        mask //= 2
+    return masks
+
+
+def everywhere(values):
+    if values.shape[0] <= 16:
+        count = lax.axis_size("dp") * lax.axis_size("mp")
+        copies = jnp.broadcast_to(values[None], (count,) + values.shape)
+        return jnp.sum(lax.all_to_all(copies, ("dp", "mp"), 0, 0, tiled=True), 0)
+    for axis in ("mp", "dp"):
+        mask = 1
+        while mask < lax.axis_size(axis):
+            values = values + swap(values, (axis, mask))
+            mask *= 2
+    return values
+
+
+def pack(block):
+    lead, rows, cols = block.shape
+    parts = block.reshape(lead, rows, cols // 128, 128).transpose(0, 2, 1, 3)
+    return parts.reshape(-1, 128)
+
+
+def column_bits():
+    return [("mp", mask) for mask in high_bits("mp")[:-1]]
+
+
+def row_bits():
+    return [("dp", mask) for mask in high_bits("dp")]
+
+
+def lanes_of(rows):
+    first = rows // 32 * 16
+    return ((0, first), (first, rows))
+
+
+def merged(parts, bits, dims):
+    if not bits:
+        return parts[0]
+    high = bit_of(*bits[-1]) > 0
+    half = len(parts) // 2
+    first = [jnp.where(high, parts[half + at], parts[at]) for at in range(half)]
+    second = [jnp.where(high, parts[at], parts[half + at]) for at in range(half)]
+    pair = [merged(first, bits[:-1], dims), merged(second, bits[:-1], dims)]
+    return jnp.concatenate(pair, dims.index(bits[-1]))
+
+
+class Gather:
+    def __init__(self, rows, lanes=True):
+        self.dims = column_bits() + row_bits()
+        near = row_bits()[-1:]
+        if lanes:
+            self.steps = [[row_bits()[:-1]], [near, column_bits()], [column_bits(), near]]
+            self.spans = lanes_of(rows.shape[0])
+        else:
+            self.steps = [[row_bits()[:-1]], [near + column_bits()]]
+            self.spans = ((0, rows.shape[0]),)
+        self.parts = [([rows.reshape((1,) * len(self.dims) + rows.shape)], [])]
+        self.step = 0
+
+    def pending(self):
+        return [values for values, bits in self.parts]
+
+    def resume(self, values):
+        self.parts = [(value, bits) for value, (_, bits) in zip(values, self.parts)]
+
+    def launch(self):
+        values = [merged(parts, bits, self.dims) for parts, bits in self.parts]
+        if self.step < len(self.steps):
+            groups = self.steps[self.step]
+            if len(groups) > len(values):
+                values = [values[0][..., low:high, :] for low, high in self.spans]
+            self.parts = [
+                ([value] + [swap(value, *bits) for bits in subsets(group)[1:]], group)
+                for value, group in zip(values, groups)
+            ]
+        else:
+            value = jnp.concatenate(values, -2) if len(values) > 1 else values[0]
+            self.parts = [([value, swap(value, ("mp", 1))], [])]
+        self.step += 1
+
+    def bundles(self):
+        shape = (1 << len(column_bits()), lax.axis_size("dp")) + self.parts[0][0][0].shape[-2:]
+        return [value.reshape(shape) for value in self.parts[0][0]]
+
+
+class Scatter:
+    def __init__(self, keep, send, lanes=True):
+        self.dims = column_bits() + row_bits()
+        shape = (2,) * len(self.dims) + keep.shape[2:]
+        near = row_bits()[-1:]
+        far = row_bits()[:-1]
+        if lanes:
+            self.steps = [None, [column_bits(), near], [near, column_bits()], [far, far]]
+            self.spans = lanes_of(keep.shape[2])
+        else:
+            self.steps = [None, [column_bits() + near], [far]]
+            self.spans = (None,)
+        self.lanes = [[] for _ in self.spans]
+        self.raw = [keep.reshape(shape), send.reshape(shape)]
+        self.step = 0
+
+    def pending(self):
+        return self.raw
+
+    def resume(self, values):
+        self.raw = list(values)
+
+    def fold(self, lane, group=(), turned=()):
+        total = 0.0
+        for index, settled, span in self.lanes[lane]:
+            value = self.raw[index]
+            for bit in settled + list(group):
+                place = bit_of(*bit)
+                place = 1 - place if bit in turned else place
+                value = lax.dynamic_slice_in_dim(value, place, 1, self.dims.index(bit))
+            if span is not None:
+                value = value[..., span[0] : span[1], :]
+            total = total + value.astype(jnp.float32)
+        return total
+
+    def settle(self, lane, group, arrived, span):
+        old = [(index, settled + group, part) for index, settled, part in self.lanes[lane]]
+        self.lanes[lane] = old + [(index, [], span) for index in arrived]
+
+    def launch(self):
+        groups = self.steps[self.step]
+        whole = self.step == len(self.steps) - 1
+        if groups is None:
+            self.raw[1] = swap(self.raw[1], ("mp", 1))
+            for lane, span in zip(self.lanes, self.spans):
+                lane += [(0, [], span), (1, [], span)]
+        elif whole:
+            arrived = []
+            for bits in subsets(groups[0])[1:]:
+                out = [
+                    self.fold(lane, groups[0], bits).astype(jnp.bfloat16)
+                    for lane in range(len(self.lanes))
+                ]
+                out = jnp.concatenate(out, -2) if len(out) > 1 else out[0]
+                arrived.append(len(self.raw))
+                self.raw.append(swap(out, *bits))
+            for lane, span in enumerate(self.spans):
+                self.settle(lane, groups[lane], arrived, span)
+        else:
+            for lane, group in enumerate(groups):
+                arrived = []
+                for bits in subsets(group)[1:]:
+                    out = self.fold(lane, group, bits).astype(jnp.bfloat16)
+                    arrived.append(len(self.raw))
+                    self.raw.append(swap(out, *bits))
+                self.settle(lane, group, arrived, None)
+        self.step += 1
+
+    def rows(self):
+        total = [self.fold(lane) for lane in range(len(self.lanes))]
+        total = jnp.concatenate(total, -2) if len(total) > 1 else total[0]
+        return total.reshape(total.shape[-2:])
+
+
+def wave(flows, anchor=()):
+    anchor, values = lax.optimization_barrier((anchor, [flow.pending() for flow in flows]))
+    for flow, value in zip(flows, values):
+        flow.resume(value)
+        flow.launch()
+    return anchor
+
+
+def chunk_kernel(units, columns, rows_ref, cols_ref, *refs):
+    outs = refs[-2:]
+    product = lax.dot_general(
+        rows_ref[...], cols_ref[...], (((0,), (0,)), ((), ())), preferred_element_type=jnp.float32
+    ).astype(jnp.bfloat16)
+    groups = outs[0].shape[0]
+    chunks = outs[0].shape[1]
+    for half, out in enumerate(outs):
+        for group in range(groups):
+            for part in range(columns):
+                place = ((half * groups + group) * columns + part) * 128
+                block = product[:, place : place + 128].reshape(chunks, units, 128)
+                out[group, :, part * units : (part + 1) * units, :] = block
+
+
+def chunks_into(bundle, total, start, rows_of, cols_of, lead, units, columns):
+    count = lax.axis_size("dp")
+    groups = 1 << len(column_bits())
+    columns = columns // 128
+    pixels = cols_of.shape[0]
+    height = units * columns
+    if lead > 1:
+        steps, wide, chunks = lead, count * units, count
+        place = lambda step: (0, 0, start // height + step, 0)
+    else:
+        steps, wide, chunks = count, units, 1
+        place = lambda step: (0, step, start // height, 0)
+    shape = jax.ShapeDtypeStruct((groups, count, total, 128), jnp.bfloat16)
+    block = pl.BlockSpec((groups, chunks, height, 128), place)
+    earlier = () if bundle is None else tuple(bundle)
+    return pl.pallas_call(
+        functools.partial(chunk_kernel, units, columns),
+        grid=(steps,),
+        in_specs=[
+            pl.BlockSpec((pixels, wide), lambda step: (0, step)),
+            pl.BlockSpec(cols_of.shape, lambda step: (0, 0)),
+        ]
+        + [pl.BlockSpec(memory_space=pltpu.HBM)] * len(earlier),
+        out_specs=[block, block],
+        out_shape=[shape, shape],
+        input_output_aliases={2 + place: place for place in range(len(earlier))},
+        compiler_params=pltpu.CompilerParams(vmem_limit_bytes=24 * 2**20),
+        cost_estimate=pl.CostEstimate(
+            flops=2 * rows_of.size * cols_of.shape[1],
+            bytes_accessed=2 * (rows_of.size + cols_of.size)
+            + 2 * rows_of.shape[1] * cols_of.shape[1],
+            transcendentals=0,
+        ),
+    )(rows_of, cols_of, *earlier)
+
+
+def total_of(ref):
+    return jnp.sum(ref[...], 0) if len(ref.shape) == 3 else ref[...]
+
+
+def as_row(block):
+    return jnp.concatenate([block[place : place + 1] for place in range(block.shape[0])], 1)
+
+
+def as_rows(row):
+    return jnp.concatenate(
+        [row[:, place : place + 128] for place in range(0, row.shape[1], 128)], 0
+    )
+
+
+def hand_out(out, rows):
+    missing = out.shape[-2] - sum(row.shape[0] for row in rows)
+    if missing:
+        rows = rows + [jnp.zeros((missing, 128), jnp.float32)]
+    block = jnp.concatenate(rows, 0)
+    out[...] = jnp.broadcast_to(block[None], out.shape) if len(out.shape) == 3 else block
+
+
+def levels(total, first, width, count):
+    rows = width // 128
+    mean = total[first : first + rows] / count
+    scale = lax.rsqrt(total[first + rows : first + 2 * rows] / count - mean * mean + EPS_NORM)
+    return (as_row(mean), as_row(scale))
+
+
+def standard(values, level):
+    return (values - level[0]) * level[1]
+
+
+def back_through(grad, centred, level, gain, mask, total, first, bias_first, count):
+    rows = grad.shape[1] // 128
+    gain_sum = as_row(total[first : first + rows] / count)
+    bias_sum = as_row(total[bias_first : bias_first + rows] / count)
+    return (gain * level[1]) * (grad - mask * (bias_sum + centred * gain_sum))
+
+
+def column_sums(values, mask):
+    weighted = values * mask
+    return [
+        as_rows(jnp.sum(weighted, 0, keepdims=True)),
+        as_rows(jnp.sum(weighted * values, 0, keepdims=True)),
+    ]
+
+
+def product_sums(grad, centred):
+    return as_rows(jnp.sum(grad * centred, 0, keepdims=True))
+
+
+def plain_sums(grad):
+    return as_rows(jnp.sum(grad, 0, keepdims=True))
+
+
+def fetch(bundles, held, sems, start):
+    rows = held.shape[3]
+    copies = [
+        pltpu.make_async_copy(ref.at[:, :, pl.ds(start, rows), :], held.at[half], sems.at[half])
+        for half, ref in enumerate(bundles)
+    ]
+    for copy in copies:
+        copy.start()
+    return copies
+
+
+def arrive(copies):
+    for copy in copies:
+        copy.wait()
+
+
+def weight_part(held, chunk, chunks, start, units, columns):
+    return jnp.concatenate(
+        [
+            held[half, group, chunk : chunk + chunks, start + part * units : start + (part + 1) * units, :]
+            .reshape(chunks * units, 128)
+            for half in range(2)
+            for group in range(held.shape[1])
+            for part in range(columns)
+        ],
+        1,
+    )
+
+
+def spots(core, groups, width):
+    return [
+        pl.multiple_of((2 * group + (core if half == 0 else 1 - core)) * width, 128)
+        for half in range(2)
+        for group in range(groups)
+    ]
+
+
+def in_turn(ref, core, groups):
+    width = ref.shape[1] // (2 * groups)
+    return jnp.concatenate([ref[:, pl.ds(at, width)] for at in spots(core, groups, width)], 1)
+
+
+def in_order(ref, values, core, groups):
+    width = ref.shape[1] // (2 * groups)
+    for place, at in enumerate(spots(core, groups, width)):
+        ref[:, pl.ds(at, width)] = values[:, place * width : (place + 1) * width]
+
+
+def product(first, second):
+    return lax.dot_general(
+        first, second, (((1,), (0,)), ((), ())), preferred_element_type=jnp.float32
+    )
+
+
+def product_turned(first, second):
+    return lax.dot_general(
+        first, second, (((1,), (1,)), ((), ())), preferred_element_type=jnp.float32
+    )
+
+
+def many_in(values, held, units, columns):
+    chunks = max(1, 256 // units)
+    total = 0.0
+    for chunk in range(0, held.shape[2], chunks):
+        part = weight_part(held, chunk, chunks, 0, units, columns)
+        total = total + product(
+            values[:, chunk * units : (chunk + chunks) * units], part
+        )
+    return total
+
+
+def many_out(values, held, units, columns):
+    chunks = max(1, 256 // units)
+    return [
+        product_turned(values, weight_part(held, chunk, chunks, 0, units, columns))
+        for chunk in range(0, held.shape[2], chunks)
+    ]
+
+
+def slid(values, offset):
+    count = values.shape[0]
+    return pltpu.roll(values, (-offset) % count, 0) if offset % count else values
+
+
+def within(inside, drow, dcol):
+    place = 3 * (drow + 1) + dcol + 1
+    return inside[:, place : place + 1]
+
+
+def first_layer(core, raw, mask, first, second, field, out, sums, held, sems):
+    copies = fetch((first, second), held, sems, 0)
+    core = core[0]
+    weights = mask[...]
+    width = raw.shape[2]
+    for place in range(raw.shape[0]):
+        part = raw[place].astype(jnp.float32) * weights
+        field[:, place * width : (place + 1) * width] = part.astype(jnp.bfloat16)
+    arrive(copies)
+    result = many_in(field, held, held.shape[3], 1)
+    in_order(out, result, core, held.shape[1])
+    rows = column_sums(out[...], weights)
+    pixels = weights.shape[0] // 4
+    for part in (weights, weights[:pixels]):
+        rows.append(jnp.broadcast_to(jnp.sum(part, 0, keepdims=True), (1, 128)))
+    hand_out(sums, rows)
+
+
+def side_layer(start, core, field, mask, first, second, out, sums, held, sems):
+    copies = fetch((first, second), held, sems, start)
+    core = core[0]
+    pixels = mask.shape[0]
+    arrive(copies)
+    columns = out.shape[1] // (2 * held.shape[1] * 128)
+    result = many_in(field[:pixels, :], held, held.shape[3] // columns, columns)
+    in_order(out, result, core, held.shape[1])
+    hand_out(sums, column_sums(out[...], mask[...]))
+
+
+def spread_layer(start, norm, taps, core, before, sums_in, counts, tables, keep, mask_in, mask, inside,
+                 first, second, cols, out, sums, held, sems):
+    copies = fetch((first, second), held, sems, start)
+    core = core[0]
+    pixels = mask.shape[0]
+    width = before.shape[1]
+    counted = 0 if before.shape[0] > pixels else 1
+    level = levels(total_of(sums_in), 0, width, counts[counted : counted + 1, :])
+    act = standard(before[...], level) * tables[2 * norm : 2 * norm + 1, :] + tables[2 * norm + 1 : 2 * norm + 2, :]
+    row = norm // 2
+    hidden = jax.nn.silu(act) * mask_in[...] * keep[row : row + 1, :]
+    for tap, phase, drow, dcol in taps:
+        source = hidden[phase * pixels : (phase + 1) * pixels]
+        moved = slid(source, drow * WO + dcol) * within(inside, drow, dcol)
+        cols[:, tap * width : (tap + 1) * width] = moved.astype(jnp.bfloat16)
+    arrive(copies)
+    units = held.shape[3] // 9
+    total = 0.0
+    for tap in range(9):
+        part = weight_part(held, 0, held.shape[2], tap * units, units, 1)
+        total = total + product(cols[:, tap * width : (tap + 1) * width], part)
+    in_order(out, total, core, held.shape[1])
+    hand_out(sums, column_sums(out[...], mask[...]))
+
+
+def widen_layer(start, norm, core, before, sums_in, counts, tables, keep, mask, first, second,
+                hidden, out, sums, held, scratch, sems):
+    copies = fetch((first, second), held, sems, start)
+    core = core[0]
+    level = levels(total_of(sums_in), 0, before.shape[1], counts[1:2, :])
+    act = standard(before[...], level) * tables[2 * norm : 2 * norm + 1, :] + tables[2 * norm + 1 : 2 * norm + 2, :]
+    row = norm // 2
+    scratch[...] = jax.nn.silu(act) * mask[...] * keep[row : row + 1, :]
+    hidden[...] = in_turn(scratch, core, held.shape[1]).astype(jnp.bfloat16)
+    arrive(copies)
+    parts = many_out(hidden[...], held, held.shape[3], 1)
+    size = out.shape[1] // len(parts)
+    for place, part in enumerate(parts):
+        out[:, place * size : (place + 1) * size] = part
+    hand_out(sums, column_sums(out[...], mask[...]))
+
+
+def joined_acts(total, third, side, wide, count):
+    width = third.shape[1]
+    rows = width // 128
+    centred_third = standard(third[...], levels(total, 0, width, count))
+    centred_side = standard(side[...], levels(total, 2 * rows, width, count))
+    act = (
+        centred_third * wide[0:1, :]
+        + wide[1:2, :]
+        + (centred_side * wide[2:3, :] + wide[3:4, :])
+    )
+    return (centred_third, centred_side, act)
+
+
+def narrow_layer(start, core, third, side, sums_in, counts, wide, mask, first, second,
+                 above, out, sums, held, sems):
+    copies = fetch((first, second), held, sems, start)
+    core = core[0]
+    centred_third, centred_side, act = joined_acts(
+        sums_in[...], third, side, wide, counts[1:2, :]
+    )
+    above[...] = (jax.nn.silu(act) * mask[...]).astype(jnp.bfloat16)
+    arrive(copies)
+    result = many_in(above, held, held.shape[3], 1)
+    in_order(out, result, core, held.shape[1])
+    hand_out(sums, column_sums(out[...], mask[...]))
+
+
+def last_layer(sixth, sums_in, counts, wide, above, cotangent, mask, out, grad, sums):
+    level = levels(sums_in[...], 0, sixth.shape[1], counts[1:2, :])
+    centred = standard(sixth[...], level)
+    act = centred * wide[4:5, :] + wide[5:6, :] + above[...].astype(jnp.float32)
+    weights = mask[...]
+    result = (jax.nn.silu(act) * weights).astype(jnp.bfloat16)
+    inner = weights * slope(act)
+    width = out.shape[2]
+    for place in range(out.shape[0]):
+        span = slice(place * width, (place + 1) * width)
+        out[place] = result[:, span]
+        grad[:, span] = cotangent[place].astype(jnp.float32) * inner[:, span]
+    result = grad[...]
+    hand_out(sums, [product_sums(result, centred), plain_sums(result)])
+
+
+def narrow_grad(grad, before, sums_in, counts, tables, norm, keep, mask):
+    counted = 0 if norm == 0 else 1
+    level = levels(total_of(sums_in), 0, before.shape[1], counts[counted : counted + 1, :])
+    centred = standard(before[...], level)
+    act = centred * tables[2 * norm : 2 * norm + 1, :] + tables[2 * norm + 1 : 2 * norm + 2, :]
+    row = norm // 2
+    result = grad * keep[row : row + 1, :] * mask * slope(act)
+    return (result, [product_sums(result, centred), plain_sums(result)])
+
+
+def narrow_back(norm, grad, before, sums_in, sums_back, counts, tables, mask):
+    counted = 0 if norm == 0 else 1
+    count = counts[counted : counted + 1, :]
+    width = before.shape[1]
+    level = levels(total_of(sums_in), 0, width, count)
+    return back_through(
+        grad[...],
+        standard(before[...], level),
+        level,
+        tables[2 * norm : 2 * norm + 1, :],
+        mask,
+        total_of(sums_back),
+        0,
+        width // 128,
+        count,
+    )
+
+
+def last_back(start, norm, core, grad, sixth, sums_six, back_six, counts, wide, before, sums_in, tables,
+              keep, mask, first, second, grad_out, grad_in, sums, held, scratch, sems):
+    copies = fetch((first, second), held, sems, start)
+    core = core[0]
+    width = sixth.shape[1]
+    count = counts[1:2, :]
+    level = levels(sums_six[...], 0, width, count)
+    grad_out[...] = back_through(
+        grad[...], standard(sixth[...], level), level, wide[4:5, :], mask[...], back_six[...], 0,
+        width // 128, count,
+    ).astype(jnp.bfloat16)
+    arrive(copies)
+    in_order(scratch, many_in(grad_out, held, held.shape[3], 1), core, held.shape[1])
+    result, rows = narrow_grad(scratch[...], before, sums_in, counts, tables, norm, keep, mask[...])
+    grad_in[...] = result
+    hand_out(sums, rows)
+
+
+def pair_back(start, norm, core, grad, third, side, sums_pair, back_pair, counts, wide, before, sums_in,
+              tables, keep, mask, first, second, grad_third, grad_side, grad_in, sums, held, scratch,
+              big, sems):
+    copies = fetch((first, second), held, sems, start)
+    core = core[0]
+    width = third.shape[1]
+    rows = width // 128
+    count = counts[1:2, :]
+    total = sums_pair[...]
+    back = back_pair[...]
+    groups = held.shape[1]
+    level = levels(total, 0, width, count)
+    grad_third[...] = back_through(
+        grad[...], standard(third[...], level), level, wide[0:1, :], mask[...], back, 0, 2 * rows, count
+    ).astype(jnp.bfloat16)
+    arrive(copies)
+    in_order(scratch, many_in(grad_third, held, held.shape[3], 1), core, groups)
+    result, parts = narrow_grad(scratch[...], before, sums_in, counts, tables, norm, keep, mask[...])
+    grad_in[...] = result
+    hand_out(sums, parts)
+    level = levels(total, 2 * rows, width, count)
+    big[...] = back_through(
+        grad[...], standard(side[...], level), level, wide[2:3, :], mask[...], back, rows, 2 * rows, count
+    )
+    grad_side[...] = in_turn(big, core, groups).astype(jnp.bfloat16)
+
+
+def spread_back(start, norm, taps, core, grad, after, sums_after, back_after, counts, tables, before,
+                sums_in, keep, mask_in, mask, inside, first, second, grad_out, grad_in, sums, held,
+                scratch, sems):
+    copies = fetch((first, second), held, sems, start)
+    core = core[0]
+    pixels = mask.shape[0]
+    phases = before.shape[0] // pixels
+    scratch[...] = narrow_back(norm + 1, grad, after, sums_after, back_after, counts, tables, mask[...])
+    grad_out[...] = in_turn(scratch, core, held.shape[1]).astype(jnp.bfloat16)
+    arrive(copies)
+    units = held.shape[3] // 9
+    totals = [0.0] * phases
+    for tap, phase, drow, dcol in taps:
+        part = weight_part(held, 0, held.shape[2], tap * units, units, 1)
+        moved = product_turned(grad_out[...], part)
+        totals[phase] = totals[phase] + slid(moved, -drow * WO - dcol) * within(inside, -drow, -dcol)
+    hidden = jnp.concatenate(totals, 0) if phases > 1 else totals[0]
+    result, rows = narrow_grad(hidden, before, sums_in, counts, tables, norm, keep, mask_in[...])
+    grad_in[...] = result
+    hand_out(sums, rows)
+
+
+def narrow_layer_back(start, core, grad, fourth, sums_four, back_four, counts, tables, mask, grad_two,
+                      third, side, sums_pair, wide, first, second, grad_out, grad_in, sums, held,
+                      scratch, big, sems):
+    copies = fetch((first, second), held, sems, start)
+    core = core[0]
+    scratch[...] = narrow_back(2, grad, fourth, sums_four, back_four, counts, tables, mask[...])
+    grad_out[...] = in_turn(scratch, core, held.shape[1]).astype(jnp.bfloat16)
+    arrive(copies)
+    parts = many_out(grad_out[...], held, held.shape[3], 1)
+    size = big.shape[1] // len(parts)
+    for place, part in enumerate(parts):
+        big[:, place * size : (place + 1) * size] = part
+    centred_third, centred_side, act = joined_acts(
+        sums_pair[...], third, side, wide, counts[1:2, :]
+    )
+    result = (grad_two[...] + big[...]) * mask[...] * slope(act)
+    grad_in[...] = result
+    hand_out(
+        sums,
+        [
+            product_sums(result, centred_third),
+            product_sums(result, centred_side),
+            plain_sums(result),
+        ],
+    )
+
+
+def side_back(start, grad, first, second, out, held, sems):
+    copies = fetch((first, second), held, sems, start)
+    arrive(copies)
+    columns = grad.shape[1] // (2 * held.shape[1] * 128)
+    parts = many_out(grad[...], held, held.shape[3] // columns, columns)
+    size = out.shape[1] // len(parts)
+    for place, part in enumerate(parts):
+        out[:, place * size : (place + 1) * size] = part
+
+
+def first_back(core, grad, before, sums_in, sums_back, counts, tables, mask, side, first, second,
+               grad_out, out, held, scratch, sems):
+    copies = fetch((first, second), held, sems, 0)
+    core = core[0]
+    scratch[...] = narrow_back(0, grad, before, sums_in, sums_back, counts, tables, mask[...])
+    grad_out[...] = in_turn(scratch, core, held.shape[1]).astype(jnp.bfloat16)
+    arrive(copies)
+    parts = many_out(grad_out[...], held, held.shape[3], 1)
+    size = side.shape[1] // len(parts)
+    pixels = side.shape[0]
+    weights = mask[...]
+    width = out.shape[2]
+    for place, part in enumerate(parts):
+        owner = place * size // width
+        span = slice(place * size % width, place * size % width + size)
+        beside = side[:, place * size : (place + 1) * size]
+        out[owner, :pixels, span] = ((part[:pixels] + beside) * weights[:pixels]).astype(jnp.bfloat16)
+        out[owner, pixels:, span] = (part[pixels:] * weights[pixels:]).astype(jnp.bfloat16)
+
+
+class Far:
+    def __init__(self, value):
+        self.value = value
+
+
+class Coming:
+    def __init__(self, ref, copy):
+        self.ref = ref
+        self.copy = copy
+        self.shape = ref.shape
+
+    def settle(self):
+        if self.copy is not None:
+            self.copy.wait()
+            self.copy = None
+
+    def __getitem__(self, place):
+        self.settle()
+        return self.ref[place]
+
+
+def framed(kernel, places, count, *refs):
+    refs = list(refs)
+    rest, held, sems = refs[: len(refs) - len(places) - 1], refs[-len(places) - 1 : -1], refs[-1]
+    coming = []
+    for at, place in enumerate(places):
+        copy = pltpu.make_async_copy(rest[place], held[at], sems.at[at])
+        copy.start()
+        rest[place] = Coming(held[at], copy)
+        coming.append(rest[place])
+    kernel(*rest)
+    for value in coming:
+        value.settle()
+
+
+def launch(kernel, shapes, values, bundles=(), rows=0, scratch=(), work=0):
+    held = []
+    sems = []
+    if bundles:
+        held = [pltpu.VMEM((2,) + bundles[0].shape[:2] + (rows, 128), jnp.bfloat16)]
+        sems = [pltpu.SemaphoreType.DMA((2,))]
+    places = [place for place, value in enumerate(values) if isinstance(value, Far)]
+    values = [value.value if isinstance(value, Far) else value for value in values]
+    moved = sum(value.size * value.dtype.itemsize for value in list(values) + list(shapes))
+    specs = []
+    for place, value in enumerate(values):
+        space = pltpu.SMEM if value.dtype == jnp.int32 else pltpu.VMEM
+        specs.append(pl.BlockSpec(memory_space=pltpu.HBM if place in places else space))
+    late = []
+    if places:
+        kernel = functools.partial(framed, kernel, places, len(values))
+        late = [pltpu.VMEM(values[place].shape, values[place].dtype) for place in places]
+        late.append(pltpu.SemaphoreType.DMA((len(places),)))
+    return pl.pallas_call(
+        kernel,
+        in_specs=specs + [pl.BlockSpec(memory_space=pltpu.HBM)] * len(bundles),
+        out_specs=[pl.BlockSpec(memory_space=pltpu.VMEM)] * len(shapes),
+        out_shape=list(shapes),
+        scratch_shapes=held + [pltpu.VMEM(shape, jnp.float32) for shape in scratch] + sems + late,
+        compiler_params=pltpu.CompilerParams(vmem_limit_bytes=40 * 2**20),
+        cost_estimate=pl.CostEstimate(
+            flops=2 * work, bytes_accessed=moved + rows * 16 * 512, transcendentals=0
+        ),
+    )(*values, *bundles)
+
+
+def moved_by(grad, mean, square, weight, mean_out, square_out, update_out, at):
+    first_fix = 1.0 - BETA_ONE**STEP
+    second_fix = 1.0 - BETA_TWO**STEP
+    old = weight[at]
+    mean_next, square_next, step = adapt(grad, mean[at], square[at], first_fix, second_fix)
+    update = step + DECAY * old
+    mean_out[at] = mean_next
+    square_out[at] = square_next
+    update_out[at] = update
+    result = []
+    for value in (old, update):
+        power = value * value
+        while len(power.shape) > 2:
+            power = jnp.sum(power, 0)
+        row = jnp.sum(power, 0, keepdims=True)
+        result.append(
+            sum(row[:, place : place + 128] for place in range(0, row.shape[1], 128))
+        )
+    return result
+
+
+def early_moves(columns, rows_a, rows_c, short_m, short_v, short_w, last_m, last_v, last_w, second_m, second_v,
+                second_w, short_mo, short_vo, short_uo, last_mo, last_vo, last_uo, second_mo, second_vo,
+                second_uo, powers):
+    unit_in = short_w.shape[0]
+    unit_out = second_w.shape[0]
+    parts = short_w.shape[1] // 128
+    every = (slice(None), slice(None))
+    grad = jnp.concatenate(
+        [rows_c[part * unit_in : (part + 1) * unit_in, :] for part in range(parts)], 1
+    )
+    found = moved_by(grad, short_m, short_v, short_w, short_mo, short_vo, short_uo, every)
+    start = parts * unit_in
+    for block, rows in enumerate((rows_c[start : start + unit_out, :], rows_a[...])):
+        found += moved_by(
+            jnp.transpose(rows), last_m, last_v, last_w, last_mo, last_vo, last_uo, block
+        )
+    start += unit_out
+    found += moved_by(
+        rows_c[start : start + unit_out, :], second_m, second_v, second_w, second_mo, second_vo,
+        second_uo, every,
+    )
+    powers[...] = jnp.concatenate(found, 0)
+
+
+def late_moves(rows_b, rows_d, rows_e, powers_in, first_m, first_v, first_w, mid_m, mid_v, mid_w, first_mo,
+               first_vo, first_uo, mid_mo, mid_vo, mid_uo, powers):
+    every = (slice(None), slice(None))
+    found = moved_by(
+        rows_e[...], first_m, first_v, first_w, first_mo, first_vo, first_uo, every
+    )
+    shape = mid_w.shape[1:]
+    middle = []
+    for block, rows in enumerate((rows_d, rows_b)):
+        middle += moved_by(
+            rows[...].reshape(shape), mid_m, mid_v, mid_w, mid_mo, mid_vo, mid_uo, block
+        )
+    early = powers_in[...]
+    order = [found[0], found[1], early[0:2]] + middle + [early[2:8]]
+    hand_out(powers, order)
+
+
+def final_moves(powers, first_w, first_u, short_w, short_u, mid_w, mid_u, last_w, last_u, second_w, second_u,
+                norms, first_o, short_o, mid_o, last_o, second_o, first_c, short_c, mid_c, last_c, second_c):
+    total = jnp.sqrt(jnp.sum(jnp.sum(powers[...], 0), 1, keepdims=True))
+    norms[...] = jnp.broadcast_to(total, norms.shape)
+
+    def step(row, weight, update, out, copy, at):
+        ratio = total[2 * row : 2 * row + 1] / (total[2 * row + 1 : 2 * row + 2] + EPS_TRUST)
+        fresh = weight[at] - (RATE * ratio) * update[at]
+        out[at] = fresh
+        copy[at] = fresh.astype(jnp.bfloat16)
+
+    every = (slice(None), slice(None))
+    step(0, first_w, first_u, first_o, first_c, every)
+    step(1, short_w, short_u, short_o, short_c, every)
+    for block in range(2):
+        for tap in range(mid_w.shape[1]):
+            step(2 + block, mid_w, mid_u, mid_o, mid_c, (block, tap))
+        step(4 + block, last_w, last_u, last_o, last_c, block)
+    step(6, second_w, second_u, second_o, second_c, every)
+
+
+def exchange(copies):
+    return lax.all_to_all(copies, ("dp", "mp"), 0, 0, tiled=True)
+
+
+def by_image(
+    inputs,
+    pixel_mask,
+    widths,
+    output_grad,
+    first_weight,
+    shortcut_weight,
+    middle_weight,
+    last_weight,
+    second_weight,
+    narrow_norms,
+    wide_norms,
+    first_mean,
+    first_square,
+    shortcut_mean,
+    shortcut_square,
+    middle_mean,
+    middle_square,
+    last_mean,
+    last_square,
+    second_mean,
+    second_square,
+    narrow_mean,
+    narrow_square,
+    wide_mean,
+    wide_square,
+):
+    ranks = lax.axis_size("mp")
+    rank = lax.axis_index("mp")
+    pixels = pixel_mask.shape[1] // ranks
+    narrow = first_weight.shape[1] * ranks
+    wide = shortcut_weight.shape[1] * ranks
+    low = jnp.bfloat16
+    channels = inputs.shape[0]
+    field = inputs.reshape(channels, 4, ranks, pixels).transpose(2, 1, 3, 0)
+    field = field.reshape(ranks, 4 * pixels, channels)
+    flow_a = Gather(pack(first_weight.astype(low)[None]), False)
+    flow_b = Gather(pack(middle_weight[0].astype(low)))
+    flow_c = Gather(
+        jnp.concatenate(
+            [
+                pack(shortcut_weight.astype(low)[None]),
+                pack(last_weight[0].astype(low).T[None]),
+                pack(second_weight.astype(low)[None]),
+            ]
+        )
+    )
+    flow_d = Gather(
+        jnp.concatenate(
+            [pack(last_weight[1].astype(low).T[None]), pack(middle_weight[1].astype(low))]
+        )
+    )
+    field = wave([flow_a, flow_b], field)
+    field = lax.all_to_all(field, "mp", 0, 0, tiled=True)
+    wave([flow_a, flow_b])
+    field = wave([flow_a, flow_b, flow_c], field)
+    unit_in, column = first_weight.shape
+    column_wide = shortcut_weight.shape[1]
+    unit_mid = middle_weight.shape[2]
+    unit_out = second_weight.shape[0]
+    size_short = unit_in * column_wide // 128
+    size_out = unit_out * column // 128
+    size_mid = 9 * unit_mid * column // 128
+    tables = jnp.concatenate([narrow_norms.reshape(-1, 128), wide_norms.reshape(-1, 128)], 0)
+    tables = jnp.broadcast_to(tables[None], (ranks,) + tables.shape)
+    tables = lax.all_to_all(tables, "mp", 0, 0, tiled=True)
+    split = narrow_norms.size // 128
+    narrow_all = (
+        tables[:, :split].reshape(ranks, 4, 2, -1).transpose(1, 2, 0, 3).reshape(4, 2, narrow)
+    )
+    wide_all = tables[:, split:].reshape(ranks, 3, 2, -1).transpose(1, 2, 0, 3).reshape(3, 2, wide)
+
+    narrow_all = narrow_all.reshape(8, narrow)
+    wide_all = jnp.concatenate([wide_all.reshape(6, wide), jnp.zeros((2, wide), jnp.float32)], 0)
+
+    own_mask = lax.dynamic_slice_in_dim(pixel_mask, rank * pixels, pixels, 1).astype(jnp.float32)
+    mask_in = own_mask.reshape(-1, 1)
+    mask = own_mask[0][:, None]
+    channel = lax.iota(jnp.int32, narrow)[None]
+    keep = (channel < widths[:, None]).astype(jnp.float32)
+    keep = jnp.concatenate([keep, jnp.zeros((6, narrow), jnp.float32)], 0)
+    place = lax.iota(jnp.int32, pixels)[:, None]
+    step = lax.iota(jnp.int32, 9)[None]
+    row_at = place // WO % HO + step // 3 - 1
+    col_at = place % WO + step % 3 - 1
+    inside = (row_at >= 0) & (row_at < HO) & (col_at >= 0) & (col_at < WO)
+    inside = inside.astype(jnp.float32)
+    core = bit_of("mp", 1)[None]
+
+    above = output_grad.reshape(-1, ranks, pixels).transpose(1, 2, 0)
+    above = lax.all_to_all(above, "mp", 0, 0, tiled=True)
+
+    devices = ranks * lax.axis_size("dp")
+    full = 4 * pixels
+
+    def real(*shape):
+        return jax.ShapeDtypeStruct(shape, jnp.float32)
+
+    def short(*shape):
+        return jax.ShapeDtypeStruct(shape, low)
+
+    size = narrow // 128
+    wide_rows = wide // 128
+    copies = real(devices, 2 * size, 128)
+    bundle_a = flow_a.bundles()
+    field, pre_one, sums = launch(
+        first_layer,
+        [short(full, ranks * channels), real(full, narrow), real(devices, 2 * size + 8, 128)],
+        [core, field, Far(mask_in)],
+        bundle_a,
+        unit_in,
+        work=field.size * narrow,
+    )
+    sums = wave([flow_b, flow_c], sums)
+    sums_one = exchange(sums)
+    sums_one = wave([flow_c, flow_d], sums_one)
+    counts = jnp.sum(sums_one[:, 2 * size :], 0)
+    bundle_b = flow_b.bundles()
+    cols_one, pre_two, sums = launch(
+        functools.partial(spread_layer, 0, 0, STRIDED_TAPS),
+        [short(pixels, 9 * narrow), real(pixels, narrow), copies],
+        [core, pre_one, sums_one, Far(counts), Far(narrow_all), Far(keep), Far(mask_in), Far(mask), Far(inside)],
+        bundle_b,
+        size_mid,
+        work=9 * pixels * narrow * narrow,
+    )
+    sums_two = exchange(sums)
+    sums_two = wave([flow_c, flow_d], sums_two)
+    bundle_c = flow_c.bundles()
+    pre_side, side_sums = launch(
+        functools.partial(side_layer, 0),
+        [real(pixels, wide), real(2 * wide_rows, 128)],
+        [core, Far(field), Far(mask)],
+        bundle_c,
+        size_short,
+        work=pixels * field.shape[1] * wide,
+    )
+    hid_two, pre_three, sums = launch(
+        functools.partial(widen_layer, size_short, 1),
+        [short(pixels, narrow), real(pixels, wide), real(2 * wide_rows, 128)],
+        [core, pre_two, sums_two, Far(counts), Far(narrow_all), Far(keep), Far(mask)],
+        bundle_c,
+        size_out,
+        [(pixels, narrow)],
+        work=pixels * narrow * wide,
+    )
+    sums = wave([flow_d], jnp.concatenate([sums, side_sums], 0))
+    sums_pair = everywhere(sums)
+    out_one, pre_four, sums = launch(
+        functools.partial(narrow_layer, size_short + size_out),
+        [short(pixels, wide), real(pixels, narrow), copies],
+        [core, pre_three, Far(pre_side), sums_pair, Far(counts), Far(wide_all), Far(mask)],
+        bundle_c,
+        size_out,
+        work=pixels * narrow * wide,
+    )
+    sums_four = exchange(sums)
+    sums_four = wave([flow_d], sums_four)
+    bundle_d = flow_d.bundles()
+    cols_four, pre_five, sums = launch(
+        functools.partial(spread_layer, size_out, 2, PLAIN_TAPS),
+        [short(pixels, 9 * narrow), real(pixels, narrow), copies],
+        [core, pre_four, sums_four, Far(counts), Far(narrow_all), Far(keep), Far(mask), Far(mask), Far(inside)],
+        bundle_d,
+        size_mid,
+        work=9 * pixels * narrow * narrow,
+    )
+    sums_five = exchange(sums)
+    hid_five, pre_six, sums = launch(
+        functools.partial(widen_layer, 0, 3),
+        [short(pixels, narrow), real(pixels, wide), real(2 * wide_rows, 128)],
+        [core, pre_five, sums_five, Far(counts), Far(narrow_all), Far(keep), Far(mask)],
+        bundle_d,
+        size_out,
+        [(pixels, narrow)],
+        work=pixels * narrow * wide,
+    )
+    sums_six = everywhere(sums)
+    block_output, grad_two, sums = launch(
+        last_layer,
+        [short(*above.shape), real(pixels, wide), real(2 * wide_rows, 128)],
+        [pre_six, sums_six, Far(counts), Far(wide_all), Far(out_one), Far(above), Far(mask)],
+    )
+    back_six = everywhere(sums)
+    block_output = lax.all_to_all(block_output, "mp", 0, 0, tiled=True)
+    block_output = block_output.transpose(2, 0, 1).reshape(-1, ranks * pixels)
+
+    grad_six, act_five_grad, sums = launch(
+        functools.partial(last_back, 0, 3),
+        [short(pixels, wide), real(pixels, narrow), copies],
+        [core, grad_two, Far(pre_six), Far(sums_six), back_six, Far(counts), Far(wide_all), Far(pre_five),
+         Far(sums_five), Far(narrow_all), Far(keep), Far(mask)],
+        bundle_d,
+        size_out,
+        [(pixels, narrow)],
+        work=pixels * narrow * wide,
+    )
+    bundle = chunks_into(None, size_out, 0, grad_six, hid_five, 1, unit_out, column)
+    back_a = Scatter(*bundle)
+    back_five = exchange(sums)
+    back_five = wave([back_a], back_five)
+    grad_five, act_four_grad, sums = launch(
+        functools.partial(spread_back, size_out, 2, PLAIN_TAPS),
+        [short(pixels, narrow), real(pixels, narrow), copies],
+        [core, act_five_grad, Far(pre_five), Far(sums_five), back_five, Far(counts), Far(narrow_all),
+         Far(pre_four), Far(sums_four), Far(keep), Far(mask), Far(mask), Far(inside)],
+        bundle_d,
+        size_mid,
+        [(pixels, narrow)],
+        work=9 * pixels * narrow * narrow,
+    )
+    sums = wave([back_a], sums)
+    back_four = exchange(sums)
+    bundle = chunks_into(None, size_mid, 0, cols_four, grad_five, 9, unit_mid, column)
+    back_b = Scatter(*bundle)
+    back_four = wave([back_b], back_four)
+    grad_four, grad_one, sums = launch(
+        functools.partial(narrow_layer_back, size_short + size_out),
+        [short(pixels, narrow), real(pixels, wide), real(3 * wide_rows, 128)],
+        [core, act_four_grad, Far(pre_four), Far(sums_four), back_four, Far(counts), Far(narrow_all), Far(mask),
+         Far(grad_two), Far(pre_three), Far(pre_side), Far(sums_pair), Far(wide_all)],
+        bundle_c,
+        size_out,
+        [(pixels, narrow), (pixels, wide)],
+        work=pixels * narrow * wide,
+    )
+    sums = wave([back_a, back_b], sums)
+    back_pair = everywhere(sums)
+    total = size_short + 2 * size_out
+    bundle = chunks_into(
+        None, total, size_short + size_out, out_one, grad_four, 1, unit_out, column
+    )
+    back_pair, bundle = lax.optimization_barrier((back_pair, bundle))
+    grad_three, grad_side, act_two_grad, sums = launch(
+        functools.partial(pair_back, size_short, 1),
+        [short(pixels, wide), short(pixels, wide), real(pixels, narrow), copies],
+        [core, grad_one, Far(pre_three), Far(pre_side), Far(sums_pair), back_pair, Far(counts), Far(wide_all),
+         Far(pre_two), Far(sums_two), Far(narrow_all), Far(keep), Far(mask)],
+        bundle_c,
+        size_out,
+        [(pixels, narrow), (pixels, wide)],
+        work=pixels * narrow * wide,
+    )
+    sums = wave([back_a, back_b], sums)
+    back_two = exchange(sums)
+    bundle = chunks_into(bundle, total, size_short, grad_three, hid_two, 1, unit_out, column)
+    bundle = chunks_into(bundle, total, 0, field, grad_side, 1, unit_in, column_wide)
+    back_c = Scatter(*bundle)
+    back_two = wave([back_c], back_two)
+    grad_mid, act_one_grad, sums = launch(
+        functools.partial(spread_back, 0, 0, STRIDED_TAPS),
+        [short(pixels, narrow), real(full, narrow), copies],
+        [core, act_two_grad, Far(pre_two), Far(sums_two), back_two, Far(counts), Far(narrow_all), Far(pre_one),
+         Far(sums_one), Far(keep), Far(mask_in), Far(mask), Far(inside)],
+        bundle_b,
+        size_mid,
+        [(pixels, narrow)],
+        work=9 * pixels * narrow * narrow,
+    )
+    sums = wave([back_b, back_c], sums)
+    back_one = exchange(sums)
+    bundle = chunks_into(None, size_mid, 0, cols_one, grad_mid, 9, unit_mid, column)
+    back_d = Scatter(*bundle)
+    (side_grad,) = launch(
+        functools.partial(side_back, 0),
+        [real(pixels, field.shape[1])],
+        [grad_side],
+        bundle_c,
+        size_short,
+        work=pixels * field.shape[1] * wide,
+    )
+    back_one, side_grad = wave([back_d], (back_one, side_grad))
+    grad_first, field_grad = launch(
+        first_back,
+        [short(full, narrow), short(ranks, full, channels)],
+        [core, act_one_grad, Far(pre_one), Far(sums_one), back_one, Far(counts), Far(narrow_all), Far(mask_in),
+         Far(side_grad)],
+        bundle_a,
+        unit_in,
+        [(full, narrow)],
+        work=field.size * narrow,
+    )
+    bundle = chunks_into(None, unit_in * column // 128, 0, field, grad_first, 1, unit_in, column)
+    back_e = Scatter(*bundle, False)
+    field_grad = wave([back_c, back_d, back_e], field_grad)
+    input_grad = lax.all_to_all(field_grad, "mp", 0, 0, tiled=True)
+    input_grad = input_grad.reshape(ranks, 4, pixels, channels).transpose(3, 1, 0, 2)
+    input_grad = input_grad.reshape(inputs.shape)
+    wave([back_c, back_d, back_e])
+    wave([back_d, back_e])
+    rows_a, rows_b, rows_c, rows_d, rows_e = [
+        flow.rows() for flow in (back_a, back_b, back_c, back_d, back_e)
+    ]
+    first_fix = 1.0 - BETA_ONE**STEP
+    second_fix = 1.0 - BETA_TWO**STEP
+
+    def like(*values):
+        return [real(*value.shape) for value in values for _ in range(3)]
+
+    early = launch(
+        functools.partial(early_moves, column),
+        like(shortcut_weight, last_weight, second_weight) + [real(8, 128)],
+        [rows_a, rows_c]
+        + [
+            Far(value)
+            for value in (
+                shortcut_mean, shortcut_square, shortcut_weight, last_mean, last_square, last_weight,
+                second_mean, second_square, second_weight,
+            )
+        ],
+    )
+    late = launch(
+        late_moves,
+        like(first_weight, middle_weight) + [real(devices, 16, 128)],
+        [rows_b, rows_d, rows_e, early[-1]]
+        + [
+            Far(value)
+            for value in (
+                first_mean, first_square, first_weight, middle_mean, middle_square, middle_weight,
+            )
+        ],
+    )
+    powers = exchange(late[-1])
+    weights = (first_weight, shortcut_weight, middle_weight, last_weight, second_weight)
+    updates = (late[2], early[2], late[5], early[5], early[8])
+    norms, *fresh = launch(
+        final_moves,
+        [real(16, 128)]
+        + [real(*value.shape) for value in weights]
+        + [short(*value.shape) for value in weights],
+        [powers]
+        + [Far(value) for pair in zip(weights, updates) for value in pair],
+    )
+    matrix_norms = norms[:14, 0].reshape(7, 2)
+    first_next, short_next, middle_next, last_next, second_next = fresh[:5]
+    states = [late[0:2], early[0:2], late[3:5], early[3:5], early[6:8]]
+
+    def own_channels(values):
+        width = values.shape[-1] // ranks
+        return lax.dynamic_slice_in_dim(values, rank * width, width, values.ndim - 1)
+
+    narrow_grads = jnp.stack([jnp.sum(rows, 0) for rows in (back_one, back_two, back_four, back_five)])
+    narrow_grad = own_channels(narrow_grads.reshape(4, 2, narrow))
+    gain_three, gain_side, bias_pair = back_pair.reshape(3, wide)
+    wide_grad = own_channels(
+        jnp.stack(
+            [
+                jnp.stack([gain_three, bias_pair]),
+                jnp.stack([gain_side, bias_pair]),
+                back_six.reshape(2, wide),
+            ]
+        )
+    )
+    narrow_mean_next, narrow_square_next, narrow_step = adapt(
+        narrow_grad, narrow_mean, narrow_square, first_fix, second_fix
+    )
+    wide_mean_next, wide_square_next, wide_step = adapt(
+        wide_grad, wide_mean, wide_square, first_fix, second_fix
+    )
+    return (
+        block_output,
+        input_grad,
+        states[0][0],
+        states[0][1],
+        first_next,
+        states[1][0],
+        states[1][1],
+        short_next,
+        states[2][0],
+        states[2][1],
+        middle_next,
+        states[3][0],
+        states[3][1],
+        last_next,
+        states[4][0],
+        states[4][1],
+        second_next,
+        narrow_mean_next,
+        narrow_square_next,
+        narrow_norms - RATE_NORM * narrow_step,
+        wide_mean_next,
+        wide_square_next,
+        wide_norms - RATE_NORM * wide_step,
+        matrix_norms,
+        *fresh[5:],
+    )
+
+
 def solution(mesh):
     in_specs = (
         P("mp", None, "dp"),
@@ -518,4 +1728,10 @@
         P(None, "mp", "dp"),
         P("dp", "mp"),
     )
-    return jax.shard_map(shards, mesh=mesh, in_specs=in_specs, out_specs=out_specs, check_vma=False)
+    return jax.shard_map(
+        lambda *values: (by_image if fits(mesh, values[1]) else shards)(*values),
+        mesh=mesh,
+        in_specs=in_specs,
+        out_specs=out_specs,
+        check_vma=False,
+    )

time: 1320 us -> 656 us (0.50)
  waiting for transfers between devices: 691 us -> 220 us
  blocking collectives: 364 us -> 21.3 us
  starting transfers between devices: 1 us -> 153 us
  matrix products: 110 us -> 0 us
  Pallas kernels: 0 us -> 77.6 us
  local copies, waits for them, and re-layouts: 21 us -> 97.6 us
  other arithmetic: 104 us -> 72.3 us
  between operations: 19 us -> 3.89 us
    reduce_scatter x11 -> x0, waiting for transfers between devices: 539 us -> none  [the longest x2 108 us: output_mix(): lax.psum_scatter(jnp.einsum('kc,kp->cp', kernel, hidden, preferred_elemen...]
    psum x13 -> x0, blocking collectives: 290 us -> none  [the longest x12 250 us: over_images(): return lax.psum((first, second), 'dp')]
    ppermute x0 -> x90, waiting for transfers between devices: none -> 205 us  [the longest x55 101 us: swap(): lax.ppermute(values, 'dp', [(at, at ^ masks['dp']) for at in range(sizes[...]
    all_gather x8 -> x0, waiting for transfers between devices: 152 us -> none  [the longest x2 48.4 us: output_back(): piece = lax.all_gather(grad_b, 'mp', axis=0, tiled=True)]
    dot_general x69 -> x0, matrix products: 110 us -> none  [the longest x18 26.4 us: conv_forward(): jnp.einsum('kc,kp->cp', kernel[tap], source, preferred_element_type=jnp.f...]
    ppermute x0 -> x90, starting transfers between devices: none -> 107 us  [the longest x55 76.5 us: swap(): lax.ppermute(values, 'dp', [(at, at ^ masks['dp']) for at in range(sizes[...]
    pallas_call x0 -> x25, Pallas kernels: none -> 77.6 us  [the longest x18 57.2 us: launch(): pl.pallas_call(kernel, in_specs=specs + [pl.BlockSpec(memory_space=pltpu....]
    unnamed x398 -> x380, local copies, waits for them, and re-layouts: 12 us -> 89.3 us
  transfers between devices with their start and end apart: 19 -> 102, of which waited for: 18 -> 51; matrix products, arithmetic and copies ran while one was open for 9% -> 9% of each run, Pallas kernels for 0% -> 10%
where the time goes in v3:
time: 656 us; the launch traced here: 646 us
  waiting for transfers between devices  220 us (34%)
  starting transfers between devices  153 us (23%)
  local copies, waits for them, and re-layouts  97.6 us (15%)
  Pallas kernels  77.6 us (12%)
  other arithmetic  72.3 us (11%)
  blocking collectives  21.3 us (3%)
    ppermute x55, waiting for transfers between devices, swap(): lax.ppermute(values, 'dp', [(at, at ^ masks['dp']) for at in range(sizes[...  101 us
    unnamed x380, local copies, waits for them, and re-layouts  89.3 us
    ppermute x33, waiting for transfers between devices, swap(): lax.ppermute(values, 'mp', [(at, at ^ masks['mp']) for at in range(sizes[...  87.3 us
    ppermute x55, starting transfers between devices, swap(): lax.ppermute(values, 'dp', [(at, at ^ masks['dp']) for at in range(sizes[...  76.5 us
    pallas_call x18, Pallas kernels, launch(): pl.pallas_call(kernel, in_specs=specs + [pl.BlockSpec(memory_space=pltpu....  57.2 us
    all_to_all x7, starting transfers between devices, exchange(): return lax.all_to_all(copies, ('dp', 'mp'), 0, 0, tiled=True)  26.2 us
    ppermute x33, starting transfers between devices, swap(): lax.ppermute(values, 'mp', [(at, at ^ masks['mp']) for at in range(sizes[...  25 us
    convert_element_type x13, other arithmetic, launch(): out = self.fold(lane, group, bits).astype(jnp.bfloat16)  22 us
  transfers between devices with their start and end apart: 102, of which 51 were waited for; matrix products, arithmetic and copies ran while one was open for 9% of the time, Pallas kernels for 10%

profile of v3, /device:TPU:0, one launch (start us, length us, event | category | flops | bytes accessed | tf_op | source)
XLA Modules:
  0.0 646.0 jit_solution(6753435679406262458)
XLA Ops:
  4.0 5.0 collective-permute-start.5
  9.6 3.8 collective-permute-start.2
  13.4 6.9 %collective-permute-done.2 = bf16[1,1,1,1,128,128]{5,4,3,2,1,0:T(8,128)(2,1)S(1)} collective-permute-done((bf16[1,1,1,1,128,128]{5,4,3,2,1,0:T(8,128)(2,1)S(1)}, bf16[1,1,1,1,128,128]{5,4,3,2,1,0:T(8,128)(2,1)S(1)}, u32[]{:S(2)}, u32[]{:S(2)}) %collective-permute-start.2) | collective-permute-done | bytes 32800 | tf_op jit(solution)/shard_map/ppermute | solution.py:478
  20.4 4.1 collective-permute-start
  24.5 3.6 all-to-all-start
  28.3 3.0 collective-permute-start.8
  36.5 14.5 %collective-permute-done.8 = bf16[1,2,2,1,128,128]{5,4,3,2,1,0:T(8,128)(2,1)} collective-permute-done((bf16[1,2,2,1,128,128]{5,4,3,2,1,0:T(8,128)(2,1)S(1)}, bf16[1,2,2,1,128,128]{5,4,3,2,1,0:T(8,128)(2,1)}, u32[]{:S(2)}, u32[]{:S(2)}) %collective-permute-start.8) | collective-permute-done | bytes 131104 | tf_op jit(solution)/shard_map/ppermute | solution.py:480
  52.9 5.7 collective-permute-done.10
  66.8 3.0 collective-permute-start.14
  76.7 6.4 collective-permute-done.15
  83.0 7.0 %collective-permute-done.14 = bf16[1,1,1,1,1024,128]{5,4,3,2,1,0:T(8,128)(2,1)} collective-permute-done((bf16[1,1,1,1,1024,128]{5,4,3,2,1,0:T(8,128)(2,1)}, bf16[1,1,1,1,1024,128]{5,4,3,2,1,0:T(8,128)(2,1)}, u32[]{:S(2)}, u32[]{:S(2)}) %collective-permute-start.14) | collective-permute-done | bytes 262176 | tf_op jit(solution)/shard_map/ppermute | solution.py:478
  90.1 3.0 all-to-all-start.1
  104.4 3.3 all-to-all-start.2
  107.7 6.3 collective-permute-done.18
  124.1 3.5 shard_map.465
  129.4 5.1 all-to-all-start.3
  134.5 3.8 collective-permute-start.24
  139.0 7.4 %collective-permute-done.24 = bf16[1,1,1,1,832,128]{5,4,3,2,1,0:T(8,128)(2,1)S(1)} collective-permute-done((bf16[1,1,1,1,832,128]{5,4,3,2,1,0:T(8,128)(2,1)}, bf16[1,1,1,1,832,128]{5,4,3,2,1,0:T(8,128)(2,1)S(1)}, u32[]{:S(2)}, u32[]{:S(2)}) %collective-permute-start.24) | collective-permute-done | bytes 213024 | tf_op jit(solution)/shard_map/ppermute | solution.py:478
  146.3 4.2 collective-permute-done.23
  150.5 8.8 %collective-permute-done.22 = bf16[1,1,1,1,832,128]{5,4,3,2,1,0:T(8,128)(2,1)S(1)} collective-permute-done((bf16[1,1,1,1,832,128]{5,4,3,2,1,0:T(8,128)(2,1)}, bf16[1,1,1,1,832,128]{5,4,3,2,1,0:T(8,128)(2,1)S(1)}, u32[]{:S(2)}, u32[]{:S(2)}) %collective-permute-start.22) | collective-permute-done | bytes 213024 | tf_op jit(solution)/shard_map/ppermute | solution.py:478
  167.8 3.2 collective-permute-done.25
  184.5 16.9 %collective-permute-done.29 = f32[64,128]{1,0:T(8,128)S(1)} collective-permute-done((f32[64,128]{1,0:T(8,128)S(1)}, f32[64,128]{1,0:T(8,128)S(1)}, u32[]{:S(2)}, u32[]{:S(2)}) %collective-permute-start.29) | collective-permute-done | bytes 32800 | tf_op jit(solution)/shard_map/ppermute | solution.py:476
  201.9 3.4 collective-permute-done.30
  205.3 3.9 collective-permute-done.31
  209.5 4.5 collective-permute-done.32
  221.1 10.7 %all_to_all.70.refs_2_.refs_8_.refs_3_ = f32[32,8,128]{2,1,0:T(8,128)S(1)} all-to-all(f32[32,8,128]{2,1,0:T(8,128)S(1)} %get-tuple-element.301), channel_id=1, replica_groups=mesh['dp'=8,'mp'=4] {'dp','mp'}, dimensions={0} | all-to-all | bytes 262144 | tf_op jit(solution)/shard_map/all_to_all | solution.py:1281
  235.6 5.8 collective-permute-done.35
  246.0 10.6 %all_to_all.71.refs_2_.refs_8_.refs_3_ = f32[32,8,128]{2,1,0:T(8,128)} all-to-all(f32[32,8,128]{2,1,0:T(8,128)S(1)} %get-tuple-element.312), channel_id=1, replica_groups=mesh['dp'=8,'mp'=4] {'dp','mp'}, dimensions={0} | all-to-all | bytes 262144 | tf_op jit(solution)/shard_map/all_to_all | solution.py:1281
  256.6 4.4 all-to-all-start.6
  273.2 3.1 collective-permute-done.38
  276.9 3.1 collective-permute-done.39
  280.8 3.9 collective-permute-done.40
  288.0 3.2 shard_map.471
  296.9 3.1 collective-permute-done.43
  300.7 3.0 collective-permute-done.44
  304.5 3.9 collective-permute-done.45
  315.2 3.3 all-to-all-start.8
  334.6 4.8 shard_map.474
  341.5 4.3 all-to-all-start.9
  348.3 3.5 shard_map.475
  367.1 6.9 %shard_map.476 = (bf16[176,512]{1,0:T(8,128)(2,1)S(1)}, f32[176,2048]{1,0:T(8,128)S(1)}, f32[48,128]{1,0:T(8,128)S(1)}) custom-call(s32[1]{0:T(128)} %bitcast.refs_0_, f32[176,512]{1,0:T(8,128)S(1)} %copy-done.111, f32[176,512]{1,0:T(8,128)S(1)} %copy-done.44, f32[32,8,128]{2,1,0:T(8,128)S(1)} %copy-done.69, f32[32,8,128]{2,1,0:T(8,128)} %all-to-all-done.9.refs_4_, ...), custom_call_target="tpu_custom_call" | custom-call | flops 369098752 | bytes 9171652 | tf_op jit(solution)/shard_map/pallas_call | solution.py:1184
  382.6 12.0 %collective-permute-done.51 = f32[48,128]{1,0:T(8,128)} collective-permute-done((f32[48,128]{1,0:T(8,128)S(1)}, f32[48,128]{1,0:T(8,128)}, u32[]{:S(2)}, u32[]{:S(2)}) %collective-permute-start.51) | collective-permute-done | bytes 24608 | tf_op jit(solution)/shard_map/ppermute | solution.py:476
  413.3 4.2 shard_map.478
  425.3 3.3 all-to-all-start.10
  434.1 3.0 shard_map.480
  449.4 6.7 %shard_map.481 = (bf16[176,512]{1,0:T(8,128)(2,1)S(1)}, f32[704,512]{1,0:T(8,128)S(1)}, f32[32,8,128]{2,1,0:T(8,128)S(1)}) custom-call(s32[1]{0:T(128)} %bitcast.refs_0_, f32[176,512]{1,0:T(8,128)S(1)} %copy-done.109, f32[176,512]{1,0:T(8,128)S(1)} %copy-done.41, f32[32,8,128]{2,1,0:T(8,128)S(1)} %copy-done.66, f32[32,8,128]{2,1,0:T(8,128)} %all-to-all-done.10.refs_4_, ...), custom_call_target="tpu_custom_call" | custom-call | flops 830472192 | bytes 9205380 | tf_op jit(solution)/shard_map/pallas_call | solution.py:1184
  458.5 3.8 all-to-all-start.11
  469.7 3.5 shard_map.483
  476.4 3.5 all-to-all-start.7
  481.5 9.3 %all-to-all-done.7 = bf16[4,176,512]{2,1,0:T(8,128)(2,1)S(1)} async-done(((bf16[4,176,512]{2,1,0:T(8,128)(2,1)}), bf16[4,176,512]{2,1,0:T(8,128)(2,1)S(1)}, u32[]{:S(2)}, u32[]{:S(2)}) %all-to-all-start.7) | async-done | bytes 720928 | tf_op jit(solution)/shard_map/all_to_all | solution.py:1468
  506.0 2.9 shard_map.484
  508.9 3.1 shard_map.485
  512.0 7.7 %collective-permute-done.62 = bf16[1,2,2,2,512,128]{5,4,3,2,1,0:T(8,128)(2,1)S(1)} collective-permute-done((bf16[1,2,2,2,512,128]{5,4,3,2,1,0:T(8,128)(2,1)S(1)}, bf16[1,2,2,2,512,128]{5,4,3,2,1,0:T(8,128)(2,1)S(1)}, u32[]{:S(2)}, u32[]{:S(2)}) %collective-permute-start.62) | collective-permute-done | bytes 1048608 | tf_op jit(solution)/shard_map/ppermute | solution.py:476
  534.5 4.1 collective-permute-done.65
  542.4 11.0 %collective-permute-done.69 = bf16[1,2,2,1,512,128]{5,4,3,2,1,0:T(8,128)(2,1)S(1)} collective-permute-done((bf16[1,2,2,1,512,128]{5,4,3,2,1,0:T(8,128)(2,1)S(1)}, bf16[1,2,2,1,512,128]{5,4,3,2,1,0:T(8,128)(2,1)S(1)}, u32[]{:S(2)}, u32[]{:S(2)}) %collective-permute-start.69) | collective-permute-done | bytes 524320 | tf_op jit(solution)/shard_map/ppermute | solution.py:476
  563.7 4.7 all-to-all-start.12
  569.6 3.0 collective-permute-start.77
  576.8 6.2 collective-permute-done.87
  593.2 5.8 collective-permute-done.74
  599.9 2.9 collective-permute-start.81
  613.2 4.3 collective-permute-done.80
  617.5 4.7 collective-permute-done.78
  625.9 3.5 all-to-all-start.13
  635.7 4.2 all-to-all-done.13.refs_0_
  (690 shorter events, 307.0 us)
Async XLA Ops:
  4.0 24.2 %collective-permute-start.5 = (bf16[1,1,1,1,576,128]{5,4,3,2,1,0:T(8,128)(2,1)S(1)}, bf16[1,1,1,1,576,128]{5,4,3,2,1,0:T(8,128)(2,1)S(1)}, u32[]{:S(2)}, u32[]{:S(2)}) collective-permute-start(bf16[1,1,1,1,576,128]{5,4,3,2,1,0:T(8,128)(2,1)S(1)} %bitcast.151), channel_id=1, source_target_pairs={{0,24},{4,28},{8,16},{12,20},{16,8},{20,12},{24,0},{28,4},{1,25},{... | collective-permute-start | bytes 442376 | tf_op jit(solution)/shard_map/ppermute | solution.py:478
  9.0 19.1 %collective-permute-start.4 = (bf16[1,1,1,1,576,128]{5,4,3,2,1,0:T(8,128)(2,1)S(1)}, bf16[1,1,1,1,576,128]{5,4,3,2,1,0:T(8,128)(2,1)S(1)}, u32[]{:S(2)}, u32[]{:S(2)}) collective-permute-start(bf16[1,1,1,1,576,128]{5,4,3,2,1,0:T(8,128)(2,1)S(1)} %bitcast.152), channel_id=1, source_target_pairs={{0,8},{4,12},{8,0},{12,4},{16,24},{20,28},{24,16},{28,20},{1,9},{5... | collective-permute-start | bytes 442376 | tf_op jit(solution)/shard_map/ppermute | solution.py:478
  9.1 19.2 %collective-permute-start.3 = (bf16[1,1,1,1,576,128]{5,4,3,2,1,0:T(8,128)(2,1)S(1)}, bf16[1,1,1,1,576,128]{5,4,3,2,1,0:T(8,128)(2,1)S(1)}, u32[]{:S(2)}, u32[]{:S(2)}) collective-permute-start(bf16[1,1,1,1,576,128]{5,4,3,2,1,0:T(8,128)(2,1)S(1)} %bitcast.153), channel_id=1, source_target_pairs={{0,16},{4,20},{8,24},{12,28},{16,0},{20,4},{24,8},{28,12},{1,17},{... | collective-permute-start | bytes 442376 | tf_op jit(solution)/shard_map/ppermute | solution.py:478
  13.4 14.7 %collective-permute-start.1 = (bf16[1,1,1,1,128,128]{5,4,3,2,1,0:T(8,128)(2,1)S(1)}, bf16[1,1,1,1,128,128]{5,4,3,2,1,0:T(8,128)(2,1)S(1)}, u32[]{:S(2)}, u32[]{:S(2)}) collective-permute-start(bf16[1,1,1,1,128,128]{5,4,3,2,1,0:T(8,128)(2,1)S(1)} %convert_bitcast_fusion), channel_id=1, source_target_pairs={{0,8},{4,12},{8,0},{12,4},{16,24},{20,28},{24,16},{28,20},{1,9},{5... | collective-permute-start | bytes 98312 | tf_op jit(solution)/shard_map/ppermute | solution.py:478
  24.5 34.9 %all-to-all-start = ((bf16[4,704,256]{2,1,0:T(8,128)(2,1)}), bf16[4,704,256]{2,1,0:T(8,128)(2,1)S(1)}, u32[]{:S(2)}, u32[]{:S(2)}) async-start(bf16[4,704,256]{2,1,0:T(8,128)(2,1)} %bitcast.3), calls=%async_computation | async-start | bytes 2883584 | tf_op jit(solution)/shard_map/all_to_all | solution.py:1337
  28.3 22.8 %collective-permute-start.8 = (bf16[1,2,2,1,128,128]{5,4,3,2,1,0:T(8,128)(2,1)S(1)}, bf16[1,2,2,1,128,128]{5,4,3,2,1,0:T(8,128)(2,1)}, u32[]{:S(2)}, u32[]{:S(2)}) collective-permute-start(bf16[1,2,2,1,128,128]{5,4,3,2,1,0:T(8,128)(2,1)S(1)} %maximum_maximum_fusion.7), channel_id=1, source_target_pairs={{0,6},{1,7},{2,4},{3,5},{4,2},{5,3},{6,0},{7,1},{8,14},{9,15},{10,... | collective-permute-start | bytes 393224 | tf_op jit(solution)/shard_map/ppermute | solution.py:480
  31.2 21.7 %collective-permute-start.7 = (bf16[1,2,2,1,128,128]{5,4,3,2,1,0:T(8,128)(2,1)S(1)}, bf16[1,2,2,1,128,128]{5,4,3,2,1,0:T(8,128)(2,1)}, u32[]{:S(2)}, u32[]{:S(2)}) collective-permute-start(bf16[1,2,2,1,128,128]{5,4,3,2,1,0:T(8,128)(2,1)S(1)} %maximum_maximum_fusion.7), channel_id=1, source_target_pairs={{0,2},{1,3},{2,0},{3,1},{4,6},{5,7},{6,4},{7,5},{8,10},{9,11},{10,... | collective-permute-start | bytes 393224 | tf_op jit(solution)/shard_map/ppermute | solution.py:476
  31.3 21.6 %collective-permute-start.6 = (bf16[1,2,2,1,128,128]{5,4,3,2,1,0:T(8,128)(2,1)S(1)}, bf16[1,2,2,1,128,128]{5,4,3,2,1,0:T(8,128)(2,1)}, u32[]{:S(2)}, u32[]{:S(2)}) collective-permute-start(bf16[1,2,2,1,128,128]{5,4,3,2,1,0:T(8,128)(2,1)S(1)} %maximum_maximum_fusion.7), channel_id=1, source_target_pairs={{0,4},{4,0},{8,12},{12,8},{16,20},{20,16},{24,28},{28,24},{1,5},{5... | collective-permute-start | bytes 393224 | tf_op jit(solution)/shard_map/ppermute | solution.py:478
  32.0 26.6 %collective-permute-start.10 = (bf16[1,2,2,1,288,128]{5,4,3,2,1,0:T(8,128)(2,1)S(1)}, bf16[1,2,2,1,288,128]{5,4,3,2,1,0:T(8,128)(2,1)S(1)}, u32[]{:S(2)}, u32[]{:S(2)}) collective-permute-start(bf16[1,2,2,1,288,128]{5,4,3,2,1,0:T(8,128)(2,1)S(1)} %get-tuple-element.266), channel_id=1, source_target_pairs={{0,2},{1,3},{2,0},{3,1},{4,6},{5,7},{6,4},{7,5},{8,10},{9,11},{10,... | collective-permute-start | bytes 884744 | tf_op jit(solution)/shard_map/ppermute | solution.py:476
  34.0 24.7 %collective-permute-start.9 = (bf16[1,2,2,1,288,128]{5,4,3,2,1,0:T(8,128)(2,1)S(1)}, bf16[1,2,2,1,288,128]{5,4,3,2,1,0:T(8,128)(2,1)}, u32[]{:S(2)}, u32[]{:S(2)}) collective-permute-start(bf16[1,2,2,1,288,128]{5,4,3,2,1,0:T(8,128)(2,1)S(1)} %get-tuple-element.264), channel_id=1, source_target_pairs={{0,4},{4,0},{8,12},{12,8},{16,20},{20,16},{24,28},{28,24},{1,5},{5... | collective-permute-start | bytes 884744 | tf_op jit(solution)/shard_map/ppermute | solution.py:478
  62.7 27.3 %collective-permute-start.12 = (bf16[1,2,2,2,288,128]{5,4,3,2,1,0:T(8,128)(2,1)}, bf16[1,2,2,2,288,128]{5,4,3,2,1,0:T(8,128)(2,1)}, u32[]{:S(2)}, u32[]{:S(2)}) collective-permute-start(bf16[1,2,2,2,288,128]{5,4,3,2,1,0:T(8,128)(2,1)} %pad_maximum_fusion.4), channel_id=1, source_target_pairs={{0,2},{1,3},{2,0},{3,1},{4,6},{5,7},{6,4},{7,5},{8,10},{9,11},{10,... | collective-permute-start | bytes 1769480 | tf_op jit(solution)/shard_map/ppermute | solution.py:476
  64.0 26.1 %collective-permute-start.13 = (bf16[2,2,2,1,288,128]{5,4,3,2,1,0:T(8,128)(2,1)}, bf16[2,2,2,1,288,128]{5,4,3,2,1,0:T(8,128)(2,1)}, u32[]{:S(2)}, u32[]{:S(2)}) collective-permute-start(bf16[2,2,2,1,288,128]{5,4,3,2,1,0:T(8,128)(2,1)} %pad_maximum_fusion.5), channel_id=1, source_target_pairs={{0,4},{4,0},{8,12},{12,8},{16,20},{20,16},{24,28},{28,24},{1,5},{5... | collective-permute-start | bytes 1769480 | tf_op jit(solution)/shard_map/ppermute | solution.py:478
  66.8 16.2 %collective-permute-start.15 = (bf16[1,1,1,1,1024,128]{5,4,3,2,1,0:T(8,128)(2,1)}, bf16[1,1,1,1,1024,128]{5,4,3,2,1,0:T(8,128)(2,1)}, u32[]{:S(2)}, u32[]{:S(2)}) collective-permute-start(bf16[1,1,1,1,1024,128]{5,4,3,2,1,0:T(8,128)(2,1)} %maximum_bitcast_fusion.3), channel_id=1, source_target_pairs={{0,8},{4,12},{8,0},{12,4},{16,24},{20,28},{24,16},{28,20},{1,9},{5... | collective-permute-start | bytes 786440 | tf_op jit(solution)/shard_map/ppermute | solution.py:478
  66.8 23.2 %collective-permute-start.14 = (bf16[1,1,1,1,1024,128]{5,4,3,2,1,0:T(8,128)(2,1)}, bf16[1,1,1,1,1024,128]{5,4,3,2,1,0:T(8,128)(2,1)}, u32[]{:S(2)}, u32[]{:S(2)}) collective-permute-start(bf16[1,1,1,1,1024,128]{5,4,3,2,1,0:T(8,128)(2,1)} %maximum_bitcast_fusion.3), channel_id=1, source_target_pairs={{0,16},{4,20},{8,24},{12,28},{16,0},{20,4},{24,8},{28,12},{1,17},{... | collective-permute-start | bytes 786440 | tf_op jit(solution)/shard_map/ppermute | solution.py:478
  90.1 13.7 %all-to-all-start.1 = ((f32[32,16,128]{2,1,0:T(8,128)}), f32[32,16,128]{2,1,0:T(8,128)S(1)}, u32[]{:S(2)}, u32[]{:S(2)}) async-start(f32[32,16,128]{2,1,0:T(8,128)} %get-tuple-element.268), calls=%async_computation.1 | async-start | bytes 524288 | tf_op jit(solution)/shard_map/all_to_all | solution.py:1281
  96.0 26.1 %collective-permute-start.19 = (bf16[2,2,2,2,576,128]{5,4,3,2,1,0:T(8,128)(2,1)S(1)}, bf16[2,2,2,2,576,128]{5,4,3,2,1,0:T(8,128)(2,1)}, u32[]{:S(2)}, u32[]{:S(2)}) collective-permute-start(bf16[2,2,2,2,576,128]{5,4,3,2,1,0:T(8,128)(2,1)S(1)} %maximum_maximum_fusion.2), channel_id=1, source_target_pairs={{0,1},{1,0},{2,3},{3,2},{4,5},{5,4},{6,7},{7,6},{8,9},{9,8},{10,11... | collective-permute-start | bytes 7077896 | tf_op jit(solution)/shard_map/ppermute | solution.py:476
  99.2 14.8 %collective-permute-start.18 = (bf16[1,2,2,1,512,128]{5,4,3,2,1,0:T(8,128)(2,1)}, bf16[1,2,2,1,512,128]{5,4,3,2,1,0:T(8,128)(2,1)}, u32[]{:S(2)}, u32[]{:S(2)}) collective-permute-start(bf16[1,2,2,1,512,128]{5,4,3,2,1,0:T(8,128)(2,1)} %get-tuple-element.283), channel_id=1, source_target_pairs={{0,2},{1,3},{2,0},{3,1},{4,6},{5,7},{6,4},{7,5},{8,10},{9,11},{10,... | collective-permute-start | bytes 1572872 | tf_op jit(solution)/shard_map/ppermute | solution.py:476
  101.0 14.1 %collective-permute-start.17 = (bf16[1,2,2,1,512,128]{5,4,3,2,1,0:T(8,128)(2,1)}, bf16[1,2,2,1,512,128]{5,4,3,2,1,0:T(8,128)(2,1)}, u32[]{:S(2)}, u32[]{:S(2)}) collective-permute-start(bf16[1,2,2,1,512,128]{5,4,3,2,1,0:T(8,128)(2,1)} %get-tuple-element.281), channel_id=1, source_target_pairs={{0,4},{4,0},{8,12},{12,8},{16,20},{20,16},{24,28},{28,24},{1,5},{5... | collective-permute-start | bytes 1572872 | tf_op jit(solution)/shard_map/ppermute | solution.py:478
  104.4 17.6 %all-to-all-start.2 = ((f32[4,32,128]{2,1,0:T(8,128)}), f32[4,32,128]{2,1,0:T(8,128)S(1)}, u32[]{:S(2)}, u32[]{:S(2)}) async-start(f32[4,32,128]{2,1,0:T(8,128)} %broadcast_in_dim.5), calls=%async_computation.2 | async-start | bytes 131072 | tf_op jit(solution)/shard_map/all_to_all | solution.py:1349
  117.4 41.9 %collective-permute-start.21 = (bf16[2,2,2,1,512,128]{5,4,3,2,1,0:T(8,128)(2,1)}, bf16[2,2,2,1,512,128]{5,4,3,2,1,0:T(8,128)(2,1)}, u32[]{:S(2)}, u32[]{:S(2)}) collective-permute-start(bf16[2,2,2,1,512,128]{5,4,3,2,1,0:T(8,128)(2,1)} %pad_maximum_fusion.1), channel_id=1, source_target_pairs={{0,4},{4,0},{8,12},{12,8},{16,20},{20,16},{24,28},{28,24},{1,5},{5... | collective-permute-start | bytes 3145736 | tf_op jit(solution)/shard_map/ppermute | solution.py:478
  121.1 38.2 %collective-permute-start.20 = (bf16[1,2,2,2,512,128]{5,4,3,2,1,0:T(8,128)(2,1)}, bf16[1,2,2,2,512,128]{5,4,3,2,1,0:T(8,128)(2,1)}, u32[]{:S(2)}, u32[]{:S(2)}) collective-permute-start(bf16[1,2,2,2,512,128]{5,4,3,2,1,0:T(8,128)(2,1)} %pad_maximum_fusion), channel_id=1, source_target_pairs={{0,2},{1,3},{2,0},{3,1},{4,6},{5,7},{6,4},{7,5},{8,10},{9,11},{10,... | collective-permute-start | bytes 3145736 | tf_op jit(solution)/shard_map/ppermute | solution.py:476
  129.4 30.6 %all-to-all-start.3 = ((f32[32,8,128]{2,1,0:T(8,128)}), f32[32,8,128]{2,1,0:T(8,128)S(1)}, u32[]{:S(2)}, u32[]{:S(2)}) async-start(f32[32,8,128]{2,1,0:T(8,128)} %copy-done.134), calls=%async_computation.3 | async-start | bytes 262144 | tf_op jit(solution)/shard_map/all_to_all | solution.py:1281
  138.3 12.2 %collective-permute-start.23 = (bf16[1,1,1,1,832,128]{5,4,3,2,1,0:T(8,128)(2,1)}, bf16[1,1,1,1,832,128]{5,4,3,2,1,0:T(8,128)(2,1)S(1)}, u32[]{:S(2)}, u32[]{:S(2)}) collective-permute-start(bf16[1,1,1,1,832,128]{5,4,3,2,1,0:T(8,128)(2,1)} %maximum_bitcast_fusion.4), channel_id=1, source_target_pairs={{0,8},{4,12},{8,0},{12,4},{16,24},{20,28},{24,16},{28,20},{1,9},{5... | collective-permute-start | bytes 638984 | tf_op jit(solution)/shard_map/ppermute | solution.py:478
  138.3 21.0 %collective-permute-start.22 = (bf16[1,1,1,1,832,128]{5,4,3,2,1,0:T(8,128)(2,1)}, bf16[1,1,1,1,832,128]{5,4,3,2,1,0:T(8,128)(2,1)S(1)}, u32[]{:S(2)}, u32[]{:S(2)}) collective-permute-start(bf16[1,1,1,1,832,128]{5,4,3,2,1,0:T(8,128)(2,1)} %maximum_bitcast_fusion.4), channel_id=1, source_target_pairs={{0,16},{4,20},{8,24},{12,28},{16,0},{20,4},{24,8},{28,12},{1,17},{... | collective-permute-start | bytes 638984 | tf_op jit(solution)/shard_map/ppermute | solution.py:478
  178.7 53.2 %collective-permute-start.34 = (bf16[2,2,2,1,416,128]{5,4,3,2,1,0:T(8,128)(2,1)}, bf16[2,2,2,1,416,128]{5,4,3,2,1,0:T(8,128)(2,1)}, u32[]{:S(2)}, u32[]{:S(2)}) collective-permute-start(bf16[2,2,2,1,416,128]{5,4,3,2,1,0:T(8,128)(2,1)} %pad_maximum_fusion.3), channel_id=1, source_target_pairs={{0,4},{4,0},{8,12},{12,8},{16,20},{20,16},{24,28},{28,24},{1,5},{5... | collective-permute-start | bytes 2555912 | tf_op jit(solution)/shard_map/ppermute | solution.py:478
  181.2 50.6 %collective-permute-start.33 = (bf16[1,2,2,2,416,128]{5,4,3,2,1,0:T(8,128)(2,1)}, bf16[1,2,2,2,416,128]{5,4,3,2,1,0:T(8,128)(2,1)}, u32[]{:S(2)}, u32[]{:S(2)}) collective-permute-start(bf16[1,2,2,2,416,128]{5,4,3,2,1,0:T(8,128)(2,1)} %pad_maximum_fusion.2), channel_id=1, source_target_pairs={{0,2},{1,3},{2,0},{3,1},{4,6},{5,7},{6,4},{7,5},{8,10},{9,11},{10,... | collective-permute-start | bytes 2555912 | tf_op jit(solution)/shard_map/ppermute | solution.py:476
  183.0 18.4 %collective-permute-start.29 = (f32[64,128]{1,0:T(8,128)S(1)}, f32[64,128]{1,0:T(8,128)S(1)}, u32[]{:S(2)}, u32[]{:S(2)}) collective-permute-start(f32[64,128]{1,0:T(8,128)S(1)} %add.2733), channel_id=1, source_target_pairs={{0,2},{1,3},{2,0},{3,1},{4,6},{5,7},{6,4},{7,5},{8,10},{9,11},{10,... | collective-permute-start | bytes 98312 | tf_op jit(solution)/shard_map/ppermute | solution.py:476
  256.6 28.1 %all-to-all-start.6 = ((bf16[4,176,512]{2,1,0:T(8,128)(2,1)}), bf16[4,176,512]{2,1,0:T(8,128)(2,1)}, u32[]{:S(2)}, u32[]{:S(2)}) async-start(bf16[4,176,512]{2,1,0:T(8,128)(2,1)} %bitcast.149), calls=%async_computation.6 | async-start | bytes 1441792 | tf_op jit(solution)/shard_map/all_to_all | solution.py:1374
  326.7 14.7 %collective-permute-start.46 = (bf16[2,2,2,2,256,128]{5,4,3,2,1,0:T(8,128)(2,1)}, bf16[2,2,2,2,256,128]{5,4,3,2,1,0:T(8,128)(2,1)}, u32[]{:S(2)}, u32[]{:S(2)}) collective-permute-start(bf16[2,2,2,2,256,128]{5,4,3,2,1,0:T(8,128)(2,1)} %bitcast.144), channel_id=1, source_target_pairs={{0,1},{1,0},{2,3},{3,2},{4,5},{5,4},{6,7},{7,6},{8,9},{9,8},{10,11... | collective-permute-start | bytes 3145736 | tf_op jit(solution)/shard_map/ppermute | solution.py:476
  341.5 13.1 %all-to-all-start.9 = ((f32[32,8,128]{2,1,0:T(8,128)}), f32[32,8,128]{2,1,0:T(8,128)}, u32[]{:S(2)}, u32[]{:S(2)}) async-start(f32[32,8,128]{2,1,0:T(8,128)} %copy-done.135), calls=%async_computation.9 | async-start | bytes 262144 | tf_op jit(solution)/shard_map/all_to_all | solution.py:1281
  354.6 19.5 %collective-permute-start.49 = (bf16[2,2,2,2,576,128]{5,4,3,2,1,0:T(8,128)(2,1)}, bf16[2,2,2,2,576,128]{5,4,3,2,1,0:T(8,128)(2,1)}, u32[]{:S(2)}, u32[]{:S(2)}) collective-permute-start(bf16[2,2,2,2,576,128]{5,4,3,2,1,0:T(8,128)(2,1)} %bitcast.143), channel_id=1, source_target_pairs={{0,1},{1,0},{2,3},{3,2},{4,5},{5,4},{6,7},{7,6},{8,9},{9,8},{10,11... | collective-permute-start | bytes 7077896 | tf_op jit(solution)/shard_map/ppermute | solution.py:476
  356.7 17.3 %collective-permute-start.47 = (bf16[1,2,2,2,128,128]{5,4,3,2,1,0:T(8,128)(2,1)}, bf16[1,2,2,2,128,128]{5,4,3,2,1,0:T(8,128)(2,1)}, u32[]{:S(2)}, u32[]{:S(2)}) collective-permute-start(bf16[1,2,2,2,128,128]{5,4,3,2,1,0:T(8,128)(2,1)} %add_convert_fusion.13), channel_id=1, source_target_pairs={{0,2},{1,3},{2,0},{3,1},{4,6},{5,7},{6,4},{7,5},{8,10},{9,11},{10,... | collective-permute-start | bytes 786440 | tf_op jit(solution)/shard_map/ppermute | solution.py:476
  360.2 13.9 %collective-permute-start.48 = (bf16[2,2,2,1,128,128]{5,4,3,2,1,0:T(8,128)(2,1)}, bf16[2,2,2,1,128,128]{5,4,3,2,1,0:T(8,128)(2,1)}, u32[]{:S(2)}, u32[]{:S(2)}) collective-permute-start(bf16[2,2,2,1,128,128]{5,4,3,2,1,0:T(8,128)(2,1)} %add_convert_fusion.12), channel_id=1, source_target_pairs={{0,4},{4,0},{8,12},{12,8},{16,20},{20,16},{24,28},{28,24},{1,5},{5... | collective-permute-start | bytes 786440 | tf_op jit(solution)/shard_map/ppermute | solution.py:478
  378.7 45.9 %collective-permute-start.57 = (bf16[1,2,2,2,288,128]{5,4,3,2,1,0:T(8,128)(2,1)}, bf16[1,2,2,2,288,128]{5,4,3,2,1,0:T(8,128)(2,1)}, u32[]{:S(2)}, u32[]{:S(2)}) collective-permute-start(bf16[1,2,2,2,288,128]{5,4,3,2,1,0:T(8,128)(2,1)} %add_convert_fusion.5), channel_id=1, source_target_pairs={{0,2},{1,3},{2,0},{3,1},{4,6},{5,7},{6,4},{7,5},{8,10},{9,11},{10,... | collective-permute-start | bytes 1769480 | tf_op jit(solution)/shard_map/ppermute | solution.py:476
  379.3 46.0 %collective-permute-start.58 = (bf16[2,2,2,1,288,128]{5,4,3,2,1,0:T(8,128)(2,1)}, bf16[2,2,2,1,288,128]{5,4,3,2,1,0:T(8,128)(2,1)}, u32[]{:S(2)}, u32[]{:S(2)}) collective-permute-start(bf16[2,2,2,1,288,128]{5,4,3,2,1,0:T(8,128)(2,1)} %add_convert_fusion.4), channel_id=1, source_target_pairs={{0,4},{4,0},{8,12},{12,8},{16,20},{20,16},{24,28},{28,24},{1,5},{5... | collective-permute-start | bytes 1769480 | tf_op jit(solution)/shard_map/ppermute | solution.py:478
  380.9 13.7 %collective-permute-start.51 = (f32[48,128]{1,0:T(8,128)S(1)}, f32[48,128]{1,0:T(8,128)}, u32[]{:S(2)}, u32[]{:S(2)}) collective-permute-start(f32[48,128]{1,0:T(8,128)S(1)} %add.2752), channel_id=1, source_target_pairs={{0,2},{1,3},{2,0},{3,1},{4,6},{5,7},{6,4},{7,5},{8,10},{9,11},{10,... | collective-permute-start | bytes 73736 | tf_op jit(solution)/shard_map/ppermute | solution.py:476
  397.2 26.8 %collective-permute-start.56 = (bf16[1,2,2,1,128,128]{5,4,3,2,1,0:T(8,128)(2,1)S(1)}, bf16[1,2,2,1,128,128]{5,4,3,2,1,0:T(8,128)(2,1)S(1)}, u32[]{:S(2)}, u32[]{:S(2)}) collective-permute-start(bf16[1,2,2,1,128,128]{5,4,3,2,1,0:T(8,128)(2,1)S(1)} %get-tuple-element.633), channel_id=1, source_target_pairs={{0,2},{1,3},{2,0},{3,1},{4,6},{5,7},{6,4},{7,5},{8,10},{9,11},{10,... | collective-permute-start | bytes 393224 | tf_op jit(solution)/shard_map/ppermute | solution.py:476
  397.6 26.4 %collective-permute-start.55 = (bf16[1,2,2,1,128,128]{5,4,3,2,1,0:T(8,128)(2,1)S(1)}, bf16[1,2,2,1,128,128]{5,4,3,2,1,0:T(8,128)(2,1)S(1)}, u32[]{:S(2)}, u32[]{:S(2)}) collective-permute-start(bf16[1,2,2,1,128,128]{5,4,3,2,1,0:T(8,128)(2,1)S(1)} %get-tuple-element.634), channel_id=1, source_target_pairs={{0,4},{4,0},{8,12},{12,8},{16,20},{20,16},{24,28},{28,24},{1,5},{5... | collective-permute-start | bytes 393224 | tf_op jit(solution)/shard_map/ppermute | solution.py:478
  425.3 15.8 %all-to-all-start.10 = ((f32[32,8,128]{2,1,0:T(8,128)}), f32[32,8,128]{2,1,0:T(8,128)}, u32[]{:S(2)}, u32[]{:S(2)}) async-start(f32[32,8,128]{2,1,0:T(8,128)} %copy-done.132), calls=%async_computation.10 | async-start | bytes 262144 | tf_op jit(solution)/shard_map/all_to_all | solution.py:1281
  441.1 17.5 %collective-permute-start.61 = (bf16[2,2,2,2,1024,128]{5,4,3,2,1,0:T(8,128)(2,1)}, bf16[2,2,2,2,1024,128]{5,4,3,2,1,0:T(8,128)(2,1)}, u32[]{:S(2)}, u32[]{:S(2)}) collective-permute-start(bf16[2,2,2,2,1024,128]{5,4,3,2,1,0:T(8,128)(2,1)} %bitcast.111), channel_id=1, source_target_pairs={{0,1},{1,0},{2,3},{3,2},{4,5},{5,4},{6,7},{7,6},{8,9},{9,8},{10,11... | collective-permute-start | bytes 12582920 | tf_op jit(solution)/shard_map/ppermute | solution.py:476
  442.9 15.6 %collective-permute-start.60 = (bf16[1,2,2,1,288,128]{5,4,3,2,1,0:T(8,128)(2,1)S(1)}, bf16[1,2,2,1,288,128]{5,4,3,2,1,0:T(8,128)(2,1)}, u32[]{:S(2)}, u32[]{:S(2)}) collective-permute-start(bf16[1,2,2,1,288,128]{5,4,3,2,1,0:T(8,128)(2,1)S(1)} %get-tuple-element.620), channel_id=1, source_target_pairs={{0,2},{1,3},{2,0},{3,1},{4,6},{5,7},{6,4},{7,5},{8,10},{9,11},{10,... | collective-permute-start | bytes 884744 | tf_op jit(solution)/shard_map/ppermute | solution.py:476
  444.6 13.9 %collective-permute-start.59 = (bf16[1,2,2,1,288,128]{5,4,3,2,1,0:T(8,128)(2,1)S(1)}, bf16[1,2,2,1,288,128]{5,4,3,2,1,0:T(8,128)(2,1)}, u32[]{:S(2)}, u32[]{:S(2)}) collective-permute-start(bf16[1,2,2,1,288,128]{5,4,3,2,1,0:T(8,128)(2,1)S(1)} %get-tuple-element.621), channel_id=1, source_target_pairs={{0,4},{4,0},{8,12},{12,8},{16,20},{20,16},{24,28},{28,24},{1,5},{5... | collective-permute-start | bytes 884744 | tf_op jit(solution)/shard_map/ppermute | solution.py:478
  458.5 17.6 %all-to-all-start.11 = ((f32[32,8,128]{2,1,0:T(8,128)}), f32[32,8,128]{2,1,0:T(8,128)S(1)}, u32[]{:S(2)}, u32[]{:S(2)}) async-start(f32[32,8,128]{2,1,0:T(8,128)} %copy-done.133), calls=%async_computation.11 | async-start | bytes 262144 | tf_op jit(solution)/shard_map/all_to_all | solution.py:1281
  476.2 47.6 %collective-permute-start.64 = (bf16[2,2,2,2,576,128]{5,4,3,2,1,0:T(8,128)(2,1)}, bf16[2,2,2,2,576,128]{5,4,3,2,1,0:T(8,128)(2,1)}, u32[]{:S(2)}, u32[]{:S(2)}) collective-permute-start(bf16[2,2,2,2,576,128]{5,4,3,2,1,0:T(8,128)(2,1)} %bitcast.142), channel_id=1, source_target_pairs={{0,1},{1,0},{2,3},{3,2},{4,5},{5,4},{6,7},{7,6},{8,9},{9,8},{10,11... | collective-permute-start | bytes 7077896 | tf_op jit(solution)/shard_map/ppermute | solution.py:476
  476.4 14.4 %all-to-all-start.7 = ((bf16[4,176,512]{2,1,0:T(8,128)(2,1)}), bf16[4,176,512]{2,1,0:T(8,128)(2,1)S(1)}, u32[]{:S(2)}, u32[]{:S(2)}) async-start(bf16[4,176,512]{2,1,0:T(8,128)(2,1)} %get-tuple-element.316), calls=%async_computation.7 | async-start | bytes 1441792 | tf_op jit(solution)/shard_map/all_to_all | solution.py:1468
  495.0 24.8 %collective-permute-start.62 = (bf16[1,2,2,2,512,128]{5,4,3,2,1,0:T(8,128)(2,1)S(1)}, bf16[1,2,2,2,512,128]{5,4,3,2,1,0:T(8,128)(2,1)S(1)}, u32[]{:S(2)}, u32[]{:S(2)}) collective-permute-start(bf16[1,2,2,2,512,128]{5,4,3,2,1,0:T(8,128)(2,1)S(1)} %add_convert_fusion.1), channel_id=1, source_target_pairs={{0,2},{1,3},{2,0},{3,1},{4,6},{5,7},{6,4},{7,5},{8,10},{9,11},{10,... | collective-permute-start | bytes 3145736 | tf_op jit(solution)/shard_map/ppermute | solution.py:476
  497.3 25.0 %collective-permute-start.63 = (bf16[2,2,2,1,512,128]{5,4,3,2,1,0:T(8,128)(2,1)S(1)}, bf16[2,2,2,1,512,128]{5,4,3,2,1,0:T(8,128)(2,1)S(1)}, u32[]{:S(2)}, u32[]{:S(2)}) collective-permute-start(bf16[2,2,2,1,512,128]{5,4,3,2,1,0:T(8,128)(2,1)S(1)} %add_convert_fusion), channel_id=1, source_target_pairs={{0,4},{4,0},{8,12},{12,8},{16,20},{20,16},{24,28},{28,24},{1,5},{5... | collective-permute-start | bytes 3145736 | tf_op jit(solution)/shard_map/ppermute | solution.py:478
  500.2 27.2 %collective-permute-start.85 = (bf16[1,1,1,1,256,128]{5,4,3,2,1,0:T(8,128)(2,1)S(1)}, bf16[1,1,1,1,256,128]{5,4,3,2,1,0:T(8,128)(2,1)S(1)}, u32[]{:S(2)}, u32[]{:S(2)}) collective-permute-start(bf16[1,1,1,1,256,128]{5,4,3,2,1,0:T(8,128)(2,1)S(1)} %pad_maximum_fusion.16), channel_id=1, source_target_pairs={{0,8},{4,12},{8,0},{12,4},{16,24},{20,28},{24,16},{28,20},{1,9},{5... | collective-permute-start | bytes 196616 | tf_op jit(solution)/shard_map/ppermute | solution.py:478
  501.7 27.0 %collective-permute-start.86 = (bf16[1,1,1,1,256,128]{5,4,3,2,1,0:T(8,128)(2,1)S(1)}, bf16[1,1,1,1,256,128]{5,4,3,2,1,0:T(8,128)(2,1)S(1)}, u32[]{:S(2)}, u32[]{:S(2)}) collective-permute-start(bf16[1,1,1,1,256,128]{5,4,3,2,1,0:T(8,128)(2,1)S(1)} %pad_maximum_fusion.17), channel_id=1, source_target_pairs={{0,24},{4,28},{8,16},{12,20},{16,8},{20,12},{24,0},{28,4},{1,25},{... | collective-permute-start | bytes 196616 | tf_op jit(solution)/shard_map/ppermute | solution.py:478
  528.7 25.5 %collective-permute-start.70 = (bf16[1,2,2,2,288,128]{5,4,3,2,1,0:T(8,128)(2,1)S(1)}, bf16[1,2,2,2,288,128]{5,4,3,2,1,0:T(8,128)(2,1)S(1)}, u32[]{:S(2)}, u32[]{:S(2)}) collective-permute-start(bf16[1,2,2,2,288,128]{5,4,3,2,1,0:T(8,128)(2,1)S(1)} %add_convert_fusion.3), channel_id=1, source_target_pairs={{0,2},{1,3},{2,0},{3,1},{4,6},{5,7},{6,4},{7,5},{8,10},{9,11},{10,... | collective-permute-start | bytes 1769480 | tf_op jit(solution)/shard_map/ppermute | solution.py:476
  530.1 24.1 %collective-permute-start.71 = (bf16[2,2,2,1,288,128]{5,4,3,2,1,0:T(8,128)(2,1)S(1)}, bf16[2,2,2,1,288,128]{5,4,3,2,1,0:T(8,128)(2,1)S(1)}, u32[]{:S(2)}, u32[]{:S(2)}) collective-permute-start(bf16[2,2,2,1,288,128]{5,4,3,2,1,0:T(8,128)(2,1)S(1)} %add_convert_fusion.2), channel_id=1, source_target_pairs={{0,4},{4,0},{8,12},{12,8},{16,20},{20,16},{24,28},{28,24},{1,5},{5... | collective-permute-start | bytes 1769480 | tf_op jit(solution)/shard_map/ppermute | solution.py:478
  533.9 19.5 %collective-permute-start.69 = (bf16[1,2,2,1,512,128]{5,4,3,2,1,0:T(8,128)(2,1)S(1)}, bf16[1,2,2,1,512,128]{5,4,3,2,1,0:T(8,128)(2,1)S(1)}, u32[]{:S(2)}, u32[]{:S(2)}) collective-permute-start(bf16[1,2,2,1,512,128]{5,4,3,2,1,0:T(8,128)(2,1)S(1)} %get-tuple-element.594), channel_id=1, source_target_pairs={{0,2},{1,3},{2,0},{3,1},{4,6},{5,7},{6,4},{7,5},{8,10},{9,11},{10,... | collective-permute-start | bytes 1572872 | tf_op jit(solution)/shard_map/ppermute | solution.py:476
  538.7 15.6 %collective-permute-start.68 = (bf16[1,2,2,1,512,128]{5,4,3,2,1,0:T(8,128)(2,1)S(1)}, bf16[1,2,2,1,512,128]{5,4,3,2,1,0:T(8,128)(2,1)S(1)}, u32[]{:S(2)}, u32[]{:S(2)}) collective-permute-start(bf16[1,2,2,1,512,128]{5,4,3,2,1,0:T(8,128)(2,1)S(1)} %get-tuple-element.595), channel_id=1, source_target_pairs={{0,4},{4,0},{8,12},{12,8},{16,20},{20,16},{24,28},{28,24},{1,5},{5... | collective-permute-start | bytes 1572872 | tf_op jit(solution)/shard_map/ppermute | solution.py:478
  557.4 17.3 %collective-permute-start.88 = (bf16[1,1,1,1,1024,128]{5,4,3,2,1,0:T(8,128)(2,1)}, bf16[1,1,1,1,1024,128]{5,4,3,2,1,0:T(8,128)(2,1)}, u32[]{:S(2)}, u32[]{:S(2)}) collective-permute-start(bf16[1,1,1,1,1024,128]{5,4,3,2,1,0:T(8,128)(2,1)} %pad_maximum_fusion.7), channel_id=1, source_target_pairs={{0,8},{4,12},{8,0},{12,4},{16,24},{20,28},{24,16},{28,20},{1,9},{5... | collective-permute-start | bytes 786440 | tf_op jit(solution)/shard_map/ppermute | solution.py:478
  559.8 15.0 %collective-permute-start.89 = (bf16[1,1,1,1,1024,128]{5,4,3,2,1,0:T(8,128)(2,1)}, bf16[1,1,1,1,1024,128]{5,4,3,2,1,0:T(8,128)(2,1)}, u32[]{:S(2)}, u32[]{:S(2)}) collective-permute-start(bf16[1,1,1,1,1024,128]{5,4,3,2,1,0:T(8,128)(2,1)} %pad_maximum_fusion.8), channel_id=1, source_target_pairs={{0,24},{4,28},{8,16},{12,20},{16,8},{20,12},{24,0},{28,4},{1,25},{... | collective-permute-start | bytes 786440 | tf_op jit(solution)/shard_map/ppermute | solution.py:478
  563.0 20.0 %collective-permute-start.87 = (bf16[1,1,1,1,1024,128]{5,4,3,2,1,0:T(8,128)(2,1)}, bf16[1,1,1,1,1024,128]{5,4,3,2,1,0:T(8,128)(2,1)}, u32[]{:S(2)}, u32[]{:S(2)}) collective-permute-start(bf16[1,1,1,1,1024,128]{5,4,3,2,1,0:T(8,128)(2,1)} %pad_maximum_fusion.6), channel_id=1, source_target_pairs={{0,16},{4,20},{8,24},{12,28},{16,0},{20,4},{24,8},{28,12},{1,17},{... | collective-permute-start | bytes 786440 | tf_op jit(solution)/shard_map/ppermute | solution.py:478
  563.7 62.1 %all-to-all-start.12 = ((bf16[4,704,256]{2,1,0:T(8,128)(2,1)}), bf16[4,704,256]{2,1,0:T(8,128)(2,1)}, u32[]{:S(2)}, u32[]{:S(2)}) async-start(bf16[4,704,256]{2,1,0:T(8,128)(2,1)} %copy-done.77), calls=%async_computation.12 | async-start | bytes 2883584 | tf_op jit(solution)/shard_map/all_to_all | solution.py:1569
  569.6 21.7 %collective-permute-start.77 = (bf16[1,2,2,1,128,128]{5,4,3,2,1,0:T(8,128)(2,1)S(1)}, bf16[1,2,2,1,128,128]{5,4,3,2,1,0:T(8,128)(2,1)S(1)}, u32[]{:S(2)}, u32[]{:S(2)}) collective-permute-start(bf16[1,2,2,1,128,128]{5,4,3,2,1,0:T(8,128)(2,1)S(1)} %get-tuple-element.650), channel_id=1, source_target_pairs={{0,6},{1,7},{2,4},{3,5},{4,2},{5,3},{6,0},{7,1},{8,14},{9,15},{10,... | collective-permute-start | bytes 393224 | tf_op jit(solution)/shard_map/ppermute | solution.py:480
  572.6 18.7 %collective-permute-start.76 = (bf16[1,2,2,1,128,128]{5,4,3,2,1,0:T(8,128)(2,1)S(1)}, bf16[1,2,2,1,128,128]{5,4,3,2,1,0:T(8,128)(2,1)S(1)}, u32[]{:S(2)}, u32[]{:S(2)}) collective-permute-start(bf16[1,2,2,1,128,128]{5,4,3,2,1,0:T(8,128)(2,1)S(1)} %get-tuple-element.651), channel_id=1, source_target_pairs={{0,4},{4,0},{8,12},{12,8},{16,20},{20,16},{24,28},{28,24},{1,5},{5... | collective-permute-start | bytes 393224 | tf_op jit(solution)/shard_map/ppermute | solution.py:478
  574.7 18.4 %collective-permute-start.75 = (bf16[1,2,2,1,128,128]{5,4,3,2,1,0:T(8,128)(2,1)S(1)}, bf16[1,2,2,1,128,128]{5,4,3,2,1,0:T(8,128)(2,1)S(1)}, u32[]{:S(2)}, u32[]{:S(2)}) collective-permute-start(bf16[1,2,2,1,128,128]{5,4,3,2,1,0:T(8,128)(2,1)S(1)} %get-tuple-element.652), channel_id=1, source_target_pairs={{0,2},{1,3},{2,0},{3,1},{4,6},{5,7},{6,4},{7,5},{8,10},{9,11},{10,... | collective-permute-start | bytes 393224 | tf_op jit(solution)/shard_map/ppermute | solution.py:476
  574.9 24.1 %collective-permute-start.74 = (bf16[1,2,2,1,288,128]{5,4,3,2,1,0:T(8,128)(2,1)S(1)}, bf16[1,2,2,1,288,128]{5,4,3,2,1,0:T(8,128)(2,1)S(1)}, u32[]{:S(2)}, u32[]{:S(2)}) collective-permute-start(bf16[1,2,2,1,288,128]{5,4,3,2,1,0:T(8,128)(2,1)S(1)} %get-tuple-element.615), channel_id=1, source_target_pairs={{0,2},{1,3},{2,0},{3,1},{4,6},{5,7},{6,4},{7,5},{8,10},{9,11},{10,... | collective-permute-start | bytes 884744 | tf_op jit(solution)/shard_map/ppermute | solution.py:476
  583.0 16.0 %collective-permute-start.73 = (bf16[1,2,2,1,288,128]{5,4,3,2,1,0:T(8,128)(2,1)S(1)}, bf16[1,2,2,1,288,128]{5,4,3,2,1,0:T(8,128)(2,1)S(1)}, u32[]{:S(2)}, u32[]{:S(2)}) collective-permute-start(bf16[1,2,2,1,288,128]{5,4,3,2,1,0:T(8,128)(2,1)S(1)} %get-tuple-element.616), channel_id=1, source_target_pairs={{0,4},{4,0},{8,12},{12,8},{16,20},{20,16},{24,28},{28,24},{1,5},{5... | collective-permute-start | bytes 884744 | tf_op jit(solution)/shard_map/ppermute | solution.py:478
  610.3 11.9 %collective-permute-start.78 = (bf16[1,1,1,1,576,128]{5,4,3,2,1,0:T(8,128)(2,1)S(1)}, bf16[1,1,1,1,576,128]{5,4,3,2,1,0:T(8,128)(2,1)S(1)}, u32[]{:S(2)}, u32[]{:S(2)}) collective-permute-start(bf16[1,1,1,1,576,128]{5,4,3,2,1,0:T(8,128)(2,1)S(1)} %pad_maximum_fusion.12), channel_id=1, source_target_pairs={{0,16},{4,20},{8,24},{12,28},{16,0},{20,4},{24,8},{28,12},{1,17},{... | collective-permute-start | bytes 442376 | tf_op jit(solution)/shard_map/ppermute | solution.py:478
  625.9 14.1 %all-to-all-start.13 = ((f32[32,16,128]{2,1,0:T(8,128)}), f32[32,16,128]{2,1,0:T(8,128)S(1)}, u32[]{:S(2)}, u32[]{:S(2)}) async-start(f32[32,16,128]{2,1,0:T(8,128)} %get-tuple-element.436), calls=%async_computation.13 | async-start | bytes 524288 | tf_op jit(solution)/shard_map/all_to_all | solution.py:1281
  (227 other events, 2028.5 us)

commit v4 on v3

--- a/solution.py
+++ b/solution.py
@@ -463,6 +463,9 @@
     )
 
 
+VMEM_BYTES = 62 * 2**20
+
+
 def fits(mesh, pixel_mask):
     sizes = (mesh.shape["dp"], mesh.shape["mp"])
     powers = all(size >= 2 and size & (size - 1) == 0 for size in sizes)
@@ -502,17 +505,14 @@
     return masks
 
 
-def everywhere(values):
-    if values.shape[0] <= 16:
-        count = lax.axis_size("dp") * lax.axis_size("mp")
-        copies = jnp.broadcast_to(values[None], (count,) + values.shape)
-        return jnp.sum(lax.all_to_all(copies, ("dp", "mp"), 0, 0, tiled=True), 0)
-    for axis in ("mp", "dp"):
-        mask = 1
-        while mask < lax.axis_size(axis):
-            values = values + swap(values, (axis, mask))
-            mask *= 2
-    return values
+def everywhere(values, flows=()):
+    mask = 1
+    while mask < lax.axis_size("mp"):
+        values = values + swap(values, ("mp", mask))
+        mask *= 2
+    copies = jnp.broadcast_to(values[None], (lax.axis_size("dp"),) + values.shape)
+    arrived = lax.all_to_all(copies, "dp", 0, 0, tiled=True)
+    return wave(flows, values, arrived) if flows else arrived
 
 
 def pack(block):
@@ -534,27 +534,64 @@
     return ((0, first), (first, rows))
 
 
-def merged(parts, bits, dims):
-    if not bits:
-        return parts[0]
-    high = bit_of(*bits[-1]) > 0
-    half = len(parts) // 2
-    first = [jnp.where(high, parts[half + at], parts[at]) for at in range(half)]
-    second = [jnp.where(high, parts[at], parts[half + at]) for at in range(half)]
-    pair = [merged(first, bits[:-1], dims), merged(second, bits[:-1], dims)]
-    return jnp.concatenate(pair, dims.index(bits[-1]))
+def moves_kernel(tasks, count, places, *refs):
+    sources, outs, sems = refs[:count], refs[count:-1], refs[-1]
+    copies = []
+    for at, (source, span, out, turns, rows) in enumerate(tasks):
+        dims = len(sources[source].shape) - 2
+        every = [slice(None)] * dims
+        start = [
+            pl.ds(1 - places[dim] if turns[dim] else places[dim], 1) if dim in turns else slice(None)
+            for dim in range(dims)
+        ]
+        copies.append(
+            pltpu.make_async_copy(
+                sources[source].at[(*every, pl.ds(*span), slice(None))],
+                outs[out].at[(*start, pl.ds(*rows), slice(None))],
+                sems.at[at],
+            )
+        )
+        copies[-1].start()
+    for copy in copies:
+        copy.wait()
+
+
+def moves(wanted):
+    sources = []
+    tasks = []
+    for out, (shape, pieces) in enumerate(wanted):
+        for source, span, turns, rows in pieces:
+            tasks.append((len(sources), span, out, turns, rows))
+            sources.append(source)
+    bits = column_bits() + row_bits()
+    places = jnp.stack([bit_of(*bit) for bit in bits]).astype(jnp.int32)
+    return pl.pallas_call(
+        functools.partial(moves_kernel, tasks, len(sources)),
+        in_specs=[pl.BlockSpec(memory_space=pltpu.SMEM)]
+        + [pl.BlockSpec(memory_space=pltpu.HBM)] * len(sources),
+        out_specs=[pl.BlockSpec(memory_space=pltpu.VMEM)] * len(wanted),
+        out_shape=[jax.ShapeDtypeStruct(shape, jnp.bfloat16) for shape, _ in wanted],
+        scratch_shapes=[pltpu.SemaphoreType.DMA((len(tasks),))],
+        compiler_params=pltpu.CompilerParams(vmem_limit_bytes=VMEM_BYTES),
+        cost_estimate=pl.CostEstimate(
+            flops=0,
+            bytes_accessed=sum(2 * source.size * 2 for source in sources),
+            transcendentals=0,
+        ),
+    )(places, *sources)
 
 
 class Gather:
     def __init__(self, rows, lanes=True):
         self.dims = column_bits() + row_bits()
         near = row_bits()[-1:]
+        self.rows = rows.shape[0]
         if lanes:
             self.steps = [[row_bits()[:-1]], [near, column_bits()], [column_bits(), near]]
-            self.spans = lanes_of(rows.shape[0])
+            self.spans = lanes_of(self.rows)
         else:
             self.steps = [[row_bits()[:-1]], [near + column_bits()]]
-            self.spans = ((0, rows.shape[0]),)
+            self.spans = ((0, self.rows),)
         self.parts = [([rows.reshape((1,) * len(self.dims) + rows.shape)], [])]
         self.step = 0
 
@@ -564,20 +601,47 @@
     def resume(self, values):
         self.parts = [(value, bits) for value, (_, bits) in zip(values, self.parts)]
 
-    def launch(self):
-        values = [merged(parts, bits, self.dims) for parts, bits in self.parts]
+    def wanted(self):
+        if not self.parts[0][1]:
+            return []
+        last = self.step == len(self.steps)
+        split = not last and len(self.steps[self.step]) > len(self.parts)
+        lanes = [(low, high - low) for low, high in self.spans]
+        result = []
+        for lane, (values, bits) in enumerate(self.parts):
+            shape = [
+                2 if bit in bits else size
+                for bit, size in zip(self.dims, values[0].shape)
+            ]
+            pieces = [
+                (value, {self.dims.index(bit): bit in turned for bit in bits})
+                for value, turned in zip(values, subsets(bits))
+            ]
+            height = values[0].shape[-2]
+            for low, size in lanes if split else [(0, height)]:
+                block = [(value, (low, size), turns, (0, size)) for value, turns in pieces]
+                result.append((tuple(shape) + (size, 128), block))
+        if last:
+            pieces = [
+                (value, span, turns, lanes[lane])
+                for lane, (_, block) in enumerate(result)
+                for value, span, turns, _ in block
+            ]
+            result = [(result[0][0][:-2] + (self.rows, 128), pieces)]
+        return result
+
+    def launch(self, values):
+        if not values:
+            values = [self.parts[0][0][0]]
         if self.step < len(self.steps):
-            groups = self.steps[self.step]
-            if len(groups) > len(values):
-                values = [values[0][..., low:high, :] for low, high in self.spans]
             self.parts = [
                 ([value] + [swap(value, *bits) for bits in subsets(group)[1:]], group)
-                for value, group in zip(values, groups)
+                for value, group in zip(values, self.steps[self.step])
             ]
         else:
-            value = jnp.concatenate(values, -2) if len(values) > 1 else values[0]
-            self.parts = [([value, swap(value, ("mp", 1))], [])]
+            self.parts = [([values[0], swap(values[0], ("mp", 1))], [])]
         self.step += 1
+        return values
 
     def bundles(self):
         shape = (1 << len(column_bits()), lax.axis_size("dp")) + self.parts[0][0][0].shape[-2:]
@@ -623,10 +687,15 @@
         old = [(index, settled + group, part) for index, settled, part in self.lanes[lane]]
         self.lanes[lane] = old + [(index, [], span) for index in arrived]
 
-    def launch(self):
+    def wanted(self):
+        return []
+
+    def launch(self, values):
         groups = self.steps[self.step]
         whole = self.step == len(self.steps) - 1
+        sent = []
         if groups is None:
+            sent.append(self.raw[1])
             self.raw[1] = swap(self.raw[1], ("mp", 1))
             for lane, span in zip(self.lanes, self.spans):
                 lane += [(0, [], span), (1, [], span)]
@@ -639,6 +708,7 @@
                 ]
                 out = jnp.concatenate(out, -2) if len(out) > 1 else out[0]
                 arrived.append(len(self.raw))
+                sent.append(out)
                 self.raw.append(swap(out, *bits))
             for lane, span in enumerate(self.spans):
                 self.settle(lane, groups[lane], arrived, span)
@@ -648,9 +718,11 @@
                 for bits in subsets(group)[1:]:
                     out = self.fold(lane, group, bits).astype(jnp.bfloat16)
                     arrived.append(len(self.raw))
+                    sent.append(out)
                     self.raw.append(swap(out, *bits))
                 self.settle(lane, group, arrived, None)
         self.step += 1
+        return sent
 
     def rows(self):
         total = [self.fold(lane) for lane in range(len(self.lanes))]
@@ -658,12 +730,21 @@
         return total.reshape(total.shape[-2:])
 
 
-def wave(flows, anchor=()):
-    anchor, values = lax.optimization_barrier((anchor, [flow.pending() for flow in flows]))
+def wave(flows, after=None, before=None):
+    values = [flow.pending() for flow in flows]
+    if after is not None:
+        values, _ = lax.optimization_barrier((values, after))
     for flow, value in zip(flows, values):
         flow.resume(value)
-        flow.launch()
-    return anchor
+    wanted = [flow.wanted() for flow in flows]
+    joined = [value for part in wanted for value in part]
+    made = list(moves(joined)) if joined else []
+    sent = []
+    for flow, part in zip(flows, wanted):
+        sent += flow.launch([made.pop(0) for _ in part])
+    if before is not None:
+        before, _ = lax.optimization_barrier((before, sent))
+    return before
 
 
 def chunk_kernel(units, columns, rows_ref, cols_ref, *refs):
@@ -707,7 +788,7 @@
         out_specs=[block, block],
         out_shape=[shape, shape],
         input_output_aliases={2 + place: place for place in range(len(earlier))},
-        compiler_params=pltpu.CompilerParams(vmem_limit_bytes=24 * 2**20),
+        compiler_params=pltpu.CompilerParams(vmem_limit_bytes=VMEM_BYTES),
         cost_estimate=pl.CostEstimate(
             flops=2 * rows_of.size * cols_of.shape[1],
             bytes_accessed=2 * (rows_of.size + cols_of.size)
@@ -951,7 +1032,7 @@
     copies = fetch((first, second), held, sems, start)
     core = core[0]
     centred_third, centred_side, act = joined_acts(
-        sums_in[...], third, side, wide, counts[1:2, :]
+        total_of(sums_in), third, side, wide, counts[1:2, :]
     )
     above[...] = (jax.nn.silu(act) * mask[...]).astype(jnp.bfloat16)
     arrive(copies)
@@ -961,7 +1042,7 @@
 
 
 def last_layer(sixth, sums_in, counts, wide, above, cotangent, mask, out, grad, sums):
-    level = levels(sums_in[...], 0, sixth.shape[1], counts[1:2, :])
+    level = levels(total_of(sums_in), 0, sixth.shape[1], counts[1:2, :])
     centred = standard(sixth[...], level)
     act = centred * wide[4:5, :] + wide[5:6, :] + above[...].astype(jnp.float32)
     weights = mask[...]
@@ -1010,9 +1091,9 @@
     core = core[0]
     width = sixth.shape[1]
     count = counts[1:2, :]
-    level = levels(sums_six[...], 0, width, count)
+    level = levels(total_of(sums_six), 0, width, count)
     grad_out[...] = back_through(
-        grad[...], standard(sixth[...], level), level, wide[4:5, :], mask[...], back_six[...], 0,
+        grad[...], standard(sixth[...], level), level, wide[4:5, :], mask[...], total_of(back_six), 0,
         width // 128, count,
     ).astype(jnp.bfloat16)
     arrive(copies)
@@ -1030,8 +1111,8 @@
     width = third.shape[1]
     rows = width // 128
     count = counts[1:2, :]
-    total = sums_pair[...]
-    back = back_pair[...]
+    total = total_of(sums_pair)
+    back = total_of(back_pair)
     groups = held.shape[1]
     level = levels(total, 0, width, count)
     grad_third[...] = back_through(
@@ -1084,7 +1165,7 @@
     for place, part in enumerate(parts):
         big[:, place * size : (place + 1) * size] = part
     centred_third, centred_side, act = joined_acts(
-        sums_pair[...], third, side, wide, counts[1:2, :]
+        total_of(sums_pair), third, side, wide, counts[1:2, :]
     )
     result = (grad_two[...] + big[...]) * mask[...] * slope(act)
     grad_in[...] = result
@@ -1128,11 +1209,6 @@
         out[owner, pixels:, span] = (part[pixels:] * weights[pixels:]).astype(jnp.bfloat16)
 
 
-class Far:
-    def __init__(self, value):
-        self.value = value
-
-
 class Coming:
     def __init__(self, ref, copy):
         self.ref = ref
@@ -1169,8 +1245,7 @@
     if bundles:
         held = [pltpu.VMEM((2,) + bundles[0].shape[:2] + (rows, 128), jnp.bfloat16)]
         sems = [pltpu.SemaphoreType.DMA((2,))]
-    places = [place for place, value in enumerate(values) if isinstance(value, Far)]
-    values = [value.value if isinstance(value, Far) else value for value in values]
+    places = [place for place, value in enumerate(values) if value.dtype != jnp.int32]
     moved = sum(value.size * value.dtype.itemsize for value in list(values) + list(shapes))
     specs = []
     for place, value in enumerate(values):
@@ -1187,7 +1262,7 @@
         out_specs=[pl.BlockSpec(memory_space=pltpu.VMEM)] * len(shapes),
         out_shape=list(shapes),
         scratch_shapes=held + [pltpu.VMEM(shape, jnp.float32) for shape in scratch] + sems + late,
-        compiler_params=pltpu.CompilerParams(vmem_limit_bytes=40 * 2**20),
+        compiler_params=pltpu.CompilerParams(vmem_limit_bytes=VMEM_BYTES),
         cost_estimate=pl.CostEstimate(
             flops=2 * work, bytes_accessed=moved + rows * 16 * 512, transcendentals=0
         ),
@@ -1333,10 +1408,10 @@
             [pack(last_weight[1].astype(low).T[None]), pack(middle_weight[1].astype(low))]
         )
     )
-    field = wave([flow_a, flow_b], field)
     field = lax.all_to_all(field, "mp", 0, 0, tiled=True)
     wave([flow_a, flow_b])
-    field = wave([flow_a, flow_b, flow_c], field)
+    wave([flow_a, flow_b, flow_c], field)
+    wave([flow_a, flow_b, flow_d])
     unit_in, column = first_weight.shape
     column_wide = shortcut_weight.shape[1]
     unit_mid = middle_weight.shape[2]
@@ -1389,31 +1464,29 @@
     field, pre_one, sums = launch(
         first_layer,
         [short(full, ranks * channels), real(full, narrow), real(devices, 2 * size + 8, 128)],
-        [core, field, Far(mask_in)],
+        [core, field, mask_in],
         bundle_a,
         unit_in,
         work=field.size * narrow,
     )
-    sums = wave([flow_b, flow_c], sums)
-    sums_one = exchange(sums)
-    sums_one = wave([flow_c, flow_d], sums_one)
+    sums_one = wave([flow_b, flow_c], sums, exchange(sums))
     counts = jnp.sum(sums_one[:, 2 * size :], 0)
     bundle_b = flow_b.bundles()
     cols_one, pre_two, sums = launch(
         functools.partial(spread_layer, 0, 0, STRIDED_TAPS),
         [short(pixels, 9 * narrow), real(pixels, narrow), copies],
-        [core, pre_one, sums_one, Far(counts), Far(narrow_all), Far(keep), Far(mask_in), Far(mask), Far(inside)],
+        [core, pre_one, sums_one, counts, narrow_all, keep, mask_in, mask, inside],
         bundle_b,
         size_mid,
         work=9 * pixels * narrow * narrow,
     )
-    sums_two = exchange(sums)
-    sums_two = wave([flow_c, flow_d], sums_two)
+    sums_two = wave([flow_c], sums, exchange(sums))
+    wave([flow_c, flow_d], sums_two)
     bundle_c = flow_c.bundles()
     pre_side, side_sums = launch(
         functools.partial(side_layer, 0),
         [real(pixels, wide), real(2 * wide_rows, 128)],
-        [core, Far(field), Far(mask)],
+        [core, field, mask],
         bundle_c,
         size_short,
         work=pixels * field.shape[1] * wide,
@@ -1421,29 +1494,27 @@
     hid_two, pre_three, sums = launch(
         functools.partial(widen_layer, size_short, 1),
         [short(pixels, narrow), real(pixels, wide), real(2 * wide_rows, 128)],
-        [core, pre_two, sums_two, Far(counts), Far(narrow_all), Far(keep), Far(mask)],
+        [core, pre_two, sums_two, counts, narrow_all, keep, mask],
         bundle_c,
         size_out,
         [(pixels, narrow)],
         work=pixels * narrow * wide,
     )
-    sums = wave([flow_d], jnp.concatenate([sums, side_sums], 0))
-    sums_pair = everywhere(sums)
+    sums_pair = everywhere(jnp.concatenate([sums, side_sums], 0), [flow_d])
     out_one, pre_four, sums = launch(
         functools.partial(narrow_layer, size_short + size_out),
         [short(pixels, wide), real(pixels, narrow), copies],
-        [core, pre_three, Far(pre_side), sums_pair, Far(counts), Far(wide_all), Far(mask)],
+        [core, pre_three, pre_side, sums_pair, counts, wide_all, mask],
         bundle_c,
         size_out,
         work=pixels * narrow * wide,
     )
-    sums_four = exchange(sums)
-    sums_four = wave([flow_d], sums_four)
+    sums_four = wave([flow_d], sums, exchange(sums))
     bundle_d = flow_d.bundles()
     cols_four, pre_five, sums = launch(
         functools.partial(spread_layer, size_out, 2, PLAIN_TAPS),
         [short(pixels, 9 * narrow), real(pixels, narrow), copies],
-        [core, pre_four, sums_four, Far(counts), Far(narrow_all), Far(keep), Far(mask), Far(mask), Far(inside)],
+        [core, pre_four, sums_four, counts, narrow_all, keep, mask, mask, inside],
         bundle_d,
         size_mid,
         work=9 * pixels * narrow * narrow,
@@ -1452,7 +1523,7 @@
     hid_five, pre_six, sums = launch(
         functools.partial(widen_layer, 0, 3),
         [short(pixels, narrow), real(pixels, wide), real(2 * wide_rows, 128)],
-        [core, pre_five, sums_five, Far(counts), Far(narrow_all), Far(keep), Far(mask)],
+        [core, pre_five, sums_five, counts, narrow_all, keep, mask],
         bundle_d,
         size_out,
         [(pixels, narrow)],
@@ -1462,7 +1533,7 @@
     block_output, grad_two, sums = launch(
         last_layer,
         [short(*above.shape), real(pixels, wide), real(2 * wide_rows, 128)],
-        [pre_six, sums_six, Far(counts), Far(wide_all), Far(out_one), Far(above), Far(mask)],
+        [pre_six, sums_six, counts, wide_all, out_one, above, mask],
     )
     back_six = everywhere(sums)
     block_output = lax.all_to_all(block_output, "mp", 0, 0, tiled=True)
@@ -1471,8 +1542,8 @@
     grad_six, act_five_grad, sums = launch(
         functools.partial(last_back, 0, 3),
         [short(pixels, wide), real(pixels, narrow), copies],
-        [core, grad_two, Far(pre_six), Far(sums_six), back_six, Far(counts), Far(wide_all), Far(pre_five),
-         Far(sums_five), Far(narrow_all), Far(keep), Far(mask)],
+        [core, grad_two, pre_six, sums_six, back_six, counts, wide_all, pre_five,
+         sums_five, narrow_all, keep, mask],
         bundle_d,
         size_out,
         [(pixels, narrow)],
@@ -1480,35 +1551,32 @@
     )
     bundle = chunks_into(None, size_out, 0, grad_six, hid_five, 1, unit_out, column)
     back_a = Scatter(*bundle)
-    back_five = exchange(sums)
-    back_five = wave([back_a], back_five)
+    back_five = wave([back_a], sums, exchange(sums))
     grad_five, act_four_grad, sums = launch(
         functools.partial(spread_back, size_out, 2, PLAIN_TAPS),
         [short(pixels, narrow), real(pixels, narrow), copies],
-        [core, act_five_grad, Far(pre_five), Far(sums_five), back_five, Far(counts), Far(narrow_all),
-         Far(pre_four), Far(sums_four), Far(keep), Far(mask), Far(mask), Far(inside)],
+        [core, act_five_grad, pre_five, sums_five, back_five, counts, narrow_all,
+         pre_four, sums_four, keep, mask, mask, inside],
         bundle_d,
         size_mid,
         [(pixels, narrow)],
         work=9 * pixels * narrow * narrow,
     )
-    sums = wave([back_a], sums)
     back_four = exchange(sums)
     bundle = chunks_into(None, size_mid, 0, cols_four, grad_five, 9, unit_mid, column)
     back_b = Scatter(*bundle)
-    back_four = wave([back_b], back_four)
+    back_four = wave([back_a, back_b], sums, back_four)
     grad_four, grad_one, sums = launch(
         functools.partial(narrow_layer_back, size_short + size_out),
         [short(pixels, narrow), real(pixels, wide), real(3 * wide_rows, 128)],
-        [core, act_four_grad, Far(pre_four), Far(sums_four), back_four, Far(counts), Far(narrow_all), Far(mask),
-         Far(grad_two), Far(pre_three), Far(pre_side), Far(sums_pair), Far(wide_all)],
+        [core, act_four_grad, pre_four, sums_four, back_four, counts, narrow_all, mask,
+         grad_two, pre_three, pre_side, sums_pair, wide_all],
         bundle_c,
         size_out,
         [(pixels, narrow), (pixels, wide)],
         work=pixels * narrow * wide,
     )
-    sums = wave([back_a, back_b], sums)
-    back_pair = everywhere(sums)
+    back_pair = everywhere(sums, [back_a, back_b])
     total = size_short + 2 * size_out
     bundle = chunks_into(
         None, total, size_short + size_out, out_one, grad_four, 1, unit_out, column
@@ -1517,31 +1585,29 @@
     grad_three, grad_side, act_two_grad, sums = launch(
         functools.partial(pair_back, size_short, 1),
         [short(pixels, wide), short(pixels, wide), real(pixels, narrow), copies],
-        [core, grad_one, Far(pre_three), Far(pre_side), Far(sums_pair), back_pair, Far(counts), Far(wide_all),
-         Far(pre_two), Far(sums_two), Far(narrow_all), Far(keep), Far(mask)],
+        [core, grad_one, pre_three, pre_side, sums_pair, back_pair, counts, wide_all,
+         pre_two, sums_two, narrow_all, keep, mask],
         bundle_c,
         size_out,
         [(pixels, narrow), (pixels, wide)],
         work=pixels * narrow * wide,
     )
-    sums = wave([back_a, back_b], sums)
-    back_two = exchange(sums)
+    back_two = wave([back_a, back_b], sums, exchange(sums))
     bundle = chunks_into(bundle, total, size_short, grad_three, hid_two, 1, unit_out, column)
     bundle = chunks_into(bundle, total, 0, field, grad_side, 1, unit_in, column_wide)
     back_c = Scatter(*bundle)
-    back_two = wave([back_c], back_two)
+    back_two = wave([back_c], sums, back_two)
     grad_mid, act_one_grad, sums = launch(
         functools.partial(spread_back, 0, 0, STRIDED_TAPS),
         [short(pixels, narrow), real(full, narrow), copies],
-        [core, act_two_grad, Far(pre_two), Far(sums_two), back_two, Far(counts), Far(narrow_all), Far(pre_one),
-         Far(sums_one), Far(keep), Far(mask_in), Far(mask), Far(inside)],
+        [core, act_two_grad, pre_two, sums_two, back_two, counts, narrow_all, pre_one,
+         sums_one, keep, mask_in, mask, inside],
         bundle_b,
         size_mid,
         [(pixels, narrow)],
         work=9 * pixels * narrow * narrow,
     )
-    sums = wave([back_b, back_c], sums)
-    back_one = exchange(sums)
+    back_one = wave([back_b, back_c], sums, exchange(sums))
     bundle = chunks_into(None, size_mid, 0, cols_one, grad_mid, 9, unit_mid, column)
     back_d = Scatter(*bundle)
     (side_grad,) = launch(
@@ -1552,12 +1618,14 @@
         size_short,
         work=pixels * field.shape[1] * wide,
     )
-    back_one, side_grad = wave([back_d], (back_one, side_grad))
+    back_one = wave([back_d], sums, back_one)
+    back_one, side_grad = lax.optimization_barrier((back_one, side_grad))
+    wave([back_c, back_d], back_one)
     grad_first, field_grad = launch(
         first_back,
         [short(full, narrow), short(ranks, full, channels)],
-        [core, act_one_grad, Far(pre_one), Far(sums_one), back_one, Far(counts), Far(narrow_all), Far(mask_in),
-         Far(side_grad)],
+        [core, act_one_grad, pre_one, sums_one, back_one, counts, narrow_all, mask_in,
+         side_grad],
         bundle_a,
         unit_in,
         [(full, narrow)],
@@ -1565,7 +1633,7 @@
     )
     bundle = chunks_into(None, unit_in * column // 128, 0, field, grad_first, 1, unit_in, column)
     back_e = Scatter(*bundle, False)
-    field_grad = wave([back_c, back_d, back_e], field_grad)
+    wave([back_e])
     input_grad = lax.all_to_all(field_grad, "mp", 0, 0, tiled=True)
     input_grad = input_grad.reshape(ranks, 4, pixels, channels).transpose(3, 1, 0, 2)
     input_grad = input_grad.reshape(inputs.shape)
@@ -1585,23 +1653,15 @@
         like(shortcut_weight, last_weight, second_weight) + [real(8, 128)],
         [rows_a, rows_c]
         + [
-            Far(value)
-            for value in (
-                shortcut_mean, shortcut_square, shortcut_weight, last_mean, last_square, last_weight,
-                second_mean, second_square, second_weight,
-            )
+            shortcut_mean, shortcut_square, shortcut_weight, last_mean, last_square, last_weight,
+            second_mean, second_square, second_weight,
         ],
     )
     late = launch(
         late_moves,
         like(first_weight, middle_weight) + [real(devices, 16, 128)],
         [rows_b, rows_d, rows_e, early[-1]]
-        + [
-            Far(value)
-            for value in (
-                first_mean, first_square, first_weight, middle_mean, middle_square, middle_weight,
-            )
-        ],
+        + [first_mean, first_square, first_weight, middle_mean, middle_square, middle_weight],
     )
     powers = exchange(late[-1])
     weights = (first_weight, shortcut_weight, middle_weight, last_weight, second_weight)
@@ -1612,7 +1672,7 @@
         + [real(*value.shape) for value in weights]
         + [short(*value.shape) for value in weights],
         [powers]
-        + [Far(value) for pair in zip(weights, updates) for value in pair],
+        + [value for pair in zip(weights, updates) for value in pair],
     )
     matrix_norms = norms[:14, 0].reshape(7, 2)
     first_next, short_next, middle_next, last_next, second_next = fresh[:5]
@@ -1624,13 +1684,13 @@
 
     narrow_grads = jnp.stack([jnp.sum(rows, 0) for rows in (back_one, back_two, back_four, back_five)])
     narrow_grad = own_channels(narrow_grads.reshape(4, 2, narrow))
-    gain_three, gain_side, bias_pair = back_pair.reshape(3, wide)
+    gain_three, gain_side, bias_pair = jnp.sum(back_pair, 0).reshape(3, wide)
     wide_grad = own_channels(
         jnp.stack(
             [
                 jnp.stack([gain_three, bias_pair]),
                 jnp.stack([gain_side, bias_pair]),
-                back_six.reshape(2, wide),
+                jnp.sum(back_six, 0).reshape(2, wide),
             ]
         )
     )

time: 656 us -> 635 us (0.968)
  Pallas kernels: 77.6 us -> 164 us
  local copies, waits for them, and re-layouts: 97.6 us -> 29.7 us
  waiting for transfers between devices: 220 us -> 176 us
  blocking collectives: 21.3 us -> 54.8 us
  other arithmetic: 72.3 us -> 56 us
  starting transfers between devices: 153 us -> 138 us
    unnamed x380 -> x164, local copies, waits for them, and re-layouts: 89.3 us -> 15 us
    ppermute x33, waiting for transfers between devices: 87.3 us -> 34 us  [swap(): lax.ppermute(values, 'mp', [(at, at ^ masks['mp']) for at in range(sizes[...]
    pallas_call x18, Pallas kernels: 57.2 us -> 88.4 us  [launch(): pl.pallas_call(kernel, in_specs=specs + [pl.BlockSpec(memory_space=pltpu....]
    ppermute x55 -> x43, waiting for transfers between devices: 101 us -> 71.8 us  [swap(): lax.ppermute(values, 'dp', [(at, at ^ masks['dp']) for at in range(sizes[...]
    pallas_call x7, Pallas kernels: 20.4 us -> 48.5 us  [chunks_into(): pl.pallas_call(functools.partial(chunk_kernel, units, columns), grid=(ste...]
    pallas_call x0 -> x7, Pallas kernels: none -> 27.5 us  [moves(): pl.pallas_call(functools.partial(moves_kernel, tasks, len(sources)), in_s...]
    all_to_all x7 -> x6, waiting for transfers between devices: 6.38 us -> 30.4 us  [exchange(): return lax.all_to_all(copies, ('dp', 'mp'), 0, 0, tiled=True)]
    all_to_all x0 -> x2, blocking collectives: none -> 20.8 us  [everywhere(): arrived = lax.all_to_all(copies, 'dp', 0, 0, tiled=True)]
  transfers between devices with their start and end apart: 102 -> 91, of which waited for: 51 -> 37; matrix products, arithmetic and copies ran while one was open for 9% -> 11% of each run, Pallas kernels for 10% -> 15%
where the time goes in v4:
time: 635 us; the launch traced here: 622 us
  waiting for transfers between devices  176 us (28%)
  Pallas kernels  164 us (26%)
  starting transfers between devices  138 us (22%)
  other arithmetic  56 us (9%)
  blocking collectives  54.8 us (9%)
  local copies, waits for them, and re-layouts  29.7 us (5%)
    pallas_call x18, Pallas kernels, launch(): pl.pallas_call(kernel, in_specs=specs + [pl.BlockSpec(memory_space=pltpu....  88.4 us
    ppermute x43, waiting for transfers between devices, swap(): lax.ppermute(values, 'dp', [(at, at ^ masks['dp']) for at in range(sizes[...  71.8 us
    ppermute x43, starting transfers between devices, swap(): lax.ppermute(values, 'dp', [(at, at ^ masks['dp']) for at in range(sizes[...  61.3 us
    pallas_call x7, Pallas kernels, chunks_into(): pl.pallas_call(functools.partial(chunk_kernel, units, columns), grid=(ste...  48.5 us
    ppermute x33, waiting for transfers between devices, swap(): lax.ppermute(values, 'mp', [(at, at ^ masks['mp']) for at in range(sizes[...  34 us
    all_to_all x3, blocking collectives, exchange(): return lax.all_to_all(copies, ('dp', 'mp'), 0, 0, tiled=True)  34 us
    all_to_all x6, waiting for transfers between devices, exchange(): return lax.all_to_all(copies, ('dp', 'mp'), 0, 0, tiled=True)  30.4 us
    ppermute x33, starting transfers between devices, swap(): lax.ppermute(values, 'mp', [(at, at ^ masks['mp']) for at in range(sizes[...  28.5 us
  transfers between devices with their start and end apart: 91, of which 37 were waited for; matrix products, arithmetic and copies ran while one was open for 11% of the time, Pallas kernels for 15%

profile of v4, /device:TPU:0, one launch (start us, length us, event | category | flops | bytes accessed | tf_op | source)
XLA Modules:
  0.0 622.2 jit_solution(13013364314478547612)
XLA Ops:
  3.3 4.3 all-to-all-start
  7.7 4.5 collective-permute-start.2
  19.5 11.4 %collective-permute-done.refs_1_ = bf16[1,1,1,1,128,128]{5,4,3,2,1,0:T(8,128)(2,1)S(1)} collective-permute-done((bf16[1,1,1,1,128,128]{5,4,3,2,1,0:T(8,128)(2,1)S(1)}, bf16[1,1,1,1,128,128]{5,4,3,2,1,0:T(8,128)(2,1)S(1)}, u32[]{:S(2)}, u32[]{:S(2)}) %collective-permute-start) | collective-permute-done | bytes 32800 | tf_op jit(solution)/shard_map/ppermute | solution.py:481
  41.9 7.3 %collective-permute-done.8.refs_3_ = bf16[1,2,2,1,128,128]{5,4,3,2,1,0:T(8,128)(2,1)S(1)} collective-permute-done((bf16[1,2,2,1,128,128]{5,4,3,2,1,0:T(8,128)(2,1)}, bf16[1,2,2,1,128,128]{5,4,3,2,1,0:T(8,128)(2,1)S(1)}, u32[]{:S(2)}, u32[]{:S(2)}) %collective-permute-start.8) | collective-permute-done | bytes 131104 | tf_op jit(solution)/shard_map/ppermute | solution.py:483
  52.0 3.4 shard_map.465
  64.4 4.2 shard_map.466
  68.7 7.9 %collective-permute-done.15.refs_6_.refs_10_ = bf16[1,1,1,1,1024,128]{5,4,3,2,1,0:T(8,128)(2,1)} collective-permute-done((bf16[1,1,1,1,1024,128]{5,4,3,2,1,0:T(8,128)(2,1)S(1)}, bf16[1,1,1,1,1024,128]{5,4,3,2,1,0:T(8,128)(2,1)}, u32[]{:S(2)}, u32[]{:S(2)}) %collective-permute-start.15) | collective-permute-done | bytes 262176 | tf_op jit(solution)/shard_map/ppermute | solution.py:481
  76.5 4.5 collective-permute-done.14.refs_5_.refs_9_
  81.1 4.4 shard_map.467
  86.3 3.3 all-to-all-start.2
  93.7 3.4 all-to-all-start.1
  102.3 5.4 all-to-all-done.1.refs_2_.refs_8_.refs_3_
  108.4 5.6 shard_map.468
  115.7 3.6 shard_map.469
  121.4 4.3 all-to-all-start.3
  125.7 3.7 collective-permute-start.24
  130.2 16.3 %all-to-all-done.3.refs_2_.refs_9_.refs_3_ = f32[32,8,128]{2,1,0:T(8,128)S(1)} async-done(((f32[32,8,128]{2,1,0:T(8,128)}), f32[32,8,128]{2,1,0:T(8,128)S(1)}, u32[]{:S(2)}, u32[]{:S(2)}) %all-to-all-start.3) | async-done | bytes 131104 | tf_op jit(solution)/shard_map/all_to_all | solution.py:1356
  146.5 4.0 collective-permute-done.22.refs_5_.refs_9_
  152.2 5.4 shard_map.470
  160.7 4.5 collective-permute-done.25
  165.2 3.8 shard_map.471
  169.0 4.9 shard_map.472
  181.9 3.3 shard_map.473
  189.7 3.9 all-to-all-start.4
  194.3 15.0 %all-to-all-done.4.refs_3_.refs_11_.refs_4_ = f32[8,64,128]{2,1,0:T(8,128)S(1)} async-done(((f32[8,64,128]{2,1,0:T(8,128)}), f32[8,64,128]{2,1,0:T(8,128)S(1)}, u32[]{:S(2)}, u32[]{:S(2)}) %all-to-all-start.4) | async-done | bytes 262176 | tf_op jit(solution)/shard_map/all_to_all | solution.py:514
  210.0 4.5 shard_map.474
  215.8 4.5 shard_map.475
  220.4 10.9 %all_to_all.90.refs_2_.refs_8_.refs_3_ = f32[32,8,128]{2,1,0:T(8,128)} all-to-all(f32[32,8,128]{2,1,0:T(8,128)S(1)} %copy-done.61), channel_id=1, replica_groups=mesh['dp'=8,'mp'=4] {'dp','mp'}, dimensions={0} | all-to-all | bytes 262144 | tf_op jit(solution)/shard_map/all_to_all | solution.py:1356
  231.4 5.2 shard_map.476
  236.5 11.5 %all_to_all.91.refs_2_.refs_8_.refs_3_ = f32[32,8,128]{2,1,0:T(8,128)} all-to-all(f32[32,8,128]{2,1,0:T(8,128)} %get-tuple-element.290), channel_id=1, replica_groups=mesh['dp'=8,'mp'=4] {'dp','mp'}, dimensions={0} | all-to-all | bytes 262144 | tf_op jit(solution)/shard_map/all_to_all | solution.py:1356
  248.0 3.5 all-to-all-start.8
  251.5 3.9 shard_map.477
  262.9 10.4 %all_to_all.92.refs_1_.refs_3_ = f32[8,32,128]{2,1,0:T(8,128)} all-to-all(f32[8,32,128]{2,1,0:T(8,128)S(1)} %broadcast_in_dim.15), channel_id=1, replica_groups=mesh['dp'=8,'mp'=4] {'dp'}, dimensions={0} | all-to-all | bytes 262144 | tf_op jit(solution)/shard_map/all_to_all | solution.py:514
  273.3 4.5 shard_map.478
  283.7 10.4 %all_to_all.93.refs_4_ = f32[8,32,128]{2,1,0:T(8,128)} all-to-all(f32[8,32,128]{2,1,0:T(8,128)S(1)} %broadcast_in_dim.16), channel_id=1, replica_groups=mesh['dp'=8,'mp'=4] {'dp'}, dimensions={0} | all-to-all | bytes 262144 | tf_op jit(solution)/shard_map/all_to_all | solution.py:514
  294.1 4.7 shard_map.479
  298.7 6.3 %shard_map.480 = (bf16[2,8,256,128]{3,2,1,0:T(8,128)(2,1)}, bf16[2,8,256,128]{3,2,1,0:T(8,128)(2,1)}) custom-call(bf16[176,2048]{1,0:T(8,128)(2,1)} %get-tuple-element.299.rows_ref, bf16[176,512]{1,0:T(8,128)(2,1)} %get-tuple-element.300.cols_ref), custom_call_target="tpu_custom_call" | custom-call | flops 369098752 | bytes 2998272 | tf_op jit(solution)/shard_map/pallas_call | solution.py:780
  305.1 11.5 %all_to_all.94.refs_4_ = f32[32,8,128]{2,1,0:T(8,128)} all-to-all(f32[32,8,128]{2,1,0:T(8,128)} %get-tuple-element.298), channel_id=1, replica_groups=mesh['dp'=8,'mp'=4] {'dp','mp'}, dimensions={0} | all-to-all | bytes 262144 | tf_op jit(solution)/shard_map/all_to_all | solution.py:1356
  316.6 6.0 shard_map.481
  322.6 8.1 %shard_map.482 = (bf16[2,8,576,128]{3,2,1,0:T(8,128)(2,1)}, bf16[2,8,576,128]{3,2,1,0:T(8,128)(2,1)}) custom-call(bf16[176,4608]{1,0:T(8,128)(2,1)} %get-tuple-element.308.rows_ref, bf16[176,512]{1,0:T(8,128)(2,1)} %get-tuple-element.309.cols_ref), custom_call_target="tpu_custom_call" | custom-call | flops 830472192 | bytes 6520832 | tf_op jit(solution)/shard_map/pallas_call | solution.py:780
  342.7 7.2 %shard_map.483 = (bf16[176,512]{1,0:T(8,128)(2,1)}, f32[176,2048]{1,0:T(8,128)}, f32[48,128]{1,0:T(8,128)}) custom-call(s32[1]{0:T(128)} %bitcast.refs_0_, f32[176,512]{1,0:T(8,128)} %get-tuple-element.305.refs_1_, f32[176,512]{1,0:T(8,128)} %get-tuple-element.282.refs_1_.refs_7_.refs_2_, f32[32,8,128]{2,1,0:T(8,128)} %all_to_all.90.refs_2_.refs_8_.refs_3_, ...), custom_call_target="tpu_custom_call" | custom-call | flops 369098752 | bytes 9401028 | tf_op jit(solution)/shard_map/pallas_call | solution.py:1259
  352.5 6.3 %shard_map.484 = (bf16[2,8,1024,128]{3,2,1,0:T(8,128)(2,1)}, bf16[2,8,1024,128]{3,2,1,0:T(8,128)(2,1)}) custom-call(bf16[176,2048]{1,0:T(8,128)(2,1)} %get-tuple-element.293.refs_4_.rows_ref, bf16[176,512]{1,0:T(8,128)(2,1)} %get-tuple-element.326.cols_ref), custom_call_target="tpu_custom_call" | custom-call | flops 369098752 | bytes 2998272 | tf_op jit(solution)/shard_map/pallas_call | solution.py:780
  359.5 3.4 all-to-all-start.13
  371.8 5.9 shard_map.485
  377.7 6.3 %shard_map.486 = (bf16[2,8,1024,128]{3,2,1,0:T(8,128)(2,1)}, bf16[2,8,1024,128]{3,2,1,0:T(8,128)(2,1)}) custom-call(bf16[176,2048]{1,0:T(8,128)(2,1)} %get-tuple-element.344.rows_ref, bf16[176,512]{1,0:T(8,128)(2,1)} %get-tuple-element.345.cols_ref, ...), custom_call_target="tpu_custom_call", output_to_operand_aliasing={{0}: (2, {}), {1}: (3, {})} | custom-call | flops 369098752 | bytes 2998272 | tf_op jit(solution)/shard_map/pallas_call | solution.py:780
  384.0 6.6 %shard_map.487 = (bf16[2,8,1024,128]{3,2,1,0:T(8,128)(2,1)}, bf16[2,8,1024,128]{3,2,1,0:T(8,128)(2,1)}) custom-call(bf16[704,1024]{1,0:T(8,128)(2,1)} %get-tuple-element.269.refs_1_.rows_ref, bf16[176,2048]{1,0:T(8,128)(2,1)} %get-tuple-element.343.cols_ref.refs_0_, ...), custom_call_target="tpu_custom_call", output_to_operand_aliasing={{0}: (2, {}), {1}: (3, {})} | custom-call | flops 2952790016 | bytes 6356992 | tf_op jit(solution)/shard_map/pallas_call | solution.py:780
  394.7 3.5 all-to-all-start.14
  398.3 12.4 %collective-permute-done.44 = bf16[1,2,2,1,128,128]{5,4,3,2,1,0:T(8,128)(2,1)S(1)} collective-permute-done((bf16[1,2,2,1,128,128]{5,4,3,2,1,0:T(8,128)(2,1)S(1)}, bf16[1,2,2,1,128,128]{5,4,3,2,1,0:T(8,128)(2,1)S(1)}, u32[]{:S(2)}, u32[]{:S(2)}) %collective-permute-start.44) | collective-permute-done | bytes 131104 | tf_op jit(solution)/shard_map/ppermute | solution.py:479
  419.7 7.5 %shard_map.488 = (bf16[176,512]{1,0:T(8,128)(2,1)}, f32[704,512]{1,0:T(8,128)}, f32[32,8,128]{2,1,0:T(8,128)}) custom-call(s32[1]{0:T(128)} %bitcast.refs_0_, f32[176,512]{1,0:T(8,128)} %get-tuple-element.330.refs_1_, f32[176,512]{1,0:T(8,128)} %get-tuple-element.250.refs_1_.refs_8_.refs_2_, f32[32,8,128]{2,1,0:T(8,128)} %copy-done.11, ...), custom_call_target="tpu_custom_call" | custom-call | flops 830472192 | bytes 9205380 | tf_op jit(solution)/shard_map/pallas_call | solution.py:1259
  427.3 8.1 %shard_map.489 = (bf16[2,8,576,128]{3,2,1,0:T(8,128)(2,1)}, bf16[2,8,576,128]{3,2,1,0:T(8,128)(2,1)}) custom-call(bf16[176,4608]{1,0:T(8,128)(2,1)} %get-tuple-element.366.rows_ref, bf16[176,512]{1,0:T(8,128)(2,1)} %get-tuple-element.367.cols_ref), custom_call_target="tpu_custom_call" | custom-call | flops 830472192 | bytes 6520832 | tf_op jit(solution)/shard_map/pallas_call | solution.py:780
  435.4 4.8 shard_map.490.refs_8_
  452.6 3.5 all-to-all-start.9
  456.1 5.3 shard_map.491
  461.4 6.8 %shard_map.492 = (bf16[2,8,128,128]{3,2,1,0:T(8,128)(2,1)}, bf16[2,8,128,128]{3,2,1,0:T(8,128)(2,1)}) custom-call(bf16[704,1024]{1,0:T(8,128)(2,1)} %get-tuple-element.269.refs_1_.rows_ref, bf16[704,512]{1,0:T(8,128)(2,1)} %get-tuple-element.378.cols_ref), custom_call_target="tpu_custom_call" | custom-call | flops 738197504 | bytes 3211264 | tf_op jit(solution)/shard_map/pallas_call | solution.py:780
  479.6 3.6 collective-permute-start.72
  486.2 12.1 %collective-permute-done.66 = bf16[1,2,2,1,128,128]{5,4,3,2,1,0:T(8,128)(2,1)S(1)} collective-permute-done((bf16[1,2,2,1,128,128]{5,4,3,2,1,0:T(8,128)(2,1)S(1)}, bf16[1,2,2,1,128,128]{5,4,3,2,1,0:T(8,128)(2,1)S(1)}, u32[]{:S(2)}, u32[]{:S(2)}) %collective-permute-start.66) | collective-permute-done | bytes 131104 | tf_op jit(solution)/shard_map/ppermute | solution.py:483
  502.3 3.9 all-to-all-start.16
  534.0 13.0 %collective-permute-done.73 = bf16[1,2,2,1,512,128]{5,4,3,2,1,0:T(8,128)(2,1)S(1)} collective-permute-done((bf16[1,2,2,1,512,128]{5,4,3,2,1,0:T(8,128)(2,1)S(1)}, bf16[1,2,2,1,512,128]{5,4,3,2,1,0:T(8,128)(2,1)S(1)}, u32[]{:S(2)}, u32[]{:S(2)}) %collective-permute-start.73) | collective-permute-done | bytes 524320 | tf_op jit(solution)/shard_map/ppermute | solution.py:481
  557.6 3.5 collective-permute-done.57
  570.4 17.6 %collective-permute-done.75 = bf16[1,1,1,1,1024,128]{5,4,3,2,1,0:T(8,128)(2,1)S(1)} collective-permute-done((bf16[1,1,1,1,1024,128]{5,4,3,2,1,0:T(8,128)(2,1)S(1)}, bf16[1,1,1,1,1024,128]{5,4,3,2,1,0:T(8,128)(2,1)S(1)}, u32[]{:S(2)}, u32[]{:S(2)}) %collective-permute-start.75) | collective-permute-done | bytes 262176 | tf_op jit(solution)/shard_map/ppermute | solution.py:481
  590.2 3.5 shard_map.493
  595.9 3.8 shard_map.494
  599.8 5.3 all-to-all-start.17
  609.2 6.5 %all-to-all-done.17.refs_0_ = f32[32,16,128]{2,1,0:T(8,128)S(1)} async-done(((f32[32,16,128]{2,1,0:T(8,128)}), f32[32,16,128]{2,1,0:T(8,128)S(1)}, u32[]{:S(2)}, u32[]{:S(2)}) %all-to-all-start.17) | async-done | bytes 262176 | tf_op jit(solution)/shard_map/all_to_all | solution.py:1356
  (420 shorter events, 211.1 us)
Async XLA Ops:
  3.3 29.0 %all-to-all-start = ((bf16[4,704,256]{2,1,0:T(8,128)(2,1)}), bf16[4,704,256]{2,1,0:T(8,128)(2,1)S(1)}, u32[]{:S(2)}, u32[]{:S(2)}) async-start(bf16[4,704,256]{2,1,0:T(8,128)(2,1)} %bitcast.3), calls=%async_computation | async-start | bytes 2883584 | tf_op jit(solution)/shard_map/all_to_all | solution.py:1411
  12.9 18.0 %collective-permute-start.5 = (bf16[1,1,1,1,576,128]{5,4,3,2,1,0:T(8,128)(2,1)S(1)}, bf16[1,1,1,1,576,128]{5,4,3,2,1,0:T(8,128)(2,1)S(1)}, u32[]{:S(2)}, u32[]{:S(2)}) collective-permute-start(bf16[1,1,1,1,576,128]{5,4,3,2,1,0:T(8,128)(2,1)S(1)} %bitcast.131), channel_id=1, source_target_pairs={{0,24},{4,28},{8,16},{12,20},{16,8},{20,12},{24,0},{28,4},{1,25},{... | collective-permute-start | bytes 442376 | tf_op jit(solution)/shard_map/ppermute | solution.py:481
  13.8 17.1 %collective-permute-start.4 = (bf16[1,1,1,1,576,128]{5,4,3,2,1,0:T(8,128)(2,1)S(1)}, bf16[1,1,1,1,576,128]{5,4,3,2,1,0:T(8,128)(2,1)S(1)}, u32[]{:S(2)}, u32[]{:S(2)}) collective-permute-start(bf16[1,1,1,1,576,128]{5,4,3,2,1,0:T(8,128)(2,1)S(1)} %bitcast.132), channel_id=1, source_target_pairs={{0,8},{4,12},{8,0},{12,4},{16,24},{20,28},{24,16},{28,20},{1,9},{5... | collective-permute-start | bytes 442376 | tf_op jit(solution)/shard_map/ppermute | solution.py:481
  14.9 16.0 %collective-permute-start.3 = (bf16[1,1,1,1,576,128]{5,4,3,2,1,0:T(8,128)(2,1)S(1)}, bf16[1,1,1,1,576,128]{5,4,3,2,1,0:T(8,128)(2,1)S(1)}, u32[]{:S(2)}, u32[]{:S(2)}) collective-permute-start(bf16[1,1,1,1,576,128]{5,4,3,2,1,0:T(8,128)(2,1)S(1)} %bitcast.133), channel_id=1, source_target_pairs={{0,16},{4,20},{8,24},{12,28},{16,0},{20,4},{24,8},{28,12},{1,17},{... | collective-permute-start | bytes 442376 | tf_op jit(solution)/shard_map/ppermute | solution.py:481
  18.3 12.6 %collective-permute-start = (bf16[1,1,1,1,128,128]{5,4,3,2,1,0:T(8,128)(2,1)S(1)}, bf16[1,1,1,1,128,128]{5,4,3,2,1,0:T(8,128)(2,1)S(1)}, u32[]{:S(2)}, u32[]{:S(2)}) collective-permute-start(bf16[1,1,1,1,128,128]{5,4,3,2,1,0:T(8,128)(2,1)S(1)} %convert_bitcast_fusion.refs_0_), channel_id=1, source_target_pairs={{0,16},{4,20},{8,24},{12,28},{16,0},{20,4},{24,8},{28,12},{1,17},{... | collective-permute-start | bytes 98312 | tf_op jit(solution)/shard_map/ppermute | solution.py:481
  35.2 15.4 %collective-permute-start.9 = (bf16[1,2,2,1,288,128]{5,4,3,2,1,0:T(8,128)(2,1)}, bf16[1,2,2,1,288,128]{5,4,3,2,1,0:T(8,128)(2,1)S(1)}, u32[]{:S(2)}, u32[]{:S(2)}) collective-permute-start(bf16[1,2,2,1,288,128]{5,4,3,2,1,0:T(8,128)(2,1)} %get-tuple-element.230.refs_4_), channel_id=1, source_target_pairs={{0,4},{4,0},{8,12},{12,8},{16,20},{20,16},{24,28},{28,24},{1,5},{5... | collective-permute-start | bytes 884744 | tf_op jit(solution)/shard_map/ppermute | solution.py:481
  36.7 14.6 %collective-permute-start.10 = (bf16[1,2,2,1,288,128]{5,4,3,2,1,0:T(8,128)(2,1)}, bf16[1,2,2,1,288,128]{5,4,3,2,1,0:T(8,128)(2,1)}, u32[]{:S(2)}, u32[]{:S(2)}) collective-permute-start(bf16[1,2,2,1,288,128]{5,4,3,2,1,0:T(8,128)(2,1)} %get-tuple-element.231.refs_6_), channel_id=1, source_target_pairs={{0,2},{1,3},{2,0},{3,1},{4,6},{5,7},{6,4},{7,5},{8,10},{9,11},{10,... | collective-permute-start | bytes 884744 | tf_op jit(solution)/shard_map/ppermute | solution.py:479
  38.7 11.9 %collective-permute-start.7 = (bf16[1,2,2,1,128,128]{5,4,3,2,1,0:T(8,128)(2,1)}, bf16[1,2,2,1,128,128]{5,4,3,2,1,0:T(8,128)(2,1)S(1)}, u32[]{:S(2)}, u32[]{:S(2)}) collective-permute-start(bf16[1,2,2,1,128,128]{5,4,3,2,1,0:T(8,128)(2,1)} %get-tuple-element.229.refs_0_), channel_id=1, source_target_pairs={{0,2},{1,3},{2,0},{3,1},{4,6},{5,7},{6,4},{7,5},{8,10},{9,11},{10,... | collective-permute-start | bytes 393224 | tf_op jit(solution)/shard_map/ppermute | solution.py:479
  55.5 25.6 %collective-permute-start.12 = (bf16[1,2,2,2,288,128]{5,4,3,2,1,0:T(8,128)(2,1)}, bf16[1,2,2,2,288,128]{5,4,3,2,1,0:T(8,128)(2,1)}, u32[]{:S(2)}, u32[]{:S(2)}) collective-permute-start(bf16[1,2,2,2,288,128]{5,4,3,2,1,0:T(8,128)(2,1)} %get-tuple-element.238.refs_0_), channel_id=1, source_target_pairs={{0,2},{1,3},{2,0},{3,1},{4,6},{5,7},{6,4},{7,5},{8,10},{9,11},{10,... | collective-permute-start | bytes 1769480 | tf_op jit(solution)/shard_map/ppermute | solution.py:479
  57.2 23.9 %collective-permute-start.13 = (bf16[2,2,2,1,288,128]{5,4,3,2,1,0:T(8,128)(2,1)}, bf16[2,2,2,1,288,128]{5,4,3,2,1,0:T(8,128)(2,1)}, u32[]{:S(2)}, u32[]{:S(2)}) collective-permute-start(bf16[2,2,2,1,288,128]{5,4,3,2,1,0:T(8,128)(2,1)} %get-tuple-element.240.refs_2_), channel_id=1, source_target_pairs={{0,4},{4,0},{8,12},{12,8},{16,20},{20,16},{24,28},{28,24},{1,5},{5... | collective-permute-start | bytes 1769480 | tf_op jit(solution)/shard_map/ppermute | solution.py:481
  59.4 17.1 %collective-permute-start.15 = (bf16[1,1,1,1,1024,128]{5,4,3,2,1,0:T(8,128)(2,1)S(1)}, bf16[1,1,1,1,1024,128]{5,4,3,2,1,0:T(8,128)(2,1)}, u32[]{:S(2)}, u32[]{:S(2)}) collective-permute-start(bf16[1,1,1,1,1024,128]{5,4,3,2,1,0:T(8,128)(2,1)S(1)} %maximum_bitcast_fusion.3.refs_4_.refs_8_), channel_id=1, source_target_pairs={{0,8},{4,12},{8,0},{12,4},{16,24},{20,28},{24,16},{28,20},{1,9},{5... | collective-permute-start | bytes 786440 | tf_op jit(solution)/shard_map/ppermute | solution.py:481
  59.4 21.7 %collective-permute-start.14 = (bf16[1,1,1,1,1024,128]{5,4,3,2,1,0:T(8,128)(2,1)S(1)}, bf16[1,1,1,1,1024,128]{5,4,3,2,1,0:T(8,128)(2,1)}, u32[]{:S(2)}, u32[]{:S(2)}) collective-permute-start(bf16[1,1,1,1,1024,128]{5,4,3,2,1,0:T(8,128)(2,1)S(1)} %maximum_bitcast_fusion.3.refs_4_.refs_8_), channel_id=1, source_target_pairs={{0,16},{4,20},{8,24},{12,28},{16,0},{20,4},{24,8},{28,12},{1,17},{... | collective-permute-start | bytes 786440 | tf_op jit(solution)/shard_map/ppermute | solution.py:481
  85.5 22.9 %collective-permute-start.17 = (bf16[2,2,2,2,576,128]{5,4,3,2,1,0:T(8,128)(2,1)}, bf16[2,2,2,2,576,128]{5,4,3,2,1,0:T(8,128)(2,1)}, u32[]{:S(2)}, u32[]{:S(2)}) collective-permute-start(bf16[2,2,2,2,576,128]{5,4,3,2,1,0:T(8,128)(2,1)} %get-tuple-element.246), channel_id=1, source_target_pairs={{0,1},{1,0},{2,3},{3,2},{4,5},{5,4},{6,7},{7,6},{8,9},{9,8},{10,11... | collective-permute-start | bytes 7077896 | tf_op jit(solution)/shard_map/ppermute | solution.py:479
  93.7 14.0 %all-to-all-start.1 = ((f32[32,16,128]{2,1,0:T(8,128)}), f32[32,16,128]{2,1,0:T(8,128)S(1)}, u32[]{:S(2)}, u32[]{:S(2)}) async-start(f32[32,16,128]{2,1,0:T(8,128)} %get-tuple-element.234), calls=%async_computation.1 | async-start | bytes 524288 | tf_op jit(solution)/shard_map/all_to_all | solution.py:1356
  97.7 16.7 %collective-permute-start.18 = (bf16[1,2,2,1,512,128]{5,4,3,2,1,0:T(8,128)(2,1)}, bf16[1,2,2,1,512,128]{5,4,3,2,1,0:T(8,128)(2,1)S(1)}, u32[]{:S(2)}, u32[]{:S(2)}) collective-permute-start(bf16[1,2,2,1,512,128]{5,4,3,2,1,0:T(8,128)(2,1)} %get-tuple-element.252.refs_0_), channel_id=1, source_target_pairs={{0,4},{4,0},{8,12},{12,8},{16,20},{20,16},{24,28},{28,24},{1,5},{5... | collective-permute-start | bytes 1572872 | tf_op jit(solution)/shard_map/ppermute | solution.py:481
  99.5 15.4 %collective-permute-start.19 = (bf16[1,2,2,1,512,128]{5,4,3,2,1,0:T(8,128)(2,1)}, bf16[1,2,2,1,512,128]{5,4,3,2,1,0:T(8,128)(2,1)S(1)}, u32[]{:S(2)}, u32[]{:S(2)}) collective-permute-start(bf16[1,2,2,1,512,128]{5,4,3,2,1,0:T(8,128)(2,1)} %get-tuple-element.254.refs_2_), channel_id=1, source_target_pairs={{0,2},{1,3},{2,0},{3,1},{4,6},{5,7},{6,4},{7,5},{8,10},{9,11},{10,... | collective-permute-start | bytes 1572872 | tf_op jit(solution)/shard_map/ppermute | solution.py:479
  119.3 31.2 %collective-permute-start.20 = (bf16[1,2,2,2,512,128]{5,4,3,2,1,0:T(8,128)(2,1)}, bf16[1,2,2,2,512,128]{5,4,3,2,1,0:T(8,128)(2,1)S(1)}, u32[]{:S(2)}, u32[]{:S(2)}) collective-permute-start(bf16[1,2,2,2,512,128]{5,4,3,2,1,0:T(8,128)(2,1)} %get-tuple-element.259.refs_0_), channel_id=1, source_target_pairs={{0,2},{1,3},{2,0},{3,1},{4,6},{5,7},{6,4},{7,5},{8,10},{9,11},{10,... | collective-permute-start | bytes 3145736 | tf_op jit(solution)/shard_map/ppermute | solution.py:479
  120.5 30.7 %collective-permute-start.21 = (bf16[2,2,2,1,512,128]{5,4,3,2,1,0:T(8,128)(2,1)}, bf16[2,2,2,1,512,128]{5,4,3,2,1,0:T(8,128)(2,1)}, u32[]{:S(2)}, u32[]{:S(2)}) collective-permute-start(bf16[2,2,2,1,512,128]{5,4,3,2,1,0:T(8,128)(2,1)} %get-tuple-element.261.refs_2_), channel_id=1, source_target_pairs={{0,4},{4,0},{8,12},{12,8},{16,20},{20,16},{24,28},{28,24},{1,5},{5... | collective-permute-start | bytes 3145736 | tf_op jit(solution)/shard_map/ppermute | solution.py:481
  121.4 25.1 %all-to-all-start.3 = ((f32[32,8,128]{2,1,0:T(8,128)}), f32[32,8,128]{2,1,0:T(8,128)S(1)}, u32[]{:S(2)}, u32[]{:S(2)}) async-start(f32[32,8,128]{2,1,0:T(8,128)} %get-tuple-element.251), calls=%async_computation.3 | async-start | bytes 262144 | tf_op jit(solution)/shard_map/all_to_all | solution.py:1356
  125.7 20.8 %collective-permute-start.24 = (bf16[1,1,1,1,832,128]{5,4,3,2,1,0:T(8,128)(2,1)S(1)}, bf16[1,1,1,1,832,128]{5,4,3,2,1,0:T(8,128)(2,1)S(1)}, u32[]{:S(2)}, u32[]{:S(2)}) collective-permute-start(bf16[1,1,1,1,832,128]{5,4,3,2,1,0:T(8,128)(2,1)S(1)} %maximum_bitcast_fusion.4.refs_4_.refs_8_), channel_id=1, source_target_pairs={{0,24},{4,28},{8,16},{12,20},{16,8},{20,12},{24,0},{28,4},{1,25},{... | collective-permute-start | bytes 638984 | tf_op jit(solution)/shard_map/ppermute | solution.py:481
  129.4 17.1 %collective-permute-start.23 = (bf16[1,1,1,1,832,128]{5,4,3,2,1,0:T(8,128)(2,1)S(1)}, bf16[1,1,1,1,832,128]{5,4,3,2,1,0:T(8,128)(2,1)S(1)}, u32[]{:S(2)}, u32[]{:S(2)}) collective-permute-start(bf16[1,1,1,1,832,128]{5,4,3,2,1,0:T(8,128)(2,1)S(1)} %maximum_bitcast_fusion.4.refs_4_.refs_8_), channel_id=1, source_target_pairs={{0,8},{4,12},{8,0},{12,4},{16,24},{20,28},{24,16},{28,20},{1,9},{5... | collective-permute-start | bytes 638984 | tf_op jit(solution)/shard_map/ppermute | solution.py:481
  129.4 21.1 %collective-permute-start.22 = (bf16[1,1,1,1,832,128]{5,4,3,2,1,0:T(8,128)(2,1)S(1)}, bf16[1,1,1,1,832,128]{5,4,3,2,1,0:T(8,128)(2,1)S(1)}, u32[]{:S(2)}, u32[]{:S(2)}) collective-permute-start(bf16[1,1,1,1,832,128]{5,4,3,2,1,0:T(8,128)(2,1)S(1)} %maximum_bitcast_fusion.4.refs_4_.refs_8_), channel_id=1, source_target_pairs={{0,16},{4,20},{8,24},{12,28},{16,0},{20,4},{24,8},{28,12},{1,17},{... | collective-permute-start | bytes 638984 | tf_op jit(solution)/shard_map/ppermute | solution.py:481
  157.7 22.7 %collective-permute-start.28 = (bf16[1,2,2,1,416,128]{5,4,3,2,1,0:T(8,128)(2,1)}, bf16[1,2,2,1,416,128]{5,4,3,2,1,0:T(8,128)(2,1)S(1)}, u32[]{:S(2)}, u32[]{:S(2)}) collective-permute-start(bf16[1,2,2,1,416,128]{5,4,3,2,1,0:T(8,128)(2,1)} %get-tuple-element.275.refs_0_), channel_id=1, source_target_pairs={{0,4},{4,0},{8,12},{12,8},{16,20},{20,16},{24,28},{28,24},{1,5},{5... | collective-permute-start | bytes 1277960 | tf_op jit(solution)/shard_map/ppermute | solution.py:481
  159.2 21.2 %collective-permute-start.29 = (bf16[1,2,2,1,416,128]{5,4,3,2,1,0:T(8,128)(2,1)}, bf16[1,2,2,1,416,128]{5,4,3,2,1,0:T(8,128)(2,1)S(1)}, u32[]{:S(2)}, u32[]{:S(2)}) collective-permute-start(bf16[1,2,2,1,416,128]{5,4,3,2,1,0:T(8,128)(2,1)} %get-tuple-element.277.refs_2_), channel_id=1, source_target_pairs={{0,2},{1,3},{2,0},{3,1},{4,6},{5,7},{6,4},{7,5},{8,10},{9,11},{10,... | collective-permute-start | bytes 1277960 | tf_op jit(solution)/shard_map/ppermute | solution.py:479
  185.2 29.4 %collective-permute-start.30 = (bf16[1,2,2,2,416,128]{5,4,3,2,1,0:T(8,128)(2,1)}, bf16[1,2,2,2,416,128]{5,4,3,2,1,0:T(8,128)(2,1)S(1)}, u32[]{:S(2)}, u32[]{:S(2)}) collective-permute-start(bf16[1,2,2,2,416,128]{5,4,3,2,1,0:T(8,128)(2,1)} %get-tuple-element.284.refs_0_), channel_id=1, source_target_pairs={{0,2},{1,3},{2,0},{3,1},{4,6},{5,7},{6,4},{7,5},{8,10},{9,11},{10,... | collective-permute-start | bytes 2555912 | tf_op jit(solution)/shard_map/ppermute | solution.py:479
  186.7 27.9 %collective-permute-start.31 = (bf16[2,2,2,1,416,128]{5,4,3,2,1,0:T(8,128)(2,1)}, bf16[2,2,2,1,416,128]{5,4,3,2,1,0:T(8,128)(2,1)S(1)}, u32[]{:S(2)}, u32[]{:S(2)}) collective-permute-start(bf16[2,2,2,1,416,128]{5,4,3,2,1,0:T(8,128)(2,1)} %get-tuple-element.286.refs_2_), channel_id=1, source_target_pairs={{0,4},{4,0},{8,12},{12,8},{16,20},{20,16},{24,28},{28,24},{1,5},{5... | collective-permute-start | bytes 2555912 | tf_op jit(solution)/shard_map/ppermute | solution.py:481
  189.7 19.6 %all-to-all-start.4 = ((f32[8,64,128]{2,1,0:T(8,128)}), f32[8,64,128]{2,1,0:T(8,128)S(1)}, u32[]{:S(2)}, u32[]{:S(2)}) async-start(f32[8,64,128]{2,1,0:T(8,128)} %broadcast_in_dim.14), calls=%async_computation.4 | async-start | bytes 524288 | tf_op jit(solution)/shard_map/all_to_all | solution.py:514
  248.0 14.8 %all-to-all-start.8 = ((bf16[4,176,512]{2,1,0:T(8,128)(2,1)}), bf16[4,176,512]{2,1,0:T(8,128)(2,1)S(1)}, u32[]{:S(2)}, u32[]{:S(2)}) async-start(bf16[4,176,512]{2,1,0:T(8,128)(2,1)} %bitcast.33), calls=%async_computation.8 | async-start | bytes 1441792 | tf_op jit(solution)/shard_map/all_to_all | solution.py:1449
  305.1 25.7 %collective-permute-start.37 = (bf16[2,2,2,2,256,128]{5,4,3,2,1,0:T(8,128)(2,1)}, bf16[2,2,2,2,256,128]{5,4,3,2,1,0:T(8,128)(2,1)}, u32[]{:S(2)}, u32[]{:S(2)}) collective-permute-start(bf16[2,2,2,2,256,128]{5,4,3,2,1,0:T(8,128)(2,1)} %bitcast.156), channel_id=1, source_target_pairs={{0,1},{1,0},{2,3},{3,2},{4,5},{5,4},{6,7},{7,6},{8,9},{9,8},{10,11... | collective-permute-start | bytes 3145736 | tf_op jit(solution)/shard_map/ppermute | solution.py:479
  330.8 32.2 %collective-permute-start.42 = (bf16[2,2,2,2,576,128]{5,4,3,2,1,0:T(8,128)(2,1)}, bf16[2,2,2,2,576,128]{5,4,3,2,1,0:T(8,128)(2,1)}, u32[]{:S(2)}, u32[]{:S(2)}) collective-permute-start(bf16[2,2,2,2,576,128]{5,4,3,2,1,0:T(8,128)(2,1)} %bitcast.155), channel_id=1, source_target_pairs={{0,1},{1,0},{2,3},{3,2},{4,5},{5,4},{6,7},{7,6},{8,9},{9,8},{10,11... | collective-permute-start | bytes 7077896 | tf_op jit(solution)/shard_map/ppermute | solution.py:479
  335.5 27.4 %collective-permute-start.40 = (bf16[1,2,2,2,128,128]{5,4,3,2,1,0:T(8,128)(2,1)}, bf16[1,2,2,2,128,128]{5,4,3,2,1,0:T(8,128)(2,1)S(1)}, u32[]{:S(2)}, u32[]{:S(2)}) collective-permute-start(bf16[1,2,2,2,128,128]{5,4,3,2,1,0:T(8,128)(2,1)} %add_convert_fusion.13), channel_id=1, source_target_pairs={{0,2},{1,3},{2,0},{3,1},{4,6},{5,7},{6,4},{7,5},{8,10},{9,11},{10,... | collective-permute-start | bytes 786440 | tf_op jit(solution)/shard_map/ppermute | solution.py:479
  338.3 24.7 %collective-permute-start.41 = (bf16[2,2,2,1,128,128]{5,4,3,2,1,0:T(8,128)(2,1)S(1)}, bf16[2,2,2,1,128,128]{5,4,3,2,1,0:T(8,128)(2,1)S(1)}, u32[]{:S(2)}, u32[]{:S(2)}) collective-permute-start(bf16[2,2,2,1,128,128]{5,4,3,2,1,0:T(8,128)(2,1)S(1)} %add_convert_fusion.12), channel_id=1, source_target_pairs={{0,4},{4,0},{8,12},{12,8},{16,20},{20,16},{24,28},{28,24},{1,5},{5... | collective-permute-start | bytes 786440 | tf_op jit(solution)/shard_map/ppermute | solution.py:481
  359.5 11.6 %all-to-all-start.13 = ((f32[8,48,128]{2,1,0:T(8,128)}), f32[8,48,128]{2,1,0:T(8,128)S(1)}, u32[]{:S(2)}, u32[]{:S(2)}) async-start(f32[8,48,128]{2,1,0:T(8,128)} %broadcast_in_dim.17), calls=%async_computation.13 | async-start | bytes 393216 | tf_op jit(solution)/shard_map/all_to_all | solution.py:514
  390.7 52.5 %collective-permute-start.49 = (bf16[2,2,2,2,1024,128]{5,4,3,2,1,0:T(8,128)(2,1)}, bf16[2,2,2,2,1024,128]{5,4,3,2,1,0:T(8,128)(2,1)}, u32[]{:S(2)}, u32[]{:S(2)}) collective-permute-start(bf16[2,2,2,2,1024,128]{5,4,3,2,1,0:T(8,128)(2,1)} %bitcast.105), channel_id=1, source_target_pairs={{0,1},{1,0},{2,3},{3,2},{4,5},{5,4},{6,7},{7,6},{8,9},{9,8},{10,11... | collective-permute-start | bytes 12582920 | tf_op jit(solution)/shard_map/ppermute | solution.py:479
  390.7 21.3 %collective-permute-start.45 = (bf16[1,2,2,2,288,128]{5,4,3,2,1,0:T(8,128)(2,1)}, bf16[1,2,2,2,288,128]{5,4,3,2,1,0:T(8,128)(2,1)S(1)}, u32[]{:S(2)}, u32[]{:S(2)}) collective-permute-start(bf16[1,2,2,2,288,128]{5,4,3,2,1,0:T(8,128)(2,1)} %add_convert_fusion.5), channel_id=1, source_target_pairs={{0,2},{1,3},{2,0},{3,1},{4,6},{5,7},{6,4},{7,5},{8,10},{9,11},{10,... | collective-permute-start | bytes 1769480 | tf_op jit(solution)/shard_map/ppermute | solution.py:479
  392.4 19.6 %collective-permute-start.46 = (bf16[2,2,2,1,288,128]{5,4,3,2,1,0:T(8,128)(2,1)S(1)}, bf16[2,2,2,1,288,128]{5,4,3,2,1,0:T(8,128)(2,1)S(1)}, u32[]{:S(2)}, u32[]{:S(2)}) collective-permute-start(bf16[2,2,2,1,288,128]{5,4,3,2,1,0:T(8,128)(2,1)S(1)} %add_convert_fusion.4), channel_id=1, source_target_pairs={{0,4},{4,0},{8,12},{12,8},{16,20},{20,16},{24,28},{28,24},{1,5},{5... | collective-permute-start | bytes 1769480 | tf_op jit(solution)/shard_map/ppermute | solution.py:481
  393.3 17.3 %collective-permute-start.44 = (bf16[1,2,2,1,128,128]{5,4,3,2,1,0:T(8,128)(2,1)S(1)}, bf16[1,2,2,1,128,128]{5,4,3,2,1,0:T(8,128)(2,1)S(1)}, u32[]{:S(2)}, u32[]{:S(2)}) collective-permute-start(bf16[1,2,2,1,128,128]{5,4,3,2,1,0:T(8,128)(2,1)S(1)} %get-tuple-element.585), channel_id=1, source_target_pairs={{0,2},{1,3},{2,0},{3,1},{4,6},{5,7},{6,4},{7,5},{8,10},{9,11},{10,... | collective-permute-start | bytes 393224 | tf_op jit(solution)/shard_map/ppermute | solution.py:479
  393.7 18.3 %collective-permute-start.43 = (bf16[1,2,2,1,128,128]{5,4,3,2,1,0:T(8,128)(2,1)S(1)}, bf16[1,2,2,1,128,128]{5,4,3,2,1,0:T(8,128)(2,1)S(1)}, u32[]{:S(2)}, u32[]{:S(2)}) collective-permute-start(bf16[1,2,2,1,128,128]{5,4,3,2,1,0:T(8,128)(2,1)S(1)} %get-tuple-element.586), channel_id=1, source_target_pairs={{0,4},{4,0},{8,12},{12,8},{16,20},{20,16},{24,28},{28,24},{1,5},{5... | collective-permute-start | bytes 393224 | tf_op jit(solution)/shard_map/ppermute | solution.py:481
  394.7 24.3 %all-to-all-start.14 = ((f32[32,8,128]{2,1,0:T(8,128)}), f32[32,8,128]{2,1,0:T(8,128)S(1)}, u32[]{:S(2)}, u32[]{:S(2)}) async-start(f32[32,8,128]{2,1,0:T(8,128)} %get-tuple-element.331), calls=%async_computation.14 | async-start | bytes 262144 | tf_op jit(solution)/shard_map/all_to_all | solution.py:1356
  414.6 28.5 %collective-permute-start.48 = (bf16[1,2,2,1,288,128]{5,4,3,2,1,0:T(8,128)(2,1)}, bf16[1,2,2,1,288,128]{5,4,3,2,1,0:T(8,128)(2,1)S(1)}, u32[]{:S(2)}, u32[]{:S(2)}) collective-permute-start(bf16[1,2,2,1,288,128]{5,4,3,2,1,0:T(8,128)(2,1)} %get-tuple-element.572), channel_id=1, source_target_pairs={{0,2},{1,3},{2,0},{3,1},{4,6},{5,7},{6,4},{7,5},{8,10},{9,11},{10,... | collective-permute-start | bytes 884744 | tf_op jit(solution)/shard_map/ppermute | solution.py:479
  415.1 28.1 %collective-permute-start.47 = (bf16[1,2,2,1,288,128]{5,4,3,2,1,0:T(8,128)(2,1)S(1)}, bf16[1,2,2,1,288,128]{5,4,3,2,1,0:T(8,128)(2,1)S(1)}, u32[]{:S(2)}, u32[]{:S(2)}) collective-permute-start(bf16[1,2,2,1,288,128]{5,4,3,2,1,0:T(8,128)(2,1)S(1)} %get-tuple-element.573), channel_id=1, source_target_pairs={{0,4},{4,0},{8,12},{12,8},{16,20},{20,16},{24,28},{28,24},{1,5},{5... | collective-permute-start | bytes 884744 | tf_op jit(solution)/shard_map/ppermute | solution.py:481
  435.4 75.9 %collective-permute-start.55 = (bf16[2,2,2,2,576,128]{5,4,3,2,1,0:T(8,128)(2,1)}, bf16[2,2,2,2,576,128]{5,4,3,2,1,0:T(8,128)(2,1)}, u32[]{:S(2)}, u32[]{:S(2)}) collective-permute-start(bf16[2,2,2,2,576,128]{5,4,3,2,1,0:T(8,128)(2,1)} %bitcast.154), channel_id=1, source_target_pairs={{0,1},{1,0},{2,3},{3,2},{4,5},{5,4},{6,7},{7,6},{8,9},{9,8},{10,11... | collective-permute-start | bytes 7077896 | tf_op jit(solution)/shard_map/ppermute | solution.py:479
  440.2 12.4 %all-to-all-start.15 = ((f32[32,8,128]{2,1,0:T(8,128)}), f32[32,8,128]{2,1,0:T(8,128)S(1)}, u32[]{:S(2)}, u32[]{:S(2)}) async-start(f32[32,8,128]{2,1,0:T(8,128)} %get-tuple-element.355), calls=%async_computation.15 | async-start | bytes 262144 | tf_op jit(solution)/shard_map/all_to_all | solution.py:1356
  452.6 20.2 %all-to-all-start.9 = ((bf16[4,176,512]{2,1,0:T(8,128)(2,1)}), bf16[4,176,512]{2,1,0:T(8,128)(2,1)S(1)}, u32[]{:S(2)}, u32[]{:S(2)}) async-start(bf16[4,176,512]{2,1,0:T(8,128)(2,1)} %get-tuple-element.294), calls=%async_computation.9 | async-start | bytes 1441792 | tf_op jit(solution)/shard_map/all_to_all | solution.py:1539
  468.6 43.2 %collective-permute-start.53 = (bf16[1,2,2,2,512,128]{5,4,3,2,1,0:T(8,128)(2,1)}, bf16[1,2,2,2,512,128]{5,4,3,2,1,0:T(8,128)(2,1)S(1)}, u32[]{:S(2)}, u32[]{:S(2)}) collective-permute-start(bf16[1,2,2,2,512,128]{5,4,3,2,1,0:T(8,128)(2,1)} %add_convert_fusion.1), channel_id=1, source_target_pairs={{0,2},{1,3},{2,0},{3,1},{4,6},{5,7},{6,4},{7,5},{8,10},{9,11},{10,... | collective-permute-start | bytes 3145736 | tf_op jit(solution)/shard_map/ppermute | solution.py:479
  470.3 43.0 %collective-permute-start.54 = (bf16[2,2,2,1,512,128]{5,4,3,2,1,0:T(8,128)(2,1)}, bf16[2,2,2,1,512,128]{5,4,3,2,1,0:T(8,128)(2,1)}, u32[]{:S(2)}, u32[]{:S(2)}) collective-permute-start(bf16[2,2,2,1,512,128]{5,4,3,2,1,0:T(8,128)(2,1)} %add_convert_fusion), channel_id=1, source_target_pairs={{0,4},{4,0},{8,12},{12,8},{16,20},{20,16},{24,28},{28,24},{1,5},{5... | collective-permute-start | bytes 3145736 | tf_op jit(solution)/shard_map/ppermute | solution.py:481
  483.2 15.1 %collective-permute-start.66 = (bf16[1,2,2,1,128,128]{5,4,3,2,1,0:T(8,128)(2,1)S(1)}, bf16[1,2,2,1,128,128]{5,4,3,2,1,0:T(8,128)(2,1)S(1)}, u32[]{:S(2)}, u32[]{:S(2)}) collective-permute-start(bf16[1,2,2,1,128,128]{5,4,3,2,1,0:T(8,128)(2,1)S(1)} %get-tuple-element.590), channel_id=1, source_target_pairs={{0,6},{1,7},{2,4},{3,5},{4,2},{5,3},{6,0},{7,1},{8,14},{9,15},{10,... | collective-permute-start | bytes 393224 | tf_op jit(solution)/shard_map/ppermute | solution.py:483
  485.7 20.6 %collective-permute-start.65 = (bf16[1,2,2,1,128,128]{5,4,3,2,1,0:T(8,128)(2,1)S(1)}, bf16[1,2,2,1,128,128]{5,4,3,2,1,0:T(8,128)(2,1)}, u32[]{:S(2)}, u32[]{:S(2)}) collective-permute-start(bf16[1,2,2,1,128,128]{5,4,3,2,1,0:T(8,128)(2,1)S(1)} %get-tuple-element.591), channel_id=1, source_target_pairs={{0,4},{4,0},{8,12},{12,8},{16,20},{20,16},{24,28},{28,24},{1,5},{5... | collective-permute-start | bytes 393224 | tf_op jit(solution)/shard_map/ppermute | solution.py:481
  502.3 97.4 %all-to-all-start.16 = ((bf16[4,704,256]{2,1,0:T(8,128)(2,1)}), bf16[4,704,256]{2,1,0:T(8,128)(2,1)S(1)}, u32[]{:S(2)}, u32[]{:S(2)}) async-start(bf16[4,704,256]{2,1,0:T(8,128)(2,1)} %get-tuple-element.374), calls=%async_computation.16 | async-start | bytes 2883584 | tf_op jit(solution)/shard_map/all_to_all | solution.py:1637
  506.3 13.5 %collective-permute-start.50 = (bf16[1,1,1,1,576,128]{5,4,3,2,1,0:T(8,128)(2,1)}, bf16[1,1,1,1,576,128]{5,4,3,2,1,0:T(8,128)(2,1)S(1)}, u32[]{:S(2)}, u32[]{:S(2)}) collective-permute-start(bf16[1,1,1,1,576,128]{5,4,3,2,1,0:T(8,128)(2,1)} %pad_maximum_fusion.3), channel_id=1, source_target_pairs={{0,16},{4,20},{8,24},{12,28},{16,0},{20,4},{24,8},{28,12},{1,17},{... | collective-permute-start | bytes 442376 | tf_op jit(solution)/shard_map/ppermute | solution.py:481
  508.8 13.1 %collective-permute-start.51 = (bf16[1,1,1,1,576,128]{5,4,3,2,1,0:T(8,128)(2,1)}, bf16[1,1,1,1,576,128]{5,4,3,2,1,0:T(8,128)(2,1)S(1)}, u32[]{:S(2)}, u32[]{:S(2)}) collective-permute-start(bf16[1,1,1,1,576,128]{5,4,3,2,1,0:T(8,128)(2,1)} %pad_maximum_fusion.4), channel_id=1, source_target_pairs={{0,8},{4,12},{8,0},{12,4},{16,24},{20,28},{24,16},{28,20},{1,9},{5... | collective-permute-start | bytes 442376 | tf_op jit(solution)/shard_map/ppermute | solution.py:481
  511.8 13.9 %collective-permute-start.67 = (bf16[1,1,1,1,128,128]{5,4,3,2,1,0:T(8,128)(2,1)S(1)}, bf16[1,1,1,1,128,128]{5,4,3,2,1,0:T(8,128)(2,1)S(1)}, u32[]{:S(2)}, u32[]{:S(2)}) collective-permute-start(bf16[1,1,1,1,128,128]{5,4,3,2,1,0:T(8,128)(2,1)S(1)} %get-tuple-element.587), channel_id=1, source_target_pairs={{0,16},{4,20},{8,24},{12,28},{16,0},{20,4},{24,8},{28,12},{1,17},{... | collective-permute-start | bytes 98312 | tf_op jit(solution)/shard_map/ppermute | solution.py:481
  513.3 15.3 %collective-permute-start.69 = (bf16[1,1,1,1,128,128]{5,4,3,2,1,0:T(8,128)(2,1)S(1)}, bf16[1,1,1,1,128,128]{5,4,3,2,1,0:T(8,128)(2,1)S(1)}, u32[]{:S(2)}, u32[]{:S(2)}) collective-permute-start(bf16[1,1,1,1,128,128]{5,4,3,2,1,0:T(8,128)(2,1)S(1)} %get-tuple-element.588), channel_id=1, source_target_pairs={{0,24},{4,28},{8,16},{12,20},{16,8},{20,12},{24,0},{28,4},{1,25},{... | collective-permute-start | bytes 98312 | tf_op jit(solution)/shard_map/ppermute | solution.py:481
  519.8 31.0 %collective-permute-start.56 = (bf16[1,2,2,2,288,128]{5,4,3,2,1,0:T(8,128)(2,1)S(1)}, bf16[1,2,2,2,288,128]{5,4,3,2,1,0:T(8,128)(2,1)S(1)}, u32[]{:S(2)}, u32[]{:S(2)}) collective-permute-start(bf16[1,2,2,2,288,128]{5,4,3,2,1,0:T(8,128)(2,1)S(1)} %add_convert_fusion.3), channel_id=1, source_target_pairs={{0,2},{1,3},{2,0},{3,1},{4,6},{5,7},{6,4},{7,5},{8,10},{9,11},{10,... | collective-permute-start | bytes 1769480 | tf_op jit(solution)/shard_map/ppermute | solution.py:479
  521.9 28.9 %collective-permute-start.58 = (bf16[2,2,2,1,288,128]{5,4,3,2,1,0:T(8,128)(2,1)S(1)}, bf16[2,2,2,1,288,128]{5,4,3,2,1,0:T(8,128)(2,1)S(1)}, u32[]{:S(2)}, u32[]{:S(2)}) collective-permute-start(bf16[2,2,2,1,288,128]{5,4,3,2,1,0:T(8,128)(2,1)S(1)} %add_convert_fusion.2), channel_id=1, source_target_pairs={{0,4},{4,0},{8,12},{12,8},{16,20},{20,16},{24,28},{28,24},{1,5},{5... | collective-permute-start | bytes 1769480 | tf_op jit(solution)/shard_map/ppermute | solution.py:481
  522.4 24.7 %collective-permute-start.73 = (bf16[1,2,2,1,512,128]{5,4,3,2,1,0:T(8,128)(2,1)S(1)}, bf16[1,2,2,1,512,128]{5,4,3,2,1,0:T(8,128)(2,1)S(1)}, u32[]{:S(2)}, u32[]{:S(2)}) collective-permute-start(bf16[1,2,2,1,512,128]{5,4,3,2,1,0:T(8,128)(2,1)S(1)} %get-tuple-element.546), channel_id=1, source_target_pairs={{0,4},{4,0},{8,12},{12,8},{16,20},{20,16},{24,28},{28,24},{1,5},{5... | collective-permute-start | bytes 1572872 | tf_op jit(solution)/shard_map/ppermute | solution.py:481
  525.7 23.1 %collective-permute-start.74 = (bf16[1,2,2,1,512,128]{5,4,3,2,1,0:T(8,128)(2,1)S(1)}, bf16[1,2,2,1,512,128]{5,4,3,2,1,0:T(8,128)(2,1)S(1)}, u32[]{:S(2)}, u32[]{:S(2)}) collective-permute-start(bf16[1,2,2,1,512,128]{5,4,3,2,1,0:T(8,128)(2,1)S(1)} %get-tuple-element.547), channel_id=1, source_target_pairs={{0,2},{1,3},{2,0},{3,1},{4,6},{5,7},{6,4},{7,5},{8,10},{9,11},{10,... | collective-permute-start | bytes 1572872 | tf_op jit(solution)/shard_map/ppermute | solution.py:479
  553.2 15.5 %collective-permute-start.76 = (bf16[1,1,1,1,1024,128]{5,4,3,2,1,0:T(8,128)(2,1)S(1)}, bf16[1,1,1,1,1024,128]{5,4,3,2,1,0:T(8,128)(2,1)S(1)}, u32[]{:S(2)}, u32[]{:S(2)}) collective-permute-start(bf16[1,1,1,1,1024,128]{5,4,3,2,1,0:T(8,128)(2,1)S(1)} %pad_maximum_fusion.1), channel_id=1, source_target_pairs={{0,8},{4,12},{8,0},{12,4},{16,24},{20,28},{24,16},{28,20},{1,9},{5... | collective-permute-start | bytes 786440 | tf_op jit(solution)/shard_map/ppermute | solution.py:481
  555.0 15.3 %collective-permute-start.77 = (bf16[1,1,1,1,1024,128]{5,4,3,2,1,0:T(8,128)(2,1)S(1)}, bf16[1,1,1,1,1024,128]{5,4,3,2,1,0:T(8,128)(2,1)S(1)}, u32[]{:S(2)}, u32[]{:S(2)}) collective-permute-start(bf16[1,1,1,1,1024,128]{5,4,3,2,1,0:T(8,128)(2,1)S(1)} %pad_maximum_fusion.2), channel_id=1, source_target_pairs={{0,24},{4,28},{8,16},{12,20},{16,8},{20,12},{24,0},{28,4},{1,25},{... | collective-permute-start | bytes 786440 | tf_op jit(solution)/shard_map/ppermute | solution.py:481
  557.5 30.4 %collective-permute-start.75 = (bf16[1,1,1,1,1024,128]{5,4,3,2,1,0:T(8,128)(2,1)S(1)}, bf16[1,1,1,1,1024,128]{5,4,3,2,1,0:T(8,128)(2,1)S(1)}, u32[]{:S(2)}, u32[]{:S(2)}) collective-permute-start(bf16[1,1,1,1,1024,128]{5,4,3,2,1,0:T(8,128)(2,1)S(1)} %pad_maximum_fusion), channel_id=1, source_target_pairs={{0,16},{4,20},{8,24},{12,28},{16,0},{20,4},{24,8},{28,12},{1,17},{... | collective-permute-start | bytes 786440 | tf_op jit(solution)/shard_map/ppermute | solution.py:481
  563.3 30.4 %collective-permute-start.61 = (bf16[1,1,1,1,576,128]{5,4,3,2,1,0:T(8,128)(2,1)}, bf16[1,1,1,1,576,128]{5,4,3,2,1,0:T(8,128)(2,1)S(1)}, u32[]{:S(2)}, u32[]{:S(2)}) collective-permute-start(bf16[1,1,1,1,576,128]{5,4,3,2,1,0:T(8,128)(2,1)} %pad_maximum_fusion.7), channel_id=1, source_target_pairs={{0,8},{4,12},{8,0},{12,4},{16,24},{20,28},{24,16},{28,20},{1,9},{5... | collective-permute-start | bytes 442376 | tf_op jit(solution)/shard_map/ppermute | solution.py:481
  565.6 28.1 %collective-permute-start.62 = (bf16[1,1,1,1,576,128]{5,4,3,2,1,0:T(8,128)(2,1)}, bf16[1,1,1,1,576,128]{5,4,3,2,1,0:T(8,128)(2,1)}, u32[]{:S(2)}, u32[]{:S(2)}) collective-permute-start(bf16[1,1,1,1,576,128]{5,4,3,2,1,0:T(8,128)(2,1)} %pad_maximum_fusion.8), channel_id=1, source_target_pairs={{0,24},{4,28},{8,16},{12,20},{16,8},{20,12},{24,0},{28,4},{1,25},{... | collective-permute-start | bytes 442376 | tf_op jit(solution)/shard_map/ppermute | solution.py:481
  568.7 25.0 %collective-permute-start.60 = (bf16[1,1,1,1,576,128]{5,4,3,2,1,0:T(8,128)(2,1)}, bf16[1,1,1,1,576,128]{5,4,3,2,1,0:T(8,128)(2,1)}, u32[]{:S(2)}, u32[]{:S(2)}) collective-permute-start(bf16[1,1,1,1,576,128]{5,4,3,2,1,0:T(8,128)(2,1)} %pad_maximum_fusion.6), channel_id=1, source_target_pairs={{0,16},{4,20},{8,24},{12,28},{16,0},{20,4},{24,8},{28,12},{1,17},{... | collective-permute-start | bytes 442376 | tf_op jit(solution)/shard_map/ppermute | solution.py:481
  599.8 15.9 %all-to-all-start.17 = ((f32[32,16,128]{2,1,0:T(8,128)}), f32[32,16,128]{2,1,0:T(8,128)S(1)}, u32[]{:S(2)}, u32[]{:S(2)}) async-start(f32[32,16,128]{2,1,0:T(8,128)} %get-tuple-element.388), calls=%async_computation.17 | async-start | bytes 524288 | tf_op jit(solution)/shard_map/all_to_all | solution.py:1356
  (106 other events, 986.8 us)

commit v5 on v4

--- a/solution.py
+++ b/solution.py
@@ -464,6 +464,7 @@
 
 
 VMEM_BYTES = 62 * 2**20
+LIGHT = pl.CostEstimate(flops=1024, bytes_accessed=1024, transcendentals=0)
 
 
 def fits(mesh, pixel_mask):
@@ -573,11 +574,7 @@
         out_shape=[jax.ShapeDtypeStruct(shape, jnp.bfloat16) for shape, _ in wanted],
         scratch_shapes=[pltpu.SemaphoreType.DMA((len(tasks),))],
         compiler_params=pltpu.CompilerParams(vmem_limit_bytes=VMEM_BYTES),
-        cost_estimate=pl.CostEstimate(
-            flops=0,
-            bytes_accessed=sum(2 * source.size * 2 for source in sources),
-            transcendentals=0,
-        ),
+        cost_estimate=LIGHT,
     )(places, *sources)
 
 
@@ -789,12 +786,7 @@
         out_shape=[shape, shape],
         input_output_aliases={2 + place: place for place in range(len(earlier))},
         compiler_params=pltpu.CompilerParams(vmem_limit_bytes=VMEM_BYTES),
-        cost_estimate=pl.CostEstimate(
-            flops=2 * rows_of.size * cols_of.shape[1],
-            bytes_accessed=2 * (rows_of.size + cols_of.size)
-            + 2 * rows_of.shape[1] * cols_of.shape[1],
-            transcendentals=0,
-        ),
+        cost_estimate=LIGHT,
     )(rows_of, cols_of, *earlier)
 
 
@@ -1239,14 +1231,13 @@
         value.settle()
 
 
-def launch(kernel, shapes, values, bundles=(), rows=0, scratch=(), work=0):
+def launch(kernel, shapes, values, bundles=(), rows=0, scratch=()):
     held = []
     sems = []
     if bundles:
         held = [pltpu.VMEM((2,) + bundles[0].shape[:2] + (rows, 128), jnp.bfloat16)]
         sems = [pltpu.SemaphoreType.DMA((2,))]
     places = [place for place, value in enumerate(values) if value.dtype != jnp.int32]
-    moved = sum(value.size * value.dtype.itemsize for value in list(values) + list(shapes))
     specs = []
     for place, value in enumerate(values):
         space = pltpu.SMEM if value.dtype == jnp.int32 else pltpu.VMEM
@@ -1263,9 +1254,7 @@
         out_shape=list(shapes),
         scratch_shapes=held + [pltpu.VMEM(shape, jnp.float32) for shape in scratch] + sems + late,
         compiler_params=pltpu.CompilerParams(vmem_limit_bytes=VMEM_BYTES),
-        cost_estimate=pl.CostEstimate(
-            flops=2 * work, bytes_accessed=moved + rows * 16 * 512, transcendentals=0
-        ),
+        cost_estimate=LIGHT,
     )(*values, *bundles)
 
 
@@ -1467,7 +1456,6 @@
         [core, field, mask_in],
         bundle_a,
         unit_in,
-        work=field.size * narrow,
     )
     sums_one = wave([flow_b, flow_c], sums, exchange(sums))
     counts = jnp.sum(sums_one[:, 2 * size :], 0)
@@ -1478,7 +1466,6 @@
         [core, pre_one, sums_one, counts, narrow_all, keep, mask_in, mask, inside],
         bundle_b,
         size_mid,
-        work=9 * pixels * narrow * narrow,
     )
     sums_two = wave([flow_c], sums, exchange(sums))
     wave([flow_c, flow_d], sums_two)
@@ -1489,7 +1476,6 @@
         [core, field, mask],
         bundle_c,
         size_short,
-        work=pixels * field.shape[1] * wide,
     )
     hid_two, pre_three, sums = launch(
         functools.partial(widen_layer, size_short, 1),
@@ -1498,7 +1484,6 @@
         bundle_c,
         size_out,
         [(pixels, narrow)],
-        work=pixels * narrow * wide,
     )
     sums_pair = everywhere(jnp.concatenate([sums, side_sums], 0), [flow_d])
     out_one, pre_four, sums = launch(
@@ -1507,7 +1492,6 @@
         [core, pre_three, pre_side, sums_pair, counts, wide_all, mask],
         bundle_c,
         size_out,
-        work=pixels * narrow * wide,
     )
     sums_four = wave([flow_d], sums, exchange(sums))
     bundle_d = flow_d.bundles()
@@ -1517,7 +1501,6 @@
         [core, pre_four, sums_four, counts, narrow_all, keep, mask, mask, inside],
         bundle_d,
         size_mid,
-        work=9 * pixels * narrow * narrow,
     )
     sums_five = exchange(sums)
     hid_five, pre_six, sums = launch(
@@ -1527,7 +1510,6 @@
         bundle_d,
         size_out,
         [(pixels, narrow)],
-        work=pixels * narrow * wide,
     )
     sums_six = everywhere(sums)
     block_output, grad_two, sums = launch(
@@ -1547,7 +1529,6 @@
         bundle_d,
         size_out,
         [(pixels, narrow)],
-        work=pixels * narrow * wide,
     )
     bundle = chunks_into(None, size_out, 0, grad_six, hid_five, 1, unit_out, column)
     back_a = Scatter(*bundle)
@@ -1560,7 +1541,6 @@
         bundle_d,
         size_mid,
         [(pixels, narrow)],
-        work=9 * pixels * narrow * narrow,
     )
     back_four = exchange(sums)
     bundle = chunks_into(None, size_mid, 0, cols_four, grad_five, 9, unit_mid, column)
@@ -1574,7 +1554,6 @@
         bundle_c,
         size_out,
         [(pixels, narrow), (pixels, wide)],
-        work=pixels * narrow * wide,
     )
     back_pair = everywhere(sums, [back_a, back_b])
     total = size_short + 2 * size_out
@@ -1590,7 +1569,6 @@
         bundle_c,
         size_out,
         [(pixels, narrow), (pixels, wide)],
-        work=pixels * narrow * wide,
     )
     back_two = wave([back_a, back_b], sums, exchange(sums))
     bundle = chunks_into(bundle, total, size_short, grad_three, hid_two, 1, unit_out, column)
@@ -1605,9 +1583,9 @@
         bundle_b,
         size_mid,
         [(pixels, narrow)],
-        work=9 * pixels * narrow * narrow,
-    )
-    back_one = wave([back_b, back_c], sums, exchange(sums))
+    )
+    sums = wave([back_c], None, sums)
+    back_one = wave([back_b], sums, exchange(sums))
     bundle = chunks_into(None, size_mid, 0, cols_one, grad_mid, 9, unit_mid, column)
     back_d = Scatter(*bundle)
     (side_grad,) = launch(
@@ -1616,11 +1594,10 @@
         [grad_side],
         bundle_c,
         size_short,
-        work=pixels * field.shape[1] * wide,
     )
     back_one = wave([back_d], sums, back_one)
+    back_one = wave([back_c], None, back_one)
     back_one, side_grad = lax.optimization_barrier((back_one, side_grad))
-    wave([back_c, back_d], back_one)
     grad_first, field_grad = launch(
         first_back,
         [short(full, narrow), short(ranks, full, channels)],
@@ -1629,15 +1606,15 @@
         bundle_a,
         unit_in,
         [(full, narrow)],
-        work=field.size * narrow,
-    )
+    )
+    grad_first = wave([back_c, back_d], back_one, grad_first)
     bundle = chunks_into(None, unit_in * column // 128, 0, field, grad_first, 1, unit_in, column)
     back_e = Scatter(*bundle, False)
     wave([back_e])
     input_grad = lax.all_to_all(field_grad, "mp", 0, 0, tiled=True)
     input_grad = input_grad.reshape(ranks, 4, pixels, channels).transpose(3, 1, 0, 2)
     input_grad = input_grad.reshape(inputs.shape)
-    wave([back_c, back_d, back_e])
+    wave([back_d, back_e])
     wave([back_d, back_e])
     rows_a, rows_b, rows_c, rows_d, rows_e = [
         flow.rows() for flow in (back_a, back_b, back_c, back_d, back_e)

time: 635 us -> 628 us (0.989)
  waiting for transfers between devices: 176 us -> 169 us
    all_to_all x1, waiting for transfers between devices: 0.01 us -> 27 us  [by_image(): block_output = lax.all_to_all(block_output, 'mp', 0, 0, tiled=True)]
    ppermute x43, waiting for transfers between devices: 71.8 us -> 45.7 us  [swap(): lax.ppermute(values, 'dp', [(at, at ^ masks['dp']) for at in range(sizes[...]
    ppermute x2, waiting for transfers between devices: 19.5 us -> 9.6 us  [swap(): lax.ppermute(values, ('dp', 'mp'), [(at, at ^ mask) for at in range(sizes...]
    unnamed x164 -> x160, local copies, waits for them, and re-layouts: 15 us -> 16.9 us
  transfers between devices with their start and end apart: 91 -> 91, of which waited for: 37 -> 36; matrix products, arithmetic and copies ran while one was open for 11% -> 11% of each run, Pallas kernels for 15% -> 15%
where the time goes in v5:
time: 628 us; the launch traced here: 616 us
  waiting for transfers between devices  169 us (27%)
  Pallas kernels  164 us (26%)
  starting transfers between devices  133 us (21%)
  other arithmetic  61.6 us (10%)
  blocking collectives  54.8 us (9%)
  local copies, waits for them, and re-layouts  31.3 us (5%)
    pallas_call x18, Pallas kernels, launch(): pl.pallas_call(kernel, in_specs=specs + [pl.BlockSpec(memory_space=pltpu....  88.3 us
    ppermute x43, starting transfers between devices, swap(): lax.ppermute(values, 'dp', [(at, at ^ masks['dp']) for at in range(sizes[...  59.4 us
    pallas_call x7, Pallas kernels, chunks_into(): pl.pallas_call(functools.partial(chunk_kernel, units, columns), grid=(ste...  48.4 us
    ppermute x43, waiting for transfers between devices, swap(): lax.ppermute(values, 'dp', [(at, at ^ masks['dp']) for at in range(sizes[...  45.7 us
    ppermute x33, waiting for transfers between devices, swap(): lax.ppermute(values, 'mp', [(at, at ^ masks['mp']) for at in range(sizes[...  35.9 us
    all_to_all x3, blocking collectives, exchange(): return lax.all_to_all(copies, ('dp', 'mp'), 0, 0, tiled=True)  33.9 us
    all_to_all x6, waiting for transfers between devices, exchange(): return lax.all_to_all(copies, ('dp', 'mp'), 0, 0, tiled=True)  30.4 us
    convert_element_type x13, other arithmetic, launch(): out = self.fold(lane, group, bits).astype(jnp.bfloat16)  28.5 us
  transfers between devices with their start and end apart: 91, of which 36 were waited for; matrix products, arithmetic and copies ran while one was open for 11% of the time, Pallas kernels for 15%

profile of v5, /device:TPU:0, one launch (start us, length us, event | category | flops | bytes accessed | tf_op | source)
XLA Modules:
  0.0 615.7 jit_solution(10065652717987962514)
XLA Ops:
  3.3 4.3 all-to-all-start
  7.7 4.5 collective-permute-start.2
  19.5 11.4 %collective-permute-done.refs_1_ = bf16[1,1,1,1,128,128]{5,4,3,2,1,0:T(8,128)(2,1)S(1)} collective-permute-done((bf16[1,1,1,1,128,128]{5,4,3,2,1,0:T(8,128)(2,1)S(1)}, bf16[1,1,1,1,128,128]{5,4,3,2,1,0:T(8,128)(2,1)S(1)}, u32[]{:S(2)}, u32[]{:S(2)}) %collective-permute-start) | collective-permute-done | bytes 32800 | tf_op jit(solution)/shard_map/ppermute | solution.py:482
  41.9 7.3 %collective-permute-done.8.refs_3_ = bf16[1,2,2,1,128,128]{5,4,3,2,1,0:T(8,128)(2,1)S(1)} collective-permute-done((bf16[1,2,2,1,128,128]{5,4,3,2,1,0:T(8,128)(2,1)}, bf16[1,2,2,1,128,128]{5,4,3,2,1,0:T(8,128)(2,1)S(1)}, u32[]{:S(2)}, u32[]{:S(2)}) %collective-permute-start.8) | collective-permute-done | bytes 131104 | tf_op jit(solution)/shard_map/ppermute | solution.py:484
  52.0 3.4 shard_map.465
  64.4 4.2 shard_map.466
  68.7 7.9 %collective-permute-done.15.refs_6_.refs_10_ = bf16[1,1,1,1,1024,128]{5,4,3,2,1,0:T(8,128)(2,1)} collective-permute-done((bf16[1,1,1,1,1024,128]{5,4,3,2,1,0:T(8,128)(2,1)S(1)}, bf16[1,1,1,1,1024,128]{5,4,3,2,1,0:T(8,128)(2,1)}, u32[]{:S(2)}, u32[]{:S(2)}) %collective-permute-start.15) | collective-permute-done | bytes 262176 | tf_op jit(solution)/shard_map/ppermute | solution.py:482
  76.6 4.5 collective-permute-done.14.refs_5_.refs_9_
  81.1 4.4 shard_map.467
  86.3 3.3 all-to-all-start.2
  93.7 3.4 all-to-all-start.1
  102.4 5.3 all-to-all-done.1.refs_2_.refs_8_.refs_3_
  108.4 5.6 shard_map.468
  115.5 3.6 shard_map.469
  121.1 4.2 all-to-all-start.3
  125.4 3.7 collective-permute-start.24
  129.8 16.7 %all-to-all-done.3.refs_2_.refs_9_.refs_3_ = f32[32,8,128]{2,1,0:T(8,128)S(1)} async-done(((f32[32,8,128]{2,1,0:T(8,128)}), f32[32,8,128]{2,1,0:T(8,128)S(1)}, u32[]{:S(2)}, u32[]{:S(2)}) %all-to-all-start.3) | async-done | bytes 131104 | tf_op jit(solution)/shard_map/all_to_all | solution.py:1345
  146.5 3.6 collective-permute-done.22.refs_5_.refs_9_
  151.8 5.4 shard_map.470
  160.3 4.5 collective-permute-done.25
  164.8 4.8 shard_map.472
  169.7 3.8 shard_map.471
  181.5 3.3 shard_map.473
  189.3 3.9 all-to-all-start.4
  193.9 15.0 %all-to-all-done.4.refs_3_.refs_11_.refs_4_ = f32[8,64,128]{2,1,0:T(8,128)S(1)} async-done(((f32[8,64,128]{2,1,0:T(8,128)}), f32[8,64,128]{2,1,0:T(8,128)S(1)}, u32[]{:S(2)}, u32[]{:S(2)}) %all-to-all-start.4) | async-done | bytes 262176 | tf_op jit(solution)/shard_map/all_to_all | solution.py:515
  209.6 4.5 shard_map.474
  215.4 4.5 shard_map.475
  220.0 10.9 %all_to_all.90.refs_2_.refs_8_.refs_3_ = f32[32,8,128]{2,1,0:T(8,128)} all-to-all(f32[32,8,128]{2,1,0:T(8,128)S(1)} %copy-done.58), channel_id=1, replica_groups=mesh['dp'=8,'mp'=4] {'dp','mp'}, dimensions={0} | all-to-all | bytes 262144 | tf_op jit(solution)/shard_map/all_to_all | solution.py:1345
  230.9 5.2 shard_map.476
  236.1 11.5 %all_to_all.91.refs_2_.refs_8_.refs_3_ = f32[32,8,128]{2,1,0:T(8,128)} all-to-all(f32[32,8,128]{2,1,0:T(8,128)} %get-tuple-element.293), channel_id=1, replica_groups=mesh['dp'=8,'mp'=4] {'dp','mp'}, dimensions={0} | all-to-all | bytes 262144 | tf_op jit(solution)/shard_map/all_to_all | solution.py:1345
  247.6 3.5 all-to-all-start.8
  251.1 3.8 shard_map.477
  259.1 3.3 collective-permute-done.34
  262.4 10.4 %all_to_all.92.refs_1_.refs_3_ = f32[8,32,128]{2,1,0:T(8,128)} all-to-all(f32[8,32,128]{2,1,0:T(8,128)S(1)} %broadcast_in_dim.15), channel_id=1, replica_groups=mesh['dp'=8,'mp'=4] {'dp'}, dimensions={0} | all-to-all | bytes 262144 | tf_op jit(solution)/shard_map/all_to_all | solution.py:515
  272.8 4.5 shard_map.478
  283.3 10.4 %all_to_all.93.refs_4_ = f32[8,32,128]{2,1,0:T(8,128)} all-to-all(f32[8,32,128]{2,1,0:T(8,128)S(1)} %broadcast_in_dim.16), channel_id=1, replica_groups=mesh['dp'=8,'mp'=4] {'dp'}, dimensions={0} | all-to-all | bytes 262144 | tf_op jit(solution)/shard_map/all_to_all | solution.py:515
  293.7 4.6 shard_map.479
  298.3 6.3 %shard_map.480 = (bf16[2,8,256,128]{3,2,1,0:T(8,128)(2,1)}, bf16[2,8,256,128]{3,2,1,0:T(8,128)(2,1)}) custom-call(bf16[176,2048]{1,0:T(8,128)(2,1)} %get-tuple-element.302.rows_ref, bf16[176,512]{1,0:T(8,128)(2,1)} %get-tuple-element.303.cols_ref), custom_call_target="tpu_custom_call" | custom-call | flops 1024 | bytes 1024 | tf_op jit(solution)/shard_map/pallas_call | solution.py:777
  304.6 11.5 %all_to_all.94.refs_4_ = f32[32,8,128]{2,1,0:T(8,128)} all-to-all(f32[32,8,128]{2,1,0:T(8,128)} %get-tuple-element.301), channel_id=1, replica_groups=mesh['dp'=8,'mp'=4] {'dp','mp'}, dimensions={0} | all-to-all | bytes 262144 | tf_op jit(solution)/shard_map/all_to_all | solution.py:1345
  316.1 6.1 shard_map.481
  322.2 8.1 %shard_map.482 = (bf16[2,8,576,128]{3,2,1,0:T(8,128)(2,1)}, bf16[2,8,576,128]{3,2,1,0:T(8,128)(2,1)}) custom-call(bf16[176,4608]{1,0:T(8,128)(2,1)} %get-tuple-element.311.rows_ref, bf16[176,512]{1,0:T(8,128)(2,1)} %get-tuple-element.312.cols_ref), custom_call_target="tpu_custom_call" | custom-call | flops 1024 | bytes 1024 | tf_op jit(solution)/shard_map/pallas_call | solution.py:777
  342.2 7.2 %shard_map.483 = (bf16[176,512]{1,0:T(8,128)(2,1)}, f32[176,2048]{1,0:T(8,128)}, f32[48,128]{1,0:T(8,128)}) custom-call(s32[1]{0:T(128)} %bitcast.refs_0_, f32[176,512]{1,0:T(8,128)} %get-tuple-element.308.refs_1_, f32[176,512]{1,0:T(8,128)} %get-tuple-element.285.refs_1_.refs_7_.refs_2_, f32[32,8,128]{2,1,0:T(8,128)} %all_to_all.90.refs_2_.refs_8_.refs_3_, ...), custom_call_target="tpu_custom_call" | custom-call | flops 1024 | bytes 1024 | tf_op jit(solution)/shard_map/pallas_call | solution.py:1250
  352.0 6.3 %shard_map.484 = (bf16[2,8,1024,128]{3,2,1,0:T(8,128)(2,1)}, bf16[2,8,1024,128]{3,2,1,0:T(8,128)(2,1)}) custom-call(bf16[176,2048]{1,0:T(8,128)(2,1)} %get-tuple-element.296.refs_4_.rows_ref, bf16[176,512]{1,0:T(8,128)(2,1)} %get-tuple-element.329.cols_ref), custom_call_target="tpu_custom_call" | custom-call | flops 1024 | bytes 1024 | tf_op jit(solution)/shard_map/pallas_call | solution.py:777
  359.0 3.4 all-to-all-start.13
  371.3 5.9 shard_map.485
  377.2 6.3 %shard_map.486 = (bf16[2,8,1024,128]{3,2,1,0:T(8,128)(2,1)}, bf16[2,8,1024,128]{3,2,1,0:T(8,128)(2,1)}) custom-call(bf16[176,2048]{1,0:T(8,128)(2,1)} %get-tuple-element.347.rows_ref, bf16[176,512]{1,0:T(8,128)(2,1)} %get-tuple-element.348.cols_ref, ...), custom_call_target="tpu_custom_call", output_to_operand_aliasing={{0}: (2, {}), {1}: (3, {})} | custom-call | flops 1024 | bytes 1024 | tf_op jit(solution)/shard_map/pallas_call | solution.py:777
  383.5 6.6 %shard_map.487 = (bf16[2,8,1024,128]{3,2,1,0:T(8,128)(2,1)}, bf16[2,8,1024,128]{3,2,1,0:T(8,128)(2,1)}) custom-call(bf16[704,1024]{1,0:T(8,128)(2,1)} %get-tuple-element.272.refs_1_.rows_ref, bf16[176,2048]{1,0:T(8,128)(2,1)} %get-tuple-element.346.cols_ref.refs_0_, ...), custom_call_target="tpu_custom_call", output_to_operand_aliasing={{0}: (2, {}), {1}: (3, {})} | custom-call | flops 1024 | bytes 1024 | tf_op jit(solution)/shard_map/pallas_call | solution.py:777
  394.2 3.9 all-to-all-start.14
  398.0 12.1 %collective-permute-done.44 = bf16[1,2,2,1,128,128]{5,4,3,2,1,0:T(8,128)(2,1)S(1)} collective-permute-done((bf16[1,2,2,1,128,128]{5,4,3,2,1,0:T(8,128)(2,1)S(1)}, bf16[1,2,2,1,128,128]{5,4,3,2,1,0:T(8,128)(2,1)S(1)}, u32[]{:S(2)}, u32[]{:S(2)}) %collective-permute-start.44) | collective-permute-done | bytes 131104 | tf_op jit(solution)/shard_map/ppermute | solution.py:480
  417.9 7.5 %shard_map.488 = (bf16[176,512]{1,0:T(8,128)(2,1)}, f32[704,512]{1,0:T(8,128)}, f32[32,8,128]{2,1,0:T(8,128)}) custom-call(s32[1]{0:T(128)} %bitcast.refs_0_, f32[176,512]{1,0:T(8,128)} %get-tuple-element.333.refs_1_, f32[176,512]{1,0:T(8,128)} %get-tuple-element.253.refs_1_.refs_8_.refs_2_, f32[32,8,128]{2,1,0:T(8,128)} %copy-done.8, ...), custom_call_target="tpu_custom_call" | custom-call | flops 1024 | bytes 1024 | tf_op jit(solution)/shard_map/pallas_call | solution.py:1250
  425.4 8.2 %shard_map.489 = (bf16[2,8,576,128]{3,2,1,0:T(8,128)(2,1)}, bf16[2,8,576,128]{3,2,1,0:T(8,128)(2,1)}) custom-call(bf16[176,4608]{1,0:T(8,128)(2,1)} %get-tuple-element.368.rows_ref, bf16[176,512]{1,0:T(8,128)(2,1)} %get-tuple-element.369.cols_ref), custom_call_target="tpu_custom_call" | custom-call | flops 1024 | bytes 1024 | tf_op jit(solution)/shard_map/pallas_call | solution.py:777
  440.4 4.2 all-to-all-start.9
  445.9 27.0 %all-to-all-done.9 = bf16[4,176,512]{2,1,0:T(8,128)(2,1)} async-done(((bf16[4,176,512]{2,1,0:T(8,128)(2,1)}), bf16[4,176,512]{2,1,0:T(8,128)(2,1)}, u32[]{:S(2)}, u32[]{:S(2)}) %all-to-all-start.9) | async-done | bytes 720928 | tf_op jit(solution)/shard_map/all_to_all | solution.py:1521
  474.8 3.5 add_convert_fusion.6
  481.7 4.8 shard_map.490.refs_8_
  498.1 5.2 shard_map.491
  515.8 6.7 %shard_map.492 = (bf16[2,8,128,128]{3,2,1,0:T(8,128)(2,1)}, bf16[2,8,128,128]{3,2,1,0:T(8,128)(2,1)}) custom-call(bf16[704,1024]{1,0:T(8,128)(2,1)} %get-tuple-element.272.refs_1_.rows_ref, bf16[704,512]{1,0:T(8,128)(2,1)} %get-tuple-element.388.cols_ref), custom_call_target="tpu_custom_call" | custom-call | flops 1024 | bytes 1024 | tf_op jit(solution)/shard_map/pallas_call | solution.py:777
  536.6 3.8 all-to-all-start.16
  548.2 4.2 collective-permute-done.75
  557.1 3.5 shard_map.493
  579.3 3.3 collective-permute-done.64
  582.6 6.3 %collective-permute-done.62 = bf16[1,1,1,1,576,128]{5,4,3,2,1,0:T(8,128)(2,1)S(1)} collective-permute-done((bf16[1,1,1,1,576,128]{5,4,3,2,1,0:T(8,128)(2,1)S(1)}, bf16[1,1,1,1,576,128]{5,4,3,2,1,0:T(8,128)(2,1)S(1)}, u32[]{:S(2)}, u32[]{:S(2)}) %collective-permute-start.62) | collective-permute-done | bytes 147488 | tf_op jit(solution)/shard_map/ppermute | solution.py:482
  590.9 3.8 shard_map.494
  601.6 6.5 %all-to-all-done.17.refs_0_ = f32[32,16,128]{2,1,0:T(8,128)S(1)} async-done(((f32[32,16,128]{2,1,0:T(8,128)}), f32[32,16,128]{2,1,0:T(8,128)S(1)}, u32[]{:S(2)}, u32[]{:S(2)}) %all-to-all-start.17) | async-done | bytes 262176 | tf_op jit(solution)/shard_map/all_to_all | solution.py:1345
  (416 shorter events, 212.2 us)
Async XLA Ops:
  3.3 29.0 %all-to-all-start = ((bf16[4,704,256]{2,1,0:T(8,128)(2,1)}), bf16[4,704,256]{2,1,0:T(8,128)(2,1)S(1)}, u32[]{:S(2)}, u32[]{:S(2)}) async-start(bf16[4,704,256]{2,1,0:T(8,128)(2,1)} %bitcast.3), calls=%async_computation | async-start | bytes 2883584 | tf_op jit(solution)/shard_map/all_to_all | solution.py:1400
  12.9 18.0 %collective-permute-start.5 = (bf16[1,1,1,1,576,128]{5,4,3,2,1,0:T(8,128)(2,1)S(1)}, bf16[1,1,1,1,576,128]{5,4,3,2,1,0:T(8,128)(2,1)S(1)}, u32[]{:S(2)}, u32[]{:S(2)}) collective-permute-start(bf16[1,1,1,1,576,128]{5,4,3,2,1,0:T(8,128)(2,1)S(1)} %bitcast.130), channel_id=1, source_target_pairs={{0,24},{4,28},{8,16},{12,20},{16,8},{20,12},{24,0},{28,4},{1,25},{... | collective-permute-start | bytes 442376 | tf_op jit(solution)/shard_map/ppermute | solution.py:482
  13.8 17.1 %collective-permute-start.4 = (bf16[1,1,1,1,576,128]{5,4,3,2,1,0:T(8,128)(2,1)S(1)}, bf16[1,1,1,1,576,128]{5,4,3,2,1,0:T(8,128)(2,1)S(1)}, u32[]{:S(2)}, u32[]{:S(2)}) collective-permute-start(bf16[1,1,1,1,576,128]{5,4,3,2,1,0:T(8,128)(2,1)S(1)} %bitcast.131), channel_id=1, source_target_pairs={{0,8},{4,12},{8,0},{12,4},{16,24},{20,28},{24,16},{28,20},{1,9},{5... | collective-permute-start | bytes 442376 | tf_op jit(solution)/shard_map/ppermute | solution.py:482
  14.9 16.0 %collective-permute-start.3 = (bf16[1,1,1,1,576,128]{5,4,3,2,1,0:T(8,128)(2,1)S(1)}, bf16[1,1,1,1,576,128]{5,4,3,2,1,0:T(8,128)(2,1)S(1)}, u32[]{:S(2)}, u32[]{:S(2)}) collective-permute-start(bf16[1,1,1,1,576,128]{5,4,3,2,1,0:T(8,128)(2,1)S(1)} %bitcast.132), channel_id=1, source_target_pairs={{0,16},{4,20},{8,24},{12,28},{16,0},{20,4},{24,8},{28,12},{1,17},{... | collective-permute-start | bytes 442376 | tf_op jit(solution)/shard_map/ppermute | solution.py:482
  18.3 12.6 %collective-permute-start = (bf16[1,1,1,1,128,128]{5,4,3,2,1,0:T(8,128)(2,1)S(1)}, bf16[1,1,1,1,128,128]{5,4,3,2,1,0:T(8,128)(2,1)S(1)}, u32[]{:S(2)}, u32[]{:S(2)}) collective-permute-start(bf16[1,1,1,1,128,128]{5,4,3,2,1,0:T(8,128)(2,1)S(1)} %convert_bitcast_fusion.refs_0_), channel_id=1, source_target_pairs={{0,16},{4,20},{8,24},{12,28},{16,0},{20,4},{24,8},{28,12},{1,17},{... | collective-permute-start | bytes 98312 | tf_op jit(solution)/shard_map/ppermute | solution.py:482
  35.2 15.4 %collective-permute-start.9 = (bf16[1,2,2,1,288,128]{5,4,3,2,1,0:T(8,128)(2,1)}, bf16[1,2,2,1,288,128]{5,4,3,2,1,0:T(8,128)(2,1)S(1)}, u32[]{:S(2)}, u32[]{:S(2)}) collective-permute-start(bf16[1,2,2,1,288,128]{5,4,3,2,1,0:T(8,128)(2,1)} %get-tuple-element.233.refs_4_), channel_id=1, source_target_pairs={{0,4},{4,0},{8,12},{12,8},{16,20},{20,16},{24,28},{28,24},{1,5},{5... | collective-permute-start | bytes 884744 | tf_op jit(solution)/shard_map/ppermute | solution.py:482
  36.7 14.6 %collective-permute-start.10 = (bf16[1,2,2,1,288,128]{5,4,3,2,1,0:T(8,128)(2,1)}, bf16[1,2,2,1,288,128]{5,4,3,2,1,0:T(8,128)(2,1)}, u32[]{:S(2)}, u32[]{:S(2)}) collective-permute-start(bf16[1,2,2,1,288,128]{5,4,3,2,1,0:T(8,128)(2,1)} %get-tuple-element.234.refs_6_), channel_id=1, source_target_pairs={{0,2},{1,3},{2,0},{3,1},{4,6},{5,7},{6,4},{7,5},{8,10},{9,11},{10,... | collective-permute-start | bytes 884744 | tf_op jit(solution)/shard_map/ppermute | solution.py:480
  38.7 11.9 %collective-permute-start.7 = (bf16[1,2,2,1,128,128]{5,4,3,2,1,0:T(8,128)(2,1)}, bf16[1,2,2,1,128,128]{5,4,3,2,1,0:T(8,128)(2,1)S(1)}, u32[]{:S(2)}, u32[]{:S(2)}) collective-permute-start(bf16[1,2,2,1,128,128]{5,4,3,2,1,0:T(8,128)(2,1)} %get-tuple-element.232.refs_0_), channel_id=1, source_target_pairs={{0,2},{1,3},{2,0},{3,1},{4,6},{5,7},{6,4},{7,5},{8,10},{9,11},{10,... | collective-permute-start | bytes 393224 | tf_op jit(solution)/shard_map/ppermute | solution.py:480
  55.5 25.6 %collective-permute-start.12 = (bf16[1,2,2,2,288,128]{5,4,3,2,1,0:T(8,128)(2,1)}, bf16[1,2,2,2,288,128]{5,4,3,2,1,0:T(8,128)(2,1)}, u32[]{:S(2)}, u32[]{:S(2)}) collective-permute-start(bf16[1,2,2,2,288,128]{5,4,3,2,1,0:T(8,128)(2,1)} %get-tuple-element.241.refs_0_), channel_id=1, source_target_pairs={{0,2},{1,3},{2,0},{3,1},{4,6},{5,7},{6,4},{7,5},{8,10},{9,11},{10,... | collective-permute-start | bytes 1769480 | tf_op jit(solution)/shard_map/ppermute | solution.py:480
  57.2 23.9 %collective-permute-start.13 = (bf16[2,2,2,1,288,128]{5,4,3,2,1,0:T(8,128)(2,1)}, bf16[2,2,2,1,288,128]{5,4,3,2,1,0:T(8,128)(2,1)}, u32[]{:S(2)}, u32[]{:S(2)}) collective-permute-start(bf16[2,2,2,1,288,128]{5,4,3,2,1,0:T(8,128)(2,1)} %get-tuple-element.243.refs_2_), channel_id=1, source_target_pairs={{0,4},{4,0},{8,12},{12,8},{16,20},{20,16},{24,28},{28,24},{1,5},{5... | collective-permute-start | bytes 1769480 | tf_op jit(solution)/shard_map/ppermute | solution.py:482
  59.4 17.1 %collective-permute-start.15 = (bf16[1,1,1,1,1024,128]{5,4,3,2,1,0:T(8,128)(2,1)S(1)}, bf16[1,1,1,1,1024,128]{5,4,3,2,1,0:T(8,128)(2,1)}, u32[]{:S(2)}, u32[]{:S(2)}) collective-permute-start(bf16[1,1,1,1,1024,128]{5,4,3,2,1,0:T(8,128)(2,1)S(1)} %maximum_bitcast_fusion.3.refs_4_.refs_8_), channel_id=1, source_target_pairs={{0,8},{4,12},{8,0},{12,4},{16,24},{20,28},{24,16},{28,20},{1,9},{5... | collective-permute-start | bytes 786440 | tf_op jit(solution)/shard_map/ppermute | solution.py:482
  59.4 21.7 %collective-permute-start.14 = (bf16[1,1,1,1,1024,128]{5,4,3,2,1,0:T(8,128)(2,1)S(1)}, bf16[1,1,1,1,1024,128]{5,4,3,2,1,0:T(8,128)(2,1)}, u32[]{:S(2)}, u32[]{:S(2)}) collective-permute-start(bf16[1,1,1,1,1024,128]{5,4,3,2,1,0:T(8,128)(2,1)S(1)} %maximum_bitcast_fusion.3.refs_4_.refs_8_), channel_id=1, source_target_pairs={{0,16},{4,20},{8,24},{12,28},{16,0},{20,4},{24,8},{28,12},{1,17},{... | collective-permute-start | bytes 786440 | tf_op jit(solution)/shard_map/ppermute | solution.py:482
  85.5 22.9 %collective-permute-start.17 = (bf16[2,2,2,2,576,128]{5,4,3,2,1,0:T(8,128)(2,1)}, bf16[2,2,2,2,576,128]{5,4,3,2,1,0:T(8,128)(2,1)}, u32[]{:S(2)}, u32[]{:S(2)}) collective-permute-start(bf16[2,2,2,2,576,128]{5,4,3,2,1,0:T(8,128)(2,1)} %get-tuple-element.249), channel_id=1, source_target_pairs={{0,1},{1,0},{2,3},{3,2},{4,5},{5,4},{6,7},{7,6},{8,9},{9,8},{10,11... | collective-permute-start | bytes 7077896 | tf_op jit(solution)/shard_map/ppermute | solution.py:480
  93.7 14.0 %all-to-all-start.1 = ((f32[32,16,128]{2,1,0:T(8,128)}), f32[32,16,128]{2,1,0:T(8,128)S(1)}, u32[]{:S(2)}, u32[]{:S(2)}) async-start(f32[32,16,128]{2,1,0:T(8,128)} %get-tuple-element.237), calls=%async_computation.1 | async-start | bytes 524288 | tf_op jit(solution)/shard_map/all_to_all | solution.py:1345
  97.1 17.0 %collective-permute-start.18 = (bf16[1,2,2,1,512,128]{5,4,3,2,1,0:T(8,128)(2,1)}, bf16[1,2,2,1,512,128]{5,4,3,2,1,0:T(8,128)(2,1)S(1)}, u32[]{:S(2)}, u32[]{:S(2)}) collective-permute-start(bf16[1,2,2,1,512,128]{5,4,3,2,1,0:T(8,128)(2,1)} %get-tuple-element.255.refs_0_), channel_id=1, source_target_pairs={{0,4},{4,0},{8,12},{12,8},{16,20},{20,16},{24,28},{28,24},{1,5},{5... | collective-permute-start | bytes 1572872 | tf_op jit(solution)/shard_map/ppermute | solution.py:482
  99.0 15.7 %collective-permute-start.19 = (bf16[1,2,2,1,512,128]{5,4,3,2,1,0:T(8,128)(2,1)}, bf16[1,2,2,1,512,128]{5,4,3,2,1,0:T(8,128)(2,1)S(1)}, u32[]{:S(2)}, u32[]{:S(2)}) collective-permute-start(bf16[1,2,2,1,512,128]{5,4,3,2,1,0:T(8,128)(2,1)} %get-tuple-element.257.refs_2_), channel_id=1, source_target_pairs={{0,2},{1,3},{2,0},{3,1},{4,6},{5,7},{6,4},{7,5},{8,10},{9,11},{10,... | collective-permute-start | bytes 1572872 | tf_op jit(solution)/shard_map/ppermute | solution.py:480
  119.1 31.1 %collective-permute-start.20 = (bf16[1,2,2,2,512,128]{5,4,3,2,1,0:T(8,128)(2,1)}, bf16[1,2,2,2,512,128]{5,4,3,2,1,0:T(8,128)(2,1)S(1)}, u32[]{:S(2)}, u32[]{:S(2)}) collective-permute-start(bf16[1,2,2,2,512,128]{5,4,3,2,1,0:T(8,128)(2,1)} %get-tuple-element.262.refs_0_), channel_id=1, source_target_pairs={{0,2},{1,3},{2,0},{3,1},{4,6},{5,7},{6,4},{7,5},{8,10},{9,11},{10,... | collective-permute-start | bytes 3145736 | tf_op jit(solution)/shard_map/ppermute | solution.py:480
  120.2 30.6 %collective-permute-start.21 = (bf16[2,2,2,1,512,128]{5,4,3,2,1,0:T(8,128)(2,1)}, bf16[2,2,2,1,512,128]{5,4,3,2,1,0:T(8,128)(2,1)}, u32[]{:S(2)}, u32[]{:S(2)}) collective-permute-start(bf16[2,2,2,1,512,128]{5,4,3,2,1,0:T(8,128)(2,1)} %get-tuple-element.264.refs_2_), channel_id=1, source_target_pairs={{0,4},{4,0},{8,12},{12,8},{16,20},{20,16},{24,28},{28,24},{1,5},{5... | collective-permute-start | bytes 3145736 | tf_op jit(solution)/shard_map/ppermute | solution.py:482
  121.1 25.4 %all-to-all-start.3 = ((f32[32,8,128]{2,1,0:T(8,128)}), f32[32,8,128]{2,1,0:T(8,128)S(1)}, u32[]{:S(2)}, u32[]{:S(2)}) async-start(f32[32,8,128]{2,1,0:T(8,128)} %get-tuple-element.254), calls=%async_computation.3 | async-start | bytes 262144 | tf_op jit(solution)/shard_map/all_to_all | solution.py:1345
  125.4 21.2 %collective-permute-start.24 = (bf16[1,1,1,1,832,128]{5,4,3,2,1,0:T(8,128)(2,1)S(1)}, bf16[1,1,1,1,832,128]{5,4,3,2,1,0:T(8,128)(2,1)S(1)}, u32[]{:S(2)}, u32[]{:S(2)}) collective-permute-start(bf16[1,1,1,1,832,128]{5,4,3,2,1,0:T(8,128)(2,1)S(1)} %maximum_bitcast_fusion.4.refs_4_.refs_8_), channel_id=1, source_target_pairs={{0,24},{4,28},{8,16},{12,20},{16,8},{20,12},{24,0},{28,4},{1,25},{... | collective-permute-start | bytes 638984 | tf_op jit(solution)/shard_map/ppermute | solution.py:482
  129.0 17.5 %collective-permute-start.23 = (bf16[1,1,1,1,832,128]{5,4,3,2,1,0:T(8,128)(2,1)S(1)}, bf16[1,1,1,1,832,128]{5,4,3,2,1,0:T(8,128)(2,1)S(1)}, u32[]{:S(2)}, u32[]{:S(2)}) collective-permute-start(bf16[1,1,1,1,832,128]{5,4,3,2,1,0:T(8,128)(2,1)S(1)} %maximum_bitcast_fusion.4.refs_4_.refs_8_), channel_id=1, source_target_pairs={{0,8},{4,12},{8,0},{12,4},{16,24},{20,28},{24,16},{28,20},{1,9},{5... | collective-permute-start | bytes 638984 | tf_op jit(solution)/shard_map/ppermute | solution.py:482
  129.0 21.1 %collective-permute-start.22 = (bf16[1,1,1,1,832,128]{5,4,3,2,1,0:T(8,128)(2,1)S(1)}, bf16[1,1,1,1,832,128]{5,4,3,2,1,0:T(8,128)(2,1)S(1)}, u32[]{:S(2)}, u32[]{:S(2)}) collective-permute-start(bf16[1,1,1,1,832,128]{5,4,3,2,1,0:T(8,128)(2,1)S(1)} %maximum_bitcast_fusion.4.refs_4_.refs_8_), channel_id=1, source_target_pairs={{0,16},{4,20},{8,24},{12,28},{16,0},{20,4},{24,8},{28,12},{1,17},{... | collective-permute-start | bytes 638984 | tf_op jit(solution)/shard_map/ppermute | solution.py:482
  157.3 22.7 %collective-permute-start.28 = (bf16[1,2,2,1,416,128]{5,4,3,2,1,0:T(8,128)(2,1)}, bf16[1,2,2,1,416,128]{5,4,3,2,1,0:T(8,128)(2,1)S(1)}, u32[]{:S(2)}, u32[]{:S(2)}) collective-permute-start(bf16[1,2,2,1,416,128]{5,4,3,2,1,0:T(8,128)(2,1)} %get-tuple-element.278.refs_0_), channel_id=1, source_target_pairs={{0,4},{4,0},{8,12},{12,8},{16,20},{20,16},{24,28},{28,24},{1,5},{5... | collective-permute-start | bytes 1277960 | tf_op jit(solution)/shard_map/ppermute | solution.py:482
  158.9 21.1 %collective-permute-start.29 = (bf16[1,2,2,1,416,128]{5,4,3,2,1,0:T(8,128)(2,1)}, bf16[1,2,2,1,416,128]{5,4,3,2,1,0:T(8,128)(2,1)S(1)}, u32[]{:S(2)}, u32[]{:S(2)}) collective-permute-start(bf16[1,2,2,1,416,128]{5,4,3,2,1,0:T(8,128)(2,1)} %get-tuple-element.280.refs_2_), channel_id=1, source_target_pairs={{0,2},{1,3},{2,0},{3,1},{4,6},{5,7},{6,4},{7,5},{8,10},{9,11},{10,... | collective-permute-start | bytes 1277960 | tf_op jit(solution)/shard_map/ppermute | solution.py:480
  184.8 29.4 %collective-permute-start.30 = (bf16[1,2,2,2,416,128]{5,4,3,2,1,0:T(8,128)(2,1)}, bf16[1,2,2,2,416,128]{5,4,3,2,1,0:T(8,128)(2,1)S(1)}, u32[]{:S(2)}, u32[]{:S(2)}) collective-permute-start(bf16[1,2,2,2,416,128]{5,4,3,2,1,0:T(8,128)(2,1)} %get-tuple-element.287.refs_0_), channel_id=1, source_target_pairs={{0,2},{1,3},{2,0},{3,1},{4,6},{5,7},{6,4},{7,5},{8,10},{9,11},{10,... | collective-permute-start | bytes 2555912 | tf_op jit(solution)/shard_map/ppermute | solution.py:480
  186.3 27.9 %collective-permute-start.31 = (bf16[2,2,2,1,416,128]{5,4,3,2,1,0:T(8,128)(2,1)}, bf16[2,2,2,1,416,128]{5,4,3,2,1,0:T(8,128)(2,1)S(1)}, u32[]{:S(2)}, u32[]{:S(2)}) collective-permute-start(bf16[2,2,2,1,416,128]{5,4,3,2,1,0:T(8,128)(2,1)} %get-tuple-element.289.refs_2_), channel_id=1, source_target_pairs={{0,4},{4,0},{8,12},{12,8},{16,20},{20,16},{24,28},{28,24},{1,5},{5... | collective-permute-start | bytes 2555912 | tf_op jit(solution)/shard_map/ppermute | solution.py:482
  189.3 19.6 %all-to-all-start.4 = ((f32[8,64,128]{2,1,0:T(8,128)}), f32[8,64,128]{2,1,0:T(8,128)S(1)}, u32[]{:S(2)}, u32[]{:S(2)}) async-start(f32[8,64,128]{2,1,0:T(8,128)} %broadcast_in_dim.14), calls=%async_computation.4 | async-start | bytes 524288 | tf_op jit(solution)/shard_map/all_to_all | solution.py:515
  247.6 14.8 %all-to-all-start.8 = ((bf16[4,176,512]{2,1,0:T(8,128)(2,1)}), bf16[4,176,512]{2,1,0:T(8,128)(2,1)S(1)}, u32[]{:S(2)}, u32[]{:S(2)}) async-start(bf16[4,176,512]{2,1,0:T(8,128)(2,1)} %bitcast.33), calls=%async_computation.8 | async-start | bytes 1441792 | tf_op jit(solution)/shard_map/all_to_all | solution.py:1438
  304.6 25.7 %collective-permute-start.37 = (bf16[2,2,2,2,256,128]{5,4,3,2,1,0:T(8,128)(2,1)}, bf16[2,2,2,2,256,128]{5,4,3,2,1,0:T(8,128)(2,1)}, u32[]{:S(2)}, u32[]{:S(2)}) collective-permute-start(bf16[2,2,2,2,256,128]{5,4,3,2,1,0:T(8,128)(2,1)} %bitcast.154), channel_id=1, source_target_pairs={{0,1},{1,0},{2,3},{3,2},{4,5},{5,4},{6,7},{7,6},{8,9},{9,8},{10,11... | collective-permute-start | bytes 3145736 | tf_op jit(solution)/shard_map/ppermute | solution.py:480
  330.3 32.1 %collective-permute-start.42 = (bf16[2,2,2,2,576,128]{5,4,3,2,1,0:T(8,128)(2,1)}, bf16[2,2,2,2,576,128]{5,4,3,2,1,0:T(8,128)(2,1)}, u32[]{:S(2)}, u32[]{:S(2)}) collective-permute-start(bf16[2,2,2,2,576,128]{5,4,3,2,1,0:T(8,128)(2,1)} %bitcast.153), channel_id=1, source_target_pairs={{0,1},{1,0},{2,3},{3,2},{4,5},{5,4},{6,7},{7,6},{8,9},{9,8},{10,11... | collective-permute-start | bytes 7077896 | tf_op jit(solution)/shard_map/ppermute | solution.py:480
  335.0 27.4 %collective-permute-start.40 = (bf16[1,2,2,2,128,128]{5,4,3,2,1,0:T(8,128)(2,1)}, bf16[1,2,2,2,128,128]{5,4,3,2,1,0:T(8,128)(2,1)S(1)}, u32[]{:S(2)}, u32[]{:S(2)}) collective-permute-start(bf16[1,2,2,2,128,128]{5,4,3,2,1,0:T(8,128)(2,1)} %add_convert_fusion.13), channel_id=1, source_target_pairs={{0,2},{1,3},{2,0},{3,1},{4,6},{5,7},{6,4},{7,5},{8,10},{9,11},{10,... | collective-permute-start | bytes 786440 | tf_op jit(solution)/shard_map/ppermute | solution.py:480
  338.5 23.9 %collective-permute-start.41 = (bf16[2,2,2,1,128,128]{5,4,3,2,1,0:T(8,128)(2,1)}, bf16[2,2,2,1,128,128]{5,4,3,2,1,0:T(8,128)(2,1)}, u32[]{:S(2)}, u32[]{:S(2)}) collective-permute-start(bf16[2,2,2,1,128,128]{5,4,3,2,1,0:T(8,128)(2,1)} %add_convert_fusion.12), channel_id=1, source_target_pairs={{0,4},{4,0},{8,12},{12,8},{16,20},{20,16},{24,28},{28,24},{1,5},{5... | collective-permute-start | bytes 786440 | tf_op jit(solution)/shard_map/ppermute | solution.py:482
  390.1 43.5 %collective-permute-start.47 = (bf16[2,2,2,2,1024,128]{5,4,3,2,1,0:T(8,128)(2,1)}, bf16[2,2,2,2,1024,128]{5,4,3,2,1,0:T(8,128)(2,1)}, u32[]{:S(2)}, u32[]{:S(2)}) collective-permute-start(bf16[2,2,2,2,1024,128]{5,4,3,2,1,0:T(8,128)(2,1)} %bitcast.102), channel_id=1, source_target_pairs={{0,1},{1,0},{2,3},{3,2},{4,5},{5,4},{6,7},{7,6},{8,9},{9,8},{10,11... | collective-permute-start | bytes 12582920 | tf_op jit(solution)/shard_map/ppermute | solution.py:480
  390.1 21.5 %collective-permute-start.45 = (bf16[1,2,2,2,288,128]{5,4,3,2,1,0:T(8,128)(2,1)}, bf16[1,2,2,2,288,128]{5,4,3,2,1,0:T(8,128)(2,1)S(1)}, u32[]{:S(2)}, u32[]{:S(2)}) collective-permute-start(bf16[1,2,2,2,288,128]{5,4,3,2,1,0:T(8,128)(2,1)} %add_convert_fusion.5), channel_id=1, source_target_pairs={{0,2},{1,3},{2,0},{3,1},{4,6},{5,7},{6,4},{7,5},{8,10},{9,11},{10,... | collective-permute-start | bytes 1769480 | tf_op jit(solution)/shard_map/ppermute | solution.py:480
  391.8 19.8 %collective-permute-start.46 = (bf16[2,2,2,1,288,128]{5,4,3,2,1,0:T(8,128)(2,1)}, bf16[2,2,2,1,288,128]{5,4,3,2,1,0:T(8,128)(2,1)S(1)}, u32[]{:S(2)}, u32[]{:S(2)}) collective-permute-start(bf16[2,2,2,1,288,128]{5,4,3,2,1,0:T(8,128)(2,1)} %add_convert_fusion.4), channel_id=1, source_target_pairs={{0,4},{4,0},{8,12},{12,8},{16,20},{20,16},{24,28},{28,24},{1,5},{5... | collective-permute-start | bytes 1769480 | tf_op jit(solution)/shard_map/ppermute | solution.py:482
  392.8 17.3 %collective-permute-start.44 = (bf16[1,2,2,1,128,128]{5,4,3,2,1,0:T(8,128)(2,1)S(1)}, bf16[1,2,2,1,128,128]{5,4,3,2,1,0:T(8,128)(2,1)S(1)}, u32[]{:S(2)}, u32[]{:S(2)}) collective-permute-start(bf16[1,2,2,1,128,128]{5,4,3,2,1,0:T(8,128)(2,1)S(1)} %get-tuple-element.591), channel_id=1, source_target_pairs={{0,2},{1,3},{2,0},{3,1},{4,6},{5,7},{6,4},{7,5},{8,10},{9,11},{10,... | collective-permute-start | bytes 393224 | tf_op jit(solution)/shard_map/ppermute | solution.py:480
  393.1 18.5 %collective-permute-start.43 = (bf16[1,2,2,1,128,128]{5,4,3,2,1,0:T(8,128)(2,1)S(1)}, bf16[1,2,2,1,128,128]{5,4,3,2,1,0:T(8,128)(2,1)S(1)}, u32[]{:S(2)}, u32[]{:S(2)}) collective-permute-start(bf16[1,2,2,1,128,128]{5,4,3,2,1,0:T(8,128)(2,1)S(1)} %get-tuple-element.592), channel_id=1, source_target_pairs={{0,4},{4,0},{8,12},{12,8},{16,20},{20,16},{24,28},{28,24},{1,5},{5... | collective-permute-start | bytes 393224 | tf_op jit(solution)/shard_map/ppermute | solution.py:482
  394.2 23.0 %all-to-all-start.14 = ((f32[32,8,128]{2,1,0:T(8,128)}), f32[32,8,128]{2,1,0:T(8,128)S(1)}, u32[]{:S(2)}, u32[]{:S(2)}) async-start(f32[32,8,128]{2,1,0:T(8,128)} %get-tuple-element.334), calls=%async_computation.14 | async-start | bytes 262144 | tf_op jit(solution)/shard_map/all_to_all | solution.py:1345
  439.3 66.6 %collective-permute-start.57 = (bf16[2,2,2,2,576,128]{5,4,3,2,1,0:T(8,128)(2,1)}, bf16[2,2,2,2,576,128]{5,4,3,2,1,0:T(8,128)(2,1)}, u32[]{:S(2)}, u32[]{:S(2)}) collective-permute-start(bf16[2,2,2,2,576,128]{5,4,3,2,1,0:T(8,128)(2,1)} %bitcast.43), channel_id=1, source_target_pairs={{0,1},{1,0},{2,3},{3,2},{4,5},{5,4},{6,7},{7,6},{8,9},{9,8},{10,11... | collective-permute-start | bytes 7077896 | tf_op jit(solution)/shard_map/ppermute | solution.py:480
  439.3 35.6 %collective-permute-start.50 = (bf16[1,2,2,2,512,128]{5,4,3,2,1,0:T(8,128)(2,1)}, bf16[1,2,2,2,512,128]{5,4,3,2,1,0:T(8,128)(2,1)S(1)}, u32[]{:S(2)}, u32[]{:S(2)}) collective-permute-start(bf16[1,2,2,2,512,128]{5,4,3,2,1,0:T(8,128)(2,1)} %add_convert_fusion.1), channel_id=1, source_target_pairs={{0,2},{1,3},{2,0},{3,1},{4,6},{5,7},{6,4},{7,5},{8,10},{9,11},{10,... | collective-permute-start | bytes 3145736 | tf_op jit(solution)/shard_map/ppermute | solution.py:480
  439.5 35.4 %collective-permute-start.51 = (bf16[2,2,2,1,512,128]{5,4,3,2,1,0:T(8,128)(2,1)}, bf16[2,2,2,1,512,128]{5,4,3,2,1,0:T(8,128)(2,1)}, u32[]{:S(2)}, u32[]{:S(2)}) collective-permute-start(bf16[2,2,2,1,512,128]{5,4,3,2,1,0:T(8,128)(2,1)} %add_convert_fusion), channel_id=1, source_target_pairs={{0,4},{4,0},{8,12},{12,8},{16,20},{20,16},{24,28},{28,24},{1,5},{5... | collective-permute-start | bytes 3145736 | tf_op jit(solution)/shard_map/ppermute | solution.py:482
  440.4 32.5 %all-to-all-start.9 = ((bf16[4,176,512]{2,1,0:T(8,128)(2,1)}), bf16[4,176,512]{2,1,0:T(8,128)(2,1)}, u32[]{:S(2)}, u32[]{:S(2)}) async-start(bf16[4,176,512]{2,1,0:T(8,128)(2,1)} %get-tuple-element.297), calls=%async_computation.9 | async-start | bytes 1441792 | tf_op jit(solution)/shard_map/all_to_all | solution.py:1521
  473.5 15.6 %collective-permute-start.49 = (bf16[1,2,2,1,288,128]{5,4,3,2,1,0:T(8,128)(2,1)}, bf16[1,2,2,1,288,128]{5,4,3,2,1,0:T(8,128)(2,1)S(1)}, u32[]{:S(2)}, u32[]{:S(2)}) collective-permute-start(bf16[1,2,2,1,288,128]{5,4,3,2,1,0:T(8,128)(2,1)} %get-tuple-element.578), channel_id=1, source_target_pairs={{0,2},{1,3},{2,0},{3,1},{4,6},{5,7},{6,4},{7,5},{8,10},{9,11},{10,... | collective-permute-start | bytes 884744 | tf_op jit(solution)/shard_map/ppermute | solution.py:480
  473.9 18.0 %collective-permute-start.48 = (bf16[1,2,2,1,288,128]{5,4,3,2,1,0:T(8,128)(2,1)}, bf16[1,2,2,1,288,128]{5,4,3,2,1,0:T(8,128)(2,1)}, u32[]{:S(2)}, u32[]{:S(2)}) collective-permute-start(bf16[1,2,2,1,288,128]{5,4,3,2,1,0:T(8,128)(2,1)} %get-tuple-element.579), channel_id=1, source_target_pairs={{0,4},{4,0},{8,12},{12,8},{16,20},{20,16},{24,28},{28,24},{1,5},{5... | collective-permute-start | bytes 884744 | tf_op jit(solution)/shard_map/ppermute | solution.py:482
  478.3 25.1 %collective-permute-start.56 = (bf16[1,2,2,1,512,128]{5,4,3,2,1,0:T(8,128)(2,1)}, bf16[1,2,2,1,512,128]{5,4,3,2,1,0:T(8,128)(2,1)S(1)}, u32[]{:S(2)}, u32[]{:S(2)}) collective-permute-start(bf16[1,2,2,1,512,128]{5,4,3,2,1,0:T(8,128)(2,1)} %get-tuple-element.552), channel_id=1, source_target_pairs={{0,2},{1,3},{2,0},{3,1},{4,6},{5,7},{6,4},{7,5},{8,10},{9,11},{10,... | collective-permute-start | bytes 1572872 | tf_op jit(solution)/shard_map/ppermute | solution.py:480
  480.0 25.3 %collective-permute-start.55 = (bf16[1,2,2,1,512,128]{5,4,3,2,1,0:T(8,128)(2,1)}, bf16[1,2,2,1,512,128]{5,4,3,2,1,0:T(8,128)(2,1)}, u32[]{:S(2)}, u32[]{:S(2)}) collective-permute-start(bf16[1,2,2,1,512,128]{5,4,3,2,1,0:T(8,128)(2,1)} %get-tuple-element.553), channel_id=1, source_target_pairs={{0,4},{4,0},{8,12},{12,8},{16,20},{20,16},{24,28},{28,24},{1,5},{5... | collective-permute-start | bytes 1572872 | tf_op jit(solution)/shard_map/ppermute | solution.py:482
  489.2 33.3 %collective-permute-start.72 = (bf16[1,1,1,1,256,128]{5,4,3,2,1,0:T(8,128)(2,1)}, bf16[1,1,1,1,256,128]{5,4,3,2,1,0:T(8,128)(2,1)}, u32[]{:S(2)}, u32[]{:S(2)}) collective-permute-start(bf16[1,1,1,1,256,128]{5,4,3,2,1,0:T(8,128)(2,1)} %pad_maximum_fusion.9), channel_id=1, source_target_pairs={{0,16},{4,20},{8,24},{12,28},{16,0},{20,4},{24,8},{28,12},{1,17},{... | collective-permute-start | bytes 196616 | tf_op jit(solution)/shard_map/ppermute | solution.py:482
  491.9 32.5 %collective-permute-start.73 = (bf16[1,1,1,1,256,128]{5,4,3,2,1,0:T(8,128)(2,1)}, bf16[1,1,1,1,256,128]{5,4,3,2,1,0:T(8,128)(2,1)}, u32[]{:S(2)}, u32[]{:S(2)}) collective-permute-start(bf16[1,1,1,1,256,128]{5,4,3,2,1,0:T(8,128)(2,1)} %pad_maximum_fusion.10), channel_id=1, source_target_pairs={{0,8},{4,12},{8,0},{12,4},{16,24},{20,28},{24,16},{28,20},{1,9},{5... | collective-permute-start | bytes 196616 | tf_op jit(solution)/shard_map/ppermute | solution.py:482
  503.4 21.1 %collective-permute-start.74 = (bf16[1,1,1,1,256,128]{5,4,3,2,1,0:T(8,128)(2,1)}, bf16[1,1,1,1,256,128]{5,4,3,2,1,0:T(8,128)(2,1)}, u32[]{:S(2)}, u32[]{:S(2)}) collective-permute-start(bf16[1,1,1,1,256,128]{5,4,3,2,1,0:T(8,128)(2,1)} %pad_maximum_fusion.11), channel_id=1, source_target_pairs={{0,24},{4,28},{8,16},{12,20},{16,8},{20,12},{24,0},{28,4},{1,25},{... | collective-permute-start | bytes 196616 | tf_op jit(solution)/shard_map/ppermute | solution.py:482
  505.4 21.1 %collective-permute-start.52 = (bf16[1,1,1,1,576,128]{5,4,3,2,1,0:T(8,128)(2,1)}, bf16[1,1,1,1,576,128]{5,4,3,2,1,0:T(8,128)(2,1)}, u32[]{:S(2)}, u32[]{:S(2)}) collective-permute-start(bf16[1,1,1,1,576,128]{5,4,3,2,1,0:T(8,128)(2,1)} %pad_maximum_fusion.3), channel_id=1, source_target_pairs={{0,16},{4,20},{8,24},{12,28},{16,0},{20,4},{24,8},{28,12},{1,17},{... | collective-permute-start | bytes 442376 | tf_op jit(solution)/shard_map/ppermute | solution.py:482
  505.9 22.6 %collective-permute-start.53 = (bf16[1,1,1,1,576,128]{5,4,3,2,1,0:T(8,128)(2,1)}, bf16[1,1,1,1,576,128]{5,4,3,2,1,0:T(8,128)(2,1)}, u32[]{:S(2)}, u32[]{:S(2)}) collective-permute-start(bf16[1,1,1,1,576,128]{5,4,3,2,1,0:T(8,128)(2,1)} %pad_maximum_fusion.4), channel_id=1, source_target_pairs={{0,8},{4,12},{8,0},{12,4},{16,24},{20,28},{24,16},{28,20},{1,9},{5... | collective-permute-start | bytes 442376 | tf_op jit(solution)/shard_map/ppermute | solution.py:482
  525.5 16.9 %collective-permute-start.58 = (bf16[1,2,2,2,288,128]{5,4,3,2,1,0:T(8,128)(2,1)}, bf16[1,2,2,2,288,128]{5,4,3,2,1,0:T(8,128)(2,1)S(1)}, u32[]{:S(2)}, u32[]{:S(2)}) collective-permute-start(bf16[1,2,2,2,288,128]{5,4,3,2,1,0:T(8,128)(2,1)} %add_convert_fusion.3), channel_id=1, source_target_pairs={{0,2},{1,3},{2,0},{3,1},{4,6},{5,7},{6,4},{7,5},{8,10},{9,11},{10,... | collective-permute-start | bytes 1769480 | tf_op jit(solution)/shard_map/ppermute | solution.py:480
  526.4 18.4 %collective-permute-start.60 = (bf16[2,2,2,1,288,128]{5,4,3,2,1,0:T(8,128)(2,1)S(1)}, bf16[2,2,2,1,288,128]{5,4,3,2,1,0:T(8,128)(2,1)S(1)}, u32[]{:S(2)}, u32[]{:S(2)}) collective-permute-start(bf16[2,2,2,1,288,128]{5,4,3,2,1,0:T(8,128)(2,1)S(1)} %add_convert_fusion.2), channel_id=1, source_target_pairs={{0,4},{4,0},{8,12},{12,8},{16,20},{20,16},{24,28},{28,24},{1,5},{5... | collective-permute-start | bytes 1769480 | tf_op jit(solution)/shard_map/ppermute | solution.py:482
  531.4 21.0 %collective-permute-start.75 = (bf16[1,1,1,1,1024,128]{5,4,3,2,1,0:T(8,128)(2,1)}, bf16[1,1,1,1,1024,128]{5,4,3,2,1,0:T(8,128)(2,1)}, u32[]{:S(2)}, u32[]{:S(2)}) collective-permute-start(bf16[1,1,1,1,1024,128]{5,4,3,2,1,0:T(8,128)(2,1)} %pad_maximum_fusion), channel_id=1, source_target_pairs={{0,16},{4,20},{8,24},{12,28},{16,0},{20,4},{24,8},{28,12},{1,17},{... | collective-permute-start | bytes 786440 | tf_op jit(solution)/shard_map/ppermute | solution.py:482
  533.0 19.4 %collective-permute-start.76 = (bf16[1,1,1,1,1024,128]{5,4,3,2,1,0:T(8,128)(2,1)}, bf16[1,1,1,1,1024,128]{5,4,3,2,1,0:T(8,128)(2,1)}, u32[]{:S(2)}, u32[]{:S(2)}) collective-permute-start(bf16[1,1,1,1,1024,128]{5,4,3,2,1,0:T(8,128)(2,1)} %pad_maximum_fusion.1), channel_id=1, source_target_pairs={{0,8},{4,12},{8,0},{12,4},{16,24},{20,28},{24,16},{28,20},{1,9},{5... | collective-permute-start | bytes 786440 | tf_op jit(solution)/shard_map/ppermute | solution.py:482
  533.5 19.3 %collective-permute-start.77 = (bf16[1,1,1,1,1024,128]{5,4,3,2,1,0:T(8,128)(2,1)}, bf16[1,1,1,1,1024,128]{5,4,3,2,1,0:T(8,128)(2,1)}, u32[]{:S(2)}, u32[]{:S(2)}) collective-permute-start(bf16[1,1,1,1,1024,128]{5,4,3,2,1,0:T(8,128)(2,1)} %pad_maximum_fusion.2), channel_id=1, source_target_pairs={{0,24},{4,28},{8,16},{12,20},{16,8},{20,12},{24,0},{28,4},{1,25},{... | collective-permute-start | bytes 786440 | tf_op jit(solution)/shard_map/ppermute | solution.py:482
  536.6 58.3 %all-to-all-start.16 = ((bf16[4,704,256]{2,1,0:T(8,128)(2,1)}), bf16[4,704,256]{2,1,0:T(8,128)(2,1)S(1)}, u32[]{:S(2)}, u32[]{:S(2)}) async-start(bf16[4,704,256]{2,1,0:T(8,128)(2,1)} %get-tuple-element.377), calls=%async_computation.16 | async-start | bytes 2883584 | tf_op jit(solution)/shard_map/all_to_all | solution.py:1614
  542.4 20.4 %collective-permute-start.68 = (bf16[1,2,2,1,128,128]{5,4,3,2,1,0:T(8,128)(2,1)}, bf16[1,2,2,1,128,128]{5,4,3,2,1,0:T(8,128)(2,1)}, u32[]{:S(2)}, u32[]{:S(2)}) collective-permute-start(bf16[1,2,2,1,128,128]{5,4,3,2,1,0:T(8,128)(2,1)} %get-tuple-element.596), channel_id=1, source_target_pairs={{0,6},{1,7},{2,4},{3,5},{4,2},{5,3},{6,0},{7,1},{8,14},{9,15},{10,... | collective-permute-start | bytes 393224 | tf_op jit(solution)/shard_map/ppermute | solution.py:484
  544.9 17.9 %collective-permute-start.67 = (bf16[1,2,2,1,128,128]{5,4,3,2,1,0:T(8,128)(2,1)}, bf16[1,2,2,1,128,128]{5,4,3,2,1,0:T(8,128)(2,1)S(1)}, u32[]{:S(2)}, u32[]{:S(2)}) collective-permute-start(bf16[1,2,2,1,128,128]{5,4,3,2,1,0:T(8,128)(2,1)} %get-tuple-element.597), channel_id=1, source_target_pairs={{0,4},{4,0},{8,12},{12,8},{16,20},{20,16},{24,28},{28,24},{1,5},{5... | collective-permute-start | bytes 393224 | tf_op jit(solution)/shard_map/ppermute | solution.py:482
  552.4 12.7 %collective-permute-start.66 = (bf16[1,2,2,1,128,128]{5,4,3,2,1,0:T(8,128)(2,1)}, bf16[1,2,2,1,128,128]{5,4,3,2,1,0:T(8,128)(2,1)S(1)}, u32[]{:S(2)}, u32[]{:S(2)}) collective-permute-start(bf16[1,2,2,1,128,128]{5,4,3,2,1,0:T(8,128)(2,1)} %get-tuple-element.598), channel_id=1, source_target_pairs={{0,2},{1,3},{2,0},{3,1},{4,6},{5,7},{6,4},{7,5},{8,10},{9,11},{10,... | collective-permute-start | bytes 393224 | tf_op jit(solution)/shard_map/ppermute | solution.py:480
  552.4 17.3 %collective-permute-start.59 = (bf16[1,2,2,1,288,128]{5,4,3,2,1,0:T(8,128)(2,1)}, bf16[1,2,2,1,288,128]{5,4,3,2,1,0:T(8,128)(2,1)S(1)}, u32[]{:S(2)}, u32[]{:S(2)}) collective-permute-start(bf16[1,2,2,1,288,128]{5,4,3,2,1,0:T(8,128)(2,1)} %get-tuple-element.573), channel_id=1, source_target_pairs={{0,4},{4,0},{8,12},{12,8},{16,20},{20,16},{24,28},{28,24},{1,5},{5... | collective-permute-start | bytes 884744 | tf_op jit(solution)/shard_map/ppermute | solution.py:482
  552.8 18.2 %collective-permute-start.61 = (bf16[1,2,2,1,288,128]{5,4,3,2,1,0:T(8,128)(2,1)}, bf16[1,2,2,1,288,128]{5,4,3,2,1,0:T(8,128)(2,1)}, u32[]{:S(2)}, u32[]{:S(2)}) collective-permute-start(bf16[1,2,2,1,288,128]{5,4,3,2,1,0:T(8,128)(2,1)} %get-tuple-element.574), channel_id=1, source_target_pairs={{0,2},{1,3},{2,0},{3,1},{4,6},{5,7},{6,4},{7,5},{8,10},{9,11},{10,... | collective-permute-start | bytes 884744 | tf_op jit(solution)/shard_map/ppermute | solution.py:480
  575.1 13.8 %collective-permute-start.62 = (bf16[1,1,1,1,576,128]{5,4,3,2,1,0:T(8,128)(2,1)S(1)}, bf16[1,1,1,1,576,128]{5,4,3,2,1,0:T(8,128)(2,1)S(1)}, u32[]{:S(2)}, u32[]{:S(2)}) collective-permute-start(bf16[1,1,1,1,576,128]{5,4,3,2,1,0:T(8,128)(2,1)S(1)} %pad_maximum_fusion.6), channel_id=1, source_target_pairs={{0,16},{4,20},{8,24},{12,28},{16,0},{20,4},{24,8},{28,12},{1,17},{... | collective-permute-start | bytes 442376 | tf_op jit(solution)/shard_map/ppermute | solution.py:482
  594.8 13.2 %all-to-all-start.17 = ((f32[32,16,128]{2,1,0:T(8,128)}), f32[32,16,128]{2,1,0:T(8,128)S(1)}, u32[]{:S(2)}, u32[]{:S(2)}) async-start(f32[32,16,128]{2,1,0:T(8,128)} %get-tuple-element.394), calls=%async_computation.17 | async-start | bytes 524288 | tf_op jit(solution)/shard_map/all_to_all | solution.py:1345
  (104 other events, 1002.6 us)

commit v6 on v5

--- a/solution.py
+++ b/solution.py
@@ -742,6 +742,14 @@
     if before is not None:
         before, _ = lax.optimization_barrier((before, sent))
     return before
+
+
+def hold(flows, value):
+    value, parts = lax.optimization_barrier((value, [flow.pending() for flow in flows]))
+    for flow, part in zip(flows, parts):
+        flow.resume(part)
+    wave(flows)
+    return value
 
 
 def chunk_kernel(units, columns, rows_ref, cols_ref, *refs):
@@ -1398,8 +1406,11 @@
         )
     )
     field = lax.all_to_all(field, "mp", 0, 0, tiled=True)
+    tables = jnp.concatenate([narrow_norms.reshape(-1, 128), wide_norms.reshape(-1, 128)], 0)
+    tables = jnp.broadcast_to(tables[None], (ranks,) + tables.shape)
+    tables = lax.all_to_all(tables, "mp", 0, 0, tiled=True)
     wave([flow_a, flow_b])
-    wave([flow_a, flow_b, flow_c], field)
+    wave([flow_a, flow_b, flow_c], (field, tables))
     wave([flow_a, flow_b, flow_d])
     unit_in, column = first_weight.shape
     column_wide = shortcut_weight.shape[1]
@@ -1408,9 +1419,6 @@
     size_short = unit_in * column_wide // 128
     size_out = unit_out * column // 128
     size_mid = 9 * unit_mid * column // 128
-    tables = jnp.concatenate([narrow_norms.reshape(-1, 128), wide_norms.reshape(-1, 128)], 0)
-    tables = jnp.broadcast_to(tables[None], (ranks,) + tables.shape)
-    tables = lax.all_to_all(tables, "mp", 0, 0, tiled=True)
     split = narrow_norms.size // 128
     narrow_all = (
         tables[:, :split].reshape(ranks, 4, 2, -1).transpose(1, 2, 0, 3).reshape(4, 2, narrow)
@@ -1457,7 +1465,7 @@
         bundle_a,
         unit_in,
     )
-    sums_one = wave([flow_b, flow_c], sums, exchange(sums))
+    sums_one = hold([flow_b, flow_c], exchange(sums))
     counts = jnp.sum(sums_one[:, 2 * size :], 0)
     bundle_b = flow_b.bundles()
     cols_one, pre_two, sums = launch(
@@ -1518,7 +1526,9 @@
         [pre_six, sums_six, counts, wide_all, out_one, above, mask],
     )
     back_six = everywhere(sums)
+    back_six, block_output = lax.optimization_barrier((back_six, block_output))
     block_output = lax.all_to_all(block_output, "mp", 0, 0, tiled=True)
+    shown = block_output
     block_output = block_output.transpose(2, 0, 1).reshape(-1, ranks * pixels)
 
     grad_six, act_five_grad, sums = launch(
@@ -1532,7 +1542,8 @@
     )
     bundle = chunks_into(None, size_out, 0, grad_six, hid_five, 1, unit_out, column)
     back_a = Scatter(*bundle)
-    back_five = wave([back_a], sums, exchange(sums))
+    back_five, _ = lax.optimization_barrier((exchange(sums), shown))
+    back_five = hold([back_a], back_five)
     grad_five, act_four_grad, sums = launch(
         functools.partial(spread_back, size_out, 2, PLAIN_TAPS),
         [short(pixels, narrow), real(pixels, narrow), copies],
@@ -1545,7 +1556,8 @@
     back_four = exchange(sums)
     bundle = chunks_into(None, size_mid, 0, cols_four, grad_five, 9, unit_mid, column)
     back_b = Scatter(*bundle)
-    back_four = wave([back_a, back_b], sums, back_four)
+    back_four = wave([back_a], sums, back_four)
+    back_four = hold([back_b], back_four)
     grad_four, grad_one, sums = launch(
         functools.partial(narrow_layer_back, size_short + size_out),
         [short(pixels, narrow), real(pixels, wide), real(3 * wide_rows, 128)],
@@ -1574,7 +1586,7 @@
     bundle = chunks_into(bundle, total, size_short, grad_three, hid_two, 1, unit_out, column)
     bundle = chunks_into(bundle, total, 0, field, grad_side, 1, unit_in, column_wide)
     back_c = Scatter(*bundle)
-    back_two = wave([back_c], sums, back_two)
+    back_two = hold([back_c], back_two)
     grad_mid, act_one_grad, sums = launch(
         functools.partial(spread_back, 0, 0, STRIDED_TAPS),
         [short(pixels, narrow), real(full, narrow), copies],
@@ -1584,8 +1596,8 @@
         size_mid,
         [(pixels, narrow)],
     )
-    sums = wave([back_c], None, sums)
     back_one = wave([back_b], sums, exchange(sums))
+    back_one = wave([back_c], sums, back_one)
     bundle = chunks_into(None, size_mid, 0, cols_one, grad_mid, 9, unit_mid, column)
     back_d = Scatter(*bundle)
     (side_grad,) = launch(
@@ -1595,8 +1607,7 @@
         bundle_c,
         size_short,
     )
-    back_one = wave([back_d], sums, back_one)
-    back_one = wave([back_c], None, back_one)
+    back_one = hold([back_d], back_one)
     back_one, side_grad = lax.optimization_barrier((back_one, side_grad))
     grad_first, field_grad = launch(
         first_back,
@@ -1614,7 +1625,7 @@
     input_grad = lax.all_to_all(field_grad, "mp", 0, 0, tiled=True)
     input_grad = input_grad.reshape(ranks, 4, pixels, channels).transpose(3, 1, 0, 2)
     input_grad = input_grad.reshape(inputs.shape)
-    wave([back_d, back_e])
+    wave([back_c, back_d, back_e])
     wave([back_d, back_e])
     rows_a, rows_b, rows_c, rows_d, rows_e = [
         flow.rows() for flow in (back_a, back_b, back_c, back_d, back_e)

time: 628 us -> 640 us (1.019)
  starting transfers between devices: 133 us -> 141 us
  waiting for transfers between devices: 169 us -> 177 us
    ppermute x43, waiting for transfers between devices: 45.7 us -> 70.2 us  [swap(): lax.ppermute(values, 'dp', [(at, at ^ masks['dp']) for at in range(sizes[...]
    all_to_all x1, waiting for transfers between devices: 27 us -> 4.61 us  [by_image(): block_output = lax.all_to_all(block_output, 'mp', 0, 0, tiled=True)]
    ppermute x2, waiting for transfers between devices: 9.6 us -> 21.1 us  [swap(): lax.ppermute(values, ('dp', 'mp'), [(at, at ^ mask) for at in range(sizes...]
    unnamed x160 -> x150, local copies, waits for them, and re-layouts: 16.9 us -> 14.5 us
  transfers between devices with their start and end apart: 91 -> 91, of which waited for: 36 -> 34; matrix products, arithmetic and copies ran while one was open for 11% -> 10% of each run, Pallas kernels for 15% -> 19%
where the time goes in v6:
time: 640 us; the launch traced here: 627 us
  waiting for transfers between devices  177 us (28%)
  Pallas kernels  165 us (26%)
  starting transfers between devices  141 us (22%)
  other arithmetic  59.5 us (9%)
  blocking collectives  54.8 us (9%)
  local copies, waits for them, and re-layouts  29 us (5%)
    pallas_call x18, Pallas kernels, launch(): pl.pallas_call(kernel, in_specs=specs + [pl.BlockSpec(memory_space=pltpu....  88.6 us
    ppermute x43, waiting for transfers between devices, swap(): lax.ppermute(values, 'dp', [(at, at ^ masks['dp']) for at in range(sizes[...  70.2 us
    ppermute x43, starting transfers between devices, swap(): lax.ppermute(values, 'dp', [(at, at ^ masks['dp']) for at in range(sizes[...  60.7 us
    pallas_call x7, Pallas kernels, chunks_into(): pl.pallas_call(functools.partial(chunk_kernel, units, columns), grid=(ste...  48.4 us
    ppermute x33, waiting for transfers between devices, swap(): lax.ppermute(values, 'mp', [(at, at ^ masks['mp']) for at in range(sizes[...  39.4 us
    all_to_all x3, blocking collectives, exchange(): return lax.all_to_all(copies, ('dp', 'mp'), 0, 0, tiled=True)  34 us
    ppermute x33, starting transfers between devices, swap(): lax.ppermute(values, 'mp', [(at, at ^ masks['mp']) for at in range(sizes[...  28.8 us
    pallas_call x7, Pallas kernels, moves(): pl.pallas_call(functools.partial(moves_kernel, tasks, len(sources)), in_s...  27.5 us
  transfers between devices with their start and end apart: 91, of which 34 were waited for; matrix products, arithmetic and copies ran while one was open for 10% of the time, Pallas kernels for 19%

profile of v6, /device:TPU:0, one launch (start us, length us, event | category | flops | bytes accessed | tf_op | source)
XLA Modules:
  0.0 627.5 jit_solution(4444215690979390628)
XLA Ops:
  2.7 4.2 all-to-all-start.1
  11.7 3.7 all-to-all-start
  15.4 4.2 collective-permute-start.2
  26.9 11.4 %collective-permute-done.refs_1_ = bf16[1,1,1,1,128,128]{5,4,3,2,1,0:T(8,128)(2,1)S(1)} collective-permute-done((bf16[1,1,1,1,128,128]{5,4,3,2,1,0:T(8,128)(2,1)S(1)}, bf16[1,1,1,1,128,128]{5,4,3,2,1,0:T(8,128)(2,1)S(1)}, u32[]{:S(2)}, u32[]{:S(2)}) %collective-permute-start) | collective-permute-done | bytes 32800 | tf_op jit(solution)/shard_map/ppermute | solution.py:482
  49.3 7.3 %collective-permute-done.8.refs_3_ = bf16[1,2,2,1,128,128]{5,4,3,2,1,0:T(8,128)(2,1)S(1)} collective-permute-done((bf16[1,2,2,1,128,128]{5,4,3,2,1,0:T(8,128)(2,1)}, bf16[1,2,2,1,128,128]{5,4,3,2,1,0:T(8,128)(2,1)S(1)}, u32[]{:S(2)}, u32[]{:S(2)}) %collective-permute-start.8) | collective-permute-done | bytes 131104 | tf_op jit(solution)/shard_map/ppermute | solution.py:484
  59.4 3.4 shard_map.465
  66.8 4.2 shard_map.466
  74.1 3.7 collective-permute-start.16
  78.5 10.5 %collective-permute-done.16.refs_7_.refs_11_ = bf16[1,1,1,1,1024,128]{5,4,3,2,1,0:T(8,128)(2,1)S(1)} collective-permute-done((bf16[1,1,1,1,1024,128]{5,4,3,2,1,0:T(8,128)(2,1)S(1)}, bf16[1,1,1,1,1024,128]{5,4,3,2,1,0:T(8,128)(2,1)S(1)}, u32[]{:S(2)}, u32[]{:S(2)}) %collective-permute-start.16) | collective-permute-done | bytes 262176 | tf_op jit(solution)/shard_map/ppermute | solution.py:482
  89.1 4.0 collective-permute-done.15.refs_6_.refs_10_
  93.0 12.9 %collective-permute-done.14.refs_5_.refs_9_ = bf16[1,1,1,1,1024,128]{5,4,3,2,1,0:T(8,128)(2,1)S(1)} collective-permute-done((bf16[1,1,1,1,1024,128]{5,4,3,2,1,0:T(8,128)(2,1)S(1)}, bf16[1,1,1,1,1024,128]{5,4,3,2,1,0:T(8,128)(2,1)S(1)}, u32[]{:S(2)}, u32[]{:S(2)}) %collective-permute-start.14) | collective-permute-done | bytes 262176 | tf_op jit(solution)/shard_map/ppermute | solution.py:482
  106.6 4.4 shard_map.467
  117.5 5.6 shard_map.468
  123.1 3.4 collective-permute-done.18.refs_1_
  128.5 3.6 shard_map.469
  137.0 3.7 collective-permute-start.24
  141.4 18.0 %all-to-all-done.3.refs_2_.refs_9_.refs_3_ = f32[32,8,128]{2,1,0:T(8,128)S(1)} async-done(((f32[32,8,128]{2,1,0:T(8,128)}), f32[32,8,128]{2,1,0:T(8,128)S(1)}, u32[]{:S(2)}, u32[]{:S(2)}) %all-to-all-start.3) | async-done | bytes 131104 | tf_op jit(solution)/shard_map/all_to_all | solution.py:1353
  163.4 5.4 shard_map.470
  171.9 4.5 collective-permute-done.25
  176.4 4.8 shard_map.472
  181.2 3.8 shard_map.471
  193.2 3.3 shard_map.473
  201.0 3.6 all-to-all-start.4
  205.3 15.3 %all-to-all-done.4.refs_3_.refs_11_.refs_4_ = f32[8,64,128]{2,1,0:T(8,128)S(1)} async-done(((f32[8,64,128]{2,1,0:T(8,128)}), f32[8,64,128]{2,1,0:T(8,128)S(1)}, u32[]{:S(2)}, u32[]{:S(2)}) %all-to-all-start.4) | async-done | bytes 262176 | tf_op jit(solution)/shard_map/all_to_all | solution.py:515
  221.3 4.5 shard_map.474
  227.0 4.5 shard_map.475
  231.7 10.9 %all_to_all.90.refs_2_.refs_8_.refs_3_ = f32[32,8,128]{2,1,0:T(8,128)} all-to-all(f32[32,8,128]{2,1,0:T(8,128)S(1)} %copy-done.58), channel_id=1, replica_groups=mesh['dp'=8,'mp'=4] {'dp','mp'}, dimensions={0} | all-to-all | bytes 262144 | tf_op jit(solution)/shard_map/all_to_all | solution.py:1353
  242.6 5.2 shard_map.476
  247.8 11.5 %all_to_all.91.refs_2_.refs_8_.refs_3_ = f32[32,8,128]{2,1,0:T(8,128)} all-to-all(f32[32,8,128]{2,1,0:T(8,128)} %get-tuple-element.296), channel_id=1, replica_groups=mesh['dp'=8,'mp'=4] {'dp','mp'}, dimensions={0} | all-to-all | bytes 262144 | tf_op jit(solution)/shard_map/all_to_all | solution.py:1353
  259.3 3.5 all-to-all-start.8
  262.8 3.9 shard_map.477
  274.1 10.4 %all_to_all.92.refs_1_.refs_3_ = f32[8,32,128]{2,1,0:T(8,128)} all-to-all(f32[8,32,128]{2,1,0:T(8,128)S(1)} %broadcast_in_dim.15), channel_id=1, replica_groups=mesh['dp'=8,'mp'=4] {'dp'}, dimensions={0} | all-to-all | bytes 262144 | tf_op jit(solution)/shard_map/all_to_all | solution.py:515
  284.5 4.5 shard_map.478
  295.0 10.4 %all_to_all.93.refs_4_ = f32[8,32,128]{2,1,0:T(8,128)} all-to-all(f32[8,32,128]{2,1,0:T(8,128)S(1)} %broadcast_in_dim.16), channel_id=1, replica_groups=mesh['dp'=8,'mp'=4] {'dp'}, dimensions={0} | all-to-all | bytes 262144 | tf_op jit(solution)/shard_map/all_to_all | solution.py:515
  305.4 4.6 shard_map.479
  310.0 11.5 %all_to_all.94.refs_4_ = f32[32,8,128]{2,1,0:T(8,128)} all-to-all(f32[32,8,128]{2,1,0:T(8,128)} %get-tuple-element.306), channel_id=1, replica_groups=mesh['dp'=8,'mp'=4] {'dp','mp'}, dimensions={0} | all-to-all | bytes 262144 | tf_op jit(solution)/shard_map/all_to_all | solution.py:1353
  321.5 3.5 all-to-all-start.10
  325.0 6.3 %shard_map.480 = (bf16[2,8,256,128]{3,2,1,0:T(8,128)(2,1)}, bf16[2,8,256,128]{3,2,1,0:T(8,128)(2,1)}) custom-call(bf16[176,2048]{1,0:T(8,128)(2,1)} %get-tuple-element.308.rows_ref, bf16[176,512]{1,0:T(8,128)(2,1)} %get-tuple-element.309.cols_ref), custom_call_target="tpu_custom_call" | custom-call | flops 1024 | bytes 1024 | tf_op jit(solution)/shard_map/pallas_call | solution.py:785
  331.3 4.6 all-to-all-done.10
  335.9 6.3 %shard_map.481 = (bf16[176,512]{1,0:T(8,128)(2,1)}, f32[176,512]{1,0:T(8,128)}, f32[32,8,128]{2,1,0:T(8,128)}) custom-call(s32[1]{0:T(128)} %bitcast.refs_0_, f32[176,512]{1,0:T(8,128)} %get-tuple-element.305.refs_1_, f32[176,512]{1,0:T(8,128)} %get-tuple-element.295.refs_1_.refs_7_.refs_2_, f32[32,8,128]{2,1,0:T(8,128)} %all_to_all.91.refs_2_.refs_8_.refs_3_, ...), custom_call_target="tpu_custom_call" | custom-call | flops 1024 | bytes 1024 | tf_op jit(solution)/shard_map/pallas_call | solution.py:1258
  345.2 8.1 %shard_map.482 = (bf16[2,8,576,128]{3,2,1,0:T(8,128)(2,1)}, bf16[2,8,576,128]{3,2,1,0:T(8,128)(2,1)}) custom-call(bf16[176,4608]{1,0:T(8,128)(2,1)} %get-tuple-element.320.rows_ref, bf16[176,512]{1,0:T(8,128)(2,1)} %get-tuple-element.321.cols_ref), custom_call_target="tpu_custom_call" | custom-call | flops 1024 | bytes 1024 | tf_op jit(solution)/shard_map/pallas_call | solution.py:785
  360.2 7.2 %shard_map.483 = (bf16[176,512]{1,0:T(8,128)(2,1)}, f32[176,2048]{1,0:T(8,128)}, f32[48,128]{1,0:T(8,128)}) custom-call(s32[1]{0:T(128)} %bitcast.refs_0_, f32[176,512]{1,0:T(8,128)} %get-tuple-element.313.refs_1_, f32[176,512]{1,0:T(8,128)} %get-tuple-element.288.refs_1_.refs_7_.refs_2_, f32[32,8,128]{2,1,0:T(8,128)} %all_to_all.90.refs_2_.refs_8_.refs_3_, ...), custom_call_target="tpu_custom_call" | custom-call | flops 1024 | bytes 1024 | tf_op jit(solution)/shard_map/pallas_call | solution.py:1258
  379.7 5.9 all-to-all-start.13
  390.2 6.3 %shard_map.484 = (bf16[2,8,1024,128]{3,2,1,0:T(8,128)(2,1)}, bf16[2,8,1024,128]{3,2,1,0:T(8,128)(2,1)}) custom-call(bf16[176,2048]{1,0:T(8,128)(2,1)} %get-tuple-element.299.refs_4_.rows_ref, bf16[176,512]{1,0:T(8,128)(2,1)} %get-tuple-element.336.cols_ref), custom_call_target="tpu_custom_call" | custom-call | flops 1024 | bytes 1024 | tf_op jit(solution)/shard_map/pallas_call | solution.py:785
  397.2 5.9 shard_map.485
  403.1 4.6 all-to-all-start.14
  407.8 6.3 %shard_map.486 = (bf16[2,8,1024,128]{3,2,1,0:T(8,128)(2,1)}, bf16[2,8,1024,128]{3,2,1,0:T(8,128)(2,1)}) custom-call(bf16[176,2048]{1,0:T(8,128)(2,1)} %get-tuple-element.354.rows_ref, bf16[176,512]{1,0:T(8,128)(2,1)} %get-tuple-element.355.cols_ref, ...), custom_call_target="tpu_custom_call", output_to_operand_aliasing={{0}: (2, {}), {1}: (3, {})} | custom-call | flops 1024 | bytes 1024 | tf_op jit(solution)/shard_map/pallas_call | solution.py:785
  414.1 6.7 %shard_map.487 = (bf16[2,8,1024,128]{3,2,1,0:T(8,128)(2,1)}, bf16[2,8,1024,128]{3,2,1,0:T(8,128)(2,1)}) custom-call(bf16[704,1024]{1,0:T(8,128)(2,1)} %get-tuple-element.275.refs_1_.rows_ref, bf16[176,2048]{1,0:T(8,128)(2,1)} %get-tuple-element.353.cols_ref.refs_0_, ...), custom_call_target="tpu_custom_call", output_to_operand_aliasing={{0}: (2, {}), {1}: (3, {})} | custom-call | flops 1024 | bytes 1024 | tf_op jit(solution)/shard_map/pallas_call | solution.py:785
  428.9 7.5 %shard_map.488 = (bf16[176,512]{1,0:T(8,128)(2,1)}, f32[704,512]{1,0:T(8,128)}, f32[32,8,128]{2,1,0:T(8,128)}) custom-call(s32[1]{0:T(128)} %bitcast.refs_0_, f32[176,512]{1,0:T(8,128)} %get-tuple-element.340.refs_1_, f32[176,512]{1,0:T(8,128)} %get-tuple-element.254.refs_1_.refs_8_.refs_2_, f32[32,8,128]{2,1,0:T(8,128)} %copy-done.10, ...), custom_call_target="tpu_custom_call" | custom-call | flops 1024 | bytes 1024 | tf_op jit(solution)/shard_map/pallas_call | solution.py:1258
  436.5 3.9 all-to-all-start.15
  440.4 8.1 %shard_map.489 = (bf16[2,8,576,128]{3,2,1,0:T(8,128)(2,1)}, bf16[2,8,576,128]{3,2,1,0:T(8,128)(2,1)}) custom-call(bf16[176,4608]{1,0:T(8,128)(2,1)} %get-tuple-element.377.rows_ref, bf16[176,512]{1,0:T(8,128)(2,1)} %get-tuple-element.378.cols_ref), custom_call_target="tpu_custom_call" | custom-call | flops 1024 | bytes 1024 | tf_op jit(solution)/shard_map/pallas_call | solution.py:785
  463.6 4.9 shard_map.490.refs_8_
  473.0 5.2 shard_map.491
  478.3 5.8 collective-permute-done.53
  484.0 3.6 collective-permute-start.72
  496.2 6.7 %shard_map.492 = (bf16[2,8,128,128]{3,2,1,0:T(8,128)(2,1)}, bf16[2,8,128,128]{3,2,1,0:T(8,128)(2,1)}) custom-call(bf16[704,1024]{1,0:T(8,128)(2,1)} %get-tuple-element.275.refs_1_.rows_ref, bf16[704,512]{1,0:T(8,128)(2,1)} %get-tuple-element.394.cols_ref), custom_call_target="tpu_custom_call" | custom-call | flops 1024 | bytes 1024 | tf_op jit(solution)/shard_map/pallas_call | solution.py:785
  514.4 3.5 all-to-all-start.16
  526.8 7.4 %collective-permute-done.56 = bf16[1,2,2,2,288,128]{5,4,3,2,1,0:T(8,128)(2,1)} collective-permute-done((bf16[1,2,2,2,288,128]{5,4,3,2,1,0:T(8,128)(2,1)}, bf16[1,2,2,2,288,128]{5,4,3,2,1,0:T(8,128)(2,1)}, u32[]{:S(2)}, u32[]{:S(2)}) %collective-permute-start.56) | collective-permute-done | bytes 589856 | tf_op jit(solution)/shard_map/ppermute | solution.py:480
  539.5 13.8 %collective-permute-done.66 = bf16[1,2,2,1,128,128]{5,4,3,2,1,0:T(8,128)(2,1)S(1)} collective-permute-done((bf16[1,2,2,1,128,128]{5,4,3,2,1,0:T(8,128)(2,1)S(1)}, bf16[1,2,2,1,128,128]{5,4,3,2,1,0:T(8,128)(2,1)S(1)}, u32[]{:S(2)}, u32[]{:S(2)}) %collective-permute-start.66) | collective-permute-done | bytes 131104 | tf_op jit(solution)/shard_map/ppermute | solution.py:484
  575.6 19.2 %collective-permute-done.75 = bf16[1,1,1,1,1024,128]{5,4,3,2,1,0:T(8,128)(2,1)S(1)} collective-permute-done((bf16[1,1,1,1,1024,128]{5,4,3,2,1,0:T(8,128)(2,1)S(1)}, bf16[1,1,1,1,1024,128]{5,4,3,2,1,0:T(8,128)(2,1)S(1)}, u32[]{:S(2)}, u32[]{:S(2)}) %collective-permute-start.75) | collective-permute-done | bytes 262176 | tf_op jit(solution)/shard_map/ppermute | solution.py:482
  597.1 3.5 shard_map.493
  602.8 3.8 shard_map.494
  606.7 3.8 all-to-all-start.17
  614.6 6.5 %all-to-all-done.17.refs_0_ = f32[32,16,128]{2,1,0:T(8,128)S(1)} async-done(((f32[32,16,128]{2,1,0:T(8,128)}), f32[32,16,128]{2,1,0:T(8,128)S(1)}, u32[]{:S(2)}, u32[]{:S(2)}) %all-to-all-start.17) | async-done | bytes 262176 | tf_op jit(solution)/shard_map/all_to_all | solution.py:1353
  (408 shorter events, 212.1 us)
Async XLA Ops:
  11.7 28.0 %all-to-all-start = ((bf16[4,704,256]{2,1,0:T(8,128)(2,1)}), bf16[4,704,256]{2,1,0:T(8,128)(2,1)S(1)}, u32[]{:S(2)}, u32[]{:S(2)}) async-start(bf16[4,704,256]{2,1,0:T(8,128)(2,1)} %bitcast.3), calls=%async_computation | async-start | bytes 2883584 | tf_op jit(solution)/shard_map/all_to_all | solution.py:1408
  20.3 18.0 %collective-permute-start.5 = (bf16[1,1,1,1,576,128]{5,4,3,2,1,0:T(8,128)(2,1)S(1)}, bf16[1,1,1,1,576,128]{5,4,3,2,1,0:T(8,128)(2,1)S(1)}, u32[]{:S(2)}, u32[]{:S(2)}) collective-permute-start(bf16[1,1,1,1,576,128]{5,4,3,2,1,0:T(8,128)(2,1)S(1)} %bitcast.131), channel_id=1, source_target_pairs={{0,24},{4,28},{8,16},{12,20},{16,8},{20,12},{24,0},{28,4},{1,25},{... | collective-permute-start | bytes 442376 | tf_op jit(solution)/shard_map/ppermute | solution.py:482
  21.2 17.1 %collective-permute-start.4 = (bf16[1,1,1,1,576,128]{5,4,3,2,1,0:T(8,128)(2,1)S(1)}, bf16[1,1,1,1,576,128]{5,4,3,2,1,0:T(8,128)(2,1)S(1)}, u32[]{:S(2)}, u32[]{:S(2)}) collective-permute-start(bf16[1,1,1,1,576,128]{5,4,3,2,1,0:T(8,128)(2,1)S(1)} %bitcast.132), channel_id=1, source_target_pairs={{0,8},{4,12},{8,0},{12,4},{16,24},{20,28},{24,16},{28,20},{1,9},{5... | collective-permute-start | bytes 442376 | tf_op jit(solution)/shard_map/ppermute | solution.py:482
  22.3 16.0 %collective-permute-start.3 = (bf16[1,1,1,1,576,128]{5,4,3,2,1,0:T(8,128)(2,1)S(1)}, bf16[1,1,1,1,576,128]{5,4,3,2,1,0:T(8,128)(2,1)S(1)}, u32[]{:S(2)}, u32[]{:S(2)}) collective-permute-start(bf16[1,1,1,1,576,128]{5,4,3,2,1,0:T(8,128)(2,1)S(1)} %bitcast.133), channel_id=1, source_target_pairs={{0,16},{4,20},{8,24},{12,28},{16,0},{20,4},{24,8},{28,12},{1,17},{... | collective-permute-start | bytes 442376 | tf_op jit(solution)/shard_map/ppermute | solution.py:482
  42.6 15.4 %collective-permute-start.9 = (bf16[1,2,2,1,288,128]{5,4,3,2,1,0:T(8,128)(2,1)}, bf16[1,2,2,1,288,128]{5,4,3,2,1,0:T(8,128)(2,1)S(1)}, u32[]{:S(2)}, u32[]{:S(2)}) collective-permute-start(bf16[1,2,2,1,288,128]{5,4,3,2,1,0:T(8,128)(2,1)} %get-tuple-element.236.refs_4_), channel_id=1, source_target_pairs={{0,4},{4,0},{8,12},{12,8},{16,20},{20,16},{24,28},{28,24},{1,5},{5... | collective-permute-start | bytes 884744 | tf_op jit(solution)/shard_map/ppermute | solution.py:482
  44.2 14.6 %collective-permute-start.10 = (bf16[1,2,2,1,288,128]{5,4,3,2,1,0:T(8,128)(2,1)}, bf16[1,2,2,1,288,128]{5,4,3,2,1,0:T(8,128)(2,1)}, u32[]{:S(2)}, u32[]{:S(2)}) collective-permute-start(bf16[1,2,2,1,288,128]{5,4,3,2,1,0:T(8,128)(2,1)} %get-tuple-element.237.refs_6_), channel_id=1, source_target_pairs={{0,2},{1,3},{2,0},{3,1},{4,6},{5,7},{6,4},{7,5},{8,10},{9,11},{10,... | collective-permute-start | bytes 884744 | tf_op jit(solution)/shard_map/ppermute | solution.py:480
  62.9 43.0 %collective-permute-start.12 = (bf16[1,2,2,2,288,128]{5,4,3,2,1,0:T(8,128)(2,1)}, bf16[1,2,2,2,288,128]{5,4,3,2,1,0:T(8,128)(2,1)}, u32[]{:S(2)}, u32[]{:S(2)}) collective-permute-start(bf16[1,2,2,2,288,128]{5,4,3,2,1,0:T(8,128)(2,1)} %get-tuple-element.245.refs_0_), channel_id=1, source_target_pairs={{0,2},{1,3},{2,0},{3,1},{4,6},{5,7},{6,4},{7,5},{8,10},{9,11},{10,... | collective-permute-start | bytes 1769480 | tf_op jit(solution)/shard_map/ppermute | solution.py:480
  64.6 41.3 %collective-permute-start.13 = (bf16[2,2,2,1,288,128]{5,4,3,2,1,0:T(8,128)(2,1)}, bf16[2,2,2,1,288,128]{5,4,3,2,1,0:T(8,128)(2,1)}, u32[]{:S(2)}, u32[]{:S(2)}) collective-permute-start(bf16[2,2,2,1,288,128]{5,4,3,2,1,0:T(8,128)(2,1)} %get-tuple-element.247.refs_2_), channel_id=1, source_target_pairs={{0,4},{4,0},{8,12},{12,8},{16,20},{20,16},{24,28},{28,24},{1,5},{5... | collective-permute-start | bytes 1769480 | tf_op jit(solution)/shard_map/ppermute | solution.py:482
  71.0 34.9 %all-to-all-start.2 = ((f32[32,16,128]{2,1,0:T(8,128)}), f32[32,16,128]{2,1,0:T(8,128)S(1)}, u32[]{:S(2)}, u32[]{:S(2)}) async-start(f32[32,16,128]{2,1,0:T(8,128)} %get-tuple-element.240), calls=%async_computation.2 | async-start | bytes 524288 | tf_op jit(solution)/shard_map/all_to_all | solution.py:1353
  74.1 15.0 %collective-permute-start.16 = (bf16[1,1,1,1,1024,128]{5,4,3,2,1,0:T(8,128)(2,1)S(1)}, bf16[1,1,1,1,1024,128]{5,4,3,2,1,0:T(8,128)(2,1)S(1)}, u32[]{:S(2)}, u32[]{:S(2)}) collective-permute-start(bf16[1,1,1,1,1024,128]{5,4,3,2,1,0:T(8,128)(2,1)S(1)} %maximum_bitcast_fusion.3.refs_4_.refs_8_), channel_id=1, source_target_pairs={{0,24},{4,28},{8,16},{12,20},{16,8},{20,12},{24,0},{28,4},{1,25},{... | collective-permute-start | bytes 786440 | tf_op jit(solution)/shard_map/ppermute | solution.py:482
  77.8 15.3 %collective-permute-start.15 = (bf16[1,1,1,1,1024,128]{5,4,3,2,1,0:T(8,128)(2,1)S(1)}, bf16[1,1,1,1,1024,128]{5,4,3,2,1,0:T(8,128)(2,1)S(1)}, u32[]{:S(2)}, u32[]{:S(2)}) collective-permute-start(bf16[1,1,1,1,1024,128]{5,4,3,2,1,0:T(8,128)(2,1)S(1)} %maximum_bitcast_fusion.3.refs_4_.refs_8_), channel_id=1, source_target_pairs={{0,8},{4,12},{8,0},{12,4},{16,24},{20,28},{24,16},{28,20},{1,9},{5... | collective-permute-start | bytes 786440 | tf_op jit(solution)/shard_map/ppermute | solution.py:482
  77.8 28.1 %collective-permute-start.14 = (bf16[1,1,1,1,1024,128]{5,4,3,2,1,0:T(8,128)(2,1)S(1)}, bf16[1,1,1,1,1024,128]{5,4,3,2,1,0:T(8,128)(2,1)S(1)}, u32[]{:S(2)}, u32[]{:S(2)}) collective-permute-start(bf16[1,1,1,1,1024,128]{5,4,3,2,1,0:T(8,128)(2,1)S(1)} %maximum_bitcast_fusion.3.refs_4_.refs_8_), channel_id=1, source_target_pairs={{0,16},{4,20},{8,24},{12,28},{16,0},{20,4},{24,8},{28,12},{1,17},{... | collective-permute-start | bytes 786440 | tf_op jit(solution)/shard_map/ppermute | solution.py:482
  112.0 14.5 %collective-permute-start.18 = (bf16[1,2,2,1,512,128]{5,4,3,2,1,0:T(8,128)(2,1)}, bf16[1,2,2,1,512,128]{5,4,3,2,1,0:T(8,128)(2,1)S(1)}, u32[]{:S(2)}, u32[]{:S(2)}) collective-permute-start(bf16[1,2,2,1,512,128]{5,4,3,2,1,0:T(8,128)(2,1)} %get-tuple-element.258.refs_0_), channel_id=1, source_target_pairs={{0,4},{4,0},{8,12},{12,8},{16,20},{20,16},{24,28},{28,24},{1,5},{5... | collective-permute-start | bytes 1572872 | tf_op jit(solution)/shard_map/ppermute | solution.py:482
  132.1 29.6 %collective-permute-start.20 = (bf16[1,2,2,2,512,128]{5,4,3,2,1,0:T(8,128)(2,1)}, bf16[1,2,2,2,512,128]{5,4,3,2,1,0:T(8,128)(2,1)S(1)}, u32[]{:S(2)}, u32[]{:S(2)}) collective-permute-start(bf16[1,2,2,2,512,128]{5,4,3,2,1,0:T(8,128)(2,1)} %get-tuple-element.265.refs_0_), channel_id=1, source_target_pairs={{0,2},{1,3},{2,0},{3,1},{4,6},{5,7},{6,4},{7,5},{8,10},{9,11},{10,... | collective-permute-start | bytes 3145736 | tf_op jit(solution)/shard_map/ppermute | solution.py:480
  133.6 28.8 %collective-permute-start.21 = (bf16[2,2,2,1,512,128]{5,4,3,2,1,0:T(8,128)(2,1)}, bf16[2,2,2,1,512,128]{5,4,3,2,1,0:T(8,128)(2,1)}, u32[]{:S(2)}, u32[]{:S(2)}) collective-permute-start(bf16[2,2,2,1,512,128]{5,4,3,2,1,0:T(8,128)(2,1)} %get-tuple-element.267.refs_2_), channel_id=1, source_target_pairs={{0,4},{4,0},{8,12},{12,8},{16,20},{20,16},{24,28},{28,24},{1,5},{5... | collective-permute-start | bytes 3145736 | tf_op jit(solution)/shard_map/ppermute | solution.py:482
  134.2 25.3 %all-to-all-start.3 = ((f32[32,8,128]{2,1,0:T(8,128)}), f32[32,8,128]{2,1,0:T(8,128)S(1)}, u32[]{:S(2)}, u32[]{:S(2)}) async-start(f32[32,8,128]{2,1,0:T(8,128)} %get-tuple-element.255), calls=%async_computation.3 | async-start | bytes 262144 | tf_op jit(solution)/shard_map/all_to_all | solution.py:1353
  137.0 22.5 %collective-permute-start.24 = (bf16[1,1,1,1,832,128]{5,4,3,2,1,0:T(8,128)(2,1)S(1)}, bf16[1,1,1,1,832,128]{5,4,3,2,1,0:T(8,128)(2,1)S(1)}, u32[]{:S(2)}, u32[]{:S(2)}) collective-permute-start(bf16[1,1,1,1,832,128]{5,4,3,2,1,0:T(8,128)(2,1)S(1)} %maximum_bitcast_fusion.4.refs_4_.refs_8_), channel_id=1, source_target_pairs={{0,24},{4,28},{8,16},{12,20},{16,8},{20,12},{24,0},{28,4},{1,25},{... | collective-permute-start | bytes 638984 | tf_op jit(solution)/shard_map/ppermute | solution.py:482
  140.6 18.8 %collective-permute-start.23 = (bf16[1,1,1,1,832,128]{5,4,3,2,1,0:T(8,128)(2,1)S(1)}, bf16[1,1,1,1,832,128]{5,4,3,2,1,0:T(8,128)(2,1)S(1)}, u32[]{:S(2)}, u32[]{:S(2)}) collective-permute-start(bf16[1,1,1,1,832,128]{5,4,3,2,1,0:T(8,128)(2,1)S(1)} %maximum_bitcast_fusion.4.refs_4_.refs_8_), channel_id=1, source_target_pairs={{0,8},{4,12},{8,0},{12,4},{16,24},{20,28},{24,16},{28,20},{1,9},{5... | collective-permute-start | bytes 638984 | tf_op jit(solution)/shard_map/ppermute | solution.py:482
  140.6 21.1 %collective-permute-start.22 = (bf16[1,1,1,1,832,128]{5,4,3,2,1,0:T(8,128)(2,1)S(1)}, bf16[1,1,1,1,832,128]{5,4,3,2,1,0:T(8,128)(2,1)S(1)}, u32[]{:S(2)}, u32[]{:S(2)}) collective-permute-start(bf16[1,1,1,1,832,128]{5,4,3,2,1,0:T(8,128)(2,1)S(1)} %maximum_bitcast_fusion.4.refs_4_.refs_8_), channel_id=1, source_target_pairs={{0,16},{4,20},{8,24},{12,28},{16,0},{20,4},{24,8},{28,12},{1,17},{... | collective-permute-start | bytes 638984 | tf_op jit(solution)/shard_map/ppermute | solution.py:482
  168.9 22.7 %collective-permute-start.28 = (bf16[1,2,2,1,416,128]{5,4,3,2,1,0:T(8,128)(2,1)}, bf16[1,2,2,1,416,128]{5,4,3,2,1,0:T(8,128)(2,1)S(1)}, u32[]{:S(2)}, u32[]{:S(2)}) collective-permute-start(bf16[1,2,2,1,416,128]{5,4,3,2,1,0:T(8,128)(2,1)} %get-tuple-element.281.refs_0_), channel_id=1, source_target_pairs={{0,4},{4,0},{8,12},{12,8},{16,20},{20,16},{24,28},{28,24},{1,5},{5... | collective-permute-start | bytes 1277960 | tf_op jit(solution)/shard_map/ppermute | solution.py:482
  170.4 21.1 %collective-permute-start.29 = (bf16[1,2,2,1,416,128]{5,4,3,2,1,0:T(8,128)(2,1)}, bf16[1,2,2,1,416,128]{5,4,3,2,1,0:T(8,128)(2,1)S(1)}, u32[]{:S(2)}, u32[]{:S(2)}) collective-permute-start(bf16[1,2,2,1,416,128]{5,4,3,2,1,0:T(8,128)(2,1)} %get-tuple-element.283.refs_2_), channel_id=1, source_target_pairs={{0,2},{1,3},{2,0},{3,1},{4,6},{5,7},{6,4},{7,5},{8,10},{9,11},{10,... | collective-permute-start | bytes 1277960 | tf_op jit(solution)/shard_map/ppermute | solution.py:480
  196.5 29.4 %collective-permute-start.30 = (bf16[1,2,2,2,416,128]{5,4,3,2,1,0:T(8,128)(2,1)}, bf16[1,2,2,2,416,128]{5,4,3,2,1,0:T(8,128)(2,1)S(1)}, u32[]{:S(2)}, u32[]{:S(2)}) collective-permute-start(bf16[1,2,2,2,416,128]{5,4,3,2,1,0:T(8,128)(2,1)} %get-tuple-element.290.refs_0_), channel_id=1, source_target_pairs={{0,2},{1,3},{2,0},{3,1},{4,6},{5,7},{6,4},{7,5},{8,10},{9,11},{10,... | collective-permute-start | bytes 2555912 | tf_op jit(solution)/shard_map/ppermute | solution.py:480
  198.0 27.9 %collective-permute-start.31 = (bf16[2,2,2,1,416,128]{5,4,3,2,1,0:T(8,128)(2,1)}, bf16[2,2,2,1,416,128]{5,4,3,2,1,0:T(8,128)(2,1)S(1)}, u32[]{:S(2)}, u32[]{:S(2)}) collective-permute-start(bf16[2,2,2,1,416,128]{5,4,3,2,1,0:T(8,128)(2,1)} %get-tuple-element.292.refs_2_), channel_id=1, source_target_pairs={{0,4},{4,0},{8,12},{12,8},{16,20},{20,16},{24,28},{28,24},{1,5},{5... | collective-permute-start | bytes 2555912 | tf_op jit(solution)/shard_map/ppermute | solution.py:482
  201.0 19.6 %all-to-all-start.4 = ((f32[8,64,128]{2,1,0:T(8,128)}), f32[8,64,128]{2,1,0:T(8,128)S(1)}, u32[]{:S(2)}, u32[]{:S(2)}) async-start(f32[8,64,128]{2,1,0:T(8,128)} %broadcast_in_dim.14), calls=%async_computation.4 | async-start | bytes 524288 | tf_op jit(solution)/shard_map/all_to_all | solution.py:515
  259.3 14.8 %all-to-all-start.8 = ((bf16[4,176,512]{2,1,0:T(8,128)(2,1)}), bf16[4,176,512]{2,1,0:T(8,128)(2,1)S(1)}, u32[]{:S(2)}, u32[]{:S(2)}) async-start(bf16[4,176,512]{2,1,0:T(8,128)(2,1)} %bitcast.33), calls=%async_computation.8 | async-start | bytes 1441792 | tf_op jit(solution)/shard_map/all_to_all | solution.py:1446
  321.5 14.4 %all-to-all-start.10 = ((bf16[4,176,512]{2,1,0:T(8,128)(2,1)}), bf16[4,176,512]{2,1,0:T(8,128)(2,1)S(1)}, u32[]{:S(2)}, u32[]{:S(2)}) async-start(bf16[4,176,512]{2,1,0:T(8,128)(2,1)} %get-tuple-element.302), calls=%async_computation.10 | async-start | bytes 1441792 | tf_op jit(solution)/shard_map/all_to_all | solution.py:1530
  335.9 17.4 %collective-permute-start.37 = (bf16[2,2,2,2,256,128]{5,4,3,2,1,0:T(8,128)(2,1)}, bf16[2,2,2,2,256,128]{5,4,3,2,1,0:T(8,128)(2,1)}, u32[]{:S(2)}, u32[]{:S(2)}) collective-permute-start(bf16[2,2,2,2,256,128]{5,4,3,2,1,0:T(8,128)(2,1)} %bitcast.155), channel_id=1, source_target_pairs={{0,1},{1,0},{2,3},{3,2},{4,5},{5,4},{6,7},{7,6},{8,9},{9,8},{10,11... | collective-permute-start | bytes 3145736 | tf_op jit(solution)/shard_map/ppermute | solution.py:480
  342.2 14.6 %all-to-all-start.12 = ((f32[32,8,128]{2,1,0:T(8,128)}), f32[32,8,128]{2,1,0:T(8,128)S(1)}, u32[]{:S(2)}, u32[]{:S(2)}) async-start(f32[32,8,128]{2,1,0:T(8,128)} %get-tuple-element.314), calls=%async_computation.12 | async-start | bytes 262144 | tf_op jit(solution)/shard_map/all_to_all | solution.py:1353
  356.8 16.7 %collective-permute-start.42 = (bf16[2,2,2,2,576,128]{5,4,3,2,1,0:T(8,128)(2,1)}, bf16[2,2,2,2,576,128]{5,4,3,2,1,0:T(8,128)(2,1)}, u32[]{:S(2)}, u32[]{:S(2)}) collective-permute-start(bf16[2,2,2,2,576,128]{5,4,3,2,1,0:T(8,128)(2,1)} %bitcast.154), channel_id=1, source_target_pairs={{0,1},{1,0},{2,3},{3,2},{4,5},{5,4},{6,7},{7,6},{8,9},{9,8},{10,11... | collective-permute-start | bytes 7077896 | tf_op jit(solution)/shard_map/ppermute | solution.py:480
  357.1 16.5 %collective-permute-start.40 = (bf16[1,2,2,2,128,128]{5,4,3,2,1,0:T(8,128)(2,1)}, bf16[1,2,2,2,128,128]{5,4,3,2,1,0:T(8,128)(2,1)S(1)}, u32[]{:S(2)}, u32[]{:S(2)}) collective-permute-start(bf16[1,2,2,2,128,128]{5,4,3,2,1,0:T(8,128)(2,1)} %add_convert_fusion.13), channel_id=1, source_target_pairs={{0,2},{1,3},{2,0},{3,1},{4,6},{5,7},{6,4},{7,5},{8,10},{9,11},{10,... | collective-permute-start | bytes 786440 | tf_op jit(solution)/shard_map/ppermute | solution.py:480
  358.7 14.8 %collective-permute-start.41 = (bf16[2,2,2,1,128,128]{5,4,3,2,1,0:T(8,128)(2,1)}, bf16[2,2,2,1,128,128]{5,4,3,2,1,0:T(8,128)(2,1)S(1)}, u32[]{:S(2)}, u32[]{:S(2)}) collective-permute-start(bf16[2,2,2,1,128,128]{5,4,3,2,1,0:T(8,128)(2,1)} %add_convert_fusion.12), channel_id=1, source_target_pairs={{0,4},{4,0},{8,12},{12,8},{16,20},{20,16},{24,28},{28,24},{1,5},{5... | collective-permute-start | bytes 786440 | tf_op jit(solution)/shard_map/ppermute | solution.py:482
  378.2 42.6 %collective-permute-start.45 = (bf16[1,2,2,2,288,128]{5,4,3,2,1,0:T(8,128)(2,1)}, bf16[1,2,2,2,288,128]{5,4,3,2,1,0:T(8,128)(2,1)}, u32[]{:S(2)}, u32[]{:S(2)}) collective-permute-start(bf16[1,2,2,2,288,128]{5,4,3,2,1,0:T(8,128)(2,1)} %add_convert_fusion.5), channel_id=1, source_target_pairs={{0,2},{1,3},{2,0},{3,1},{4,6},{5,7},{6,4},{7,5},{8,10},{9,11},{10,... | collective-permute-start | bytes 1769480 | tf_op jit(solution)/shard_map/ppermute | solution.py:480
  378.7 42.1 %collective-permute-start.46 = (bf16[2,2,2,1,288,128]{5,4,3,2,1,0:T(8,128)(2,1)}, bf16[2,2,2,1,288,128]{5,4,3,2,1,0:T(8,128)(2,1)}, u32[]{:S(2)}, u32[]{:S(2)}) collective-permute-start(bf16[2,2,2,1,288,128]{5,4,3,2,1,0:T(8,128)(2,1)} %add_convert_fusion.4), channel_id=1, source_target_pairs={{0,4},{4,0},{8,12},{12,8},{16,20},{20,16},{24,28},{28,24},{1,5},{5... | collective-permute-start | bytes 1769480 | tf_op jit(solution)/shard_map/ppermute | solution.py:482
  379.7 16.8 %all-to-all-start.13 = ((f32[8,48,128]{2,1,0:T(8,128)}), f32[8,48,128]{2,1,0:T(8,128)S(1)}, u32[]{:S(2)}, u32[]{:S(2)}) async-start(f32[8,48,128]{2,1,0:T(8,128)} %broadcast_in_dim.17), calls=%async_computation.13 | async-start | bytes 393216 | tf_op jit(solution)/shard_map/all_to_all | solution.py:515
  386.7 34.0 %collective-permute-start.44 = (bf16[1,2,2,1,128,128]{5,4,3,2,1,0:T(8,128)(2,1)S(1)}, bf16[1,2,2,1,128,128]{5,4,3,2,1,0:T(8,128)(2,1)S(1)}, u32[]{:S(2)}, u32[]{:S(2)}) collective-permute-start(bf16[1,2,2,1,128,128]{5,4,3,2,1,0:T(8,128)(2,1)S(1)} %get-tuple-element.597), channel_id=1, source_target_pairs={{0,2},{1,3},{2,0},{3,1},{4,6},{5,7},{6,4},{7,5},{8,10},{9,11},{10,... | collective-permute-start | bytes 393224 | tf_op jit(solution)/shard_map/ppermute | solution.py:480
  388.2 32.5 %collective-permute-start.43 = (bf16[1,2,2,1,128,128]{5,4,3,2,1,0:T(8,128)(2,1)S(1)}, bf16[1,2,2,1,128,128]{5,4,3,2,1,0:T(8,128)(2,1)S(1)}, u32[]{:S(2)}, u32[]{:S(2)}) collective-permute-start(bf16[1,2,2,1,128,128]{5,4,3,2,1,0:T(8,128)(2,1)S(1)} %get-tuple-element.598), channel_id=1, source_target_pairs={{0,4},{4,0},{8,12},{12,8},{16,20},{20,16},{24,28},{28,24},{1,5},{5... | collective-permute-start | bytes 393224 | tf_op jit(solution)/shard_map/ppermute | solution.py:482
  403.1 22.3 %all-to-all-start.14 = ((f32[32,8,128]{2,1,0:T(8,128)}), f32[32,8,128]{2,1,0:T(8,128)S(1)}, u32[]{:S(2)}, u32[]{:S(2)}) async-start(f32[32,8,128]{2,1,0:T(8,128)} %get-tuple-element.341), calls=%async_computation.14 | async-start | bytes 262144 | tf_op jit(solution)/shard_map/all_to_all | solution.py:1353
  425.5 26.9 %collective-permute-start.49 = (bf16[2,2,2,2,1024,128]{5,4,3,2,1,0:T(8,128)(2,1)}, bf16[2,2,2,2,1024,128]{5,4,3,2,1,0:T(8,128)(2,1)}, u32[]{:S(2)}, u32[]{:S(2)}) collective-permute-start(bf16[2,2,2,2,1024,128]{5,4,3,2,1,0:T(8,128)(2,1)} %bitcast.102), channel_id=1, source_target_pairs={{0,1},{1,0},{2,3},{3,2},{4,5},{5,4},{6,7},{7,6},{8,9},{9,8},{10,11... | collective-permute-start | bytes 12582920 | tf_op jit(solution)/shard_map/ppermute | solution.py:480
  425.8 22.7 %collective-permute-start.48 = (bf16[1,2,2,1,288,128]{5,4,3,2,1,0:T(8,128)(2,1)S(1)}, bf16[1,2,2,1,288,128]{5,4,3,2,1,0:T(8,128)(2,1)S(1)}, u32[]{:S(2)}, u32[]{:S(2)}) collective-permute-start(bf16[1,2,2,1,288,128]{5,4,3,2,1,0:T(8,128)(2,1)S(1)} %get-tuple-element.584), channel_id=1, source_target_pairs={{0,2},{1,3},{2,0},{3,1},{4,6},{5,7},{6,4},{7,5},{8,10},{9,11},{10,... | collective-permute-start | bytes 884744 | tf_op jit(solution)/shard_map/ppermute | solution.py:480
  427.5 21.0 %collective-permute-start.47 = (bf16[1,2,2,1,288,128]{5,4,3,2,1,0:T(8,128)(2,1)S(1)}, bf16[1,2,2,1,288,128]{5,4,3,2,1,0:T(8,128)(2,1)S(1)}, u32[]{:S(2)}, u32[]{:S(2)}) collective-permute-start(bf16[1,2,2,1,288,128]{5,4,3,2,1,0:T(8,128)(2,1)S(1)} %get-tuple-element.585), channel_id=1, source_target_pairs={{0,4},{4,0},{8,12},{12,8},{16,20},{20,16},{24,28},{28,24},{1,5},{5... | collective-permute-start | bytes 884744 | tf_op jit(solution)/shard_map/ppermute | solution.py:482
  436.5 15.9 %all-to-all-start.15 = ((f32[32,8,128]{2,1,0:T(8,128)}), f32[32,8,128]{2,1,0:T(8,128)S(1)}, u32[]{:S(2)}, u32[]{:S(2)}) async-start(f32[32,8,128]{2,1,0:T(8,128)} %get-tuple-element.364), calls=%async_computation.15 | async-start | bytes 262144 | tf_op jit(solution)/shard_map/all_to_all | solution.py:1353
  458.1 29.9 %collective-permute-start.55 = (bf16[2,2,2,2,576,128]{5,4,3,2,1,0:T(8,128)(2,1)}, bf16[2,2,2,2,576,128]{5,4,3,2,1,0:T(8,128)(2,1)}, u32[]{:S(2)}, u32[]{:S(2)}) collective-permute-start(bf16[2,2,2,2,576,128]{5,4,3,2,1,0:T(8,128)(2,1)} %bitcast.43), channel_id=1, source_target_pairs={{0,1},{1,0},{2,3},{3,2},{4,5},{5,4},{6,7},{7,6},{8,9},{9,8},{10,11... | collective-permute-start | bytes 7077896 | tf_op jit(solution)/shard_map/ppermute | solution.py:480
  458.5 25.6 %collective-permute-start.53 = (bf16[1,2,2,2,512,128]{5,4,3,2,1,0:T(8,128)(2,1)}, bf16[1,2,2,2,512,128]{5,4,3,2,1,0:T(8,128)(2,1)S(1)}, u32[]{:S(2)}, u32[]{:S(2)}) collective-permute-start(bf16[1,2,2,2,512,128]{5,4,3,2,1,0:T(8,128)(2,1)} %add_convert_fusion.1), channel_id=1, source_target_pairs={{0,2},{1,3},{2,0},{3,1},{4,6},{5,7},{6,4},{7,5},{8,10},{9,11},{10,... | collective-permute-start | bytes 3145736 | tf_op jit(solution)/shard_map/ppermute | solution.py:480
  460.2 27.5 %collective-permute-start.54 = (bf16[2,2,2,1,512,128]{5,4,3,2,1,0:T(8,128)(2,1)}, bf16[2,2,2,1,512,128]{5,4,3,2,1,0:T(8,128)(2,1)}, u32[]{:S(2)}, u32[]{:S(2)}) collective-permute-start(bf16[2,2,2,1,512,128]{5,4,3,2,1,0:T(8,128)(2,1)} %add_convert_fusion), channel_id=1, source_target_pairs={{0,4},{4,0},{8,12},{12,8},{16,20},{20,16},{24,28},{28,24},{1,5},{5... | collective-permute-start | bytes 3145736 | tf_op jit(solution)/shard_map/ppermute | solution.py:482
  469.1 33.8 %collective-permute-start.70 = (bf16[1,1,1,1,256,128]{5,4,3,2,1,0:T(8,128)(2,1)}, bf16[1,1,1,1,256,128]{5,4,3,2,1,0:T(8,128)(2,1)}, u32[]{:S(2)}, u32[]{:S(2)}) collective-permute-start(bf16[1,1,1,1,256,128]{5,4,3,2,1,0:T(8,128)(2,1)} %pad_maximum_fusion.9), channel_id=1, source_target_pairs={{0,16},{4,20},{8,24},{12,28},{16,0},{20,4},{24,8},{28,12},{1,17},{... | collective-permute-start | bytes 196616 | tf_op jit(solution)/shard_map/ppermute | solution.py:482
  471.5 33.9 %collective-permute-start.71 = (bf16[1,1,1,1,256,128]{5,4,3,2,1,0:T(8,128)(2,1)}, bf16[1,1,1,1,256,128]{5,4,3,2,1,0:T(8,128)(2,1)}, u32[]{:S(2)}, u32[]{:S(2)}) collective-permute-start(bf16[1,1,1,1,256,128]{5,4,3,2,1,0:T(8,128)(2,1)} %pad_maximum_fusion.10), channel_id=1, source_target_pairs={{0,8},{4,12},{8,0},{12,4},{16,24},{20,28},{24,16},{28,20},{1,9},{5... | collective-permute-start | bytes 196616 | tf_op jit(solution)/shard_map/ppermute | solution.py:482
  484.0 21.4 %collective-permute-start.72 = (bf16[1,1,1,1,256,128]{5,4,3,2,1,0:T(8,128)(2,1)}, bf16[1,1,1,1,256,128]{5,4,3,2,1,0:T(8,128)(2,1)}, u32[]{:S(2)}, u32[]{:S(2)}) collective-permute-start(bf16[1,1,1,1,256,128]{5,4,3,2,1,0:T(8,128)(2,1)} %pad_maximum_fusion.11), channel_id=1, source_target_pairs={{0,24},{4,28},{8,16},{12,20},{16,8},{20,12},{24,0},{28,4},{1,25},{... | collective-permute-start | bytes 196616 | tf_op jit(solution)/shard_map/ppermute | solution.py:482
  487.6 20.4 %collective-permute-start.50 = (bf16[1,1,1,1,576,128]{5,4,3,2,1,0:T(8,128)(2,1)}, bf16[1,1,1,1,576,128]{5,4,3,2,1,0:T(8,128)(2,1)S(1)}, u32[]{:S(2)}, u32[]{:S(2)}) collective-permute-start(bf16[1,1,1,1,576,128]{5,4,3,2,1,0:T(8,128)(2,1)} %pad_maximum_fusion.3), channel_id=1, source_target_pairs={{0,16},{4,20},{8,24},{12,28},{16,0},{20,4},{24,8},{28,12},{1,17},{... | collective-permute-start | bytes 442376 | tf_op jit(solution)/shard_map/ppermute | solution.py:482
  488.0 22.2 %collective-permute-start.51 = (bf16[1,1,1,1,576,128]{5,4,3,2,1,0:T(8,128)(2,1)}, bf16[1,1,1,1,576,128]{5,4,3,2,1,0:T(8,128)(2,1)S(1)}, u32[]{:S(2)}, u32[]{:S(2)}) collective-permute-start(bf16[1,1,1,1,576,128]{5,4,3,2,1,0:T(8,128)(2,1)} %pad_maximum_fusion.4), channel_id=1, source_target_pairs={{0,8},{4,12},{8,0},{12,4},{16,24},{20,28},{24,16},{28,20},{1,9},{5... | collective-permute-start | bytes 442376 | tf_op jit(solution)/shard_map/ppermute | solution.py:482
  506.5 15.1 %collective-permute-start.74 = (bf16[1,2,2,1,512,128]{5,4,3,2,1,0:T(8,128)(2,1)}, bf16[1,2,2,1,512,128]{5,4,3,2,1,0:T(8,128)(2,1)}, u32[]{:S(2)}, u32[]{:S(2)}) collective-permute-start(bf16[1,2,2,1,512,128]{5,4,3,2,1,0:T(8,128)(2,1)} %get-tuple-element.558), channel_id=1, source_target_pairs={{0,2},{1,3},{2,0},{3,1},{4,6},{5,7},{6,4},{7,5},{8,10},{9,11},{10,... | collective-permute-start | bytes 1572872 | tf_op jit(solution)/shard_map/ppermute | solution.py:480
  508.0 15.1 %collective-permute-start.73 = (bf16[1,2,2,1,512,128]{5,4,3,2,1,0:T(8,128)(2,1)}, bf16[1,2,2,1,512,128]{5,4,3,2,1,0:T(8,128)(2,1)}, u32[]{:S(2)}, u32[]{:S(2)}) collective-permute-start(bf16[1,2,2,1,512,128]{5,4,3,2,1,0:T(8,128)(2,1)} %get-tuple-element.559), channel_id=1, source_target_pairs={{0,4},{4,0},{8,12},{12,8},{16,20},{20,16},{24,28},{28,24},{1,5},{5... | collective-permute-start | bytes 1572872 | tf_op jit(solution)/shard_map/ppermute | solution.py:482
  511.5 22.7 %collective-permute-start.56 = (bf16[1,2,2,2,288,128]{5,4,3,2,1,0:T(8,128)(2,1)}, bf16[1,2,2,2,288,128]{5,4,3,2,1,0:T(8,128)(2,1)}, u32[]{:S(2)}, u32[]{:S(2)}) collective-permute-start(bf16[1,2,2,2,288,128]{5,4,3,2,1,0:T(8,128)(2,1)} %add_convert_fusion.3), channel_id=1, source_target_pairs={{0,2},{1,3},{2,0},{3,1},{4,6},{5,7},{6,4},{7,5},{8,10},{9,11},{10,... | collective-permute-start | bytes 1769480 | tf_op jit(solution)/shard_map/ppermute | solution.py:480
  512.2 23.6 %collective-permute-start.58 = (bf16[2,2,2,1,288,128]{5,4,3,2,1,0:T(8,128)(2,1)S(1)}, bf16[2,2,2,1,288,128]{5,4,3,2,1,0:T(8,128)(2,1)}, u32[]{:S(2)}, u32[]{:S(2)}) collective-permute-start(bf16[2,2,2,1,288,128]{5,4,3,2,1,0:T(8,128)(2,1)S(1)} %add_convert_fusion.2), channel_id=1, source_target_pairs={{0,4},{4,0},{8,12},{12,8},{16,20},{20,16},{24,28},{28,24},{1,5},{5... | collective-permute-start | bytes 1769480 | tf_op jit(solution)/shard_map/ppermute | solution.py:482
  514.4 92.3 %all-to-all-start.16 = ((bf16[4,704,256]{2,1,0:T(8,128)(2,1)}), bf16[4,704,256]{2,1,0:T(8,128)(2,1)S(1)}, u32[]{:S(2)}, u32[]{:S(2)}) async-start(bf16[4,704,256]{2,1,0:T(8,128)(2,1)} %get-tuple-element.384), calls=%async_computation.16 | async-start | bytes 2883584 | tf_op jit(solution)/shard_map/all_to_all | solution.py:1625
  519.3 34.0 %collective-permute-start.66 = (bf16[1,2,2,1,128,128]{5,4,3,2,1,0:T(8,128)(2,1)S(1)}, bf16[1,2,2,1,128,128]{5,4,3,2,1,0:T(8,128)(2,1)S(1)}, u32[]{:S(2)}, u32[]{:S(2)}) collective-permute-start(bf16[1,2,2,1,128,128]{5,4,3,2,1,0:T(8,128)(2,1)S(1)} %get-tuple-element.602), channel_id=1, source_target_pairs={{0,6},{1,7},{2,4},{3,5},{4,2},{5,3},{6,0},{7,1},{8,14},{9,15},{10,... | collective-permute-start | bytes 393224 | tf_op jit(solution)/shard_map/ppermute | solution.py:484
  521.6 31.7 %collective-permute-start.65 = (bf16[1,2,2,1,128,128]{5,4,3,2,1,0:T(8,128)(2,1)S(1)}, bf16[1,2,2,1,128,128]{5,4,3,2,1,0:T(8,128)(2,1)S(1)}, u32[]{:S(2)}, u32[]{:S(2)}) collective-permute-start(bf16[1,2,2,1,128,128]{5,4,3,2,1,0:T(8,128)(2,1)S(1)} %get-tuple-element.603), channel_id=1, source_target_pairs={{0,4},{4,0},{8,12},{12,8},{16,20},{20,16},{24,28},{28,24},{1,5},{5... | collective-permute-start | bytes 393224 | tf_op jit(solution)/shard_map/ppermute | solution.py:482
  523.1 32.1 %collective-permute-start.64 = (bf16[1,2,2,1,128,128]{5,4,3,2,1,0:T(8,128)(2,1)S(1)}, bf16[1,2,2,1,128,128]{5,4,3,2,1,0:T(8,128)(2,1)S(1)}, u32[]{:S(2)}, u32[]{:S(2)}) collective-permute-start(bf16[1,2,2,1,128,128]{5,4,3,2,1,0:T(8,128)(2,1)S(1)} %get-tuple-element.604), channel_id=1, source_target_pairs={{0,2},{1,3},{2,0},{3,1},{4,6},{5,7},{6,4},{7,5},{8,10},{9,11},{10,... | collective-permute-start | bytes 393224 | tf_op jit(solution)/shard_map/ppermute | solution.py:480
  537.4 28.5 %collective-permute-start.57 = (bf16[1,2,2,1,288,128]{5,4,3,2,1,0:T(8,128)(2,1)S(1)}, bf16[1,2,2,1,288,128]{5,4,3,2,1,0:T(8,128)(2,1)S(1)}, u32[]{:S(2)}, u32[]{:S(2)}) collective-permute-start(bf16[1,2,2,1,288,128]{5,4,3,2,1,0:T(8,128)(2,1)S(1)} %get-tuple-element.579), channel_id=1, source_target_pairs={{0,4},{4,0},{8,12},{12,8},{16,20},{20,16},{24,28},{28,24},{1,5},{5... | collective-permute-start | bytes 884744 | tf_op jit(solution)/shard_map/ppermute | solution.py:482
  538.9 27.0 %collective-permute-start.59 = (bf16[1,2,2,1,288,128]{5,4,3,2,1,0:T(8,128)(2,1)S(1)}, bf16[1,2,2,1,288,128]{5,4,3,2,1,0:T(8,128)(2,1)S(1)}, u32[]{:S(2)}, u32[]{:S(2)}) collective-permute-start(bf16[1,2,2,1,288,128]{5,4,3,2,1,0:T(8,128)(2,1)S(1)} %get-tuple-element.580), channel_id=1, source_target_pairs={{0,2},{1,3},{2,0},{3,1},{4,6},{5,7},{6,4},{7,5},{8,10},{9,11},{10,... | collective-permute-start | bytes 884744 | tf_op jit(solution)/shard_map/ppermute | solution.py:480
  563.6 31.2 %collective-permute-start.75 = (bf16[1,1,1,1,1024,128]{5,4,3,2,1,0:T(8,128)(2,1)S(1)}, bf16[1,1,1,1,1024,128]{5,4,3,2,1,0:T(8,128)(2,1)S(1)}, u32[]{:S(2)}, u32[]{:S(2)}) collective-permute-start(bf16[1,1,1,1,1024,128]{5,4,3,2,1,0:T(8,128)(2,1)S(1)} %pad_maximum_fusion), channel_id=1, source_target_pairs={{0,16},{4,20},{8,24},{12,28},{16,0},{20,4},{24,8},{28,12},{1,17},{... | collective-permute-start | bytes 786440 | tf_op jit(solution)/shard_map/ppermute | solution.py:482
  568.3 32.2 %collective-permute-start.61 = (bf16[1,1,1,1,576,128]{5,4,3,2,1,0:T(8,128)(2,1)}, bf16[1,1,1,1,576,128]{5,4,3,2,1,0:T(8,128)(2,1)S(1)}, u32[]{:S(2)}, u32[]{:S(2)}) collective-permute-start(bf16[1,1,1,1,576,128]{5,4,3,2,1,0:T(8,128)(2,1)} %pad_maximum_fusion.7), channel_id=1, source_target_pairs={{0,8},{4,12},{8,0},{12,4},{16,24},{20,28},{24,16},{28,20},{1,9},{5... | collective-permute-start | bytes 442376 | tf_op jit(solution)/shard_map/ppermute | solution.py:482
  571.2 29.4 %collective-permute-start.62 = (bf16[1,1,1,1,576,128]{5,4,3,2,1,0:T(8,128)(2,1)}, bf16[1,1,1,1,576,128]{5,4,3,2,1,0:T(8,128)(2,1)}, u32[]{:S(2)}, u32[]{:S(2)}) collective-permute-start(bf16[1,1,1,1,576,128]{5,4,3,2,1,0:T(8,128)(2,1)} %pad_maximum_fusion.8), channel_id=1, source_target_pairs={{0,24},{4,28},{8,16},{12,20},{16,8},{20,12},{24,0},{28,4},{1,25},{... | collective-permute-start | bytes 442376 | tf_op jit(solution)/shard_map/ppermute | solution.py:482
  575.0 25.6 %collective-permute-start.60 = (bf16[1,1,1,1,576,128]{5,4,3,2,1,0:T(8,128)(2,1)}, bf16[1,1,1,1,576,128]{5,4,3,2,1,0:T(8,128)(2,1)}, u32[]{:S(2)}, u32[]{:S(2)}) collective-permute-start(bf16[1,1,1,1,576,128]{5,4,3,2,1,0:T(8,128)(2,1)} %pad_maximum_fusion.6), channel_id=1, source_target_pairs={{0,16},{4,20},{8,24},{12,28},{16,0},{20,4},{24,8},{28,12},{1,17},{... | collective-permute-start | bytes 442376 | tf_op jit(solution)/shard_map/ppermute | solution.py:482
  606.7 14.4 %all-to-all-start.17 = ((f32[32,16,128]{2,1,0:T(8,128)}), f32[32,16,128]{2,1,0:T(8,128)S(1)}, u32[]{:S(2)}, u32[]{:S(2)}) async-start(f32[32,16,128]{2,1,0:T(8,128)} %get-tuple-element.400), calls=%async_computation.17 | async-start | bytes 524288 | tf_op jit(solution)/shard_map/all_to_all | solution.py:1353
  (101 other events, 964.3 us)
